TPU v7x, 256 devices: a whole 4x4x8 slice. The times are simulated.
256 devices in a mesh: space: 64 (over z, y, core), mp: 4 (over x).
Axes of the slice: x: 4, y: 4, z: 8, core: 2. Of those that a mesh axis runs over, the one named last changes fastest.
Arguments:
- activations: bfloat16 [16384, 1024], P('space'), may hold values from -30 to 30
- w_query: bfloat16 [1024, 1024], P(None, 'mp'), may hold values from -1 to 1
- w_key: bfloat16 [1024, 1024], P(None, 'mp'), may hold values from -1 to 1
- w_value: bfloat16 [1024, 1024], P(None, 'mp'), may hold values from -0.1875 to 0.1875
- w_out: bfloat16 [1024, 1024], P('mp'), may hold values from -0.1875 to 0.1875
- grad_output: bfloat16 [16384, 1024], P('space', 'mp'), may hold values from -6 to 6
- neighbours: int32 [256, 9], P('space'), may hold values from 0 to 255, as said below
- pad_mask: int32 [256, 9], P('space'), may hold values from 0 to 1, as said below
Outputs:
- output: bfloat16 [16384, 1024], P('space', 'mp')
- grad_input: bfloat16 [16384, 1024], P('space', 'mp')
- weight_grads: float32 [4, 1024, 1024], P(None, 'space', 'mp')
Inputs may be any that keep to these rules, and one draw needn't show every extreme that they name: `neighbours`: patch r * 4 + c is column c of row r of patches, and row r lies on index r of space; every slot names a patch of row r - 1, r or r + 1; slot 4 names the patch itself; slots that would leave the band name the patch itself. `pad_mask`: slot 4 is always live; slots that leave the band are 0.
All inputs are finite; a program needn't handle non-finite values.
Results may differ from a plain program's by a relative error of at most 0.019.
Values may be sent and summed in bfloat16 or wider, within the bound.
No kernel may reach another device: no remote copies, remote signals or barrier semaphores. Data moves between devices by JAX's collectives and lax.ppermute only.
A program may use at most 64 MiB of HBM per device.

v0:
```python
import jax
import jax.numpy as jnp
from jax import lax
from jax.sharding import PartitionSpec as P

HD = 64
PATCH = 64
NB = 9


masked_score = -1e30


def from_behind(value, axis, steps):
    count = lax.axis_size(axis)
    initial, last = (max(0, -steps), min(count, count - steps))
    return lax.ppermute(value, axis, [(source, source + steps) for source in range(initial, last)])


def attend(queries, key_tiles, value_tiles, keep_mask, grad_attended):
    count, slots, patch_len, head_count, head_dim = key_tiles.shape
    key_flat = key_tiles.reshape(count, slots * patch_len, head_count, head_dim)
    value_flat = value_tiles.reshape(count, slots * patch_len, head_count, head_dim)
    factor = head_dim ** (-0.5)
    scores = (
        jnp.einsum("rihe,rjhe->rhij", queries, key_flat, preferred_element_type=jnp.float32)
        * factor
    )
    visible = jnp.repeat(keep_mask, patch_len, axis=1) > 0
    scores = jnp.where(visible[:, None, None, :], scores, masked_score)
    peak_score = jnp.max(scores, axis=-1, keepdims=True)
    weights = jnp.exp(scores - peak_score)
    probs = weights / jnp.sum(weights, axis=-1, keepdims=True)
    probs_low = probs.astype(jnp.bfloat16)
    attended = jnp.einsum(
        "rhij,rjhe->rihe", probs_low, value_flat, preferred_element_type=jnp.float32
    ).astype(jnp.bfloat16)
    grad_probs = jnp.einsum(
        "rihe,rjhe->rhij", grad_attended, value_flat, preferred_element_type=jnp.float32
    )
    grad_values = jnp.einsum(
        "rhij,rihe->rjhe", probs_low, grad_attended, preferred_element_type=jnp.float32
    )
    centre = jnp.sum(probs * grad_probs, axis=-1, keepdims=True)
    grad_scores = (probs * (grad_probs - centre) * factor).astype(jnp.bfloat16)
    grad_queries = jnp.einsum(
        "rhij,rjhe->rihe", grad_scores, key_flat, preferred_element_type=jnp.float32
    )
    grad_keys = jnp.einsum(
        "rhij,rihe->rjhe", grad_scores, queries, preferred_element_type=jnp.float32
    )
    return (
        attended,
        grad_queries,
        grad_keys.reshape(key_tiles.shape),
        grad_values.reshape(key_tiles.shape),
    )


def body(activations, w_query, w_key, w_value, w_out, grad_output, neighbours, pad_mask):
    head_width = w_query.shape[1]
    cycle_size = neighbours.shape[0]
    cell_count = activations.shape[0]
    head_count = head_width // HD
    query = jnp.dot(activations, w_query, preferred_element_type=jnp.float32).astype(jnp.bfloat16)
    key_part = jnp.dot(activations, w_key, preferred_element_type=jnp.float32).astype(jnp.bfloat16)
    value_part = jnp.dot(activations, w_value, preferred_element_type=jnp.float32).astype(
        jnp.bfloat16
    )
    own_pairs = jnp.stack([key_part, value_part])
    lower_pairs = from_behind(own_pairs, "space", 1)
    upper_pairs = from_behind(own_pairs, "space", -1)
    pair_table = jnp.concatenate([lower_pairs, own_pairs, upper_pairs], axis=1)
    pair_table = pair_table.reshape(2, 3 * cycle_size, PATCH, head_count, HD)
    first_patch = (lax.axis_index("space") - 1) * cycle_size
    local_slot = neighbours - first_patch
    key_tiles = pair_table[0][local_slot]
    value_tiles = pair_table[1][local_slot]
    cotangent = lax.all_gather(grad_output, "mp", axis=1, tiled=True)
    grad_attended = jnp.einsum(
        "cd,fd->cf", cotangent, w_out, preferred_element_type=jnp.float32
    ).astype(jnp.bfloat16)
    attended, grad_queries, grad_keys, grad_values = attend(
        query.reshape(cycle_size, PATCH, head_count, HD),
        key_tiles,
        value_tiles,
        pad_mask,
        grad_attended.reshape(cycle_size, PATCH, head_count, HD),
    )
    attended = attended.reshape(cell_count, head_width)
    grad_query = grad_queries.reshape(cell_count, head_width).astype(jnp.bfloat16)
    grad_tiles = jnp.stack([grad_keys, grad_values]).reshape(2, cycle_size * NB, PATCH * head_width)
    slot_sums = jnp.zeros((2, 3 * cycle_size, PATCH * head_width), jnp.float32)
    slot_sums = slot_sums.at[:, local_slot.reshape(-1)].add(grad_tiles)
    from_upper = from_behind(slot_sums[:, :cycle_size].astype(jnp.bfloat16), "space", -1).astype(
        jnp.float32
    )
    from_lower = from_behind(
        slot_sums[:, 2 * cycle_size :].astype(jnp.bfloat16), "space", 1
    ).astype(jnp.float32)
    totals = slot_sums[:, cycle_size : 2 * cycle_size] + from_upper + from_lower
    totals = totals.reshape(2, cell_count, head_width).astype(jnp.bfloat16)
    grad_key = totals[0]
    grad_value = totals[1]
    partial_out = jnp.dot(attended, w_out, preferred_element_type=jnp.float32)
    output = lax.psum_scatter(
        partial_out.astype(jnp.bfloat16), "mp", scatter_dimension=1, tiled=True
    )
    input_terms = (
        jnp.einsum("cf,df->cd", grad_query, w_query, preferred_element_type=jnp.float32)
        + jnp.einsum("cf,df->cd", grad_key, w_key, preferred_element_type=jnp.float32)
        + jnp.einsum("cf,df->cd", grad_value, w_value, preferred_element_type=jnp.float32)
    )
    grad_input = lax.psum_scatter(
        input_terms.astype(jnp.bfloat16), "mp", scatter_dimension=1, tiled=True
    )
    weight_terms = jnp.stack(
        [
            jnp.einsum("cd,cf->df", activations, grad_query, preferred_element_type=jnp.float32),
            jnp.einsum("cd,cf->df", activations, grad_key, preferred_element_type=jnp.float32),
            jnp.einsum("cd,cf->df", activations, grad_value, preferred_element_type=jnp.float32),
            jnp.einsum("cd,cf->df", cotangent, attended, preferred_element_type=jnp.float32),
        ]
    )
    weight_grads = lax.psum_scatter(weight_terms, "space", scatter_dimension=1, tiled=True)
    return (output, grad_input, weight_grads)


def solution(mesh):
    in_specs = (
        P("space", None),
        P(None, "mp"),
        P(None, "mp"),
        P(None, "mp"),
        P("mp", None),
        P("space", "mp"),
        P("space", None),
        P("space", None),
    )
    out_specs = (P("space", "mp"), P("space", "mp"), P(None, "space", "mp"))
    return jax.shard_map(body, mesh=mesh, in_specs=in_specs, out_specs=out_specs, check_vma=False)
```

profile of v0, /device:TPU:6, one launch (start us, length us, event | category | flops | bytes accessed | tf_op | source)
XLA Modules:
  0.0 371.5 jit_solution(17144713774668368492)
XLA Ops:
  8.1 0.9 copy-done
  9.0 1.3 fusion.34
  10.4 1.3 fusion.35
  11.8 1.3 collective-permute-start.1
  13.1 3.0 collective-permute-start
  16.3 0.3 convolution_convert_fusion.3
  16.6 13.3 %all_gather.3 = bf16[256,1024]{1,0:T(8,128)(2,1)S(1)} all-gather(bf16[256,256]{1,0:T(8,128)(2,1)S(1)} %copy-done.15), channel_id=1, replica_groups=mesh['space'=64,'mp'=4] {'mp'}, dimensions={1}, use_global_device_ids=true | all-gather | bytes 655360 | tf_op jit(solution)/shard_map/all_gather | solution.py:79
  29.9 0.8 copy-done.2
  30.7 0.3 convolution_convert_fusion.2
  31.2 0.1 gt.13
  31.3 0.2 reshape.82
  31.5 0.9 copy.60
  32.3 0.2 reshape.85
  32.5 0.2 copy.62
  32.9 0.3 squeeze.13
  33.2 0.2 copy.50
  33.4 0.3 squeeze.12
  33.7 0.2 copy.48
  33.9 2.5 gather_fusion
  36.4 4.5 %copy.49 = bf16[36,64,4,64]{1,0,3,2:T(8,128)(2,1)} copy(bf16[36,64,4,64]{3,1,2,0:T(8,128)(2,1)} %gather_fusion) | data formatting | bytes 2359296 | tf_op jit(solution)/shard_map/gather | solution.py:78
  40.9 4.8 %reshape.81 = bf16[4,576,4,64]{1,0,3,2:T(4,128)(2,1)} reshape(bf16[36,64,4,64]{1,0,3,2:T(8,128)(2,1)} %copy.49) | data formatting | bytes 2359296 | tf_op jit(solution)/shard_map/reshape | solution.py:23
  45.7 2.4 gather_fusion.1
  48.1 3.3 copy.51
  51.4 2.4 reshape.83
  53.8 3.5 fusion.28
  57.3 3.6 fusion.55
  60.9 3.1 fusion.24
  64.0 10.4 %fusion.25 = bf16[4,64,4,64]{1,3,2,0:T(8,128)(2,1)} fusion(f32[4,4,64,576]{3,2,1,0:T(8,128)} %fusion.28, bf16[4,576,4,64]{1,0,3,2:T(4,128)(2,1)S(1)} %copy-done.11, f32[4,4,64,576]{3,2,1,0:T(8,128)} %get-tuple-element.24, f32[4,4,64]{2,1,0:T(4,128)S(1)} %get-tuple-element.23), kind=kOutput, calls=%fused_computation.34 | convolution fusion | flops 79693376 | bytes 6033408 | tf_op jit(solution)/shard_map/rhij,rjhe->rihe/dot_general | solution.py:46
  74.4 11.2 %fusion.12 = f32[4,576,4,64]{1,3,2,0:T(8,128)} fusion(bf16[4,64,4,64]{1,3,2,0:T(8,128)(2,1)S(1)} %copy-done.14, f32[4,4,64,576]{3,2,1,0:T(8,128)} %fusion.28, f32[4,4,64,576]{3,2,1,0:T(8,128)} %get-tuple-element.24, f32[4,4,64]{2,1,0:T(4,128)S(1)} %get-tuple-element.23), kind=kOutput, calls=%fused_computation.15 | convolution fusion | flops 79627840 | bytes 7213056 | tf_op jit(solution)/shard_map/rhij,rihe->rjhe/dot_general | solution.py:49
  85.6 2.3 convolution_bitcast_fusion
  87.9 1.1 copy.55
  89.1 0.2 reshape.84
  89.3 1.8 copy.59
  91.1 1.2 convert_element_type.62
  92.3 3.3 copy.63
  95.6 5.1 %stack.35 = f32[1,36,16384]{2,1,0:T(8,128)S(1)} reshape(f32[4,576,4,64]{3,2,1,0:T(4,128)} %copy.63) | data formatting | bytes 4718592 | tf_op jit(solution)/shard_map/stack | solution.py:92
  100.7 5.0 %copy.61 = f32[4,576,4,64]{3,2,1,0:T(4,128)} copy(f32[4,576,4,64]{1,3,2,0:T(8,128)} %fusion.12) | data formatting | bytes 4718592 | tf_op jit(solution)/shard_map/rhij,rihe->rjhe/transpose | solution.py:49
  105.7 5.9 %stack.34 = f32[1,36,16384]{2,1,0:T(8,128)} reshape(f32[4,576,4,64]{3,2,1,0:T(4,128)} %copy.61) | data formatting | bytes 4718592 | tf_op jit(solution)/shard_map/stack | solution.py:92
  111.6 2.1 maximum_bitcast_fusion
  113.7 5.8 %copy.64 = f32[36,2,16384]{2,1,0:T(2,128)} copy(f32[36,2,16384]{2,0,1:T(8,128)S(1)} %maximum_bitcast_fusion) | data formatting | bytes 9437184 | tf_op jit(solution)/shard_map/stack | solution.py:92
  119.5 0.5 broadcast_in_dim.31
  120.1 18.5 %scatter_fusion = f32[2,12,16384]{2,0,1:T(2,128)S(1)} fusion(f32[2,12,16384]{2,0,1:T(2,128)S(1)} %broadcast_in_dim.31, s32[36]{0:T(128)S(1)} %fusion.44, f32[36,2,16384]{2,1,0:T(2,128)} %copy.64), kind=kCustom, calls=%fused_computation.2 | custom fusion | flops 1179648 | bytes 14155920 | tf_op jit(solution)/shard_map/scatter-add | solution.py:94
  138.5 0.6 convert.4
  139.2 0.4 fusion.53
  139.6 1.3 collective-permute-start.2
  140.9 3.3 collective-permute-start.3
  144.2 0.3 convolution_bitcast_fusion.1
  144.5 1.3 convolution_bitcast_fusion.4
  145.8 0.4 fusion.39
  146.2 1.2 slice_reduce_fusion
  147.5 0.3 convolution_bitcast_fusion.2
  147.8 0.3 convolution_bitcast_fusion.3
  148.2 2.3 pad_maximum_fusion
  150.5 5.2 %copy.65 = f32[4,1024,256]{2,0,1:T(4,128)} copy(f32[4,1024,256]{1,2,0:T(8,128)} %pad_maximum_fusion) | data formatting | bytes 8388608 | tf_op jit(solution)/shard_map/stack | solution.py:117
  155.8 0.9 copy-done.7
  156.8 1.1 convolution_convert_fusion
  158.0 0.3 fusion.58
  158.4 0.3 convolution_add_fusion.1
  158.7 0.2 copy-done.5
  158.9 1.2 fusion.20
  160.2 0.6 dynamic-slice
  161.4 201.2 %all-reduce.3.cloned.1.call-done = f32[4,1024,256]{2,0,1:T(4,128)} async-done(((f32[4,1024,256]{2,0,1:T(4,128)}), f32[4,1024,256]{2,0,1:T(4,128)}) %all-reduce.3.cloned.1.call-update) | async-done | bytes 4194320
  362.6 0.8 constant_dynamic-slice_fusion
  363.4 0.6 copy.66
  (58 shorter events, 0.8 us)
Async XLA Ops:
  8.0 1.0 copy-start
  8.0 8.1 %copy-start.16 = (s32[4,9]{1,0:T(4,128)S(1)}, s32[4,9]{1,0:T(4,128)}, u32[]{:S(2)}) copy-start(s32[4,9]{1,0:T(4,128)} %param.15) | copy-start | bytes 436
  8.0 8.1 %copy-start.17 = (s32[4,9]{1,0:T(4,128)S(1)}, s32[4,9]{1,0:T(4,128)}, u32[]{:S(2)}) copy-start(s32[4,9]{1,0:T(4,128)} %param.14) | copy-start | bytes 436
  8.0 8.2 %copy-start.8 = (bf16[1024,256]{1,0:T(8,128)(2,1)S(1)}, bf16[1024,256]{1,0:T(8,128)(2,1)}, u32[]{:S(2)}) copy-start(bf16[1024,256]{1,0:T(8,128)(2,1)} %param.9) | copy-start | bytes 1572868
  8.0 8.5 %copy-start.15 = (bf16[256,256]{1,0:T(8,128)(2,1)S(1)}, bf16[256,256]{1,0:T(8,128)(2,1)}, u32[]{:S(2)}) copy-start(bf16[256,256]{1,0:T(8,128)(2,1)} %param.13) | copy-start | bytes 393220
  8.1 22.6 %copy-start.6 = (bf16[256,1024]{1,0:T(8,128)(2,1)S(1)}, bf16[256,1024]{1,0:T(8,128)(2,1)}, u32[]{:S(2)}) copy-start(bf16[256,1024]{1,0:T(8,128)(2,1)} %param.12) | copy-start | bytes 1572868
  8.1 354.5 %all-reduce.3.cloned.1.call-start = ((), (), s32[]{:S(2)}) async-start(), calls=%async_computation.4 | async-start | bytes 8388608
  11.8 20.9 %collective-permute-start.1 = (bf16[2,256,256]{2,1,0:T(8,128)(2,1)S(1)}, bf16[2,256,256]{2,1,0:T(8,128)(2,1)S(1)}, u32[]{:S(2)}, u32[]{:S(2)}) collective-permute-start(bf16[2,256,256]{2,1,0:T(8,128)(2,1)S(1)} %pad_maximum_fusion.2), channel_id=1, source_target_pairs={{4,0},{8,4},{12,8},{16,12},{20,16},{24,20},{28,24},{32,28},{36,32}... | collective-permute-start | bytes 786440 | tf_op jit(solution)/shard_map/ppermute | solution.py:17
  13.1 19.7 %collective-permute-start = (bf16[2,256,256]{2,1,0:T(8,128)(2,1)S(1)}, bf16[2,256,256]{2,1,0:T(8,128)(2,1)S(1)}, u32[]{:S(2)}, u32[]{:S(2)}) collective-permute-start(bf16[2,256,256]{2,1,0:T(8,128)(2,1)S(1)} %pad_maximum_fusion.2), channel_id=1, source_target_pairs={{0,4},{4,8},{8,12},{12,16},{16,20},{20,24},{24,28},{28,32},{32,36}... | collective-permute-start | bytes 786440 | tf_op jit(solution)/shard_map/ppermute | solution.py:17
  29.9 0.8 copy-start.2
  53.8 3.5 copy-start.11
  57.3 3.6 copy-start.1
  64.0 10.4 %copy-start.14 = (bf16[4,64,4,64]{1,3,2,0:T(8,128)(2,1)S(1)}, bf16[4,64,4,64]{1,3,2,0:T(8,128)(2,1)}, u32[]{:S(2)}) copy-start(bf16[4,64,4,64]{1,3,2,0:T(8,128)(2,1)} %copy.60) | copy-start | bytes 393220
  138.5 5.6 %copy-start.3 = (bf16[256,1024]{1,0:T(8,128)(2,1)S(1)}, bf16[256,1024]{1,0:T(8,128)(2,1)}, u32[]{:S(2)}) copy-start(bf16[256,1024]{1,0:T(8,128)(2,1)} %copy-done.2) | copy-start | bytes 1572868
  139.6 6.2 %collective-permute-start.2 = (bf16[2,4,16384]{2,0,1:T(2,128)(2,1)S(1)}, bf16[2,4,16384]{2,0,1:T(2,128)(2,1)S(1)}, u32[]{:S(2)}, u32[]{:S(2)}) collective-permute-start(bf16[2,4,16384]{2,0,1:T(2,128)(2,1)S(1)} %get-tuple-element.19), channel_id=1, source_target_pairs={{4,0},{8,4},{12,8},{16,12},{20,16},{24,20},{28,24},{32,28},{36,32}... | collective-permute-start | bytes 786440 | tf_op jit(solution)/shard_map/ppermute | solution.py:17
  140.9 4.9 %collective-permute-start.3 = (bf16[2,4,16384]{2,0,1:T(2,128)(2,1)S(1)}, bf16[2,4,16384]{2,0,1:T(2,128)(2,1)S(1)}, u32[]{:S(2)}, u32[]{:S(2)}) collective-permute-start(bf16[2,4,16384]{2,0,1:T(2,128)(2,1)S(1)} %get-tuple-element.20), channel_id=1, source_target_pairs={{0,4},{4,8},{8,12},{12,16},{16,20},{20,24},{24,28},{28,32},{32,36}... | collective-permute-start | bytes 786440 | tf_op jit(solution)/shard_map/ppermute | solution.py:17
  146.2 2.0 copy-start.4
  147.5 3.0 copy-start.12
  155.7 1.0 copy-start.7
  155.7 2.3 copy-start.9
  155.8 2.6 copy-start.10
  155.8 2.6 copy-start.13
  155.8 208.3 %reduce-scatter.3.cloned.1.call-start = ((), (), s32[]{:S(2)}) async-start(), calls=%async_computation.2 | async-start | bytes 655360 | tf_op jit(solution)/shard_map/reduce_scatter | solution.py:106
  157.9 1.0 copy-start.5
  157.9 206.2 %reduce-scatter.5.cloned.1.call-start = ((), (), s32[]{:S(2)}) async-start(), calls=%async_computation.3 | async-start | bytes 655360 | tf_op jit(solution)/shard_map/reduce_scatter | solution.py:114
  158.4 1.8 copy-start.18
Sparse Core Ops, SparseCore 0:
  155.9 206.6 all-reduce.2
Sparse Core Ops, SparseCore 1:
  159.3 32.6 reduce-scatter.2
  195.0 23.8 reduce-scatter.4
where the time goes:
time: 373 us; the launch traced here: 372 us
  waiting for transfers between devices  201 us (54%)
  local copies, waits for them, and re-layouts  64.6 us (17%)
  matrix products  42.7 us (11%)
  other arithmetic  24 us (6%)
  between operations  16.6 us (4%)
  blocking collectives  13.3 us (4%)
  starting transfers between devices  9.06 us (2%)
    unnamed x4, waiting for transfers between devices  201 us
    scatter-add x1, other arithmetic, body(): slot_sums = slot_sums.at[:, local_slot.reshape(-1)].add(grad_tiles)  18.5 us
    another operation x3, local copies, waits for them, and re-layouts, body(): jnp.stack([grad_keys, grad_values])  16.8 us
    all_gather x1, blocking collectives, body(): cotangent = lax.all_gather(grad_output, 'mp', axis=1, tiled=True)  13.3 us
    dot_general x1, matrix products, attend(): jnp.einsum('rhij,rihe->rjhe', grad_scores, queries, preferred_element_typ...  11.2 us
    dot_general x1, matrix products, attend(): jnp.einsum('rhij,rjhe->rihe', grad_scores, key_flat, preferred_element_ty...  10.4 us
    ppermute x4, starting transfers between devices, from_behind(): lax.ppermute(value, axis, [(source, source + steps) for source in range(i...  8.94 us
  transfers between devices with their start and end apart: 7, of which 1 were waited for; matrix products, arithmetic and copies ran while one was open for 2% of the time, Pallas kernels for 0%

commit v1 on v0

v1 whole, which is shorter than its diff:
```python
import jax
import jax.numpy as jnp
from jax import lax
from jax.experimental import pallas as pl
from jax.experimental.pallas import tpu as pltpu
from jax.sharding import Mesh
from jax.sharding import PartitionSpec as P

HD = 64
PATCH = 64
D = 1024
ROW = 256
WIDTH = 256
HEADS = WIDTH // HD
KEYS = 3 * ROW
LOG2E = 1.4426950408889634
BF = jnp.bfloat16
F32 = jnp.float32
VMEM_BYTES = 56 * 1024 * 1024

NN = (((1,), (0,)), ((), ()))
NT = (((1,), (1,)), ((), ()))


def mm(a, b, dims=NN):
    return lax.dot_general(a, b, dims, preferred_element_type=F32)


def attention_kernel(
    pos, bias, a_lo, a_own, a_hi, wq, wk, wv, wo, c0, c1, c2, c3,
    att_out, gq_out, lo_out, own_out, hi_out, send_out, keep_out,
    key_s, value_s, dw_s,
):
    core, y, z, x = pos[0], pos[1], pos[2], pos[3]
    query = mm(a_own[...], wq[...]).astype(BF)
    for band, block in enumerate((a_lo, a_own, a_hi)):
        rows = slice(band * ROW, (band + 1) * ROW)
        key_s[rows, :] = mm(block[...], wk[...]).astype(BF)
        value_s[rows, :] = mm(block[...], wv[...]).astype(BF)
    cots = (c0, c1, c2, c3)
    grad_att = jnp.zeros((ROW, WIDTH), F32)
    for step in range(4):
        cols = pl.ds(pl.multiple_of(lax.rem(x + 4 - step, 4) * WIDTH, WIDTH), WIDTH)
        grad_att += mm(cots[step][...], wo[:, cols], NT)
    grad_att = grad_att.astype(BF)

    keys = key_s[...]
    values = value_s[...]
    keys_t = keys.T
    values_t = values.T
    lane_head = lax.broadcasted_iota(jnp.int32, (ROW, WIDTH), 1) // HD
    bias_rows = jnp.concatenate(
        [jnp.broadcast_to(bias[patch : patch + 1, :], (PATCH, ROW)) for patch in range(KEYS // PATCH)],
        axis=0,
    )
    grad_key = jnp.zeros((KEYS, WIDTH), F32)
    grad_value = jnp.zeros((KEYS, WIDTH), F32)
    att_rows, gq_rows = [], []
    for head in range(HEADS):
        feats = slice(head * HD, (head + 1) * HD)
        q_head = jnp.where(lane_head == head, query, jnp.zeros_like(query))
        g_head = jnp.where(lane_head == head, grad_att, jnp.zeros_like(grad_att))
        scores = mm(keys, q_head, NT) * (LOG2E * HD**-0.5) + bias_rows
        peak = jnp.max(scores, axis=0, keepdims=True)
        weights = jnp.exp2(scores - peak)
        probs = weights * (1.0 / jnp.sum(weights, axis=0, keepdims=True))
        probs_low = probs.astype(BF)
        grad_probs = mm(values, g_head, NT)
        centre = jnp.sum(probs * grad_probs, axis=0, keepdims=True)
        grad_scores = (probs * (grad_probs - centre) * HD**-0.5).astype(BF)
        att_rows.append(mm(values_t[feats, :], probs_low))
        gq_rows.append(mm(keys_t[feats, :], grad_scores))
        grad_key += mm(grad_scores, q_head)
        grad_value += mm(probs_low, g_head)
    att = jnp.concatenate(att_rows, axis=0).astype(BF).T
    gq = jnp.concatenate(gq_rows, axis=0).astype(BF).T
    att_out[...] = att
    gq_out[...] = gq
    lo_out[0], lo_out[1] = grad_key[:ROW].astype(BF), grad_value[:ROW].astype(BF)
    own_out[0], own_out[1] = grad_key[ROW : 2 * ROW], grad_value[ROW : 2 * ROW]
    hi_out[0], hi_out[1] = grad_key[2 * ROW :].astype(BF), grad_value[2 * ROW :].astype(BF)

    grad_key = grad_key.astype(BF)
    grad_value = grad_value.astype(BF)
    act_t = jnp.concatenate([a_lo[...], a_own[...], a_hi[...]], axis=0).T
    dw_s[0] = mm(act_t[:, ROW : 2 * ROW], gq)
    dw_s[1] = mm(act_t, grad_key)
    dw_s[2] = mm(act_t, grad_value)
    for step in range(4):
        rows = pl.ds(pl.multiple_of(lax.rem(x + 4 - step, 4) * WIDTH, WIDTH), WIDTH)
        dw_s[3, rows, :] = mm(cots[step][...].T, att)
    for mine, out in ((0, send_out), (1, keep_out)):
        c = core if mine else 1 - core
        for ys in range(4):
            yy = lax.rem(y + ys, 4)
            for low in range(2):
                for hs in range(4):
                    zl = lax.rem(z, 2)
                    zl = zl if low else 1 - zl
                    zz = 2 * lax.rem(z // 2 + hs, 4) + zl
                    row = pl.multiple_of(((zz * 4 + yy) * 2 + c) * 16, 16)
                    out[ys, low, hs] = dw_s[:, pl.ds(row, 16), :].astype(BF)


def input_kernel(pos, att, gq, own, from_lo, from_hi, wq, wk, wv, wo, p0, p1, p2, p3):
    x = pos[3]
    total = own[...] + from_lo[...].astype(F32) + from_hi[...].astype(F32)
    grad_key = total[0].astype(BF)
    grad_value = total[1].astype(BF)
    for step, out in enumerate((p0, p1, p2, p3)):
        block = pl.ds(pl.multiple_of(lax.rem(x + step, 4) * WIDTH, WIDTH), WIDTH)
        out[0] = mm(att[...], wo[:, block]).astype(out.dtype)
        out[1] = (
            mm(gq[...], wq[block, :], NT)
            + mm(grad_key, wk[block, :], NT)
            + mm(grad_value, wv[block, :], NT)
        ).astype(out.dtype)


def vmem(count):
    return [pl.BlockSpec(memory_space=pltpu.VMEM)] * count


def smem():
    return [pl.BlockSpec(memory_space=pltpu.SMEM)]


def shift(value, axis, steps):
    count = lax.axis_size(axis)
    return lax.ppermute(value, axis, [(i, (i + steps) % count) for i in range(count)])


def shift_open(value, axis, steps):
    count = lax.axis_size(axis)
    return lax.ppermute(
        value, axis, [(i, i + steps) for i in range(count) if 0 <= i + steps < count]
    )


def swap(value, axis):
    count = lax.axis_size(axis)
    return lax.ppermute(value, axis, [(i, i ^ 1) for i in range(count)])


def body(activations, w_query, w_key, w_value, w_out, grad_output, neighbours, pad_mask):
    space = ("z", "y", "core")
    act_lo = shift_open(activations, space, 1)
    act_hi = shift_open(activations, space, -1)
    cots = [grad_output] + [shift(grad_output, "mp", s) for s in (1, 2, 3)]
    pos = jnp.stack([lax.axis_index(a) for a in ("core", "y", "z", "mp")]).astype(jnp.int32)

    local = neighbours - (lax.axis_index(space) - 1) * 4
    table = lax.broadcasted_iota(jnp.int32, (16, 4, 9), 0)
    live = jnp.where((local[None] == table) & (pad_mask[None] > 0), 1.0, 0.0)
    count = jnp.sum(live, axis=-1)
    bias = jnp.where(count > 0, jnp.log2(jnp.maximum(count, 1.0)), -1e30)
    bias = jnp.repeat(bias, PATCH, axis=1)

    half = (4, 2, 4, 4, 16, WIDTH)
    att, gq, lo, own, hi, dw_send, dw_keep = pl.pallas_call(
        attention_kernel,
        out_shape=(
            jax.ShapeDtypeStruct((ROW, WIDTH), BF),
            jax.ShapeDtypeStruct((ROW, WIDTH), BF),
            jax.ShapeDtypeStruct((2, ROW, WIDTH), BF),
            jax.ShapeDtypeStruct((2, ROW, WIDTH), F32),
            jax.ShapeDtypeStruct((2, ROW, WIDTH), BF),
            jax.ShapeDtypeStruct(half, BF),
            jax.ShapeDtypeStruct(half, BF),
        ),
        in_specs=smem() + vmem(12),
        out_specs=tuple(vmem(7)),
        scratch_shapes=[
            pltpu.VMEM((KEYS, WIDTH), BF),
            pltpu.VMEM((KEYS, WIDTH), BF),
            pltpu.VMEM((4, D, WIDTH), F32),
        ],
        compiler_params=pltpu.CompilerParams(vmem_limit_bytes=VMEM_BYTES),
        cost_estimate=pl.CostEstimate(flops=4_000_000_000, bytes_accessed=8_000_000, transcendentals=800_000),
        name="attention",
    )(pos, bias, act_lo, activations, act_hi, w_query, w_key, w_value, w_out, *cots)

    def add(*terms):
        return sum(t.astype(F32) for t in terms)

    dw = add(dw_keep, swap(dw_send, "core")).astype(BF)
    from_lo = shift_open(hi, space, 1)
    from_hi = shift_open(lo, space, -1)
    dw = add(dw[0], *[shift(dw[s], "y", s) for s in (1, 2, 3)]).astype(BF)

    piece = (2, ROW, WIDTH)
    pieces = pl.pallas_call(
        input_kernel,
        out_shape=(jax.ShapeDtypeStruct(piece, F32),) + (jax.ShapeDtypeStruct(piece, BF),) * 3,
        in_specs=smem() + vmem(9),
        out_specs=tuple(vmem(4)),
        compiler_params=pltpu.CompilerParams(vmem_limit_bytes=VMEM_BYTES),
        cost_estimate=pl.CostEstimate(flops=540_000_000, bytes_accessed=4_000_000, transcendentals=0),
        name="input_grad",
    )(pos, att, gq, own, from_lo, from_hi, w_query, w_key, w_value, w_out)
    outs = add(pieces[0], *[shift(pieces[s], "mp", s) for s in (1, 2, 3)]).astype(BF)

    dw = add(dw[1], swap(dw[0], "z")).astype(BF)
    z_count = lax.axis_size("z")
    dw = add(
        dw[0],
        *[
            lax.ppermute(dw[s], "z", [(i, (i + 2 * s) % z_count) for i in range(z_count)])
            for s in (1, 2, 3)
        ],
    )
    return outs[0], outs[1], dw


def solution(mesh):
    fine = Mesh(mesh.devices.reshape(8, 4, 2, 4), ("z", "y", "core", "mp"))
    space = ("z", "y", "core")
    in_specs = (
        P(space, None),
        P(None, "mp"),
        P(None, "mp"),
        P(None, "mp"),
        P("mp", None),
        P(space, "mp"),
        P(space, None),
        P(space, None),
    )
    out_specs = (P(space, "mp"), P(space, "mp"), P(None, space, "mp"))
    return jax.shard_map(body, mesh=fine, in_specs=in_specs, out_specs=out_specs, check_vma=False)
```

time: 373 us -> 82.3 us (0.22)
  the two profiles are of different devices: /device:TPU:6 before, /device:TPU:16 now
where the time goes in v1:
time: 82.3 us; the launch traced here: 82 us
  starting transfers between devices  42.8 us (52%)
  waiting for transfers between devices  16.5 us (20%)
  Pallas kernels  13.8 us (17%)
  other arithmetic  4.57 us (6%)
  local copies, waits for them, and re-layouts  3.5 us (4%)
    ppermute x9, starting transfers between devices, shift(): lax.ppermute(value, axis, [(i, (i + steps) % count) for i in range(count)])  15.5 us
    ppermute x3, starting transfers between devices, body(): lax.ppermute(dw[s], 'z', [(i, (i + 2 * s) % z_count) for i in range(z_cou...  12.5 us
    ppermute x4, starting transfers between devices, shift_open(): lax.ppermute(value, axis, [(i, i + steps) for i in range(count) if 0 <= i...  11.1 us
    ppermute x9, waiting for transfers between devices, shift(): lax.ppermute(value, axis, [(i, (i + steps) % count) for i in range(count)])  10.6 us
    pallas_call x1, Pallas kernels, body(): pl.pallas_call(attention_kernel, out_shape=(jax.ShapeDtypeStruct((ROW, WI...  10.3 us
    ppermute x4, waiting for transfers between devices, shift_open(): lax.ppermute(value, axis, [(i, i + steps) for i in range(count) if 0 <= i...  3.82 us
    ppermute x2, starting transfers between devices, swap(): return lax.ppermute(value, axis, [(i, i ^ 1) for i in range(count)])  3.65 us
    pallas_call x1, Pallas kernels, body(): pl.pallas_call(input_kernel, out_shape=(jax.ShapeDtypeStruct(piece, F32),...  3.51 us
  transfers between devices with their start and end apart: 18, of which 7 were waited for; matrix products, arithmetic and copies ran while one was open for 7% of the time, Pallas kernels for 4%

profile of v1, /device:TPU:16, one launch (start us, length us, event | category | flops | bytes accessed | tf_op | source)
XLA Modules:
  0.0 82.0 jit_solution(3051747481408902833)
XLA Ops:
  0.6 3.1 %collective-permute-start.3 = (bf16[256,256]{1,0:T(8,128)(2,1)}, bf16[256,256]{1,0:T(8,128)(2,1)S(1)}, u32[]{:S(2)}, u32[]{:S(2)}) collective-permute-start(bf16[256,256]{1,0:T(8,128)(2,1)} %c0.1), channel_id=1, source_target_pairs={{0,2},{1,3},{2,0},{3,1},{4,6},{5,7},{6,4},{7,5},{8,10},{9,11},{10,... | collective-permute-start | bytes 393224 | tf_op jit(solution)/shard_map/ppermute | solution.py:130
  3.7 0.6 collective-permute-start.2
  4.3 2.6 %collective-permute-start.4 = (bf16[256,256]{1,0:T(8,128)(2,1)}, bf16[256,256]{1,0:T(8,128)(2,1)S(1)}, u32[]{:S(2)}, u32[]{:S(2)}) collective-permute-start(bf16[256,256]{1,0:T(8,128)(2,1)} %c0.1), channel_id=1, source_target_pairs={{0,3},{1,0},{2,1},{3,2},{4,7},{5,4},{6,5},{7,6},{8,11},{9,8},{10,9... | collective-permute-start | bytes 393224 | tf_op jit(solution)/shard_map/ppermute | solution.py:130
  7.0 1.9 %collective-permute-start = (bf16[256,1024]{1,0:T(8,128)(2,1)}, bf16[256,1024]{1,0:T(8,128)(2,1)S(1)}, u32[]{:S(2)}, u32[]{:S(2)}) collective-permute-start(bf16[256,1024]{1,0:T(8,128)(2,1)} %a_own.1), channel_id=1, source_target_pairs={{0,4},{4,8},{8,12},{12,16},{16,20},{20,24},{24,28},{28,32},{32,36}... | collective-permute-start | bytes 1572872 | tf_op jit(solution)/shard_map/ppermute | solution.py:135
  8.9 3.6 %collective-permute-start.1 = (bf16[256,1024]{1,0:T(8,128)(2,1)}, bf16[256,1024]{1,0:T(8,128)(2,1)S(1)}, u32[]{:S(2)}, u32[]{:S(2)}) collective-permute-start(bf16[256,1024]{1,0:T(8,128)(2,1)} %a_own.1), channel_id=1, source_target_pairs={{4,0},{8,4},{12,8},{16,12},{20,16},{24,20},{28,24},{32,28},{36,32}... | collective-permute-start | bytes 1572872 | tf_op jit(solution)/shard_map/ppermute | solution.py:135
  12.6 0.7 broadcast_subtract_fusion
  13.2 0.7 broadcast_compare_fusion
  13.9 0.1 copy.12
  14.0 0.1 copy.11
  14.1 0.1 select_reduce_fusion
  14.3 0.1 copy.13
  14.3 0.1 broadcast_in_dim.20
  14.4 0.7 reshape.18.bias
  15.1 0.6 pad_add_fusion.pos
  15.7 0.0 collective-permute-done.3.c2
  15.7 0.0 collective-permute-done.2.c1
  15.7 0.0 copy-start.6
  15.7 0.0 collective-permute-done.4.c3
  15.7 0.0 copy-start.7
  15.7 2.0 %collective-permute-done.a_lo = bf16[256,1024]{1,0:T(8,128)(2,1)S(1)} collective-permute-done((bf16[256,1024]{1,0:T(8,128)(2,1)}, bf16[256,1024]{1,0:T(8,128)(2,1)S(1)}, u32[]{:S(2)}, u32[]{:S(2)}) %collective-permute-start) | collective-permute-done | bytes 524320 | tf_op jit(solution)/shard_map/ppermute | solution.py:135
  17.7 1.9 %collective-permute-done.1.a_hi = bf16[256,1024]{1,0:T(8,128)(2,1)S(1)} collective-permute-done((bf16[256,1024]{1,0:T(8,128)(2,1)}, bf16[256,1024]{1,0:T(8,128)(2,1)S(1)}, u32[]{:S(2)}, u32[]{:S(2)}) %collective-permute-start.1) | collective-permute-done | bytes 524320 | tf_op jit(solution)/shard_map/ppermute | solution.py:135
  19.5 0.0 copy-done.5
  19.5 0.0 copy-done.6
  19.5 0.0 copy-done.7
  19.6 0.0 copy-done.3
  19.6 0.0 copy-start.4
  19.6 0.8 copy-done.4
  20.4 10.3 %attention.1 = (bf16[256,256]{1,0:T(8,128)(2,1)}, bf16[256,256]{1,0:T(8,128)(2,1)}, bf16[2,256,256]{2,1,0:T(8,128)(2,1)}, f32[2,256,256]{2,1,0:T(8,128)}, bf16[2...) custom-call(s32[4]{0:T(128)} %pad_add_fusion.pos, ...), custom_call_target="tpu_custom_call" | custom-call | flops 4000000000 | bytes 8000000 | tf_op jit(solution)/shard_map/attention/pallas_call | solution.py:160
  30.6 1.5 %collective-permute-start.10 = (bf16[4,2,4,4,16,256]{5,4,3,2,1,0:T(8,128)(2,1)}, bf16[4,2,4,4,16,256]{5,4,3,2,1,0:T(8,128)(2,1)S(1)}, u32[]{:S(2)}, u32[]{:S(2)}) collective-permute-start(bf16[4,2,4,4,16,256]{5,4,3,2,1,0:T(8,128)(2,1)} %get-tuple-element.24), channel_id=1, source_target_pairs={{0,4},{4,0},{1,5},{5,1},{2,6},{6,2},{3,7},{7,3},{8,12},{12,8},{9,1... | collective-permute-start | bytes 3145736 | tf_op jit(solution)/shard_map/ppermute | solution.py:142
  32.1 1.9 %collective-permute-start.5 = (bf16[2,256,256]{2,1,0:T(8,128)(2,1)}, bf16[2,256,256]{2,1,0:T(8,128)(2,1)S(1)}, u32[]{:S(2)}, u32[]{:S(2)}) collective-permute-start(bf16[2,256,256]{2,1,0:T(8,128)(2,1)} %get-tuple-element.17), channel_id=1, source_target_pairs={{0,4},{4,8},{8,12},{12,16},{16,20},{20,24},{24,28},{28,32},{32,36}... | collective-permute-start | bytes 786440 | tf_op jit(solution)/shard_map/ppermute | solution.py:135
  34.0 3.6 %collective-permute-start.6 = (bf16[2,256,256]{2,1,0:T(8,128)(2,1)}, bf16[2,256,256]{2,1,0:T(8,128)(2,1)S(1)}, u32[]{:S(2)}, u32[]{:S(2)}) collective-permute-start(bf16[2,256,256]{2,1,0:T(8,128)(2,1)} %get-tuple-element.18), channel_id=1, source_target_pairs={{4,0},{8,4},{12,8},{16,12},{20,16},{24,20},{28,24},{32,28},{36,32}... | collective-permute-start | bytes 786440 | tf_op jit(solution)/shard_map/ppermute | solution.py:135
  37.6 0.0 collective-permute-done.10
  37.6 1.6 %add_convert_fusion = bf16[4,2,4,4,16,256]{5,4,3,2,1,0:T(8,128)(2,1)S(1)} fusion(bf16[4,2,4,4,16,256]{5,4,3,2,1,0:T(8,128)(2,1)S(1)} %collective-permute-done.10, bf16[4,2,4,4,16,256]{5,4,3,2,1,0:T(8,128)(2,1)} %get-tuple-element.23), kind=kLoop, calls=%fused_computation | loop fusion | flops 2097152 | bytes 3145728 | tf_op jit(solution)/shard_map/convert_element_type | solution.py:186
  39.3 0.1 slice_bitcast_fusion.2
  39.3 3.8 %collective-permute-start.11 = (bf16[2,4,4,16,256]{4,3,2,1,0:T(8,128)(2,1)S(1)}, bf16[2,4,4,16,256]{4,3,2,1,0:T(8,128)(2,1)S(1)}, u32[]{:S(2)}, u32[]{:S(2)}) collective-permute-start(bf16[2,4,4,16,256]{4,3,2,1,0:T(8,128)(2,1)S(1)} %get-tuple-element.25), channel_id=1, source_target_pairs={{0,8},{8,16},{16,24},{24,0},{1,9},{9,17},{17,25},{25,1},{2,10},{10... | collective-permute-start | bytes 786440 | tf_op jit(solution)/shard_map/ppermute | solution.py:130
  43.1 0.0 collective-permute-start.13
  43.1 2.2 %collective-permute-start.12 = (bf16[2,4,4,16,256]{4,3,2,1,0:T(8,128)(2,1)S(1)}, bf16[2,4,4,16,256]{4,3,2,1,0:T(8,128)(2,1)S(1)}, u32[]{:S(2)}, u32[]{:S(2)}) collective-permute-start(bf16[2,4,4,16,256]{4,3,2,1,0:T(8,128)(2,1)S(1)} %get-tuple-element.27), channel_id=1, source_target_pairs={{0,16},{8,24},{16,0},{24,8},{1,17},{9,25},{17,1},{25,9},{2,18},{10... | collective-permute-start | bytes 786440 | tf_op jit(solution)/shard_map/ppermute | solution.py:130
  45.3 0.0 collective-permute-done.5.from_lo
  45.3 0.0 collective-permute-done.6.from_hi
  45.3 0.0 copy-start.2
  45.3 0.7 copy-done.1
  46.0 0.1 copy-done.2
  46.1 3.5 %input_grad.1 = (f32[2,256,256]{2,1,0:T(8,128)}, bf16[2,256,256]{2,1,0:T(8,128)(2,1)}, bf16[2,256,256]{2,1,0:T(8,128)(2,1)}, bf16[2,256,256]{2,1,0:T(8,128)(2,1)}) custom-call(s32[4]{0:T(128)} %pad_add_fusion.pos, bf16[256,256]{1,0:T(8,128)(2,1)} %get-tuple-element.14.att, bf16[256,256]{1,0:T(8,128)(2,1)} %get-tuple-element.15.gq, ...), custom_call_target="tpu_custom_call" | custom-call | flops 540000000 | bytes 4000000 | tf_op jit(solution)/shard_map/input_grad/pallas_call | solution.py:192
  49.6 0.0 collective-permute-start.7
  49.6 1.5 %collective-permute-start.8 = (bf16[2,256,256]{2,1,0:T(8,128)(2,1)}, bf16[2,256,256]{2,1,0:T(8,128)(2,1)S(1)}, u32[]{:S(2)}, u32[]{:S(2)}) collective-permute-start(bf16[2,256,256]{2,1,0:T(8,128)(2,1)} %get-tuple-element.21), channel_id=1, source_target_pairs={{0,2},{1,3},{2,0},{3,1},{4,6},{5,7},{6,4},{7,5},{8,10},{9,11},{10,... | collective-permute-start | bytes 786440 | tf_op jit(solution)/shard_map/ppermute | solution.py:130
  51.1 0.0 collective-permute-done.11
  51.1 1.8 %collective-permute-start.9 = (bf16[2,256,256]{2,1,0:T(8,128)(2,1)}, bf16[2,256,256]{2,1,0:T(8,128)(2,1)S(1)}, u32[]{:S(2)}, u32[]{:S(2)}) collective-permute-start(bf16[2,256,256]{2,1,0:T(8,128)(2,1)} %get-tuple-element.22), channel_id=1, source_target_pairs={{0,3},{1,0},{2,1},{3,2},{4,7},{5,4},{6,5},{7,6},{8,11},{9,8},{10,9... | collective-permute-start | bytes 786440 | tf_op jit(solution)/shard_map/ppermute | solution.py:130
  52.8 0.3 collective-permute-done.13
  53.1 0.1 collective-permute-done.12
  53.2 0.1 fusion.2
  53.4 2.2 %collective-permute-start.14 = (bf16[4,4,16,256]{3,2,1,0:T(8,128)(2,1)S(1)}, bf16[4,4,16,256]{3,2,1,0:T(8,128)(2,1)S(1)}, u32[]{:S(2)}, u32[]{:S(2)}) collective-permute-start(bf16[4,4,16,256]{3,2,1,0:T(8,128)(2,1)S(1)} %slice_bitcast_fusion.4), channel_id=1, source_target_pairs={{0,32},{32,0},{64,96},{96,64},{128,160},{160,128},{192,224},{224,1... | collective-permute-start | bytes 393224 | tf_op jit(solution)/shard_map/ppermute | solution.py:142
  55.6 8.9 %collective-permute-done.7 = bf16[2,256,256]{2,1,0:T(8,128)(2,1)S(1)} collective-permute-done((bf16[2,256,256]{2,1,0:T(8,128)(2,1)}, bf16[2,256,256]{2,1,0:T(8,128)(2,1)S(1)}, u32[]{:S(2)}, u32[]{:S(2)}) %collective-permute-start.7) | collective-permute-done | bytes 262176 | tf_op jit(solution)/shard_map/ppermute | solution.py:130
  64.5 0.0 collective-permute-done.8
  64.5 1.3 %collective-permute-done.9 = bf16[2,256,256]{2,1,0:T(8,128)(2,1)S(1)} collective-permute-done((bf16[2,256,256]{2,1,0:T(8,128)(2,1)}, bf16[2,256,256]{2,1,0:T(8,128)(2,1)S(1)}, u32[]{:S(2)}, u32[]{:S(2)}) %collective-permute-start.9) | collective-permute-done | bytes 262176 | tf_op jit(solution)/shard_map/ppermute | solution.py:130
  65.7 0.1 add_convert_fusion.1
  65.9 0.0 collective-permute-done.14
  65.9 4.5 %collective-permute-start.15 = (bf16[4,16,256]{2,1,0:T(8,128)(2,1)S(1)}, bf16[4,16,256]{2,1,0:T(8,128)(2,1)S(1)}, u32[]{:S(2)}, u32[]{:S(2)}) collective-permute-start(bf16[4,16,256]{2,1,0:T(8,128)(2,1)S(1)} %get-tuple-element.30), channel_id=1, source_target_pairs={{0,64},{32,96},{64,128},{96,160},{128,192},{160,224},{192,0},{224,... | collective-permute-start | bytes 98312 | tf_op jit(solution)/shard_map/ppermute | solution.py:208
  70.5 3.0 %collective-permute-start.17 = (bf16[4,16,256]{2,1,0:T(8,128)(2,1)S(1)}, bf16[4,16,256]{2,1,0:T(8,128)(2,1)S(1)}, u32[]{:S(2)}, u32[]{:S(2)}) collective-permute-start(bf16[4,16,256]{2,1,0:T(8,128)(2,1)S(1)} %get-tuple-element.31), channel_id=1, source_target_pairs={{0,192},{32,224},{64,0},{96,32},{128,64},{160,96},{192,128},{224,1... | collective-permute-start | bytes 98312 | tf_op jit(solution)/shard_map/ppermute | solution.py:208
  73.5 4.9 %collective-permute-start.16 = (bf16[4,16,256]{2,1,0:T(8,128)(2,1)S(1)}, bf16[4,16,256]{2,1,0:T(8,128)(2,1)S(1)}, u32[]{:S(2)}, u32[]{:S(2)}) collective-permute-start(bf16[4,16,256]{2,1,0:T(8,128)(2,1)S(1)} %get-tuple-element.32), channel_id=1, source_target_pairs={{0,128},{32,160},{64,192},{96,224},{128,0},{160,32},{192,64},{224,... | collective-permute-start | bytes 98312 | tf_op jit(solution)/shard_map/ppermute | solution.py:208
  78.4 0.7 slice_bitcast_fusion.6
  79.2 0.0 collective-permute-done.15
  79.2 0.0 collective-permute-done.17
  79.2 2.2 %collective-permute-done.16 = bf16[4,16,256]{2,1,0:T(8,128)(2,1)S(1)} collective-permute-done((bf16[4,16,256]{2,1,0:T(8,128)(2,1)S(1)}, bf16[4,16,256]{2,1,0:T(8,128)(2,1)S(1)}, u32[]{:S(2)}, u32[]{:S(2)}) %collective-permute-start.16) | collective-permute-done | bytes 32800 | tf_op jit(solution)/shard_map/ppermute | solution.py:208
  81.3 0.6 fusion.5
  (9 shorter events, 0.1 us)
Async XLA Ops:
  0.6 15.1 %collective-permute-start.3 = (bf16[256,256]{1,0:T(8,128)(2,1)}, bf16[256,256]{1,0:T(8,128)(2,1)S(1)}, u32[]{:S(2)}, u32[]{:S(2)}) collective-permute-start(bf16[256,256]{1,0:T(8,128)(2,1)} %c0.1), channel_id=1, source_target_pairs={{0,2},{1,3},{2,0},{3,1},{4,6},{5,7},{6,4},{7,5},{8,10},{9,11},{10,... | collective-permute-start | bytes 393224 | tf_op jit(solution)/shard_map/ppermute | solution.py:130
  3.7 11.9 %collective-permute-start.2 = (bf16[256,256]{1,0:T(8,128)(2,1)}, bf16[256,256]{1,0:T(8,128)(2,1)S(1)}, u32[]{:S(2)}, u32[]{:S(2)}) collective-permute-start(bf16[256,256]{1,0:T(8,128)(2,1)} %c0.1), channel_id=1, source_target_pairs={{0,1},{1,2},{2,3},{3,0},{4,5},{5,6},{6,7},{7,4},{8,9},{9,10},{10,1... | collective-permute-start | bytes 393224 | tf_op jit(solution)/shard_map/ppermute | solution.py:130
  4.3 11.4 %collective-permute-start.4 = (bf16[256,256]{1,0:T(8,128)(2,1)}, bf16[256,256]{1,0:T(8,128)(2,1)S(1)}, u32[]{:S(2)}, u32[]{:S(2)}) collective-permute-start(bf16[256,256]{1,0:T(8,128)(2,1)} %c0.1), channel_id=1, source_target_pairs={{0,3},{1,0},{2,1},{3,2},{4,7},{5,4},{6,5},{7,6},{8,11},{9,8},{10,9... | collective-permute-start | bytes 393224 | tf_op jit(solution)/shard_map/ppermute | solution.py:130
  7.0 10.7 %collective-permute-start = (bf16[256,1024]{1,0:T(8,128)(2,1)}, bf16[256,1024]{1,0:T(8,128)(2,1)S(1)}, u32[]{:S(2)}, u32[]{:S(2)}) collective-permute-start(bf16[256,1024]{1,0:T(8,128)(2,1)} %a_own.1), channel_id=1, source_target_pairs={{0,4},{4,8},{8,12},{12,16},{16,20},{20,24},{24,28},{28,32},{32,36}... | collective-permute-start | bytes 1572872 | tf_op jit(solution)/shard_map/ppermute | solution.py:135
  8.9 10.6 %collective-permute-start.1 = (bf16[256,1024]{1,0:T(8,128)(2,1)}, bf16[256,1024]{1,0:T(8,128)(2,1)S(1)}, u32[]{:S(2)}, u32[]{:S(2)}) collective-permute-start(bf16[256,1024]{1,0:T(8,128)(2,1)} %a_own.1), channel_id=1, source_target_pairs={{4,0},{8,4},{12,8},{16,12},{20,16},{24,20},{28,24},{32,28},{36,32}... | collective-permute-start | bytes 1572872 | tf_op jit(solution)/shard_map/ppermute | solution.py:135
  15.7 3.9 %copy-start.5 = (bf16[256,256]{1,0:T(8,128)(2,1)}, bf16[256,256]{1,0:T(8,128)(2,1)S(1)}, u32[]{:S(2)}) copy-start(bf16[256,256]{1,0:T(8,128)(2,1)S(1)} %collective-permute-done.3.c2) | copy-start | bytes 393220
  15.7 3.9 %copy-start.6 = (bf16[256,256]{1,0:T(8,128)(2,1)}, bf16[256,256]{1,0:T(8,128)(2,1)S(1)}, u32[]{:S(2)}) copy-start(bf16[256,256]{1,0:T(8,128)(2,1)S(1)} %collective-permute-done.2.c1) | copy-start | bytes 393220
  15.7 3.8 %copy-start.7 = (bf16[256,256]{1,0:T(8,128)(2,1)}, bf16[256,256]{1,0:T(8,128)(2,1)S(1)}, u32[]{:S(2)}) copy-start(bf16[256,256]{1,0:T(8,128)(2,1)S(1)} %collective-permute-done.4.c3) | copy-start | bytes 393220
  17.7 1.9 %copy-start.3 = (bf16[256,1024]{1,0:T(8,128)(2,1)}, bf16[256,1024]{1,0:T(8,128)(2,1)S(1)}, u32[]{:S(2)}) copy-start(bf16[256,1024]{1,0:T(8,128)(2,1)S(1)} %collective-permute-done.a_lo) | copy-start | bytes 1572868
  19.6 0.8 copy-start.4
  30.6 7.0 %collective-permute-start.10 = (bf16[4,2,4,4,16,256]{5,4,3,2,1,0:T(8,128)(2,1)}, bf16[4,2,4,4,16,256]{5,4,3,2,1,0:T(8,128)(2,1)S(1)}, u32[]{:S(2)}, u32[]{:S(2)}) collective-permute-start(bf16[4,2,4,4,16,256]{5,4,3,2,1,0:T(8,128)(2,1)} %get-tuple-element.24), channel_id=1, source_target_pairs={{0,4},{4,0},{1,5},{5,1},{2,6},{6,2},{3,7},{7,3},{8,12},{12,8},{9,1... | collective-permute-start | bytes 3145736 | tf_op jit(solution)/shard_map/ppermute | solution.py:142
  32.1 13.2 %collective-permute-start.5 = (bf16[2,256,256]{2,1,0:T(8,128)(2,1)}, bf16[2,256,256]{2,1,0:T(8,128)(2,1)S(1)}, u32[]{:S(2)}, u32[]{:S(2)}) collective-permute-start(bf16[2,256,256]{2,1,0:T(8,128)(2,1)} %get-tuple-element.17), channel_id=1, source_target_pairs={{0,4},{4,8},{8,12},{12,16},{16,20},{20,24},{24,28},{28,32},{32,36}... | collective-permute-start | bytes 786440 | tf_op jit(solution)/shard_map/ppermute | solution.py:135
  34.0 11.3 %collective-permute-start.6 = (bf16[2,256,256]{2,1,0:T(8,128)(2,1)}, bf16[2,256,256]{2,1,0:T(8,128)(2,1)S(1)}, u32[]{:S(2)}, u32[]{:S(2)}) collective-permute-start(bf16[2,256,256]{2,1,0:T(8,128)(2,1)} %get-tuple-element.18), channel_id=1, source_target_pairs={{4,0},{8,4},{12,8},{16,12},{20,16},{24,20},{28,24},{32,28},{36,32}... | collective-permute-start | bytes 786440 | tf_op jit(solution)/shard_map/ppermute | solution.py:135
  39.3 11.7 %collective-permute-start.11 = (bf16[2,4,4,16,256]{4,3,2,1,0:T(8,128)(2,1)S(1)}, bf16[2,4,4,16,256]{4,3,2,1,0:T(8,128)(2,1)S(1)}, u32[]{:S(2)}, u32[]{:S(2)}) collective-permute-start(bf16[2,4,4,16,256]{4,3,2,1,0:T(8,128)(2,1)S(1)} %get-tuple-element.25), channel_id=1, source_target_pairs={{0,8},{8,16},{16,24},{24,0},{1,9},{9,17},{17,25},{25,1},{2,10},{10... | collective-permute-start | bytes 786440 | tf_op jit(solution)/shard_map/ppermute | solution.py:130
  43.1 10.0 %collective-permute-start.13 = (bf16[2,4,4,16,256]{4,3,2,1,0:T(8,128)(2,1)S(1)}, bf16[2,4,4,16,256]{4,3,2,1,0:T(8,128)(2,1)S(1)}, u32[]{:S(2)}, u32[]{:S(2)}) collective-permute-start(bf16[2,4,4,16,256]{4,3,2,1,0:T(8,128)(2,1)S(1)} %get-tuple-element.26), channel_id=1, source_target_pairs={{0,24},{8,0},{16,8},{24,16},{1,25},{9,1},{17,9},{25,17},{2,26},{10... | collective-permute-start | bytes 786440 | tf_op jit(solution)/shard_map/ppermute | solution.py:130
  43.1 10.1 %collective-permute-start.12 = (bf16[2,4,4,16,256]{4,3,2,1,0:T(8,128)(2,1)S(1)}, bf16[2,4,4,16,256]{4,3,2,1,0:T(8,128)(2,1)S(1)}, u32[]{:S(2)}, u32[]{:S(2)}) collective-permute-start(bf16[2,4,4,16,256]{4,3,2,1,0:T(8,128)(2,1)S(1)} %get-tuple-element.27), channel_id=1, source_target_pairs={{0,16},{8,24},{16,0},{24,8},{1,17},{9,25},{17,1},{25,9},{2,18},{10... | collective-permute-start | bytes 786440 | tf_op jit(solution)/shard_map/ppermute | solution.py:130
  45.3 0.7 copy-start.1
  45.3 0.8 copy-start.2
  49.6 16.2 %copy-start = (f32[2,256,256]{2,1,0:T(8,128)S(1)}, f32[2,256,256]{2,1,0:T(8,128)}, u32[]{:S(2)}) copy-start(f32[2,256,256]{2,1,0:T(8,128)} %get-tuple-element.19) | copy-start | bytes 1572868
  49.6 14.9 %collective-permute-start.7 = (bf16[2,256,256]{2,1,0:T(8,128)(2,1)}, bf16[2,256,256]{2,1,0:T(8,128)(2,1)S(1)}, u32[]{:S(2)}, u32[]{:S(2)}) collective-permute-start(bf16[2,256,256]{2,1,0:T(8,128)(2,1)} %get-tuple-element.20), channel_id=1, source_target_pairs={{0,1},{1,2},{2,3},{3,0},{4,5},{5,6},{6,7},{7,4},{8,9},{9,10},{10,1... | collective-permute-start | bytes 786440 | tf_op jit(solution)/shard_map/ppermute | solution.py:130
  49.6 14.9 %collective-permute-start.8 = (bf16[2,256,256]{2,1,0:T(8,128)(2,1)}, bf16[2,256,256]{2,1,0:T(8,128)(2,1)S(1)}, u32[]{:S(2)}, u32[]{:S(2)}) collective-permute-start(bf16[2,256,256]{2,1,0:T(8,128)(2,1)} %get-tuple-element.21), channel_id=1, source_target_pairs={{0,2},{1,3},{2,0},{3,1},{4,6},{5,7},{6,4},{7,5},{8,10},{9,11},{10,... | collective-permute-start | bytes 786440 | tf_op jit(solution)/shard_map/ppermute | solution.py:130
  51.1 14.7 %collective-permute-start.9 = (bf16[2,256,256]{2,1,0:T(8,128)(2,1)}, bf16[2,256,256]{2,1,0:T(8,128)(2,1)S(1)}, u32[]{:S(2)}, u32[]{:S(2)}) collective-permute-start(bf16[2,256,256]{2,1,0:T(8,128)(2,1)} %get-tuple-element.22), channel_id=1, source_target_pairs={{0,3},{1,0},{2,1},{3,2},{4,7},{5,4},{6,5},{7,6},{8,11},{9,8},{10,9... | collective-permute-start | bytes 786440 | tf_op jit(solution)/shard_map/ppermute | solution.py:130
  53.4 12.5 %collective-permute-start.14 = (bf16[4,4,16,256]{3,2,1,0:T(8,128)(2,1)S(1)}, bf16[4,4,16,256]{3,2,1,0:T(8,128)(2,1)S(1)}, u32[]{:S(2)}, u32[]{:S(2)}) collective-permute-start(bf16[4,4,16,256]{3,2,1,0:T(8,128)(2,1)S(1)} %slice_bitcast_fusion.4), channel_id=1, source_target_pairs={{0,32},{32,0},{64,96},{96,64},{128,160},{160,128},{192,224},{224,1... | collective-permute-start | bytes 393224 | tf_op jit(solution)/shard_map/ppermute | solution.py:142
  65.9 13.2 %collective-permute-start.15 = (bf16[4,16,256]{2,1,0:T(8,128)(2,1)S(1)}, bf16[4,16,256]{2,1,0:T(8,128)(2,1)S(1)}, u32[]{:S(2)}, u32[]{:S(2)}) collective-permute-start(bf16[4,16,256]{2,1,0:T(8,128)(2,1)S(1)} %get-tuple-element.30), channel_id=1, source_target_pairs={{0,64},{32,96},{64,128},{96,160},{128,192},{160,224},{192,0},{224,... | collective-permute-start | bytes 98312 | tf_op jit(solution)/shard_map/ppermute | solution.py:208
  70.5 8.7 %collective-permute-start.17 = (bf16[4,16,256]{2,1,0:T(8,128)(2,1)S(1)}, bf16[4,16,256]{2,1,0:T(8,128)(2,1)S(1)}, u32[]{:S(2)}, u32[]{:S(2)}) collective-permute-start(bf16[4,16,256]{2,1,0:T(8,128)(2,1)S(1)} %get-tuple-element.31), channel_id=1, source_target_pairs={{0,192},{32,224},{64,0},{96,32},{128,64},{160,96},{192,128},{224,1... | collective-permute-start | bytes 98312 | tf_op jit(solution)/shard_map/ppermute | solution.py:208
  73.5 7.8 %collective-permute-start.16 = (bf16[4,16,256]{2,1,0:T(8,128)(2,1)S(1)}, bf16[4,16,256]{2,1,0:T(8,128)(2,1)S(1)}, u32[]{:S(2)}, u32[]{:S(2)}) collective-permute-start(bf16[4,16,256]{2,1,0:T(8,128)(2,1)S(1)} %get-tuple-element.32), channel_id=1, source_target_pairs={{0,128},{32,160},{64,192},{96,224},{128,0},{160,32},{192,64},{224,... | collective-permute-start | bytes 98312 | tf_op jit(solution)/shard_map/ppermute | solution.py:208

commit v2 on v1

v2 whole, which is shorter than its diff:
```python
import jax
import jax.numpy as jnp
from jax import lax
from jax.experimental import pallas as pl
from jax.experimental.pallas import tpu as pltpu
from jax.sharding import Mesh
from jax.sharding import PartitionSpec as P

HD = 64
PATCH = 64
D = 1024
ROW = 256
WIDTH = 256
HEADS = WIDTH // HD
KEYS = 3 * ROW
LOG2E = 1.4426950408889634
BF = jnp.bfloat16
F32 = jnp.float32
SPACE = ("z", "y", "core")

NN = (((1,), (0,)), ((), ()))
NT = (((1,), (1,)), ((), ()))


def mm(a, b, dims=NN):
    return lax.dot_general(a, b, dims, preferred_element_type=F32)


def places():
    return [lax.axis_index(a) for a in ("core", "y", "z", "mp")]


def slot_bias(nb, mask, core, y, z):
    row = (z * 4 + y) * 2 + core
    sign = 1 - 2 * core
    patch_of_lane = lax.broadcasted_iota(jnp.int32, (16, ROW), 1) // PATCH
    patch_of_row = lax.broadcasted_iota(jnp.int32, (16, ROW), 0)
    count = jnp.zeros((16, ROW), F32)
    for slot in range(9):
        named = jnp.zeros((16, ROW), jnp.int32)
        for patch in range(4):
            number = nb[patch, slot]
            band = 1 + sign * (lax.div(number, 4) - row)
            place = jnp.where(mask[patch, slot] > 0, band * 4 + lax.rem(number, 4), -1)
            named = jnp.where(patch_of_lane == patch, place, named)
        count += jnp.where(named == patch_of_row, 1.0, 0.0)
    return jnp.where(count > 0, jnp.where(count > 1, jnp.log(count) * LOG2E, 0.0), -1e30)


def columns(ref, x, step):
    return ref[:, pl.ds(pl.multiple_of(lax.rem(x + step, 4) * WIDTH, WIDTH), WIDTH)]


def own_kernel(
    act, w_q, w_k, w_v, w_o, cot, slots, live,
    wq, wk, wv, wo, query_out, key_out, value_out, act_t, grad_out, cot_t, bias_out,
    act_s, cot_s, nb, mask, sems,
):
    core, y, z, x = places()
    pairs = (
        (act, act_s), (w_q, wq), (w_k, wk), (w_v, wv), (cot, cot_s), (w_o, wo), (slots, nb), (live, mask)
    )
    copies = [pltpu.make_async_copy(a, b, sems.at[i]) for i, (a, b) in enumerate(pairs)]
    for copy in copies:
        copy.start()
    copies[0].wait()
    act_t[...] = act_s[...].T
    for index, weight, out in ((1, wq, query_out), (2, wk, key_out), (3, wv, value_out)):
        copies[index].wait()
        out[...] = mm(act_s[...], weight[...]).astype(BF)
    copies[4].wait()
    cot_t[...] = cot_s[...].T
    copies[5].wait()
    grad_out[...] = mm(cot_s[...], columns(wo, x, 0), NT)
    copies[6].wait()
    copies[7].wait()
    bias_out[...] = slot_bias(nb, mask, core, y, z)


def attention_kernel(
    a_far, a_near, wk, wv, wo, query_in, key_own, value_own, act_t, grad_in, cot_t, bias, c1, c2, c3,
    att_out, gq_out, far_out, own_out, send_out, keep_out,
    key_s, value_s, dw_s,
):
    core, y, z, x = places()
    query = query_in[...]
    key_s[ROW : 2 * ROW, :] = key_own[...]
    value_s[ROW : 2 * ROW, :] = value_own[...]
    for band, block in ((0, a_far), (2, a_near)):
        rows = slice(band * ROW, (band + 1) * ROW)
        key_s[rows, :] = mm(block[...], wk[...]).astype(BF)
        value_s[rows, :] = mm(block[...], wv[...]).astype(BF)
    grad_att = grad_in[...]
    for step, block in ((3, c1), (2, c2), (1, c3)):
        grad_att += mm(block[...], columns(wo, x, step), NT)
    grad_att = grad_att.astype(BF)

    keys = key_s[...]
    values = value_s[...]
    keys_t = keys.T
    values_t = values.T
    lane_head = lax.broadcasted_iota(jnp.int32, (ROW, WIDTH), 1) // HD
    bias_rows = jnp.concatenate(
        [jnp.broadcast_to(bias[patch : patch + 1, :], (PATCH, ROW)) for patch in range(KEYS // PATCH)],
        axis=0,
    )
    grad_key = jnp.zeros((KEYS, WIDTH), F32)
    grad_value = jnp.zeros((KEYS, WIDTH), F32)
    att_rows, gq_rows = [], []
    for head in range(HEADS):
        feats = slice(head * HD, (head + 1) * HD)
        q_head = jnp.where(lane_head == head, query, jnp.zeros_like(query))
        g_head = jnp.where(lane_head == head, grad_att, jnp.zeros_like(grad_att))
        scores = mm(keys, q_head, NT) * (LOG2E * HD**-0.5) + bias_rows
        peak = jnp.max(scores, axis=0, keepdims=True)
        weights = jnp.exp2(scores - peak)
        probs = weights * (1.0 / jnp.sum(weights, axis=0, keepdims=True))
        probs_low = probs.astype(BF)
        grad_probs = mm(values, g_head, NT)
        centre = jnp.sum(probs * grad_probs, axis=0, keepdims=True)
        grad_scores = (probs * (grad_probs - centre) * HD**-0.5).astype(BF)
        att_rows.append(mm(values_t[feats, :], probs_low))
        gq_rows.append(mm(keys_t[feats, :], grad_scores))
        grad_key += mm(grad_scores, q_head)
        grad_value += mm(probs_low, g_head)
    att = jnp.concatenate(att_rows, axis=0).astype(BF).T
    gq = jnp.concatenate(gq_rows, axis=0).astype(BF).T
    att_out[...] = att
    gq_out[...] = gq
    far_out[0], far_out[1] = grad_key[:ROW].astype(BF), grad_value[:ROW].astype(BF)
    own_out[0], own_out[1] = grad_key[ROW : 2 * ROW], grad_value[ROW : 2 * ROW]
    for part, grad in enumerate((grad_key, grad_value)):
        for block in range(16):
            rows = slice(2 * ROW + 16 * block, 2 * ROW + 16 * (block + 1))
            send_out[128 + 16 * part + block] = grad[rows].astype(BF)

    grad_key = grad_key.astype(BF)
    grad_value = grad_value.astype(BF)
    own = slice(ROW, 2 * ROW)
    far_t, near_t = a_far[...].T, a_near[...].T
    dw_s[0] = mm(act_t[...], gq)
    for index, grad in ((1, grad_key), (2, grad_value)):
        dw_s[index] = (
            mm(act_t[...], grad[own]) + mm(far_t, grad[:ROW]) + mm(near_t, grad[2 * ROW :])
        )
    for step, block_t in ((0, cot_t[...]), (3, c1[...].T), (2, c2[...].T), (1, c3[...].T)):
        rows = pl.ds(pl.multiple_of(lax.rem(x + step, 4) * WIDTH, WIDTH), WIDTH)
        dw_s[3, rows, :] = mm(block_t, att)
    for mine, out in ((0, send_out), (1, keep_out)):
        c = core if mine else 1 - core
        for ys in range(4):
            yy = lax.rem(y + ys, 4)
            for low in range(2):
                for hs in range(4):
                    zl = lax.rem(z, 2)
                    zl = zl if low else 1 - zl
                    zz = 2 * lax.rem(z // 2 + hs, 4) + zl
                    row = pl.multiple_of(((zz * 4 + yy) * 2 + c) * 16, 16)
                    block = ((ys * 2 + low) * 4 + hs) * 4
                    out[block : block + 4] = dw_s[:, pl.ds(row, 16), :].astype(BF)


def core_sum_kernel(keep, got, o0, o1, o2, o3):
    for step, out in enumerate((o0, o1, o2, o3)):
        part = slice(32 * step, 32 * (step + 1))
        out[...] = (keep[part].astype(F32) + got[part].astype(F32)).astype(out.dtype)


def input_kernel(att, gq, own, near, far, wq, wk, wv, wo, p0, p1, p2, p3):
    x = places()[3]
    grads = []
    for part in range(2):
        from_near = near[128 + 16 * part : 144 + 16 * part].reshape(ROW, WIDTH)
        grads.append((own[part] + from_near.astype(F32) + far[part].astype(F32)).astype(BF))
    grad_key, grad_value = grads
    for step, out in enumerate((p0, p1, p2, p3)):
        block = pl.ds(pl.multiple_of(lax.rem(x + step, 4) * WIDTH, WIDTH), WIDTH)
        out[0] = mm(att[...], wo[:, block]).astype(out.dtype)
        out[1] = (
            mm(gq[...], wq[block, :], NT)
            + mm(grad_key, wk[block, :], NT)
            + mm(grad_value, wv[block, :], NT)
        ).astype(out.dtype)


def y_sum_kernel(a, b, c, d, send, keep):
    for part, out in ((slice(0, 16), send), (slice(16, 32), keep)):
        total = (a[part].astype(F32) + b[part].astype(F32)) + (c[part].astype(F32) + d[part].astype(F32))
        out[...] = total.astype(out.dtype)


def pair_sum_kernel(keep, got, o0, o1, o2, o3):
    for step, out in enumerate((o0, o1, o2, o3)):
        part = slice(4 * step, 4 * (step + 1))
        out[...] = (keep[part].astype(F32) + got[part].astype(F32)).astype(out.dtype)


def last_sum_kernel(d0, d1, d2, d3, p0, p1, p2, p3, out, grad, dw):
    dw[...] = (d0[...] + d1[...].astype(F32)) + (d2[...].astype(F32) + d3[...].astype(F32))
    for part, ref in ((0, out), (1, grad)):
        total = (p0[part] + p1[part].astype(F32)) + (p2[part].astype(F32) + p3[part].astype(F32))
        ref[...] = total.astype(BF)


def on_chip(*arrays):
    return [pltpu.with_memory_space_constraint(a, pltpu.VMEM) for a in arrays]


def call(
    kernel, name, outs, arrays, apart=(), scratch=(), limit=16, flops=0, moved=1_000_000, keep=True
):
    kept = [pltpu.VMEM(shape, dtype) if keep else jax.ShapeDtypeStruct(shape, dtype) for shape, dtype in outs]
    return pl.pallas_call(
        kernel,
        out_shape=tuple(kept),
        in_specs=[pl.BlockSpec(memory_space=pltpu.HBM)] * len(apart)
        + [pl.BlockSpec(memory_space=pltpu.VMEM)] * len(arrays),
        out_specs=(pl.BlockSpec(memory_space=pltpu.VMEM),) * len(kept),
        scratch_shapes=list(scratch),
        compiler_params=pltpu.CompilerParams(vmem_limit_bytes=limit * 1024 * 1024),
        cost_estimate=pl.CostEstimate(flops=flops, bytes_accessed=moved, transcendentals=0),
        name=name,
    )(*[pltpu.with_memory_space_constraint(a, pltpu.HBM) for a in apart], *on_chip(*arrays))


def move(value, axis, target):
    count = lax.axis_size(axis)
    return lax.ppermute(
        value, axis, [(i, target(i)) for i in range(count) if 0 <= target(i) < count]
    )


def ring(value, axis, steps):
    count = lax.axis_size(axis)
    return move(value, axis, lambda i: (i + steps) % count)


def near_row(value):
    return move(value, SPACE, lambda i: i ^ 1)


def far_row(value):
    return move(value, SPACE, lambda i: i + 1 if i % 2 else i - 1)


def body(activations, w_query, w_key, w_value, w_out, grad_output, neighbours, pad_mask):
    act_far = far_row(activations)
    cots = [ring(grad_output, "mp", s) for s in (1, 2, 3)]
    act_near = near_row(activations)

    square = (ROW, WIDTH)
    wq, wk, wv, wo, *own_parts = call(
        own_kernel,
        "own_part",
        [((D, WIDTH), BF)] * 3 + [((WIDTH, D), BF)]
        + [(square, BF)] * 3 + [((D, ROW), BF), (square, F32), (square, BF), ((16, ROW), F32)],
        [],
        apart=(activations, w_query, w_key, w_value, w_out, grad_output, neighbours, pad_mask),
        scratch=[
            pltpu.VMEM((ROW, D), BF),
            pltpu.VMEM(square, BF),
            pltpu.SMEM((4, 9), jnp.int32),
            pltpu.SMEM((4, 9), jnp.int32),
            pltpu.SemaphoreType.DMA((8,)),
        ],
        flops=600_000_000,
        moved=6_000_000,
    )

    block = (16, WIDTH)
    att, gq, far, own, dw_send, dw_keep = call(
        attention_kernel,
        "attention",
        [
            (square, BF),
            (square, BF),
            ((2, ROW, WIDTH), BF),
            ((2, ROW, WIDTH), F32),
            ((160,) + block, BF),
            ((128,) + block, BF),
        ],
        [act_far, act_near, wk, wv, wo, *own_parts, *cots],
        scratch=[
            pltpu.VMEM((KEYS, WIDTH), BF),
            pltpu.VMEM((KEYS, WIDTH), BF),
            pltpu.VMEM((4, D, WIDTH), F32),
        ],
        limit=32,
        flops=4_000_000_000,
        moved=8_000_000,
    )

    got = near_row(dw_send)
    grad_far = far_row(far)
    dw = call(core_sum_kernel, "core_sum", [((32,) + block, BF)] * 4, [dw_keep, got])
    dw_y = [dw[0]] + [ring(dw[s], "y", s) for s in (1, 2, 3)]

    piece = (2, ROW, WIDTH)
    pieces = call(
        input_kernel,
        "input_grad",
        [(piece, F32)] + [(piece, BF)] * 3,
        [att, gq, own, got, grad_far, wq, wk, wv, wo],
        flops=540_000_000,
        moved=4_000_000,
    )
    outs = [pieces[0]] + [ring(pieces[s], "mp", s) for s in (1, 2, 3)]

    send, keep = call(y_sum_kernel, "y_sum", [((16,) + block, BF)] * 2, dw_y)
    pair = move(send, "z", lambda i: i ^ 1)
    dw = call(
        pair_sum_kernel, "pair_sum", [((4,) + block, F32)] + [((4,) + block, BF)] * 3, [keep, pair]
    )
    dw_z = [dw[0]] + [ring(dw[s], "z", 2 * s) for s in (1, 2, 3)]
    return call(
        last_sum_kernel,
        "last_sum",
        [((ROW, WIDTH), BF), ((ROW, WIDTH), BF), ((4,) + block, F32)],
        dw_z + outs,
        keep=False,
    )


def solution(mesh):
    fine = Mesh(mesh.devices.reshape(8, 4, 2, 4), SPACE + ("mp",))
    in_specs = (
        P(SPACE, None),
        P(None, "mp"),
        P(None, "mp"),
        P(None, "mp"),
        P("mp", None),
        P(SPACE, "mp"),
        P(SPACE, None),
        P(SPACE, None),
    )
    out_specs = (P(SPACE, "mp"), P(SPACE, "mp"), P(None, SPACE, "mp"))
    return jax.shard_map(body, mesh=fine, in_specs=in_specs, out_specs=out_specs, check_vma=False)
```

time: 82.3 us -> 64.9 us (0.79)
  the two profiles are of different devices: /device:TPU:16 before, /device:TPU:2 now
where the time goes in v2:
time: 64.9 us; the launch traced here: 64.7 us
  starting transfers between devices  32.8 us (51%)
  waiting for transfers between devices  20.3 us (31%)
  Pallas kernels  10.9 us (17%)
  between operations  0.72 us (1%)
    ppermute x17, starting transfers between devices, move(): lax.ppermute(value, axis, [(i, target(i)) for i in range(count) if 0 <= t...  32.8 us
    ppermute x17, waiting for transfers between devices, move(): lax.ppermute(value, axis, [(i, target(i)) for i in range(count) if 0 <= t...  20.3 us
    pallas_call x7, Pallas kernels, call(): pl.pallas_call(kernel, out_shape=tuple(kept), in_specs=[pl.BlockSpec(memo...  10.9 us
  transfers between devices with their start and end apart: 17, of which 9 were waited for; matrix products, arithmetic and copies ran while one was open for 0% of the time, Pallas kernels for 6%

profile of v2, /device:TPU:2, one launch (start us, length us, event | category | flops | bytes accessed | tf_op | source)
XLA Modules:
  0.0 64.7 jit_solution(14181162835120033770)
XLA Ops:
  0.6 0.7 %collective-permute-start = (bf16[256,1024]{1,0:T(8,128)(2,1)}, bf16[256,1024]{1,0:T(8,128)(2,1)S(1)}, u32[]{:S(2)}, u32[]{:S(2)}) collective-permute-start(bf16[256,1024]{1,0:T(8,128)(2,1)} %act.1), channel_id=1, source_target_pairs={{4,8},{8,4},{12,16},{16,12},{20,24},{24,20},{28,32},{32,28},{36,40... | collective-permute-start | bytes 1572872 | tf_op jit(solution)/shard_map/ppermute | solution.py:228
  1.3 3.0 %collective-permute-start.1 = (bf16[256,1024]{1,0:T(8,128)(2,1)}, bf16[256,1024]{1,0:T(8,128)(2,1)S(1)}, u32[]{:S(2)}, u32[]{:S(2)}) collective-permute-start(bf16[256,1024]{1,0:T(8,128)(2,1)} %act.1), channel_id=1, source_target_pairs={{0,4},{4,0},{8,12},{12,8},{16,20},{20,16},{24,28},{28,24},{32,36},... | collective-permute-start | bytes 1572872 | tf_op jit(solution)/shard_map/ppermute | solution.py:228
  4.3 1.5 %collective-permute-start.2 = (bf16[256,256]{1,0:T(8,128)(2,1)}, bf16[256,256]{1,0:T(8,128)(2,1)S(1)}, u32[]{:S(2)}, u32[]{:S(2)}) collective-permute-start(bf16[256,256]{1,0:T(8,128)(2,1)} %cot.1), channel_id=1, source_target_pairs={{0,1},{1,2},{2,3},{3,0},{4,5},{5,6},{6,7},{7,4},{8,9},{9,10},{10,1... | collective-permute-start | bytes 393224 | tf_op jit(solution)/shard_map/ppermute | solution.py:228
  5.8 0.5 collective-permute-start.4
  6.4 2.1 %collective-permute-start.3 = (bf16[256,256]{1,0:T(8,128)(2,1)}, bf16[256,256]{1,0:T(8,128)(2,1)S(1)}, u32[]{:S(2)}, u32[]{:S(2)}) collective-permute-start(bf16[256,256]{1,0:T(8,128)(2,1)} %cot.1), channel_id=1, source_target_pairs={{0,2},{1,3},{2,0},{3,1},{4,6},{5,7},{6,4},{7,5},{8,10},{9,11},{10,... | collective-permute-start | bytes 393224 | tf_op jit(solution)/shard_map/ppermute | solution.py:228
  8.5 3.0 %own_part.1 = (bf16[1024,256]{1,0:T(8,128)(2,1)S(1)}, bf16[1024,256]{1,0:T(8,128)(2,1)S(1)}, bf16[1024,256]{1,0:T(8,128)(2,1)S(1)}, bf16[256,1024]{1,0:T(8,128)(...) custom-call(bf16[256,1024]{1,0:T(8,128)(2,1)} %act.1, ...), custom_call_target="tpu_custom_call" | custom-call | flops 600000000 | bytes 6000000 | tf_op jit(solution)/shard_map/own_part/pallas_call | solution.py:213
  11.5 0.0 collective-permute-done.2.c1
  11.5 0.2 collective-permute-done.4.c3
  11.8 2.9 %collective-permute-done.3.c2 = bf16[256,256]{1,0:T(8,128)(2,1)S(1)} collective-permute-done((bf16[256,256]{1,0:T(8,128)(2,1)}, bf16[256,256]{1,0:T(8,128)(2,1)S(1)}, u32[]{:S(2)}, u32[]{:S(2)}) %collective-permute-start.3) | collective-permute-done | bytes 131104 | tf_op jit(solution)/shard_map/ppermute | solution.py:228
  14.7 0.0 collective-permute-done.a_far
  14.7 0.0 collective-permute-done.1.a_near
  14.7 5.9 %attention.1 = (bf16[256,256]{1,0:T(8,128)(2,1)S(1)}, bf16[256,256]{1,0:T(8,128)(2,1)S(1)}, bf16[2,256,256]{2,1,0:T(8,128)(2,1)S(1)}, f32[2,256,256]{2,1,0:T(8,1...) custom-call(bf16[256,1024]{1,0:T(8,128)(2,1)S(1)} %collective-permute-done.a_far, ...), custom_call_target="tpu_custom_call" | custom-call | flops 4000000000 | bytes 8000000 | tf_op jit(solution)/shard_map/attention/pallas_call | solution.py:213
  20.6 0.1 collective-permute-start.5
  20.7 0.7 %collective-permute-start.13 = (bf16[2,256,256]{2,1,0:T(8,128)(2,1)S(1)}, bf16[2,256,256]{2,1,0:T(8,128)(2,1)S(1)}, u32[]{:S(2)}, u32[]{:S(2)}) collective-permute-start(bf16[2,256,256]{2,1,0:T(8,128)(2,1)S(1)} %get-tuple-element.59), channel_id=1, source_target_pairs={{4,8},{8,4},{12,16},{16,12},{20,24},{24,20},{28,32},{32,28},{36,40... | collective-permute-start | bytes 786440 | tf_op jit(solution)/shard_map/ppermute | solution.py:228
  21.4 2.3 %collective-permute-done.5.got.near = bf16[160,16,256]{2,1,0:T(8,128)(2,1)S(1)} collective-permute-done((bf16[160,16,256]{2,1,0:T(8,128)(2,1)S(1)}, bf16[160,16,256]{2,1,0:T(8,128)(2,1)S(1)}, u32[]{:S(2)}, u32[]{:S(2)}) %collective-permute-start.5) | collective-permute-done | bytes 1310752 | tf_op jit(solution)/shard_map/ppermute | solution.py:228
  23.7 0.2 core_sum.1
  24.0 1.7 %collective-permute-start.6 = (bf16[32,16,256]{2,1,0:T(8,128)(2,1)S(1)}, bf16[32,16,256]{2,1,0:T(8,128)(2,1)S(1)}, u32[]{:S(2)}, u32[]{:S(2)}) collective-permute-start(bf16[32,16,256]{2,1,0:T(8,128)(2,1)S(1)} %get-tuple-element.47), channel_id=1, source_target_pairs={{0,8},{8,16},{16,24},{24,0},{1,9},{9,17},{17,25},{25,1},{2,10},{10... | collective-permute-start | bytes 786440 | tf_op jit(solution)/shard_map/ppermute | solution.py:228
  25.6 2.9 %collective-permute-start.7 = (bf16[32,16,256]{2,1,0:T(8,128)(2,1)S(1)}, bf16[32,16,256]{2,1,0:T(8,128)(2,1)S(1)}, u32[]{:S(2)}, u32[]{:S(2)}) collective-permute-start(bf16[32,16,256]{2,1,0:T(8,128)(2,1)S(1)} %get-tuple-element.48), channel_id=1, source_target_pairs={{0,16},{8,24},{16,0},{24,8},{1,17},{9,25},{17,1},{25,9},{2,18},{10... | collective-permute-start | bytes 786440 | tf_op jit(solution)/shard_map/ppermute | solution.py:228
  28.5 1.1 %collective-permute-start.8 = (bf16[32,16,256]{2,1,0:T(8,128)(2,1)S(1)}, bf16[32,16,256]{2,1,0:T(8,128)(2,1)S(1)}, u32[]{:S(2)}, u32[]{:S(2)}) collective-permute-start(bf16[32,16,256]{2,1,0:T(8,128)(2,1)S(1)} %get-tuple-element.49), channel_id=1, source_target_pairs={{0,24},{8,0},{16,8},{24,16},{1,25},{9,1},{17,9},{25,17},{2,26},{10... | collective-permute-start | bytes 786440 | tf_op jit(solution)/shard_map/ppermute | solution.py:228
  29.6 0.0 collective-permute-done.13.far
  29.6 0.7 %input_grad.1 = (f32[2,256,256]{2,1,0:T(8,128)S(1)}, bf16[2,256,256]{2,1,0:T(8,128)(2,1)S(1)}, bf16[2,256,256]{2,1,0:T(8,128)(2,1)S(1)}, bf16[2,256,256]{2,1,0:T(8,128)(2,1)S(1)}) custom-call(bf16[256,256]{1,0:T(8,128)(2,1)S(1)} %get-tuple-element.56.att, bf16[256,256]{1,0:T(8,128)(2,1)S(1)} %get-tuple-element.57.gq, ...), custom_call_target="tpu_custom_call" | custom-call | flops 540000000 | bytes 4000000 | tf_op jit(solution)/shard_map/input_grad/pallas_call | solution.py:213
  30.3 0.1 collective-permute-start.14
  30.4 2.9 %collective-permute-start.15 = (bf16[2,256,256]{2,1,0:T(8,128)(2,1)S(1)}, bf16[2,256,256]{2,1,0:T(8,128)(2,1)S(1)}, u32[]{:S(2)}, u32[]{:S(2)}) collective-permute-start(bf16[2,256,256]{2,1,0:T(8,128)(2,1)S(1)} %get-tuple-element.63), channel_id=1, source_target_pairs={{0,2},{1,3},{2,0},{3,1},{4,6},{5,7},{6,4},{7,5},{8,10},{9,11},{10,... | collective-permute-start | bytes 786440 | tf_op jit(solution)/shard_map/ppermute | solution.py:228
  33.3 0.7 %collective-permute-done.6.b = bf16[32,16,256]{2,1,0:T(8,128)(2,1)S(1)} collective-permute-done((bf16[32,16,256]{2,1,0:T(8,128)(2,1)S(1)}, bf16[32,16,256]{2,1,0:T(8,128)(2,1)S(1)}, u32[]{:S(2)}, u32[]{:S(2)}) %collective-permute-start.6) | collective-permute-done | bytes 262176 | tf_op jit(solution)/shard_map/ppermute | solution.py:228
  34.1 0.9 %collective-permute-start.16 = (bf16[2,256,256]{2,1,0:T(8,128)(2,1)S(1)}, bf16[2,256,256]{2,1,0:T(8,128)(2,1)S(1)}, u32[]{:S(2)}, u32[]{:S(2)}) collective-permute-start(bf16[2,256,256]{2,1,0:T(8,128)(2,1)S(1)} %get-tuple-element.64), channel_id=1, source_target_pairs={{0,3},{1,0},{2,1},{3,2},{4,7},{5,4},{6,5},{7,6},{8,11},{9,8},{10,9... | collective-permute-start | bytes 786440 | tf_op jit(solution)/shard_map/ppermute | solution.py:228
  35.0 6.4 %collective-permute-done.7.c = bf16[32,16,256]{2,1,0:T(8,128)(2,1)S(1)} collective-permute-done((bf16[32,16,256]{2,1,0:T(8,128)(2,1)S(1)}, bf16[32,16,256]{2,1,0:T(8,128)(2,1)S(1)}, u32[]{:S(2)}, u32[]{:S(2)}) %collective-permute-start.7) | collective-permute-done | bytes 262176 | tf_op jit(solution)/shard_map/ppermute | solution.py:228
  41.4 1.2 %collective-permute-done.8.d = bf16[32,16,256]{2,1,0:T(8,128)(2,1)S(1)} collective-permute-done((bf16[32,16,256]{2,1,0:T(8,128)(2,1)S(1)}, bf16[32,16,256]{2,1,0:T(8,128)(2,1)S(1)}, u32[]{:S(2)}, u32[]{:S(2)}) %collective-permute-start.8) | collective-permute-done | bytes 262176 | tf_op jit(solution)/shard_map/ppermute | solution.py:228
  42.5 0.1 y_sum.1
  42.7 2.8 %collective-permute-start.9 = (bf16[16,16,256]{2,1,0:T(8,128)(2,1)S(1)}, bf16[16,16,256]{2,1,0:T(8,128)(2,1)S(1)}, u32[]{:S(2)}, u32[]{:S(2)}) collective-permute-start(bf16[16,16,256]{2,1,0:T(8,128)(2,1)S(1)} %get-tuple-element.51), channel_id=1, source_target_pairs={{0,32},{32,0},{64,96},{96,64},{128,160},{160,128},{192,224},{224,1... | collective-permute-start | bytes 393224 | tf_op jit(solution)/shard_map/ppermute | solution.py:228
  45.5 3.4 %collective-permute-done.9.got = bf16[16,16,256]{2,1,0:T(8,128)(2,1)S(1)} collective-permute-done((bf16[16,16,256]{2,1,0:T(8,128)(2,1)S(1)}, bf16[16,16,256]{2,1,0:T(8,128)(2,1)S(1)}, u32[]{:S(2)}, u32[]{:S(2)}) %collective-permute-start.9) | collective-permute-done | bytes 131104 | tf_op jit(solution)/shard_map/ppermute | solution.py:228
  48.9 5.5 %collective-permute-start.10 = (bf16[4,16,256]{2,1,0:T(8,128)(2,1)S(1)}, bf16[4,16,256]{2,1,0:T(8,128)(2,1)S(1)}, u32[]{:S(2)}, u32[]{:S(2)}) collective-permute-start(bf16[4,16,256]{2,1,0:T(8,128)(2,1)S(1)} %get-tuple-element.53), channel_id=1, source_target_pairs={{0,64},{32,96},{64,128},{96,160},{128,192},{160,224},{192,0},{224,... | collective-permute-start | bytes 98312 | tf_op jit(solution)/shard_map/ppermute | solution.py:228
  54.4 4.0 %collective-permute-start.11 = (bf16[4,16,256]{2,1,0:T(8,128)(2,1)S(1)}, bf16[4,16,256]{2,1,0:T(8,128)(2,1)S(1)}, u32[]{:S(2)}, u32[]{:S(2)}) collective-permute-start(bf16[4,16,256]{2,1,0:T(8,128)(2,1)S(1)} %get-tuple-element.54), channel_id=1, source_target_pairs={{0,128},{32,160},{64,192},{96,224},{128,0},{160,32},{192,64},{224,... | collective-permute-start | bytes 98312 | tf_op jit(solution)/shard_map/ppermute | solution.py:228
  58.4 0.0 collective-permute-done.14.p1
  58.4 2.4 %collective-permute-start.12 = (bf16[4,16,256]{2,1,0:T(8,128)(2,1)S(1)}, bf16[4,16,256]{2,1,0:T(8,128)(2,1)S(1)}, u32[]{:S(2)}, u32[]{:S(2)}) collective-permute-start(bf16[4,16,256]{2,1,0:T(8,128)(2,1)S(1)} %get-tuple-element.55), channel_id=1, source_target_pairs={{0,192},{32,224},{64,0},{96,32},{128,64},{160,96},{192,128},{224,1... | collective-permute-start | bytes 98312 | tf_op jit(solution)/shard_map/ppermute | solution.py:228
  60.8 0.0 collective-permute-done.15.p2
  60.8 0.0 collective-permute-done.16.p3
  60.8 0.0 collective-permute-done.10.d1
  60.8 1.5 %collective-permute-done.11.d2 = bf16[4,16,256]{2,1,0:T(8,128)(2,1)S(1)} collective-permute-done((bf16[4,16,256]{2,1,0:T(8,128)(2,1)S(1)}, bf16[4,16,256]{2,1,0:T(8,128)(2,1)S(1)}, u32[]{:S(2)}, u32[]{:S(2)}) %collective-permute-start.11) | collective-permute-done | bytes 32800 | tf_op jit(solution)/shard_map/ppermute | solution.py:228
  62.3 1.6 %collective-permute-done.12.d3 = bf16[4,16,256]{2,1,0:T(8,128)(2,1)S(1)} collective-permute-done((bf16[4,16,256]{2,1,0:T(8,128)(2,1)S(1)}, bf16[4,16,256]{2,1,0:T(8,128)(2,1)S(1)}, u32[]{:S(2)}, u32[]{:S(2)}) %collective-permute-start.12) | collective-permute-done | bytes 32800 | tf_op jit(solution)/shard_map/ppermute | solution.py:228
  63.9 0.8 %last_sum.1 = (bf16[256,256]{1,0:T(8,128)(2,1)}, bf16[256,256]{1,0:T(8,128)(2,1)}, f32[4,16,256]{2,1,0:T(8,128)}) custom-call(f32[4,16,256]{2,1,0:T(8,128)S(1)} %get-tuple-element.52.d0, bf16[4,16,256]{2,1,0:T(8,128)(2,1)S(1)} %collective-permute-done.10.d1, bf16[4,16,256]{2,1,0:T(8,128)(2,1)S(1)} %collective-permute-done.11.d2, ...), custom_call_target="tpu_custom_call" | custom-call | bytes 1000000 | tf_op jit(solution)/shard_map/last_sum/pallas_call | solution.py:213
  (1 shorter events, 0.0 us)
Async XLA Ops:
  0.6 14.1 %collective-permute-start = (bf16[256,1024]{1,0:T(8,128)(2,1)}, bf16[256,1024]{1,0:T(8,128)(2,1)S(1)}, u32[]{:S(2)}, u32[]{:S(2)}) collective-permute-start(bf16[256,1024]{1,0:T(8,128)(2,1)} %act.1), channel_id=1, source_target_pairs={{4,8},{8,4},{12,16},{16,12},{20,24},{24,20},{28,32},{32,28},{36,40... | collective-permute-start | bytes 1572872 | tf_op jit(solution)/shard_map/ppermute | solution.py:228
  1.3 13.4 %collective-permute-start.1 = (bf16[256,1024]{1,0:T(8,128)(2,1)}, bf16[256,1024]{1,0:T(8,128)(2,1)S(1)}, u32[]{:S(2)}, u32[]{:S(2)}) collective-permute-start(bf16[256,1024]{1,0:T(8,128)(2,1)} %act.1), channel_id=1, source_target_pairs={{0,4},{4,0},{8,12},{12,8},{16,20},{20,16},{24,28},{28,24},{32,36},... | collective-permute-start | bytes 1572872 | tf_op jit(solution)/shard_map/ppermute | solution.py:228
  4.3 7.2 %collective-permute-start.2 = (bf16[256,256]{1,0:T(8,128)(2,1)}, bf16[256,256]{1,0:T(8,128)(2,1)S(1)}, u32[]{:S(2)}, u32[]{:S(2)}) collective-permute-start(bf16[256,256]{1,0:T(8,128)(2,1)} %cot.1), channel_id=1, source_target_pairs={{0,1},{1,2},{2,3},{3,0},{4,5},{5,6},{6,7},{7,4},{8,9},{9,10},{10,1... | collective-permute-start | bytes 393224 | tf_op jit(solution)/shard_map/ppermute | solution.py:228
  5.8 6.0 %collective-permute-start.4 = (bf16[256,256]{1,0:T(8,128)(2,1)}, bf16[256,256]{1,0:T(8,128)(2,1)S(1)}, u32[]{:S(2)}, u32[]{:S(2)}) collective-permute-start(bf16[256,256]{1,0:T(8,128)(2,1)} %cot.1), channel_id=1, source_target_pairs={{0,3},{1,0},{2,1},{3,2},{4,7},{5,4},{6,5},{7,6},{8,11},{9,8},{10,9... | collective-permute-start | bytes 393224 | tf_op jit(solution)/shard_map/ppermute | solution.py:228
  6.4 8.3 %collective-permute-start.3 = (bf16[256,256]{1,0:T(8,128)(2,1)}, bf16[256,256]{1,0:T(8,128)(2,1)S(1)}, u32[]{:S(2)}, u32[]{:S(2)}) collective-permute-start(bf16[256,256]{1,0:T(8,128)(2,1)} %cot.1), channel_id=1, source_target_pairs={{0,2},{1,3},{2,0},{3,1},{4,6},{5,7},{6,4},{7,5},{8,10},{9,11},{10,... | collective-permute-start | bytes 393224 | tf_op jit(solution)/shard_map/ppermute | solution.py:228
  20.6 3.1 %collective-permute-start.5 = (bf16[160,16,256]{2,1,0:T(8,128)(2,1)S(1)}, bf16[160,16,256]{2,1,0:T(8,128)(2,1)S(1)}, u32[]{:S(2)}, u32[]{:S(2)}) collective-permute-start(bf16[160,16,256]{2,1,0:T(8,128)(2,1)S(1)} %get-tuple-element.45), channel_id=1, source_target_pairs={{0,4},{4,0},{8,12},{12,8},{16,20},{20,16},{24,28},{28,24},{32,36},... | collective-permute-start | bytes 3932168 | tf_op jit(solution)/shard_map/ppermute | solution.py:228
  20.7 8.9 %collective-permute-start.13 = (bf16[2,256,256]{2,1,0:T(8,128)(2,1)S(1)}, bf16[2,256,256]{2,1,0:T(8,128)(2,1)S(1)}, u32[]{:S(2)}, u32[]{:S(2)}) collective-permute-start(bf16[2,256,256]{2,1,0:T(8,128)(2,1)S(1)} %get-tuple-element.59), channel_id=1, source_target_pairs={{4,8},{8,4},{12,16},{16,12},{20,24},{24,20},{28,32},{32,28},{36,40... | collective-permute-start | bytes 786440 | tf_op jit(solution)/shard_map/ppermute | solution.py:228
  24.0 10.1 %collective-permute-start.6 = (bf16[32,16,256]{2,1,0:T(8,128)(2,1)S(1)}, bf16[32,16,256]{2,1,0:T(8,128)(2,1)S(1)}, u32[]{:S(2)}, u32[]{:S(2)}) collective-permute-start(bf16[32,16,256]{2,1,0:T(8,128)(2,1)S(1)} %get-tuple-element.47), channel_id=1, source_target_pairs={{0,8},{8,16},{16,24},{24,0},{1,9},{9,17},{17,25},{25,1},{2,10},{10... | collective-permute-start | bytes 786440 | tf_op jit(solution)/shard_map/ppermute | solution.py:228
  25.6 15.7 %collective-permute-start.7 = (bf16[32,16,256]{2,1,0:T(8,128)(2,1)S(1)}, bf16[32,16,256]{2,1,0:T(8,128)(2,1)S(1)}, u32[]{:S(2)}, u32[]{:S(2)}) collective-permute-start(bf16[32,16,256]{2,1,0:T(8,128)(2,1)S(1)} %get-tuple-element.48), channel_id=1, source_target_pairs={{0,16},{8,24},{16,0},{24,8},{1,17},{9,25},{17,1},{25,9},{2,18},{10... | collective-permute-start | bytes 786440 | tf_op jit(solution)/shard_map/ppermute | solution.py:228
  28.5 14.0 %collective-permute-start.8 = (bf16[32,16,256]{2,1,0:T(8,128)(2,1)S(1)}, bf16[32,16,256]{2,1,0:T(8,128)(2,1)S(1)}, u32[]{:S(2)}, u32[]{:S(2)}) collective-permute-start(bf16[32,16,256]{2,1,0:T(8,128)(2,1)S(1)} %get-tuple-element.49), channel_id=1, source_target_pairs={{0,24},{8,0},{16,8},{24,16},{1,25},{9,1},{17,9},{25,17},{2,26},{10... | collective-permute-start | bytes 786440 | tf_op jit(solution)/shard_map/ppermute | solution.py:228
  30.3 28.1 %collective-permute-start.14 = (bf16[2,256,256]{2,1,0:T(8,128)(2,1)S(1)}, bf16[2,256,256]{2,1,0:T(8,128)(2,1)S(1)}, u32[]{:S(2)}, u32[]{:S(2)}) collective-permute-start(bf16[2,256,256]{2,1,0:T(8,128)(2,1)S(1)} %get-tuple-element.62), channel_id=1, source_target_pairs={{0,1},{1,2},{2,3},{3,0},{4,5},{5,6},{6,7},{7,4},{8,9},{9,10},{10,1... | collective-permute-start | bytes 786440 | tf_op jit(solution)/shard_map/ppermute | solution.py:228
  30.4 30.4 %collective-permute-start.15 = (bf16[2,256,256]{2,1,0:T(8,128)(2,1)S(1)}, bf16[2,256,256]{2,1,0:T(8,128)(2,1)S(1)}, u32[]{:S(2)}, u32[]{:S(2)}) collective-permute-start(bf16[2,256,256]{2,1,0:T(8,128)(2,1)S(1)} %get-tuple-element.63), channel_id=1, source_target_pairs={{0,2},{1,3},{2,0},{3,1},{4,6},{5,7},{6,4},{7,5},{8,10},{9,11},{10,... | collective-permute-start | bytes 786440 | tf_op jit(solution)/shard_map/ppermute | solution.py:228
  34.1 26.7 %collective-permute-start.16 = (bf16[2,256,256]{2,1,0:T(8,128)(2,1)S(1)}, bf16[2,256,256]{2,1,0:T(8,128)(2,1)S(1)}, u32[]{:S(2)}, u32[]{:S(2)}) collective-permute-start(bf16[2,256,256]{2,1,0:T(8,128)(2,1)S(1)} %get-tuple-element.64), channel_id=1, source_target_pairs={{0,3},{1,0},{2,1},{3,2},{4,7},{5,4},{6,5},{7,6},{8,11},{9,8},{10,9... | collective-permute-start | bytes 786440 | tf_op jit(solution)/shard_map/ppermute | solution.py:228
  42.7 6.2 %collective-permute-start.9 = (bf16[16,16,256]{2,1,0:T(8,128)(2,1)S(1)}, bf16[16,16,256]{2,1,0:T(8,128)(2,1)S(1)}, u32[]{:S(2)}, u32[]{:S(2)}) collective-permute-start(bf16[16,16,256]{2,1,0:T(8,128)(2,1)S(1)} %get-tuple-element.51), channel_id=1, source_target_pairs={{0,32},{32,0},{64,96},{96,64},{128,160},{160,128},{192,224},{224,1... | collective-permute-start | bytes 393224 | tf_op jit(solution)/shard_map/ppermute | solution.py:228
  48.9 11.9 %collective-permute-start.10 = (bf16[4,16,256]{2,1,0:T(8,128)(2,1)S(1)}, bf16[4,16,256]{2,1,0:T(8,128)(2,1)S(1)}, u32[]{:S(2)}, u32[]{:S(2)}) collective-permute-start(bf16[4,16,256]{2,1,0:T(8,128)(2,1)S(1)} %get-tuple-element.53), channel_id=1, source_target_pairs={{0,64},{32,96},{64,128},{96,160},{128,192},{160,224},{192,0},{224,... | collective-permute-start | bytes 98312 | tf_op jit(solution)/shard_map/ppermute | solution.py:228
  54.4 7.9 %collective-permute-start.11 = (bf16[4,16,256]{2,1,0:T(8,128)(2,1)S(1)}, bf16[4,16,256]{2,1,0:T(8,128)(2,1)S(1)}, u32[]{:S(2)}, u32[]{:S(2)}) collective-permute-start(bf16[4,16,256]{2,1,0:T(8,128)(2,1)S(1)} %get-tuple-element.54), channel_id=1, source_target_pairs={{0,128},{32,160},{64,192},{96,224},{128,0},{160,32},{192,64},{224,... | collective-permute-start | bytes 98312 | tf_op jit(solution)/shard_map/ppermute | solution.py:228
  58.4 5.5 %collective-permute-start.12 = (bf16[4,16,256]{2,1,0:T(8,128)(2,1)S(1)}, bf16[4,16,256]{2,1,0:T(8,128)(2,1)S(1)}, u32[]{:S(2)}, u32[]{:S(2)}) collective-permute-start(bf16[4,16,256]{2,1,0:T(8,128)(2,1)S(1)} %get-tuple-element.55), channel_id=1, source_target_pairs={{0,192},{32,224},{64,0},{96,32},{128,64},{160,96},{192,128},{224,1... | collective-permute-start | bytes 98312 | tf_op jit(solution)/shard_map/ppermute | solution.py:228

commit v3 on v2

--- a/solution.py
+++ b/solution.py
@@ -47,8 +47,37 @@
     return jnp.where(count > 0, jnp.where(count > 1, jnp.log(count) * LOG2E, 0.0), -1e30)
 
 
+def y_pair(y):
+    return y + 1 - 2 * (y % 2)
+
+
+def y_other(y):
+    return 3 - y
+
+
+def z_pair(z):
+    return z + 1 - 2 * (z % 2)
+
+
+def z_other(z):
+    return (z + 7 + 2 * (z % 2)) % 8
+
+
+def z_far(z):
+    ends = (z % 4) * (3 - z % 4) // 2
+    return (1 - ends) * (3 - 2 * (z % 4) + z) + ends * (7 - z)
+
+
+def target_row(y, z, y_bits, z_bits):
+    for bit, partner in zip(y_bits, (y_pair, y_other)):
+        y = partner(y) if bit else y
+    for bit, partner in zip(z_bits, (z_pair, z_other, z_far)):
+        z = partner(z) if bit else z
+    return z * 4 + y
+
+
 def columns(ref, x, step):
-    return ref[:, pl.ds(pl.multiple_of(lax.rem(x + step, 4) * WIDTH, WIDTH), WIDTH)]
+    return ref[:, pl.ds(pl.multiple_of((x ^ step) * WIDTH, WIDTH), WIDTH)]
 
 
 def own_kernel(
@@ -91,7 +120,7 @@
         key_s[rows, :] = mm(block[...], wk[...]).astype(BF)
         value_s[rows, :] = mm(block[...], wv[...]).astype(BF)
     grad_att = grad_in[...]
-    for step, block in ((3, c1), (2, c2), (1, c3)):
+    for step, block in ((1, c1), (2, c2), (3, c3)):
         grad_att += mm(block[...], columns(wo, x, step), NT)
     grad_att = grad_att.astype(BF)
 
@@ -143,27 +172,22 @@
         dw_s[index] = (
             mm(act_t[...], grad[own]) + mm(far_t, grad[:ROW]) + mm(near_t, grad[2 * ROW :])
         )
-    for step, block_t in ((0, cot_t[...]), (3, c1[...].T), (2, c2[...].T), (1, c3[...].T)):
-        rows = pl.ds(pl.multiple_of(lax.rem(x + step, 4) * WIDTH, WIDTH), WIDTH)
+    for step, block_t in ((0, cot_t[...]), (1, c1[...].T), (2, c2[...].T), (3, c3[...].T)):
+        rows = pl.ds(pl.multiple_of((x ^ step) * WIDTH, WIDTH), WIDTH)
         dw_s[3, rows, :] = mm(block_t, att)
-    for mine, out in ((0, send_out), (1, keep_out)):
-        c = core if mine else 1 - core
-        for ys in range(4):
-            yy = lax.rem(y + ys, 4)
-            for low in range(2):
-                for hs in range(4):
-                    zl = lax.rem(z, 2)
-                    zl = zl if low else 1 - zl
-                    zz = 2 * lax.rem(z // 2 + hs, 4) + zl
-                    row = pl.multiple_of(((zz * 4 + yy) * 2 + c) * 16, 16)
-                    block = ((ys * 2 + low) * 4 + hs) * 4
-                    out[block : block + 4] = dw_s[:, pl.ds(row, 16), :].astype(BF)
-
-
-def core_sum_kernel(keep, got, o0, o1, o2, o3):
-    for step, out in enumerate((o0, o1, o2, o3)):
-        part = slice(32 * step, 32 * (step + 1))
-        out[...] = (keep[part].astype(F32) + got[part].astype(F32)).astype(out.dtype)
+    for c, out in ((1 - core, send_out), (core, keep_out)):
+        for path in range(32):
+            s1, s2, s3, s4, s5 = ((path >> (4 - step)) & 1 for step in range(5))
+            y_first = target_row(y, z, (s1, s3), (s2, s4, s5))
+            z_first = target_row(y, z, (s2, s4), (s1, s3, s5))
+            row = jnp.where(c == 0, y_first, z_first) * 32 + c * 16
+            out[4 * path : 4 * path + 4] = dw_s[:, pl.ds(pl.multiple_of(row, 16), 16), :].astype(BF)
+
+
+def halve_kernel(kept, got, send, keep):
+    half = send.shape[0]
+    for part, out in ((slice(0, half), keep), (slice(half, 2 * half), send)):
+        out[...] = (kept[part].astype(F32) + got[part].astype(F32)).astype(out.dtype)
 
 
 def input_kernel(att, gq, own, near, far, wq, wk, wv, wo, p0, p1, p2, p3):
@@ -174,7 +198,7 @@
         grads.append((own[part] + from_near.astype(F32) + far[part].astype(F32)).astype(BF))
     grad_key, grad_value = grads
     for step, out in enumerate((p0, p1, p2, p3)):
-        block = pl.ds(pl.multiple_of(lax.rem(x + step, 4) * WIDTH, WIDTH), WIDTH)
+        block = pl.ds(pl.multiple_of((x ^ step) * WIDTH, WIDTH), WIDTH)
         out[0] = mm(att[...], wo[:, block]).astype(out.dtype)
         out[1] = (
             mm(gq[...], wq[block, :], NT)
@@ -183,20 +207,8 @@
         ).astype(out.dtype)
 
 
-def y_sum_kernel(a, b, c, d, send, keep):
-    for part, out in ((slice(0, 16), send), (slice(16, 32), keep)):
-        total = (a[part].astype(F32) + b[part].astype(F32)) + (c[part].astype(F32) + d[part].astype(F32))
-        out[...] = total.astype(out.dtype)
-
-
-def pair_sum_kernel(keep, got, o0, o1, o2, o3):
-    for step, out in enumerate((o0, o1, o2, o3)):
-        part = slice(4 * step, 4 * (step + 1))
-        out[...] = (keep[part].astype(F32) + got[part].astype(F32)).astype(out.dtype)
-
-
-def last_sum_kernel(d0, d1, d2, d3, p0, p1, p2, p3, out, grad, dw):
-    dw[...] = (d0[...] + d1[...].astype(F32)) + (d2[...].astype(F32) + d3[...].astype(F32))
+def last_sum_kernel(kept, got, p0, p1, p2, p3, out, grad, dw):
+    dw[...] = kept[...] + got[...].astype(F32)
     for part, ref in ((0, out), (1, grad)):
         total = (p0[part] + p1[part].astype(F32)) + (p2[part].astype(F32) + p3[part].astype(F32))
         ref[...] = total.astype(BF)
@@ -230,9 +242,8 @@
     )
 
 
-def ring(value, axis, steps):
-    count = lax.axis_size(axis)
-    return move(value, axis, lambda i: (i + steps) % count)
+def across(value, step):
+    return move(value, "mp", lambda i: i ^ step)
 
 
 def near_row(value):
@@ -245,7 +256,7 @@
 
 def body(activations, w_query, w_key, w_value, w_out, grad_output, neighbours, pad_mask):
     act_far = far_row(activations)
-    cots = [ring(grad_output, "mp", s) for s in (1, 2, 3)]
+    cots = [across(grad_output, s) for s in (1, 2, 3)]
     act_near = near_row(activations)
 
     square = (ROW, WIDTH)
@@ -290,10 +301,34 @@
         moved=8_000_000,
     )
 
+    def halve(kept, got, kept_as):
+        half = (kept.shape[0] // 2,) + block
+        return call(halve_kernel, "halve", [(half, BF), (half, kept_as)], [kept, got])
+
+    def over_chips(value, core0, core1):
+        def target(i):
+            z, y, c = i // 8, i // 2 % 4, i % 2
+            return ((core0, core1)[c](z, y)) * 2 + c
+
+        return move(value, SPACE, target)
+
+    def along_y(partner):
+        return lambda z, y: z * 4 + partner(y)
+
+    def along_z(partner):
+        return lambda z, y: partner(z) * 4 + y
+
+    steps = (
+        (along_y(y_pair), along_z(z_pair)),
+        (along_z(z_pair), along_y(y_pair)),
+        (along_y(y_other), along_z(z_other)),
+        (along_z(z_other), along_y(y_other)),
+        (along_z(z_far), along_z(z_far)),
+    )
     got = near_row(dw_send)
     grad_far = far_row(far)
-    dw = call(core_sum_kernel, "core_sum", [((32,) + block, BF)] * 4, [dw_keep, got])
-    dw_y = [dw[0]] + [ring(dw[s], "y", s) for s in (1, 2, 3)]
+    send, keep = halve(dw_keep, got, BF)
+    arrived = over_chips(send, *steps[0])
 
     piece = (2, ROW, WIDTH)
     pieces = call(
@@ -304,19 +339,16 @@
         flops=540_000_000,
         moved=4_000_000,
     )
-    outs = [pieces[0]] + [ring(pieces[s], "mp", s) for s in (1, 2, 3)]
-
-    send, keep = call(y_sum_kernel, "y_sum", [((16,) + block, BF)] * 2, dw_y)
-    pair = move(send, "z", lambda i: i ^ 1)
-    dw = call(
-        pair_sum_kernel, "pair_sum", [((4,) + block, F32)] + [((4,) + block, BF)] * 3, [keep, pair]
-    )
-    dw_z = [dw[0]] + [ring(dw[s], "z", 2 * s) for s in (1, 2, 3)]
+    outs = [pieces[0]] + [across(pieces[s], s) for s in (1, 2, 3)]
+
+    for step in steps[1:]:
+        send, keep = halve(keep, arrived, F32)
+        arrived = over_chips(send, *step)
     return call(
         last_sum_kernel,
         "last_sum",
-        [((ROW, WIDTH), BF), ((ROW, WIDTH), BF), ((4,) + block, F32)],
-        dw_z + outs,
+        [(square, BF), (square, BF), ((4,) + block, F32)],
+        [keep, arrived] + outs,
         keep=False,
     )
 

time: 64.9 us -> 65.3 us (level)
  the two profiles are of different devices: /device:TPU:2 before, /device:TPU:56 now
where the time goes in v3:
time: 65.3 us; the launch traced here: 65.2 us
  waiting for transfers between devices  31.5 us (48%)
  starting transfers between devices  22.1 us (34%)
  Pallas kernels  10.9 us (17%)
  between operations  0.75 us (1%)
    ppermute x15, waiting for transfers between devices, move(): lax.ppermute(value, axis, [(i, target(i)) for i in range(count) if 0 <= t...  31.5 us
    ppermute x15, starting transfers between devices, move(): lax.ppermute(value, axis, [(i, target(i)) for i in range(count) if 0 <= t...  22.1 us
    pallas_call x9, Pallas kernels, call(): pl.pallas_call(kernel, out_shape=tuple(kept), in_specs=[pl.BlockSpec(memo...  10.9 us
  transfers between devices with their start and end apart: 15, of which 7 were waited for; matrix products, arithmetic and copies ran while one was open for 0% of the time, Pallas kernels for 6%

profile of v3, /device:TPU:56, one launch (start us, length us, event | category | flops | bytes accessed | tf_op | source)
XLA Modules:
  0.0 65.2 jit_solution(8535489551843489810)
XLA Ops:
  0.6 2.1 %collective-permute-start = (bf16[256,1024]{1,0:T(8,128)(2,1)}, bf16[256,1024]{1,0:T(8,128)(2,1)S(1)}, u32[]{:S(2)}, u32[]{:S(2)}) collective-permute-start(bf16[256,1024]{1,0:T(8,128)(2,1)} %act.1), channel_id=1, source_target_pairs={{4,8},{8,4},{12,16},{16,12},{20,24},{24,20},{28,32},{32,28},{36,40... | collective-permute-start | bytes 1572872 | tf_op jit(solution)/shard_map/ppermute | solution.py:240
  2.7 1.6 %collective-permute-start.1 = (bf16[256,1024]{1,0:T(8,128)(2,1)}, bf16[256,1024]{1,0:T(8,128)(2,1)S(1)}, u32[]{:S(2)}, u32[]{:S(2)}) collective-permute-start(bf16[256,1024]{1,0:T(8,128)(2,1)} %act.1), channel_id=1, source_target_pairs={{0,4},{4,0},{8,12},{12,8},{16,20},{20,16},{24,28},{28,24},{32,36},... | collective-permute-start | bytes 1572872 | tf_op jit(solution)/shard_map/ppermute | solution.py:240
  4.3 1.5 %collective-permute-start.2 = (bf16[256,256]{1,0:T(8,128)(2,1)}, bf16[256,256]{1,0:T(8,128)(2,1)S(1)}, u32[]{:S(2)}, u32[]{:S(2)}) collective-permute-start(bf16[256,256]{1,0:T(8,128)(2,1)} %cot.1), channel_id=1, source_target_pairs={{0,1},{1,0},{2,3},{3,2},{4,5},{5,4},{6,7},{7,6},{8,9},{9,8},{10,11... | collective-permute-start | bytes 393224 | tf_op jit(solution)/shard_map/ppermute | solution.py:240
  5.8 2.1 %collective-permute-start.4 = (bf16[256,256]{1,0:T(8,128)(2,1)}, bf16[256,256]{1,0:T(8,128)(2,1)S(1)}, u32[]{:S(2)}, u32[]{:S(2)}) collective-permute-start(bf16[256,256]{1,0:T(8,128)(2,1)} %cot.1), channel_id=1, source_target_pairs={{0,3},{1,2},{2,1},{3,0},{4,7},{5,6},{6,5},{7,4},{8,11},{9,10},{10,... | collective-permute-start | bytes 393224 | tf_op jit(solution)/shard_map/ppermute | solution.py:240
  7.9 0.6 collective-permute-start.3
  8.6 3.0 %own_part.1 = (bf16[1024,256]{1,0:T(8,128)(2,1)S(1)}, bf16[1024,256]{1,0:T(8,128)(2,1)S(1)}, bf16[1024,256]{1,0:T(8,128)(2,1)S(1)}, bf16[256,1024]{1,0:T(8,128)(...) custom-call(bf16[256,1024]{1,0:T(8,128)(2,1)} %act.1, ...), custom_call_target="tpu_custom_call" | custom-call | flops 600000000 | bytes 6000000 | tf_op jit(solution)/shard_map/own_part/pallas_call | solution.py:225
  11.6 0.0 collective-permute-done.2.c1
  11.6 3.7 %collective-permute-done.4.c3 = bf16[256,256]{1,0:T(8,128)(2,1)S(1)} collective-permute-done((bf16[256,256]{1,0:T(8,128)(2,1)}, bf16[256,256]{1,0:T(8,128)(2,1)S(1)}, u32[]{:S(2)}, u32[]{:S(2)}) %collective-permute-start.4) | collective-permute-done | bytes 131104 | tf_op jit(solution)/shard_map/ppermute | solution.py:240
  15.3 0.0 collective-permute-done.3.c2
  15.3 0.0 collective-permute-done.a_far
  15.3 0.0 collective-permute-done.1.a_near
  15.3 5.9 %attention.1 = (bf16[256,256]{1,0:T(8,128)(2,1)S(1)}, bf16[256,256]{1,0:T(8,128)(2,1)S(1)}, bf16[2,256,256]{2,1,0:T(8,128)(2,1)S(1)}, f32[2,256,256]{2,1,0:T(8,1...) custom-call(bf16[256,1024]{1,0:T(8,128)(2,1)S(1)} %collective-permute-done.a_far, ...), custom_call_target="tpu_custom_call" | custom-call | flops 4000000000 | bytes 8000000 | tf_op jit(solution)/shard_map/attention/pallas_call | solution.py:225
  21.2 0.1 collective-permute-start.5
  21.3 3.0 %collective-permute-done.5.got.near = bf16[160,16,256]{2,1,0:T(8,128)(2,1)S(1)} collective-permute-done((bf16[160,16,256]{2,1,0:T(8,128)(2,1)S(1)}, bf16[160,16,256]{2,1,0:T(8,128)(2,1)S(1)}, u32[]{:S(2)}, u32[]{:S(2)}) %collective-permute-start.5) | collective-permute-done | bytes 1310752 | tf_op jit(solution)/shard_map/ppermute | solution.py:240
  24.3 0.2 halve.5
  24.5 0.5 collective-permute-start.6
  25.1 1.9 %collective-permute-start.11 = (bf16[2,256,256]{2,1,0:T(8,128)(2,1)S(1)}, bf16[2,256,256]{2,1,0:T(8,128)(2,1)S(1)}, u32[]{:S(2)}, u32[]{:S(2)}) collective-permute-start(bf16[2,256,256]{2,1,0:T(8,128)(2,1)S(1)} %get-tuple-element.59), channel_id=1, source_target_pairs={{4,8},{8,4},{12,16},{16,12},{20,24},{24,20},{28,32},{32,28},{36,40... | collective-permute-start | bytes 786440 | tf_op jit(solution)/shard_map/ppermute | solution.py:240
  27.0 10.3 %collective-permute-done.6.got = bf16[64,16,256]{2,1,0:T(8,128)(2,1)S(1)} collective-permute-done((bf16[64,16,256]{2,1,0:T(8,128)(2,1)S(1)}, bf16[64,16,256]{2,1,0:T(8,128)(2,1)S(1)}, u32[]{:S(2)}, u32[]{:S(2)}) %collective-permute-start.6) | collective-permute-done | bytes 524320 | tf_op jit(solution)/shard_map/ppermute | solution.py:240
  37.3 0.1 halve.6
  37.4 0.1 collective-permute-start.7
  37.5 0.0 collective-permute-done.11.far
  37.5 0.7 %input_grad.1 = (f32[2,256,256]{2,1,0:T(8,128)S(1)}, bf16[2,256,256]{2,1,0:T(8,128)(2,1)S(1)}, bf16[2,256,256]{2,1,0:T(8,128)(2,1)S(1)}, bf16[2,256,256]{2,1,0:T(8,128)(2,1)S(1)}) custom-call(bf16[256,256]{1,0:T(8,128)(2,1)S(1)} %get-tuple-element.56.att, bf16[256,256]{1,0:T(8,128)(2,1)S(1)} %get-tuple-element.57.gq, ...), custom_call_target="tpu_custom_call" | custom-call | flops 540000000 | bytes 4000000 | tf_op jit(solution)/shard_map/input_grad/pallas_call | solution.py:225
  38.2 0.3 collective-permute-start.12
  38.5 3.6 %collective-permute-start.13 = (bf16[2,256,256]{2,1,0:T(8,128)(2,1)S(1)}, bf16[2,256,256]{2,1,0:T(8,128)(2,1)S(1)}, u32[]{:S(2)}, u32[]{:S(2)}) collective-permute-start(bf16[2,256,256]{2,1,0:T(8,128)(2,1)S(1)} %get-tuple-element.63), channel_id=1, source_target_pairs={{0,2},{1,3},{2,0},{3,1},{4,6},{5,7},{6,4},{7,5},{8,10},{9,11},{10,... | collective-permute-start | bytes 786440 | tf_op jit(solution)/shard_map/ppermute | solution.py:240
  42.1 1.1 %collective-permute-start.14 = (bf16[2,256,256]{2,1,0:T(8,128)(2,1)S(1)}, bf16[2,256,256]{2,1,0:T(8,128)(2,1)S(1)}, u32[]{:S(2)}, u32[]{:S(2)}) collective-permute-start(bf16[2,256,256]{2,1,0:T(8,128)(2,1)S(1)} %get-tuple-element.64), channel_id=1, source_target_pairs={{0,3},{1,2},{2,1},{3,0},{4,7},{5,6},{6,5},{7,4},{8,11},{9,10},{10,... | collective-permute-start | bytes 786440 | tf_op jit(solution)/shard_map/ppermute | solution.py:240
  43.2 0.6 collective-permute-done.7.got
  43.9 0.4 collective-permute-start.8
  44.3 5.9 %collective-permute-done.8.got = bf16[16,16,256]{2,1,0:T(8,128)(2,1)S(1)} collective-permute-done((bf16[16,16,256]{2,1,0:T(8,128)(2,1)S(1)}, bf16[16,16,256]{2,1,0:T(8,128)(2,1)S(1)}, u32[]{:S(2)}, u32[]{:S(2)}) %collective-permute-start.8) | collective-permute-done | bytes 131104 | tf_op jit(solution)/shard_map/ppermute | solution.py:240
  50.2 4.5 %collective-permute-start.9 = (bf16[8,16,256]{2,1,0:T(8,128)(2,1)S(1)}, bf16[8,16,256]{2,1,0:T(8,128)(2,1)S(1)}, u32[]{:S(2)}, u32[]{:S(2)}) collective-permute-start(bf16[8,16,256]{2,1,0:T(8,128)(2,1)S(1)} %get-tuple-element.53), channel_id=1, source_target_pairs={{0,224},{4,28},{8,232},{12,20},{16,240},{20,12},{24,248},{28,4},{3... | collective-permute-start | bytes 196616 | tf_op jit(solution)/shard_map/ppermute | solution.py:240
  54.7 2.6 %collective-permute-done.9.got = bf16[8,16,256]{2,1,0:T(8,128)(2,1)S(1)} collective-permute-done((bf16[8,16,256]{2,1,0:T(8,128)(2,1)S(1)}, bf16[8,16,256]{2,1,0:T(8,128)(2,1)S(1)}, u32[]{:S(2)}, u32[]{:S(2)}) %collective-permute-start.9) | collective-permute-done | bytes 65568 | tf_op jit(solution)/shard_map/ppermute | solution.py:240
  57.3 1.7 %collective-permute-start.10 = (bf16[4,16,256]{2,1,0:T(8,128)(2,1)S(1)}, bf16[4,16,256]{2,1,0:T(8,128)(2,1)S(1)}, u32[]{:S(2)}, u32[]{:S(2)}) collective-permute-start(bf16[4,16,256]{2,1,0:T(8,128)(2,1)S(1)} %get-tuple-element.55), channel_id=1, source_target_pairs={{0,96},{4,100},{8,104},{12,108},{16,112},{20,116},{24,120},{28,124... | collective-permute-start | bytes 98312 | tf_op jit(solution)/shard_map/ppermute | solution.py:240
  59.0 0.0 collective-permute-done.12.p1
  59.0 0.0 collective-permute-done.13.p2
  59.0 0.0 collective-permute-done.14.p3
  59.0 5.4 %collective-permute-done.10.got = bf16[4,16,256]{2,1,0:T(8,128)(2,1)S(1)} collective-permute-done((bf16[4,16,256]{2,1,0:T(8,128)(2,1)S(1)}, bf16[4,16,256]{2,1,0:T(8,128)(2,1)S(1)}, u32[]{:S(2)}, u32[]{:S(2)}) %collective-permute-start.10) | collective-permute-done | bytes 32800 | tf_op jit(solution)/shard_map/ppermute | solution.py:240
  64.4 0.8 %last_sum.1 = (bf16[256,256]{1,0:T(8,128)(2,1)}, bf16[256,256]{1,0:T(8,128)(2,1)}, f32[4,16,256]{2,1,0:T(8,128)}) custom-call(f32[4,16,256]{2,1,0:T(8,128)S(1)} %get-tuple-element.54.kept, bf16[4,16,256]{2,1,0:T(8,128)(2,1)S(1)} %collective-permute-done.10.got, f32[2,256,256]{2,1,0:T(8,128)S(1)} %get-tuple-element.61.p0, ...), custom_call_target="tpu_custom_call" | custom-call | bytes 1000000 | tf_op jit(solution)/shard_map/last_sum/pallas_call | solution.py:225
  (3 shorter events, 0.1 us)
Async XLA Ops:
  0.6 14.6 %collective-permute-start = (bf16[256,1024]{1,0:T(8,128)(2,1)}, bf16[256,1024]{1,0:T(8,128)(2,1)S(1)}, u32[]{:S(2)}, u32[]{:S(2)}) collective-permute-start(bf16[256,1024]{1,0:T(8,128)(2,1)} %act.1), channel_id=1, source_target_pairs={{4,8},{8,4},{12,16},{16,12},{20,24},{24,20},{28,32},{32,28},{36,40... | collective-permute-start | bytes 1572872 | tf_op jit(solution)/shard_map/ppermute | solution.py:240
  2.7 12.5 %collective-permute-start.1 = (bf16[256,1024]{1,0:T(8,128)(2,1)}, bf16[256,1024]{1,0:T(8,128)(2,1)S(1)}, u32[]{:S(2)}, u32[]{:S(2)}) collective-permute-start(bf16[256,1024]{1,0:T(8,128)(2,1)} %act.1), channel_id=1, source_target_pairs={{0,4},{4,0},{8,12},{12,8},{16,20},{20,16},{24,28},{28,24},{32,36},... | collective-permute-start | bytes 1572872 | tf_op jit(solution)/shard_map/ppermute | solution.py:240
  4.3 7.3 %collective-permute-start.2 = (bf16[256,256]{1,0:T(8,128)(2,1)}, bf16[256,256]{1,0:T(8,128)(2,1)S(1)}, u32[]{:S(2)}, u32[]{:S(2)}) collective-permute-start(bf16[256,256]{1,0:T(8,128)(2,1)} %cot.1), channel_id=1, source_target_pairs={{0,1},{1,0},{2,3},{3,2},{4,5},{5,4},{6,7},{7,6},{8,9},{9,8},{10,11... | collective-permute-start | bytes 393224 | tf_op jit(solution)/shard_map/ppermute | solution.py:240
  5.8 9.5 %collective-permute-start.4 = (bf16[256,256]{1,0:T(8,128)(2,1)}, bf16[256,256]{1,0:T(8,128)(2,1)S(1)}, u32[]{:S(2)}, u32[]{:S(2)}) collective-permute-start(bf16[256,256]{1,0:T(8,128)(2,1)} %cot.1), channel_id=1, source_target_pairs={{0,3},{1,2},{2,1},{3,0},{4,7},{5,6},{6,5},{7,4},{8,11},{9,10},{10,... | collective-permute-start | bytes 393224 | tf_op jit(solution)/shard_map/ppermute | solution.py:240
  7.9 7.4 %collective-permute-start.3 = (bf16[256,256]{1,0:T(8,128)(2,1)}, bf16[256,256]{1,0:T(8,128)(2,1)S(1)}, u32[]{:S(2)}, u32[]{:S(2)}) collective-permute-start(bf16[256,256]{1,0:T(8,128)(2,1)} %cot.1), channel_id=1, source_target_pairs={{0,2},{1,3},{2,0},{3,1},{4,6},{5,7},{6,4},{7,5},{8,10},{9,11},{10,... | collective-permute-start | bytes 393224 | tf_op jit(solution)/shard_map/ppermute | solution.py:240
  21.2 3.1 %collective-permute-start.5 = (bf16[160,16,256]{2,1,0:T(8,128)(2,1)S(1)}, bf16[160,16,256]{2,1,0:T(8,128)(2,1)S(1)}, u32[]{:S(2)}, u32[]{:S(2)}) collective-permute-start(bf16[160,16,256]{2,1,0:T(8,128)(2,1)S(1)} %get-tuple-element.45), channel_id=1, source_target_pairs={{0,4},{4,0},{8,12},{12,8},{16,20},{20,16},{24,28},{28,24},{32,36},... | collective-permute-start | bytes 3932168 | tf_op jit(solution)/shard_map/ppermute | solution.py:240
  24.5 12.7 %collective-permute-start.6 = (bf16[64,16,256]{2,1,0:T(8,128)(2,1)S(1)}, bf16[64,16,256]{2,1,0:T(8,128)(2,1)S(1)}, u32[]{:S(2)}, u32[]{:S(2)}) collective-permute-start(bf16[64,16,256]{2,1,0:T(8,128)(2,1)S(1)} %get-tuple-element.47), channel_id=1, source_target_pairs={{0,8},{4,36},{8,0},{12,44},{16,24},{20,52},{24,16},{28,60},{32,40}... | collective-permute-start | bytes 1572872 | tf_op jit(solution)/shard_map/ppermute | solution.py:240
  25.1 12.4 %collective-permute-start.11 = (bf16[2,256,256]{2,1,0:T(8,128)(2,1)S(1)}, bf16[2,256,256]{2,1,0:T(8,128)(2,1)S(1)}, u32[]{:S(2)}, u32[]{:S(2)}) collective-permute-start(bf16[2,256,256]{2,1,0:T(8,128)(2,1)S(1)} %get-tuple-element.59), channel_id=1, source_target_pairs={{4,8},{8,4},{12,16},{16,12},{20,24},{24,20},{28,32},{32,28},{36,40... | collective-permute-start | bytes 786440 | tf_op jit(solution)/shard_map/ppermute | solution.py:240
  37.4 6.5 %collective-permute-start.7 = (bf16[32,16,256]{2,1,0:T(8,128)(2,1)S(1)}, bf16[32,16,256]{2,1,0:T(8,128)(2,1)S(1)}, u32[]{:S(2)}, u32[]{:S(2)}) collective-permute-start(bf16[32,16,256]{2,1,0:T(8,128)(2,1)S(1)} %get-tuple-element.49), channel_id=1, source_target_pairs={{0,32},{4,12},{8,40},{12,4},{16,48},{20,28},{24,56},{28,20},{32,0}... | collective-permute-start | bytes 786440 | tf_op jit(solution)/shard_map/ppermute | solution.py:240
  38.2 20.8 %collective-permute-start.12 = (bf16[2,256,256]{2,1,0:T(8,128)(2,1)S(1)}, bf16[2,256,256]{2,1,0:T(8,128)(2,1)S(1)}, u32[]{:S(2)}, u32[]{:S(2)}) collective-permute-start(bf16[2,256,256]{2,1,0:T(8,128)(2,1)S(1)} %get-tuple-element.62), channel_id=1, source_target_pairs={{0,1},{1,0},{2,3},{3,2},{4,5},{5,4},{6,7},{7,6},{8,9},{9,8},{10,11... | collective-permute-start | bytes 786440 | tf_op jit(solution)/shard_map/ppermute | solution.py:240
  38.5 20.5 %collective-permute-start.13 = (bf16[2,256,256]{2,1,0:T(8,128)(2,1)S(1)}, bf16[2,256,256]{2,1,0:T(8,128)(2,1)S(1)}, u32[]{:S(2)}, u32[]{:S(2)}) collective-permute-start(bf16[2,256,256]{2,1,0:T(8,128)(2,1)S(1)} %get-tuple-element.63), channel_id=1, source_target_pairs={{0,2},{1,3},{2,0},{3,1},{4,6},{5,7},{6,4},{7,5},{8,10},{9,11},{10,... | collective-permute-start | bytes 786440 | tf_op jit(solution)/shard_map/ppermute | solution.py:240
  42.1 16.9 %collective-permute-start.14 = (bf16[2,256,256]{2,1,0:T(8,128)(2,1)S(1)}, bf16[2,256,256]{2,1,0:T(8,128)(2,1)S(1)}, u32[]{:S(2)}, u32[]{:S(2)}) collective-permute-start(bf16[2,256,256]{2,1,0:T(8,128)(2,1)S(1)} %get-tuple-element.64), channel_id=1, source_target_pairs={{0,3},{1,2},{2,1},{3,0},{4,7},{5,6},{6,5},{7,4},{8,11},{9,10},{10,... | collective-permute-start | bytes 786440 | tf_op jit(solution)/shard_map/ppermute | solution.py:240
  43.9 6.3 %collective-permute-start.8 = (bf16[16,16,256]{2,1,0:T(8,128)(2,1)S(1)}, bf16[16,16,256]{2,1,0:T(8,128)(2,1)S(1)}, u32[]{:S(2)}, u32[]{:S(2)}) collective-permute-start(bf16[16,16,256]{2,1,0:T(8,128)(2,1)S(1)} %get-tuple-element.51), channel_id=1, source_target_pairs={{0,24},{4,228},{8,16},{12,236},{16,8},{20,244},{24,0},{28,252},{32... | collective-permute-start | bytes 393224 | tf_op jit(solution)/shard_map/ppermute | solution.py:240
  50.2 7.1 %collective-permute-start.9 = (bf16[8,16,256]{2,1,0:T(8,128)(2,1)S(1)}, bf16[8,16,256]{2,1,0:T(8,128)(2,1)S(1)}, u32[]{:S(2)}, u32[]{:S(2)}) collective-permute-start(bf16[8,16,256]{2,1,0:T(8,128)(2,1)S(1)} %get-tuple-element.53), channel_id=1, source_target_pairs={{0,224},{4,28},{8,232},{12,20},{16,240},{20,12},{24,248},{28,4},{3... | collective-permute-start | bytes 196616 | tf_op jit(solution)/shard_map/ppermute | solution.py:240
  57.3 7.1 %collective-permute-start.10 = (bf16[4,16,256]{2,1,0:T(8,128)(2,1)S(1)}, bf16[4,16,256]{2,1,0:T(8,128)(2,1)S(1)}, u32[]{:S(2)}, u32[]{:S(2)}) collective-permute-start(bf16[4,16,256]{2,1,0:T(8,128)(2,1)S(1)} %get-tuple-element.55), channel_id=1, source_target_pairs={{0,96},{4,100},{8,104},{12,108},{16,112},{20,116},{24,120},{28,124... | collective-permute-start | bytes 98312 | tf_op jit(solution)/shard_map/ppermute | solution.py:240

commit v4 on v3

--- a/solution.py
+++ b/solution.py
@@ -64,15 +64,25 @@
 
 
 def z_far(z):
-    ends = (z % 4) * (3 - z % 4) // 2
-    return (1 - ends) * (3 - 2 * (z % 4) + z) + ends * (7 - z)
-
-
-def target_row(y, z, y_bits, z_bits):
-    for bit, partner in zip(y_bits, (y_pair, y_other)):
-        y = partner(y) if bit else y
-    for bit, partner in zip(z_bits, (z_pair, z_other, z_far)):
-        z = partner(z) if bit else z
+    middle = (z % 4) * (3 - z % 4) // 2
+    return (1 - middle) * (3 - 2 * (z % 4) + z) + middle * (7 - z)
+
+
+def z_far_too(z):
+    return z + 4 + (1 - 2 * (z % 2)) - 8 * (z // 4)
+
+
+def target_row(z, y, path, core, stream):
+    s1, s2, s3, s4, s5 = path
+    first, second = (s1, s2) if stream == core else (s2, s1)
+    if core == 0:
+        y_steps, z_steps = ((y_pair, first), (y_other, s3)), ((z_other, second), (z_pair, s4), (z_far_too, s5))
+    else:
+        y_steps, z_steps = ((y_other, first), (y_pair, s4)), ((z_pair, second), (z_other, s3), (z_far, s5))
+    for partner, sent in y_steps:
+        y = partner(y) if sent else y
+    for partner, sent in z_steps:
+        z = partner(z) if sent else z
     return z * 4 + y
 
 
@@ -106,55 +116,68 @@
     bias_out[...] = slot_bias(nb, mask, core, y, z)
 
 
-def attention_kernel(
-    a_far, a_near, wk, wv, wo, query_in, key_own, value_own, act_t, grad_in, cot_t, bias, c1, c2, c3,
-    att_out, gq_out, far_out, own_out, send_out, keep_out,
-    key_s, value_s, dw_s,
+def forward_kernel(
+    a_far, a_near, wk, wv, query, key_own, value_own, bias,
+    keys, values, probs_out, att_out, far_t, near_t,
+):
+    keys[ROW : 2 * ROW, :] = key_own[...]
+    values[ROW : 2 * ROW, :] = value_own[...]
+    for band, block in ((0, a_far), (2, a_near)):
+        rows = slice(band * ROW, (band + 1) * ROW)
+        keys[rows, :] = mm(block[...], wk[...]).astype(BF)
+        values[rows, :] = mm(block[...], wv[...]).astype(BF)
+    values_t = values[...].T
+    lane_head = lax.broadcasted_iota(jnp.int32, (ROW, WIDTH), 1) // HD
+    bias_rows = jnp.concatenate(
+        [jnp.broadcast_to(bias[patch : patch + 1, :], (PATCH, ROW)) for patch in range(KEYS // PATCH)],
+        axis=0,
+    )
+    att_rows = []
+    for head in range(HEADS):
+        feats = slice(head * HD, (head + 1) * HD)
+        q_head = jnp.where(lane_head == head, query[...], jnp.zeros((ROW, WIDTH), BF))
+        scores = mm(keys[...], q_head, NT) * (LOG2E * HD**-0.5) + bias_rows
+        peak = jnp.max(scores, axis=0, keepdims=True)
+        weights = jnp.exp2(scores - peak)
+        probs = weights * (1.0 / jnp.sum(weights, axis=0, keepdims=True))
+        probs_out[head] = probs
+        att_rows.append(mm(values_t[feats, :], probs.astype(BF)))
+    att_out[...] = jnp.concatenate(att_rows, axis=0).astype(BF).T
+    far_t[...] = a_far[...].T
+    near_t[...] = a_near[...].T
+
+
+def backward_kernel(
+    keys, values, probs_in, att, far_t, near_t, wo, query, act_t, grad_in, cot_t, c1, c2, c3,
+    gq_out, far_out, own_out, send_out, keep_out,
+    dw_s,
 ):
     core, y, z, x = places()
-    query = query_in[...]
-    key_s[ROW : 2 * ROW, :] = key_own[...]
-    value_s[ROW : 2 * ROW, :] = value_own[...]
-    for band, block in ((0, a_far), (2, a_near)):
-        rows = slice(band * ROW, (band + 1) * ROW)
-        key_s[rows, :] = mm(block[...], wk[...]).astype(BF)
-        value_s[rows, :] = mm(block[...], wv[...]).astype(BF)
     grad_att = grad_in[...]
     for step, block in ((1, c1), (2, c2), (3, c3)):
         grad_att += mm(block[...], columns(wo, x, step), NT)
     grad_att = grad_att.astype(BF)
-
-    keys = key_s[...]
-    values = value_s[...]
-    keys_t = keys.T
-    values_t = values.T
+    for step, block_t in ((0, cot_t[...]), (1, c1[...].T), (2, c2[...].T), (3, c3[...].T)):
+        rows = pl.ds(pl.multiple_of((x ^ step) * WIDTH, WIDTH), WIDTH)
+        dw_s[3, rows, :] = mm(block_t, att[...])
+
+    keys_t = keys[...].T
     lane_head = lax.broadcasted_iota(jnp.int32, (ROW, WIDTH), 1) // HD
-    bias_rows = jnp.concatenate(
-        [jnp.broadcast_to(bias[patch : patch + 1, :], (PATCH, ROW)) for patch in range(KEYS // PATCH)],
-        axis=0,
-    )
     grad_key = jnp.zeros((KEYS, WIDTH), F32)
     grad_value = jnp.zeros((KEYS, WIDTH), F32)
-    att_rows, gq_rows = [], []
+    gq_rows = []
     for head in range(HEADS):
         feats = slice(head * HD, (head + 1) * HD)
-        q_head = jnp.where(lane_head == head, query, jnp.zeros_like(query))
+        q_head = jnp.where(lane_head == head, query[...], jnp.zeros((ROW, WIDTH), BF))
         g_head = jnp.where(lane_head == head, grad_att, jnp.zeros_like(grad_att))
-        scores = mm(keys, q_head, NT) * (LOG2E * HD**-0.5) + bias_rows
-        peak = jnp.max(scores, axis=0, keepdims=True)
-        weights = jnp.exp2(scores - peak)
-        probs = weights * (1.0 / jnp.sum(weights, axis=0, keepdims=True))
-        probs_low = probs.astype(BF)
-        grad_probs = mm(values, g_head, NT)
+        probs = probs_in[head]
+        grad_probs = mm(values[...], g_head, NT)
         centre = jnp.sum(probs * grad_probs, axis=0, keepdims=True)
         grad_scores = (probs * (grad_probs - centre) * HD**-0.5).astype(BF)
-        att_rows.append(mm(values_t[feats, :], probs_low))
         gq_rows.append(mm(keys_t[feats, :], grad_scores))
         grad_key += mm(grad_scores, q_head)
-        grad_value += mm(probs_low, g_head)
-    att = jnp.concatenate(att_rows, axis=0).astype(BF).T
+        grad_value += mm(probs.astype(BF), g_head)
     gq = jnp.concatenate(gq_rows, axis=0).astype(BF).T
-    att_out[...] = att
     gq_out[...] = gq
     far_out[0], far_out[1] = grad_key[:ROW].astype(BF), grad_value[:ROW].astype(BF)
     own_out[0], own_out[1] = grad_key[ROW : 2 * ROW], grad_value[ROW : 2 * ROW]
@@ -166,28 +189,40 @@
     grad_key = grad_key.astype(BF)
     grad_value = grad_value.astype(BF)
     own = slice(ROW, 2 * ROW)
-    far_t, near_t = a_far[...].T, a_near[...].T
     dw_s[0] = mm(act_t[...], gq)
     for index, grad in ((1, grad_key), (2, grad_value)):
         dw_s[index] = (
-            mm(act_t[...], grad[own]) + mm(far_t, grad[:ROW]) + mm(near_t, grad[2 * ROW :])
+            mm(act_t[...], grad[own]) + mm(far_t[...], grad[:ROW]) + mm(near_t[...], grad[2 * ROW :])
         )
-    for step, block_t in ((0, cot_t[...]), (1, c1[...].T), (2, c2[...].T), (3, c3[...].T)):
-        rows = pl.ds(pl.multiple_of((x ^ step) * WIDTH, WIDTH), WIDTH)
-        dw_s[3, rows, :] = mm(block_t, att)
     for c, out in ((1 - core, send_out), (core, keep_out)):
-        for path in range(32):
-            s1, s2, s3, s4, s5 = ((path >> (4 - step)) & 1 for step in range(5))
-            y_first = target_row(y, z, (s1, s3), (s2, s4, s5))
-            z_first = target_row(y, z, (s2, s4), (s1, s3, s5))
-            row = jnp.where(c == 0, y_first, z_first) * 32 + c * 16
-            out[4 * path : 4 * path + 4] = dw_s[:, pl.ds(pl.multiple_of(row, 16), 16), :].astype(BF)
+        for number in range(32):
+            path = [(number >> (4 - step)) & 1 for step in range(5)]
+            for stream in range(2):
+                row0, row1 = (target_row(z, y, path, which, stream) for which in (0, 1))
+                row = pl.multiple_of(jnp.where(c == 0, row0, row1) * 32 + c * 16, 16)
+                block = 64 * stream + 2 * number
+                out[block : block + 2] = dw_s[2 * stream : 2 * stream + 2, pl.ds(row, 16), :].astype(BF)
+
+
+def core_sum_kernel(kept, got, send0, keep0, send1, keep1):
+    for step, out in enumerate((keep0, send0, keep1, send1)):
+        part = slice(32 * step, 32 * (step + 1))
+        out[...] = (kept[part].astype(F32) + got[part].astype(F32)).astype(out.dtype)
 
 
 def halve_kernel(kept, got, send, keep):
     half = send.shape[0]
     for part, out in ((slice(0, half), keep), (slice(half, 2 * half), send)):
         out[...] = (kept[part].astype(F32) + got[part].astype(F32)).astype(out.dtype)
+
+
+def join_kernel(kept0, got0, kept1, got1, send, keep):
+    for start, out in ((0, keep), (8, send)):
+        for path in range(4):
+            for stream, (kept, got) in enumerate(((kept0, got0), (kept1, got1))):
+                here = slice(start + 2 * path, start + 2 * path + 2)
+                there = slice(4 * path + 2 * stream, 4 * path + 2 * stream + 2)
+                out[there] = (kept[here].astype(F32) + got[here].astype(F32)).astype(out.dtype)
 
 
 def input_kernel(att, gq, own, near, far, wq, wk, wv, wo, p0, p1, p2, p3):
@@ -207,11 +242,14 @@
         ).astype(out.dtype)
 
 
-def last_sum_kernel(kept, got, p0, p1, p2, p3, out, grad, dw):
-    dw[...] = kept[...] + got[...].astype(F32)
+def mp_sum_kernel(p0, p1, p2, p3, out, grad):
     for part, ref in ((0, out), (1, grad)):
         total = (p0[part] + p1[part].astype(F32)) + (p2[part].astype(F32) + p3[part].astype(F32))
         ref[...] = total.astype(BF)
+
+
+def last_sum_kernel(kept, got, dw):
+    dw[...] = kept[...] + got[...].astype(F32)
 
 
 def on_chip(*arrays):
@@ -279,25 +317,31 @@
     )
 
     block = (16, WIDTH)
-    att, gq, far, own, dw_send, dw_keep = call(
-        attention_kernel,
-        "attention",
+    query, key_own, value_own, act_t, grad_own, cot_t, bias = own_parts
+    keys, values, probs, att, far_t, near_t = call(
+        forward_kernel,
+        "forward",
+        [((KEYS, WIDTH), BF)] * 2
+        + [((HEADS, KEYS, ROW), F32), (square, BF), ((D, ROW), BF), ((D, ROW), BF)],
+        [act_far, act_near, wk, wv, query, key_own, value_own, bias],
+        limit=20,
+        flops=2_000_000_000,
+        moved=6_000_000,
+    )
+    gq, far, own, dw_send, dw_keep = call(
+        backward_kernel,
+        "backward",
         [
-            (square, BF),
             (square, BF),
             ((2, ROW, WIDTH), BF),
             ((2, ROW, WIDTH), F32),
             ((160,) + block, BF),
             ((128,) + block, BF),
         ],
-        [act_far, act_near, wk, wv, wo, *own_parts, *cots],
-        scratch=[
-            pltpu.VMEM((KEYS, WIDTH), BF),
-            pltpu.VMEM((KEYS, WIDTH), BF),
-            pltpu.VMEM((4, D, WIDTH), F32),
-        ],
-        limit=32,
-        flops=4_000_000_000,
+        [keys, values, probs, att, far_t, near_t, wo, query, act_t, grad_own, cot_t, *cots],
+        scratch=[pltpu.VMEM((4, D, WIDTH), F32)],
+        limit=24,
+        flops=3_000_000_000,
         moved=8_000_000,
     )
 
@@ -319,16 +363,19 @@
         return lambda z, y: partner(z) * 4 + y
 
     steps = (
-        (along_y(y_pair), along_z(z_pair)),
+        ((along_y(y_pair), along_z(z_pair)), (along_z(z_other), along_y(y_other))),
+        ((along_z(z_other), along_y(y_other)), (along_y(y_pair), along_z(z_pair))),
+        (along_y(y_other), along_z(z_other)),
         (along_z(z_pair), along_y(y_pair)),
-        (along_y(y_other), along_z(z_other)),
-        (along_z(z_other), along_y(y_other)),
-        (along_z(z_far), along_z(z_far)),
+        (along_z(z_far_too), along_z(z_far)),
     )
     got = near_row(dw_send)
     grad_far = far_row(far)
-    send, keep = halve(dw_keep, got, BF)
-    arrived = over_chips(send, *steps[0])
+    send0, keep0, send1, keep1 = call(
+        core_sum_kernel, "core_sum", [((32,) + block, BF)] * 4, [dw_keep, got]
+    )
+    keeps = [keep0, keep1]
+    arrived = [over_chips(send, *step) for send, step in zip((send0, send1), steps[0])]
 
     piece = (2, ROW, WIDTH)
     pieces = call(
@@ -341,16 +388,22 @@
     )
     outs = [pieces[0]] + [across(pieces[s], s) for s in (1, 2, 3)]
 
-    for step in steps[1:]:
-        send, keep = halve(keep, arrived, F32)
-        arrived = over_chips(send, *step)
-    return call(
-        last_sum_kernel,
-        "last_sum",
-        [(square, BF), (square, BF), ((4,) + block, F32)],
-        [keep, arrived] + outs,
-        keep=False,
-    )
+    for stream, step in enumerate(steps[1]):
+        send, keeps[stream] = halve(keeps[stream], arrived[stream], F32)
+        arrived[stream] = over_chips(send, *step)
+    send, keep = call(
+        join_kernel,
+        "join",
+        [((16,) + block, BF), ((16,) + block, F32)],
+        [keeps[0], arrived[0], keeps[1], arrived[1]],
+    )
+    got = over_chips(send, *steps[2])
+    for step in steps[3:]:
+        send, keep = halve(keep, got, F32)
+        got = over_chips(send, *step)
+    output, grad_input = call(mp_sum_kernel, "mp_sum", [(square, BF)] * 2, outs, keep=False)
+    (dw,) = call(last_sum_kernel, "last_sum", [((4,) + block, F32)], [keep, got], keep=False)
+    return output, grad_input, dw
 
 
 def solution(mesh):

time: 65.3 us -> 64.2 us (0.983)
  the two profiles are of different devices: /device:TPU:56 before, /device:TPU:64 now
where the time goes in v4:
time: 64.2 us; the launch traced here: 64 us
  starting transfers between devices  26.9 us (42%)
  waiting for transfers between devices  22.3 us (35%)
  Pallas kernels  14 us (22%)
  between operations  0.76 us (1%)
    ppermute x17, starting transfers between devices, move(): lax.ppermute(value, axis, [(i, target(i)) for i in range(count) if 0 <= t...  26.9 us
    ppermute x17, waiting for transfers between devices, move(): lax.ppermute(value, axis, [(i, target(i)) for i in range(count) if 0 <= t...  22.3 us
    pallas_call x12, Pallas kernels, call(): pl.pallas_call(kernel, out_shape=tuple(kept), in_specs=[pl.BlockSpec(memo...  14 us
  transfers between devices with their start and end apart: 17, of which 8 were waited for; matrix products, arithmetic and copies ran while one was open for 0% of the time, Pallas kernels for 13%

profile of v4, /device:TPU:64, one launch (start us, length us, event | category | flops | bytes accessed | tf_op | source)
XLA Modules:
  0.0 64.0 jit_solution(11586842514519690033)
XLA Ops:
  0.6 3.9 %collective-permute-start = (bf16[256,1024]{1,0:T(8,128)(2,1)}, bf16[256,1024]{1,0:T(8,128)(2,1)S(1)}, u32[]{:S(2)}, u32[]{:S(2)}) collective-permute-start(bf16[256,1024]{1,0:T(8,128)(2,1)} %act.1), channel_id=1, source_target_pairs={{4,8},{8,4},{12,16},{16,12},{20,24},{24,20},{28,32},{32,28},{36,40... | collective-permute-start | bytes 1572872 | tf_op jit(solution)/shard_map/ppermute | solution.py:278
  4.5 0.1 collective-permute-start.1
  4.6 1.6 %collective-permute-start.2 = (bf16[256,256]{1,0:T(8,128)(2,1)}, bf16[256,256]{1,0:T(8,128)(2,1)S(1)}, u32[]{:S(2)}, u32[]{:S(2)}) collective-permute-start(bf16[256,256]{1,0:T(8,128)(2,1)} %cot.1), channel_id=1, source_target_pairs={{0,1},{1,0},{2,3},{3,2},{4,5},{5,4},{6,7},{7,6},{8,9},{9,8},{10,11... | collective-permute-start | bytes 393224 | tf_op jit(solution)/shard_map/ppermute | solution.py:278
  6.2 2.1 %collective-permute-start.4 = (bf16[256,256]{1,0:T(8,128)(2,1)}, bf16[256,256]{1,0:T(8,128)(2,1)S(1)}, u32[]{:S(2)}, u32[]{:S(2)}) collective-permute-start(bf16[256,256]{1,0:T(8,128)(2,1)} %cot.1), channel_id=1, source_target_pairs={{0,3},{1,2},{2,1},{3,0},{4,7},{5,6},{6,5},{7,4},{8,11},{9,10},{10,... | collective-permute-start | bytes 393224 | tf_op jit(solution)/shard_map/ppermute | solution.py:278
  8.3 0.6 collective-permute-start.3
  9.0 3.0 %own_part.1 = (bf16[1024,256]{1,0:T(8,128)(2,1)S(1)}, bf16[1024,256]{1,0:T(8,128)(2,1)S(1)}, bf16[1024,256]{1,0:T(8,128)(2,1)S(1)}, bf16[256,1024]{1,0:T(8,128)(...) custom-call(bf16[256,1024]{1,0:T(8,128)(2,1)} %act.1, ...), custom_call_target="tpu_custom_call" | custom-call | flops 600000000 | bytes 6000000 | tf_op jit(solution)/shard_map/own_part/pallas_call | solution.py:263
  12.0 1.4 %collective-permute-done.a_far = bf16[256,1024]{1,0:T(8,128)(2,1)S(1)} collective-permute-done((bf16[256,1024]{1,0:T(8,128)(2,1)}, bf16[256,1024]{1,0:T(8,128)(2,1)S(1)}, u32[]{:S(2)}, u32[]{:S(2)}) %collective-permute-start) | collective-permute-done | bytes 524320 | tf_op jit(solution)/shard_map/ppermute | solution.py:278
  13.5 0.0 collective-permute-done.1.a_near
  13.5 3.6 %forward.1 = (bf16[768,256]{1,0:T(8,128)(2,1)S(1)}, bf16[768,256]{1,0:T(8,128)(2,1)S(1)}, f32[4,768,256]{2,1,0:T(8,128)S(1)}, bf16[256,256]{1,0:T(8,128)(2,1)S(1...) custom-call(bf16[256,1024]{1,0:T(8,128)(2,1)S(1)} %collective-permute-done.a_far, ...), custom_call_target="tpu_custom_call" | custom-call | flops 2000000000 | bytes 6000000 | tf_op jit(solution)/shard_map/forward/pallas_call | solution.py:263
  17.1 0.0 collective-permute-done.2.c1
  17.1 0.0 collective-permute-done.4.c3
  17.1 0.0 collective-permute-done.3.c2
  17.1 4.8 %backward.1 = (bf16[256,256]{1,0:T(8,128)(2,1)S(1)}, bf16[2,256,256]{2,1,0:T(8,128)(2,1)S(1)}, f32[2,256,256]{2,1,0:T(8,128)S(1)}, bf16[160,16,256]{2,1,0:T(8,128)(2,1)S(1)}, bf16[128,16,256]{2,1,0:T(8,128)(2,1)S(1)}) custom-call(bf16[768,256]{1,0:T(8,128)(2,1)S(1)} %get-tuple-element.52.keys, bf16[768,256]{1,0:T(8,128)(2,1)S(1)} %get-tuple-element.53.values, ...), custom_call_target="tpu_custom_call" | custom-call | flops 3000000000 | bytes 8000000 | tf_op jit(solution)/shard_map/backward/pallas_call | solution.py:263
  21.9 0.1 collective-permute-start.5
  22.0 3.0 %collective-permute-done.5.near.got = bf16[160,16,256]{2,1,0:T(8,128)(2,1)S(1)} collective-permute-done((bf16[160,16,256]{2,1,0:T(8,128)(2,1)S(1)}, bf16[160,16,256]{2,1,0:T(8,128)(2,1)S(1)}, u32[]{:S(2)}, u32[]{:S(2)}) %collective-permute-start.5) | collective-permute-done | bytes 1310752 | tf_op jit(solution)/shard_map/ppermute | solution.py:278
  25.0 0.2 core_sum.1
  25.3 0.1 collective-permute-start.10
  25.4 0.4 collective-permute-start.12
  25.7 4.1 %collective-permute-start.6 = (bf16[2,256,256]{2,1,0:T(8,128)(2,1)S(1)}, bf16[2,256,256]{2,1,0:T(8,128)(2,1)S(1)}, u32[]{:S(2)}, u32[]{:S(2)}) collective-permute-start(bf16[2,256,256]{2,1,0:T(8,128)(2,1)S(1)} %get-tuple-element.64), channel_id=1, source_target_pairs={{4,8},{8,4},{12,16},{16,12},{20,24},{24,20},{28,32},{32,28},{36,40... | collective-permute-start | bytes 786440 | tf_op jit(solution)/shard_map/ppermute | solution.py:278
  29.9 1.9 %collective-permute-done.10.got = bf16[32,16,256]{2,1,0:T(8,128)(2,1)S(1)} collective-permute-done((bf16[32,16,256]{2,1,0:T(8,128)(2,1)S(1)}, bf16[32,16,256]{2,1,0:T(8,128)(2,1)S(1)}, u32[]{:S(2)}, u32[]{:S(2)}) %collective-permute-start.10) | collective-permute-done | bytes 262176 | tf_op jit(solution)/shard_map/ppermute | solution.py:278
  31.7 0.1 halve.4
  31.8 0.2 collective-permute-start.11
  32.0 0.0 collective-permute-done.12.got
  32.0 0.1 halve.5
  32.1 2.6 %collective-permute-start.13 = (bf16[16,16,256]{2,1,0:T(8,128)(2,1)S(1)}, bf16[16,16,256]{2,1,0:T(8,128)(2,1)S(1)}, u32[]{:S(2)}, u32[]{:S(2)}) collective-permute-start(bf16[16,16,256]{2,1,0:T(8,128)(2,1)S(1)} %get-tuple-element.80), channel_id=1, source_target_pairs={{0,8},{4,36},{8,0},{12,44},{16,24},{20,52},{24,16},{28,60},{32,40}... | collective-permute-start | bytes 393224 | tf_op jit(solution)/shard_map/ppermute | solution.py:278
  34.7 2.5 %collective-permute-done.6.far = bf16[2,256,256]{2,1,0:T(8,128)(2,1)S(1)} collective-permute-done((bf16[2,256,256]{2,1,0:T(8,128)(2,1)S(1)}, bf16[2,256,256]{2,1,0:T(8,128)(2,1)S(1)}, u32[]{:S(2)}, u32[]{:S(2)}) %collective-permute-start.6) | collective-permute-done | bytes 262176 | tf_op jit(solution)/shard_map/ppermute | solution.py:278
  37.1 0.7 %input_grad.1 = (f32[2,256,256]{2,1,0:T(8,128)S(1)}, bf16[2,256,256]{2,1,0:T(8,128)(2,1)S(1)}, bf16[2,256,256]{2,1,0:T(8,128)(2,1)S(1)}, bf16[2,256,256]{2,1,0:T(8,128)(2,1)S(1)}) custom-call(bf16[256,256]{1,0:T(8,128)(2,1)S(1)} %get-tuple-element.51.att, bf16[256,256]{1,0:T(8,128)(2,1)S(1)} %get-tuple-element.61.gq, ...), custom_call_target="tpu_custom_call" | custom-call | flops 540000000 | bytes 4000000 | tf_op jit(solution)/shard_map/input_grad/pallas_call | solution.py:263
  37.9 1.3 %collective-permute-start.7 = (bf16[2,256,256]{2,1,0:T(8,128)(2,1)S(1)}, bf16[2,256,256]{2,1,0:T(8,128)(2,1)S(1)}, u32[]{:S(2)}, u32[]{:S(2)}) collective-permute-start(bf16[2,256,256]{2,1,0:T(8,128)(2,1)S(1)} %get-tuple-element.67), channel_id=1, source_target_pairs={{0,1},{1,0},{2,3},{3,2},{4,5},{5,4},{6,7},{7,6},{8,9},{9,8},{10,11... | collective-permute-start | bytes 786440 | tf_op jit(solution)/shard_map/ppermute | solution.py:278
  39.2 2.7 %collective-permute-start.8 = (bf16[2,256,256]{2,1,0:T(8,128)(2,1)S(1)}, bf16[2,256,256]{2,1,0:T(8,128)(2,1)S(1)}, u32[]{:S(2)}, u32[]{:S(2)}) collective-permute-start(bf16[2,256,256]{2,1,0:T(8,128)(2,1)S(1)} %get-tuple-element.68), channel_id=1, source_target_pairs={{0,2},{1,3},{2,0},{3,1},{4,6},{5,7},{6,4},{7,5},{8,10},{9,11},{10,... | collective-permute-start | bytes 786440 | tf_op jit(solution)/shard_map/ppermute | solution.py:278
  41.9 0.8 %collective-permute-start.9 = (bf16[2,256,256]{2,1,0:T(8,128)(2,1)S(1)}, bf16[2,256,256]{2,1,0:T(8,128)(2,1)S(1)}, u32[]{:S(2)}, u32[]{:S(2)}) collective-permute-start(bf16[2,256,256]{2,1,0:T(8,128)(2,1)S(1)} %get-tuple-element.69), channel_id=1, source_target_pairs={{0,3},{1,2},{2,1},{3,0},{4,7},{5,6},{6,5},{7,4},{8,11},{9,10},{10,... | collective-permute-start | bytes 786440 | tf_op jit(solution)/shard_map/ppermute | solution.py:278
  42.6 0.0 collective-permute-done.11.got0
  42.6 0.0 collective-permute-done.13.got1
  42.7 0.3 collective-permute-start.14
  43.0 6.0 %collective-permute-done.14.got = bf16[16,16,256]{2,1,0:T(8,128)(2,1)S(1)} collective-permute-done((bf16[16,16,256]{2,1,0:T(8,128)(2,1)S(1)}, bf16[16,16,256]{2,1,0:T(8,128)(2,1)S(1)}, u32[]{:S(2)}, u32[]{:S(2)}) %collective-permute-start.14) | collective-permute-done | bytes 131104 | tf_op jit(solution)/shard_map/ppermute | solution.py:278
  49.0 4.7 %collective-permute-start.15 = (bf16[8,16,256]{2,1,0:T(8,128)(2,1)S(1)}, bf16[8,16,256]{2,1,0:T(8,128)(2,1)S(1)}, u32[]{:S(2)}, u32[]{:S(2)}) collective-permute-start(bf16[8,16,256]{2,1,0:T(8,128)(2,1)S(1)} %get-tuple-element.84), channel_id=1, source_target_pairs={{0,32},{4,12},{8,40},{12,4},{16,48},{20,28},{24,56},{28,20},{32,0}... | collective-permute-start | bytes 196616 | tf_op jit(solution)/shard_map/ppermute | solution.py:278
  53.7 2.6 %collective-permute-done.15.got = bf16[8,16,256]{2,1,0:T(8,128)(2,1)S(1)} collective-permute-done((bf16[8,16,256]{2,1,0:T(8,128)(2,1)S(1)}, bf16[8,16,256]{2,1,0:T(8,128)(2,1)S(1)}, u32[]{:S(2)}, u32[]{:S(2)}) %collective-permute-start.15) | collective-permute-done | bytes 65568 | tf_op jit(solution)/shard_map/ppermute | solution.py:278
  56.4 1.4 %collective-permute-start.16 = (bf16[4,16,256]{2,1,0:T(8,128)(2,1)S(1)}, bf16[4,16,256]{2,1,0:T(8,128)(2,1)S(1)}, u32[]{:S(2)}, u32[]{:S(2)}) collective-permute-start(bf16[4,16,256]{2,1,0:T(8,128)(2,1)S(1)} %get-tuple-element.86), channel_id=1, source_target_pairs={{0,160},{4,100},{8,168},{12,108},{16,176},{20,116},{24,184},{28,12... | collective-permute-start | bytes 98312 | tf_op jit(solution)/shard_map/ppermute | solution.py:278
  57.7 0.0 collective-permute-done.7.p1
  57.7 0.0 collective-permute-done.8.p2
  57.7 0.1 collective-permute-done.9.p3
  57.8 0.8 %mp_sum.1 = (bf16[256,256]{1,0:T(8,128)(2,1)}, bf16[256,256]{1,0:T(8,128)(2,1)}) custom-call(f32[2,256,256]{2,1,0:T(8,128)S(1)} %get-tuple-element.66.p0, bf16[2,256,256]{2,1,0:T(8,128)(2,1)S(1)} %collective-permute-done.7.p1, bf16[2,256,256]{2,1,0:T(8,128)(2,1)S(1)} %collective-permute-done.8.p2, bf16[2,256,256]{2,1,0:T(8,128)(2,1)S(1)} %collective-permute-done.9.p3), custom_call_target="tpu_custom_call" | custom-call | bytes 1000000 | tf_op jit(solution)/shard_map/mp_sum/pallas_call | solution.py:263
  58.6 4.8 %collective-permute-done.16.got = bf16[4,16,256]{2,1,0:T(8,128)(2,1)S(1)} collective-permute-done((bf16[4,16,256]{2,1,0:T(8,128)(2,1)S(1)}, bf16[4,16,256]{2,1,0:T(8,128)(2,1)S(1)}, u32[]{:S(2)}, u32[]{:S(2)}) %collective-permute-start.16) | collective-permute-done | bytes 32800 | tf_op jit(solution)/shard_map/ppermute | solution.py:278
  63.4 0.6 last_sum.1
  (3 shorter events, 0.1 us)
Async XLA Ops:
  0.6 12.8 %collective-permute-start = (bf16[256,1024]{1,0:T(8,128)(2,1)}, bf16[256,1024]{1,0:T(8,128)(2,1)S(1)}, u32[]{:S(2)}, u32[]{:S(2)}) collective-permute-start(bf16[256,1024]{1,0:T(8,128)(2,1)} %act.1), channel_id=1, source_target_pairs={{4,8},{8,4},{12,16},{16,12},{20,24},{24,20},{28,32},{32,28},{36,40... | collective-permute-start | bytes 1572872 | tf_op jit(solution)/shard_map/ppermute | solution.py:278
  4.5 8.9 %collective-permute-start.1 = (bf16[256,1024]{1,0:T(8,128)(2,1)}, bf16[256,1024]{1,0:T(8,128)(2,1)S(1)}, u32[]{:S(2)}, u32[]{:S(2)}) collective-permute-start(bf16[256,1024]{1,0:T(8,128)(2,1)} %act.1), channel_id=1, source_target_pairs={{0,4},{4,0},{8,12},{12,8},{16,20},{20,16},{24,28},{28,24},{32,36},... | collective-permute-start | bytes 1572872 | tf_op jit(solution)/shard_map/ppermute | solution.py:278
  4.6 12.4 %collective-permute-start.2 = (bf16[256,256]{1,0:T(8,128)(2,1)}, bf16[256,256]{1,0:T(8,128)(2,1)S(1)}, u32[]{:S(2)}, u32[]{:S(2)}) collective-permute-start(bf16[256,256]{1,0:T(8,128)(2,1)} %cot.1), channel_id=1, source_target_pairs={{0,1},{1,0},{2,3},{3,2},{4,5},{5,4},{6,7},{7,6},{8,9},{9,8},{10,11... | collective-permute-start | bytes 393224 | tf_op jit(solution)/shard_map/ppermute | solution.py:278
  6.2 10.9 %collective-permute-start.4 = (bf16[256,256]{1,0:T(8,128)(2,1)}, bf16[256,256]{1,0:T(8,128)(2,1)S(1)}, u32[]{:S(2)}, u32[]{:S(2)}) collective-permute-start(bf16[256,256]{1,0:T(8,128)(2,1)} %cot.1), channel_id=1, source_target_pairs={{0,3},{1,2},{2,1},{3,0},{4,7},{5,6},{6,5},{7,4},{8,11},{9,10},{10,... | collective-permute-start | bytes 393224 | tf_op jit(solution)/shard_map/ppermute | solution.py:278
  8.3 8.8 %collective-permute-start.3 = (bf16[256,256]{1,0:T(8,128)(2,1)}, bf16[256,256]{1,0:T(8,128)(2,1)S(1)}, u32[]{:S(2)}, u32[]{:S(2)}) collective-permute-start(bf16[256,256]{1,0:T(8,128)(2,1)} %cot.1), channel_id=1, source_target_pairs={{0,2},{1,3},{2,0},{3,1},{4,6},{5,7},{6,4},{7,5},{8,10},{9,11},{10,... | collective-permute-start | bytes 393224 | tf_op jit(solution)/shard_map/ppermute | solution.py:278
  21.9 3.1 %collective-permute-start.5 = (bf16[160,16,256]{2,1,0:T(8,128)(2,1)S(1)}, bf16[160,16,256]{2,1,0:T(8,128)(2,1)S(1)}, u32[]{:S(2)}, u32[]{:S(2)}) collective-permute-start(bf16[160,16,256]{2,1,0:T(8,128)(2,1)S(1)} %get-tuple-element.63), channel_id=1, source_target_pairs={{0,4},{4,0},{8,12},{12,8},{16,20},{20,16},{24,28},{28,24},{32,36},... | collective-permute-start | bytes 3932168 | tf_op jit(solution)/shard_map/ppermute | solution.py:278
  25.3 6.5 %collective-permute-start.10 = (bf16[32,16,256]{2,1,0:T(8,128)(2,1)S(1)}, bf16[32,16,256]{2,1,0:T(8,128)(2,1)S(1)}, u32[]{:S(2)}, u32[]{:S(2)}) collective-permute-start(bf16[32,16,256]{2,1,0:T(8,128)(2,1)S(1)} %get-tuple-element.74), channel_id=1, source_target_pairs={{0,8},{4,36},{8,0},{12,44},{16,24},{20,52},{24,16},{28,60},{32,40}... | collective-permute-start | bytes 786440 | tf_op jit(solution)/shard_map/ppermute | solution.py:278
  25.4 6.6 %collective-permute-start.12 = (bf16[32,16,256]{2,1,0:T(8,128)(2,1)S(1)}, bf16[32,16,256]{2,1,0:T(8,128)(2,1)S(1)}, u32[]{:S(2)}, u32[]{:S(2)}) collective-permute-start(bf16[32,16,256]{2,1,0:T(8,128)(2,1)S(1)} %get-tuple-element.78), channel_id=1, source_target_pairs={{0,224},{4,28},{8,232},{12,20},{16,240},{20,12},{24,248},{28,4},{3... | collective-permute-start | bytes 786440 | tf_op jit(solution)/shard_map/ppermute | solution.py:278
  25.7 11.4 %collective-permute-start.6 = (bf16[2,256,256]{2,1,0:T(8,128)(2,1)S(1)}, bf16[2,256,256]{2,1,0:T(8,128)(2,1)S(1)}, u32[]{:S(2)}, u32[]{:S(2)}) collective-permute-start(bf16[2,256,256]{2,1,0:T(8,128)(2,1)S(1)} %get-tuple-element.64), channel_id=1, source_target_pairs={{4,8},{8,4},{12,16},{16,12},{20,24},{24,20},{28,32},{32,28},{36,40... | collective-permute-start | bytes 786440 | tf_op jit(solution)/shard_map/ppermute | solution.py:278
  31.8 10.8 %collective-permute-start.11 = (bf16[16,16,256]{2,1,0:T(8,128)(2,1)S(1)}, bf16[16,16,256]{2,1,0:T(8,128)(2,1)S(1)}, u32[]{:S(2)}, u32[]{:S(2)}) collective-permute-start(bf16[16,16,256]{2,1,0:T(8,128)(2,1)S(1)} %get-tuple-element.76), channel_id=1, source_target_pairs={{0,224},{4,28},{8,232},{12,20},{16,240},{20,12},{24,248},{28,4},{3... | collective-permute-start | bytes 393224 | tf_op jit(solution)/shard_map/ppermute | solution.py:278
  32.1 10.6 %collective-permute-start.13 = (bf16[16,16,256]{2,1,0:T(8,128)(2,1)S(1)}, bf16[16,16,256]{2,1,0:T(8,128)(2,1)S(1)}, u32[]{:S(2)}, u32[]{:S(2)}) collective-permute-start(bf16[16,16,256]{2,1,0:T(8,128)(2,1)S(1)} %get-tuple-element.80), channel_id=1, source_target_pairs={{0,8},{4,36},{8,0},{12,44},{16,24},{20,52},{24,16},{28,60},{32,40}... | collective-permute-start | bytes 393224 | tf_op jit(solution)/shard_map/ppermute | solution.py:278
  37.9 19.9 %collective-permute-start.7 = (bf16[2,256,256]{2,1,0:T(8,128)(2,1)S(1)}, bf16[2,256,256]{2,1,0:T(8,128)(2,1)S(1)}, u32[]{:S(2)}, u32[]{:S(2)}) collective-permute-start(bf16[2,256,256]{2,1,0:T(8,128)(2,1)S(1)} %get-tuple-element.67), channel_id=1, source_target_pairs={{0,1},{1,0},{2,3},{3,2},{4,5},{5,4},{6,7},{7,6},{8,9},{9,8},{10,11... | collective-permute-start | bytes 786440 | tf_op jit(solution)/shard_map/ppermute | solution.py:278
  39.2 18.6 %collective-permute-start.8 = (bf16[2,256,256]{2,1,0:T(8,128)(2,1)S(1)}, bf16[2,256,256]{2,1,0:T(8,128)(2,1)S(1)}, u32[]{:S(2)}, u32[]{:S(2)}) collective-permute-start(bf16[2,256,256]{2,1,0:T(8,128)(2,1)S(1)} %get-tuple-element.68), channel_id=1, source_target_pairs={{0,2},{1,3},{2,0},{3,1},{4,6},{5,7},{6,4},{7,5},{8,10},{9,11},{10,... | collective-permute-start | bytes 786440 | tf_op jit(solution)/shard_map/ppermute | solution.py:278
  41.9 15.9 %collective-permute-start.9 = (bf16[2,256,256]{2,1,0:T(8,128)(2,1)S(1)}, bf16[2,256,256]{2,1,0:T(8,128)(2,1)S(1)}, u32[]{:S(2)}, u32[]{:S(2)}) collective-permute-start(bf16[2,256,256]{2,1,0:T(8,128)(2,1)S(1)} %get-tuple-element.69), channel_id=1, source_target_pairs={{0,3},{1,2},{2,1},{3,0},{4,7},{5,6},{6,5},{7,4},{8,11},{9,10},{10,... | collective-permute-start | bytes 786440 | tf_op jit(solution)/shard_map/ppermute | solution.py:278
  42.7 6.3 %collective-permute-start.14 = (bf16[16,16,256]{2,1,0:T(8,128)(2,1)S(1)}, bf16[16,16,256]{2,1,0:T(8,128)(2,1)S(1)}, u32[]{:S(2)}, u32[]{:S(2)}) collective-permute-start(bf16[16,16,256]{2,1,0:T(8,128)(2,1)S(1)} %get-tuple-element.82), channel_id=1, source_target_pairs={{0,24},{4,228},{8,16},{12,236},{16,8},{20,244},{24,0},{28,252},{32... | collective-permute-start | bytes 393224 | tf_op jit(solution)/shard_map/ppermute | solution.py:278
  49.0 7.3 %collective-permute-start.15 = (bf16[8,16,256]{2,1,0:T(8,128)(2,1)S(1)}, bf16[8,16,256]{2,1,0:T(8,128)(2,1)S(1)}, u32[]{:S(2)}, u32[]{:S(2)}) collective-permute-start(bf16[8,16,256]{2,1,0:T(8,128)(2,1)S(1)} %get-tuple-element.84), channel_id=1, source_target_pairs={{0,32},{4,12},{8,40},{12,4},{16,48},{20,28},{24,56},{28,20},{32,0}... | collective-permute-start | bytes 196616 | tf_op jit(solution)/shard_map/ppermute | solution.py:278
  56.4 7.0 %collective-permute-start.16 = (bf16[4,16,256]{2,1,0:T(8,128)(2,1)S(1)}, bf16[4,16,256]{2,1,0:T(8,128)(2,1)S(1)}, u32[]{:S(2)}, u32[]{:S(2)}) collective-permute-start(bf16[4,16,256]{2,1,0:T(8,128)(2,1)S(1)} %get-tuple-element.86), channel_id=1, source_target_pairs={{0,160},{4,100},{8,168},{12,108},{16,176},{20,116},{24,184},{28,12... | collective-permute-start | bytes 98312 | tf_op jit(solution)/shard_map/ppermute | solution.py:278

commit v5 on v4

--- a/solution.py
+++ b/solution.py
@@ -12,6 +12,7 @@
 ROW = 256
 WIDTH = 256
 HEADS = WIDTH // HD
+LATE_FLOPS = 1_000_000_000
 KEYS = 3 * ROW
 LOG2E = 1.4426950408889634
 BF = jnp.bfloat16
@@ -72,112 +73,124 @@
     return z + 4 + (1 - 2 * (z % 2)) - 8 * (z // 4)
 
 
-def target_row(z, y, path, core, stream):
-    s1, s2, s3, s4, s5 = path
-    first, second = (s1, s2) if stream == core else (s2, s1)
+def target_rows(z, y, core, stream):
     if core == 0:
-        y_steps, z_steps = ((y_pair, first), (y_other, s3)), ((z_other, second), (z_pair, s4), (z_far_too, s5))
+        y_partners, z_partners = (y_pair, y_other), (z_other, z_pair, z_far_too)
     else:
-        y_steps, z_steps = ((y_other, first), (y_pair, s4)), ((z_pair, second), (z_other, s3), (z_far, s5))
-    for partner, sent in y_steps:
-        y = partner(y) if sent else y
-    for partner, sent in z_steps:
-        z = partner(z) if sent else z
-    return z * 4 + y
+        y_partners, z_partners = (y_other, y_pair), (z_pair, z_other, z_far)
+
+    def reached(start, partners):
+        places = [start]
+        for partner in partners:
+            places = [there for here in places for there in (here, partner(here))]
+        return places
+
+    ys, zs = reached(y, y_partners), reached(z, z_partners)
+    rows = []
+    for number in range(32):
+        s1, s2, s3, s4, s5 = ((number >> (4 - step)) & 1 for step in range(5))
+        first, second = (s1, s2) if stream == core else (s2, s1)
+        y_later, z_later = (s3, s4) if core == 0 else (s4, s3)
+        rows.append((zs[4 * second + 2 * z_later + s5], ys[2 * first + y_later]))
+    return rows
 
 
 def columns(ref, x, step):
     return ref[:, pl.ds(pl.multiple_of((x ^ step) * WIDTH, WIDTH), WIDTH)]
 
 
+def head_lanes():
+    return lax.broadcasted_iota(jnp.int32, (ROW, WIDTH), 1) // HD
+
+
+def stack_heads(rows, out):
+    for head in range(HEADS):
+        out[head * ROW : (head + 1) * ROW, :] = jnp.where(head_lanes() == head, rows, jnp.zeros_like(rows))
+
+
+def pick_heads(stacked):
+    total = jnp.zeros((ROW, WIDTH), F32)
+    for head in range(HEADS):
+        total = jnp.where(head_lanes() == head, stacked[head * ROW : (head + 1) * ROW], total)
+    return total.astype(BF)
+
+
 def own_kernel(
-    act, w_q, w_k, w_v, w_o, cot, slots, live,
-    wq, wk, wv, wo, query_out, key_out, value_out, act_t, grad_out, cot_t, bias_out,
+    act, w_q, w_k, w_v, w_o, cot, slots, live, a_near,
+    wq, wk, wv, wo, query_out, keys_out, values_out, act_t, near_t, grad_out, cot_t, bias_out,
     act_s, cot_s, nb, mask, sems,
 ):
     core, y, z, x = places()
     pairs = (
-        (act, act_s), (w_q, wq), (w_k, wk), (w_v, wv), (cot, cot_s), (w_o, wo), (slots, nb), (live, mask)
+        (slots, nb), (live, mask), (act, act_s), (w_k, wk), (w_v, wv), (w_q, wq), (cot, cot_s), (w_o, wo)
     )
     copies = [pltpu.make_async_copy(a, b, sems.at[i]) for i, (a, b) in enumerate(pairs)]
     for copy in copies:
         copy.start()
+    near_t[...] = a_near[...].T
     copies[0].wait()
+    copies[1].wait()
+    bias_out[...] = slot_bias(nb, mask, core, y, z)
+    copies[2].wait()
     act_t[...] = act_s[...].T
-    for index, weight, out in ((1, wq, query_out), (2, wk, key_out), (3, wv, value_out)):
+    for index, weight, out in ((3, wk, keys_out), (4, wv, values_out)):
         copies[index].wait()
-        out[...] = mm(act_s[...], weight[...]).astype(BF)
-    copies[4].wait()
+        out[:ROW, :] = mm(act_s[...], weight[...]).astype(BF)
+        out[ROW:, :] = mm(a_near[...], weight[...]).astype(BF)
+    copies[5].wait()
+    stack_heads(mm(act_s[...], wq[...]).astype(BF), query_out)
+    copies[6].wait()
     cot_t[...] = cot_s[...].T
-    copies[5].wait()
+    copies[7].wait()
     grad_out[...] = mm(cot_s[...], columns(wo, x, 0), NT)
-    copies[6].wait()
-    copies[7].wait()
-    bias_out[...] = slot_bias(nb, mask, core, y, z)
 
 
 def forward_kernel(
-    a_far, a_near, wk, wv, query, key_own, value_own, bias,
-    keys, values, probs_out, att_out, far_t, near_t,
+    a_far, wk, wv, query, keys_in, values_in, bias,
+    keys, values, probs_out, att_out, far_t,
+    probs_t,
 ):
-    keys[ROW : 2 * ROW, :] = key_own[...]
-    values[ROW : 2 * ROW, :] = value_own[...]
-    for band, block in ((0, a_far), (2, a_near)):
-        rows = slice(band * ROW, (band + 1) * ROW)
-        keys[rows, :] = mm(block[...], wk[...]).astype(BF)
-        values[rows, :] = mm(block[...], wv[...]).astype(BF)
-    values_t = values[...].T
-    lane_head = lax.broadcasted_iota(jnp.int32, (ROW, WIDTH), 1) // HD
+    keys[ROW:, :] = keys_in[...]
+    values[ROW:, :] = values_in[...]
+    keys[:ROW, :] = mm(a_far[...], wk[...]).astype(BF)
+    values[:ROW, :] = mm(a_far[...], wv[...]).astype(BF)
     bias_rows = jnp.concatenate(
         [jnp.broadcast_to(bias[patch : patch + 1, :], (PATCH, ROW)) for patch in range(KEYS // PATCH)],
         axis=0,
     )
-    att_rows = []
     for head in range(HEADS):
-        feats = slice(head * HD, (head + 1) * HD)
-        q_head = jnp.where(lane_head == head, query[...], jnp.zeros((ROW, WIDTH), BF))
-        scores = mm(keys[...], q_head, NT) * (LOG2E * HD**-0.5) + bias_rows
+        part = slice(head * ROW, (head + 1) * ROW)
+        scores = mm(keys[...], query[part, :], NT) * (LOG2E * HD**-0.5) + bias_rows
         peak = jnp.max(scores, axis=0, keepdims=True)
         weights = jnp.exp2(scores - peak)
-        probs = weights * (1.0 / jnp.sum(weights, axis=0, keepdims=True))
-        probs_out[head] = probs
-        att_rows.append(mm(values_t[feats, :], probs.astype(BF)))
-    att_out[...] = jnp.concatenate(att_rows, axis=0).astype(BF).T
+        probs = (weights * (1.0 / jnp.sum(weights, axis=0, keepdims=True))).astype(BF)
+        probs_out[:, part] = probs
+        probs_t[part, :] = probs.T
+    att_out[...] = pick_heads(mm(probs_t[...], values[...]))
     far_t[...] = a_far[...].T
-    near_t[...] = a_near[...].T
 
 
 def backward_kernel(
     keys, values, probs_in, att, far_t, near_t, wo, query, act_t, grad_in, cot_t, c1, c2, c3,
     gq_out, far_out, own_out, send_out, keep_out,
-    dw_s,
+    grad_s, scores_s, scores_t, dw_s,
 ):
     core, y, z, x = places()
     grad_att = grad_in[...]
     for step, block in ((1, c1), (2, c2), (3, c3)):
         grad_att += mm(block[...], columns(wo, x, step), NT)
-    grad_att = grad_att.astype(BF)
-    for step, block_t in ((0, cot_t[...]), (1, c1[...].T), (2, c2[...].T), (3, c3[...].T)):
-        rows = pl.ds(pl.multiple_of((x ^ step) * WIDTH, WIDTH), WIDTH)
-        dw_s[3, rows, :] = mm(block_t, att[...])
-
-    keys_t = keys[...].T
-    lane_head = lax.broadcasted_iota(jnp.int32, (ROW, WIDTH), 1) // HD
-    grad_key = jnp.zeros((KEYS, WIDTH), F32)
-    grad_value = jnp.zeros((KEYS, WIDTH), F32)
-    gq_rows = []
+    stack_heads(grad_att.astype(BF), grad_s)
     for head in range(HEADS):
-        feats = slice(head * HD, (head + 1) * HD)
-        q_head = jnp.where(lane_head == head, query[...], jnp.zeros((ROW, WIDTH), BF))
-        g_head = jnp.where(lane_head == head, grad_att, jnp.zeros_like(grad_att))
-        probs = probs_in[head]
-        grad_probs = mm(values[...], g_head, NT)
+        part = slice(head * ROW, (head + 1) * ROW)
+        probs = probs_in[:, part].astype(F32)
+        grad_probs = mm(values[...], grad_s[part, :], NT)
         centre = jnp.sum(probs * grad_probs, axis=0, keepdims=True)
-        grad_scores = (probs * (grad_probs - centre) * HD**-0.5).astype(BF)
-        gq_rows.append(mm(keys_t[feats, :], grad_scores))
-        grad_key += mm(grad_scores, q_head)
-        grad_value += mm(probs.astype(BF), g_head)
-    gq = jnp.concatenate(gq_rows, axis=0).astype(BF).T
+        grad_scores = (probs * ((grad_probs - centre) * HD**-0.5)).astype(BF)
+        scores_s[:, part] = grad_scores
+        scores_t[part, :] = grad_scores.T
+    gq = pick_heads(mm(scores_t[...], keys[...]))
+    grad_key = mm(scores_s[...], query[...])
+    grad_value = mm(probs_in[...], grad_s[...])
     gq_out[...] = gq
     far_out[0], far_out[1] = grad_key[:ROW].astype(BF), grad_value[:ROW].astype(BF)
     own_out[0], own_out[1] = grad_key[ROW : 2 * ROW], grad_value[ROW : 2 * ROW]
@@ -186,6 +199,9 @@
             rows = slice(2 * ROW + 16 * block, 2 * ROW + 16 * (block + 1))
             send_out[128 + 16 * part + block] = grad[rows].astype(BF)
 
+    for step, block_t in ((0, cot_t[...]), (1, c1[...].T), (2, c2[...].T), (3, c3[...].T)):
+        rows = pl.ds(pl.multiple_of((x ^ step) * WIDTH, WIDTH), WIDTH)
+        dw_s[3, rows, :] = mm(block_t, att[...])
     grad_key = grad_key.astype(BF)
     grad_value = grad_value.astype(BF)
     own = slice(ROW, 2 * ROW)
@@ -194,12 +210,12 @@
         dw_s[index] = (
             mm(act_t[...], grad[own]) + mm(far_t[...], grad[:ROW]) + mm(near_t[...], grad[2 * ROW :])
         )
-    for c, out in ((1 - core, send_out), (core, keep_out)):
+    for stream in range(2):
+        tables = [target_rows(z, y, which, stream) for which in (0, 1)]
         for number in range(32):
-            path = [(number >> (4 - step)) & 1 for step in range(5)]
-            for stream in range(2):
-                row0, row1 = (target_row(z, y, path, which, stream) for which in (0, 1))
-                row = pl.multiple_of(jnp.where(c == 0, row0, row1) * 32 + c * 16, 16)
+            first, second = ((zs * 4 + ys) * 32 for zs, ys in (table[number] for table in tables))
+            for c, out in ((1 - core, send_out), (core, keep_out)):
+                row = pl.multiple_of(jnp.where(c == 0, first, second) + c * 16, 16)
                 block = 64 * stream + 2 * number
                 out[block : block + 2] = dw_s[2 * stream : 2 * stream + 2, pl.ds(row, 16), :].astype(BF)
 
@@ -232,8 +248,8 @@
         from_near = near[128 + 16 * part : 144 + 16 * part].reshape(ROW, WIDTH)
         grads.append((own[part] + from_near.astype(F32) + far[part].astype(F32)).astype(BF))
     grad_key, grad_value = grads
-    for step, out in enumerate((p0, p1, p2, p3)):
-        block = pl.ds(pl.multiple_of((x ^ step) * WIDTH, WIDTH), WIDTH)
+    for place, out in enumerate((p0, p1, p2, p3)):
+        block = pl.ds(pl.multiple_of((x ^ place) * WIDTH, WIDTH), WIDTH)
         out[0] = mm(att[...], wo[:, block]).astype(out.dtype)
         out[1] = (
             mm(gq[...], wq[block, :], NT)
@@ -298,12 +314,14 @@
     act_near = near_row(activations)
 
     square = (ROW, WIDTH)
-    wq, wk, wv, wo, *own_parts = call(
+    stacked = (HEADS * ROW, WIDTH)
+    wq, wk, wv, wo, query, keys, values, act_t, near_t, grad_own, cot_t, bias = call(
         own_kernel,
         "own_part",
-        [((D, WIDTH), BF)] * 3 + [((WIDTH, D), BF)]
-        + [(square, BF)] * 3 + [((D, ROW), BF), (square, F32), (square, BF), ((16, ROW), F32)],
-        [],
+        [((D, WIDTH), BF)] * 3
+        + [((WIDTH, D), BF), (stacked, BF), ((2 * ROW, WIDTH), BF), ((2 * ROW, WIDTH), BF)]
+        + [((D, ROW), BF), ((D, ROW), BF), (square, F32), (square, BF), ((16, ROW), F32)],
+        [act_near],
         apart=(activations, w_query, w_key, w_value, w_out, grad_output, neighbours, pad_mask),
         scratch=[
             pltpu.VMEM((ROW, D), BF),
@@ -317,13 +335,12 @@
     )
 
     block = (16, WIDTH)
-    query, key_own, value_own, act_t, grad_own, cot_t, bias = own_parts
-    keys, values, probs, att, far_t, near_t = call(
+    keys, values, probs, att, far_t = call(
         forward_kernel,
         "forward",
-        [((KEYS, WIDTH), BF)] * 2
-        + [((HEADS, KEYS, ROW), F32), (square, BF), ((D, ROW), BF), ((D, ROW), BF)],
-        [act_far, act_near, wk, wv, query, key_own, value_own, bias],
+        [((KEYS, WIDTH), BF)] * 2 + [((KEYS, HEADS * ROW), BF), (square, BF), ((D, ROW), BF)],
+        [act_far, wk, wv, query, keys, values, bias],
+        scratch=[pltpu.VMEM((HEADS * ROW, KEYS), BF)],
         limit=20,
         flops=2_000_000_000,
         moved=6_000_000,
@@ -339,15 +356,20 @@
             ((128,) + block, BF),
         ],
         [keys, values, probs, att, far_t, near_t, wo, query, act_t, grad_own, cot_t, *cots],
-        scratch=[pltpu.VMEM((4, D, WIDTH), F32)],
+        scratch=[
+            pltpu.VMEM(stacked, BF),
+            pltpu.VMEM((KEYS, HEADS * ROW), BF),
+            pltpu.VMEM((HEADS * ROW, KEYS), BF),
+            pltpu.VMEM((4, D, WIDTH), F32),
+        ],
         limit=24,
         flops=3_000_000_000,
         moved=8_000_000,
     )
 
-    def halve(kept, got, kept_as):
+    def halve(kept, got, kept_as, flops=0):
         half = (kept.shape[0] // 2,) + block
-        return call(halve_kernel, "halve", [(half, BF), (half, kept_as)], [kept, got])
+        return call(halve_kernel, "halve", [(half, BF), (half, kept_as)], [kept, got], flops=flops)
 
     def over_chips(value, core0, core1):
         def target(i):
@@ -369,25 +391,15 @@
         (along_z(z_pair), along_y(y_pair)),
         (along_z(z_far_too), along_z(z_far)),
     )
-    got = near_row(dw_send)
+    from_core = near_row(dw_send)
     grad_far = far_row(far)
     send0, keep0, send1, keep1 = call(
-        core_sum_kernel, "core_sum", [((32,) + block, BF)] * 4, [dw_keep, got]
+        core_sum_kernel, "core_sum", [((32,) + block, BF)] * 4, [dw_keep, from_core]
     )
     keeps = [keep0, keep1]
     arrived = [over_chips(send, *step) for send, step in zip((send0, send1), steps[0])]
 
     piece = (2, ROW, WIDTH)
-    pieces = call(
-        input_kernel,
-        "input_grad",
-        [(piece, F32)] + [(piece, BF)] * 3,
-        [att, gq, own, got, grad_far, wq, wk, wv, wo],
-        flops=540_000_000,
-        moved=4_000_000,
-    )
-    outs = [pieces[0]] + [across(pieces[s], s) for s in (1, 2, 3)]
-
     for stream, step in enumerate(steps[1]):
         send, keeps[stream] = halve(keeps[stream], arrived[stream], F32)
         arrived[stream] = over_chips(send, *step)
@@ -398,8 +410,17 @@
         [keeps[0], arrived[0], keeps[1], arrived[1]],
     )
     got = over_chips(send, *steps[2])
+    pieces = call(
+        input_kernel,
+        "input_grad",
+        [(piece, F32)] + [(piece, BF)] * 3,
+        [att, gq, own, from_core, grad_far, wq, wk, wv, wo],
+        flops=540_000_000,
+        moved=4_000_000,
+    )
+    outs = [pieces[0]] + [across(pieces[s], s) for s in (1, 2, 3)]
     for step in steps[3:]:
-        send, keep = halve(keep, got, F32)
+        send, keep = halve(keep, got, F32, flops=LATE_FLOPS)
         got = over_chips(send, *step)
     output, grad_input = call(mp_sum_kernel, "mp_sum", [(square, BF)] * 2, outs, keep=False)
     (dw,) = call(last_sum_kernel, "last_sum", [((4,) + block, F32)], [keep, got], keep=False)

time: 64.2 us -> 65.4 us (1.019)
  the two profiles are of different devices: /device:TPU:64 before, /device:TPU:1 now
where the time goes in v5:
time: 65.4 us; the launch traced here: 65.3 us
  starting transfers between devices  29.6 us (45%)
  waiting for transfers between devices  23.1 us (35%)
  Pallas kernels  11.8 us (18%)
  between operations  0.79 us (1%)
    ppermute x17, starting transfers between devices, move(): lax.ppermute(value, axis, [(i, target(i)) for i in range(count) if 0 <= t...  29.6 us
    ppermute x17, waiting for transfers between devices, move(): lax.ppermute(value, axis, [(i, target(i)) for i in range(count) if 0 <= t...  23.1 us
    pallas_call x12, Pallas kernels, call(): pl.pallas_call(kernel, out_shape=tuple(kept), in_specs=[pl.BlockSpec(memo...  11.8 us
  transfers between devices with their start and end apart: 17, of which 6 were waited for; matrix products, arithmetic and copies ran while one was open for 0% of the time, Pallas kernels for 10%

profile of v5, /device:TPU:1, one launch (start us, length us, event | category | flops | bytes accessed | tf_op | source)
XLA Modules:
  0.0 65.3 jit_solution(934590372336972615)
XLA Ops:
  0.6 3.3 %collective-permute-start.1 = (bf16[256,1024]{1,0:T(8,128)(2,1)}, bf16[256,1024]{1,0:T(8,128)(2,1)S(1)}, u32[]{:S(2)}, u32[]{:S(2)}) collective-permute-start(bf16[256,1024]{1,0:T(8,128)(2,1)} %act.1), channel_id=1, source_target_pairs={{0,4},{4,0},{8,12},{12,8},{16,20},{20,16},{24,28},{28,24},{32,36},... | collective-permute-start | bytes 1572872 | tf_op jit(solution)/shard_map/ppermute | solution.py:294
  4.0 1.9 %collective-permute-start = (bf16[256,1024]{1,0:T(8,128)(2,1)}, bf16[256,1024]{1,0:T(8,128)(2,1)S(1)}, u32[]{:S(2)}, u32[]{:S(2)}) collective-permute-start(bf16[256,1024]{1,0:T(8,128)(2,1)} %act.1), channel_id=1, source_target_pairs={{4,8},{8,4},{12,16},{16,12},{20,24},{24,20},{28,32},{32,28},{36,40... | collective-permute-start | bytes 1572872 | tf_op jit(solution)/shard_map/ppermute | solution.py:294
  5.9 0.8 %collective-permute-start.2 = (bf16[256,256]{1,0:T(8,128)(2,1)}, bf16[256,256]{1,0:T(8,128)(2,1)S(1)}, u32[]{:S(2)}, u32[]{:S(2)}) collective-permute-start(bf16[256,256]{1,0:T(8,128)(2,1)} %cot.1), channel_id=1, source_target_pairs={{0,1},{1,0},{2,3},{3,2},{4,5},{5,4},{6,7},{7,6},{8,9},{9,8},{10,11... | collective-permute-start | bytes 393224 | tf_op jit(solution)/shard_map/ppermute | solution.py:294
  6.6 1.8 %collective-permute-start.4 = (bf16[256,256]{1,0:T(8,128)(2,1)}, bf16[256,256]{1,0:T(8,128)(2,1)S(1)}, u32[]{:S(2)}, u32[]{:S(2)}) collective-permute-start(bf16[256,256]{1,0:T(8,128)(2,1)} %cot.1), channel_id=1, source_target_pairs={{0,3},{1,2},{2,1},{3,0},{4,7},{5,6},{6,5},{7,4},{8,11},{9,10},{10,... | collective-permute-start | bytes 393224 | tf_op jit(solution)/shard_map/ppermute | solution.py:294
  8.4 0.8 %collective-permute-start.3 = (bf16[256,256]{1,0:T(8,128)(2,1)}, bf16[256,256]{1,0:T(8,128)(2,1)S(1)}, u32[]{:S(2)}, u32[]{:S(2)}) collective-permute-start(bf16[256,256]{1,0:T(8,128)(2,1)} %cot.1), channel_id=1, source_target_pairs={{0,2},{1,3},{2,0},{3,1},{4,6},{5,7},{6,4},{7,5},{8,10},{9,11},{10,... | collective-permute-start | bytes 393224 | tf_op jit(solution)/shard_map/ppermute | solution.py:294
  9.2 0.0 collective-permute-done.1.a_near
  9.2 3.1 %own_part.1 = (bf16[1024,256]{1,0:T(8,128)(2,1)S(1)}, bf16[1024,256]{1,0:T(8,128)(2,1)S(1)}, bf16[1024,256]{1,0:T(8,128)(2,1)S(1)}, bf16[256,1024]{1,0:T(8,128)(...) custom-call(bf16[256,1024]{1,0:T(8,128)(2,1)} %act.1, ...), custom_call_target="tpu_custom_call" | custom-call | flops 600000000 | bytes 6000000 | tf_op jit(solution)/shard_map/own_part/pallas_call | solution.py:279
  12.3 2.4 %collective-permute-done.a_far = bf16[256,1024]{1,0:T(8,128)(2,1)S(1)} collective-permute-done((bf16[256,1024]{1,0:T(8,128)(2,1)}, bf16[256,1024]{1,0:T(8,128)(2,1)S(1)}, u32[]{:S(2)}, u32[]{:S(2)}) %collective-permute-start) | collective-permute-done | bytes 524320 | tf_op jit(solution)/shard_map/ppermute | solution.py:294
  14.7 2.1 %forward.1 = (bf16[768,256]{1,0:T(8,128)(2,1)S(1)}, bf16[768,256]{1,0:T(8,128)(2,1)S(1)}, bf16[768,1024]{1,0:T(8,128)(2,1)S(1)}, bf16[256,256]{1,0:T(8,128)(2,1)S(1)}, bf16[1024,256]{1,0:T(8,128)(2,1)S(1)}) custom-call(bf16[256,1024]{1,0:T(8,128)(2,1)S(1)} %collective-permute-done.a_far, bf16[1024,256]{1,0:T(8,128)(2,1)S(1)} %get-tuple-element.45.wk, ...), custom_call_target="tpu_custom_call" | custom-call | flops 2000000000 | bytes 6000000 | tf_op jit(solution)/shard_map/forward/pallas_call | solution.py:279
  16.7 0.0 collective-permute-done.2.c1
  16.8 0.0 collective-permute-done.4.c3
  16.8 0.0 collective-permute-done.3.c2
  16.8 4.0 %backward.1 = (bf16[256,256]{1,0:T(8,128)(2,1)S(1)}, bf16[2,256,256]{2,1,0:T(8,128)(2,1)S(1)}, f32[2,256,256]{2,1,0:T(8,128)S(1)}, bf16[160,16,256]{2,1,0:T(8,128)(2,1)S(1)}, bf16[128,16,256]{2,1,0:T(8,128)(2,1)S(1)}) custom-call(bf16[768,256]{1,0:T(8,128)(2,1)S(1)} %get-tuple-element.52.keys, bf16[768,256]{1,0:T(8,128)(2,1)S(1)} %get-tuple-element.53.values, ...), custom_call_target="tpu_custom_call" | custom-call | flops 3000000000 | bytes 8000000 | tf_op jit(solution)/shard_map/backward/pallas_call | solution.py:279
  20.8 0.1 collective-permute-start.5
  20.9 3.0 %collective-permute-done.5.near.got = bf16[160,16,256]{2,1,0:T(8,128)(2,1)S(1)} collective-permute-done((bf16[160,16,256]{2,1,0:T(8,128)(2,1)S(1)}, bf16[160,16,256]{2,1,0:T(8,128)(2,1)S(1)}, u32[]{:S(2)}, u32[]{:S(2)}) %collective-permute-start.5) | collective-permute-done | bytes 1310752 | tf_op jit(solution)/shard_map/ppermute | solution.py:294
  24.0 0.2 core_sum.1
  24.2 2.1 %collective-permute-start.10 = (bf16[32,16,256]{2,1,0:T(8,128)(2,1)S(1)}, bf16[32,16,256]{2,1,0:T(8,128)(2,1)S(1)}, u32[]{:S(2)}, u32[]{:S(2)}) collective-permute-start(bf16[32,16,256]{2,1,0:T(8,128)(2,1)S(1)} %get-tuple-element.74), channel_id=1, source_target_pairs={{0,8},{4,36},{8,0},{12,44},{16,24},{20,52},{24,16},{28,60},{32,40}... | collective-permute-start | bytes 786440 | tf_op jit(solution)/shard_map/ppermute | solution.py:294
  26.2 3.1 %collective-permute-start.12 = (bf16[32,16,256]{2,1,0:T(8,128)(2,1)S(1)}, bf16[32,16,256]{2,1,0:T(8,128)(2,1)S(1)}, u32[]{:S(2)}, u32[]{:S(2)}) collective-permute-start(bf16[32,16,256]{2,1,0:T(8,128)(2,1)S(1)} %get-tuple-element.78), channel_id=1, source_target_pairs={{0,224},{4,28},{8,232},{12,20},{16,240},{20,12},{24,248},{28,4},{3... | collective-permute-start | bytes 786440 | tf_op jit(solution)/shard_map/ppermute | solution.py:294
  29.3 5.6 %collective-permute-start.6 = (bf16[2,256,256]{2,1,0:T(8,128)(2,1)S(1)}, bf16[2,256,256]{2,1,0:T(8,128)(2,1)S(1)}, u32[]{:S(2)}, u32[]{:S(2)}) collective-permute-start(bf16[2,256,256]{2,1,0:T(8,128)(2,1)S(1)} %get-tuple-element.64), channel_id=1, source_target_pairs={{4,8},{8,4},{12,16},{16,12},{20,24},{24,20},{28,32},{32,28},{36,40... | collective-permute-start | bytes 786440 | tf_op jit(solution)/shard_map/ppermute | solution.py:294
  34.9 0.0 collective-permute-done.10.got
  35.0 0.1 halve.4
  35.0 0.1 collective-permute-start.11
  35.1 0.0 collective-permute-done.12.got
  35.1 0.1 halve.5
  35.2 0.3 collective-permute-start.13
  35.5 5.0 %collective-permute-done.11.got0 = bf16[16,16,256]{2,1,0:T(8,128)(2,1)S(1)} collective-permute-done((bf16[16,16,256]{2,1,0:T(8,128)(2,1)S(1)}, bf16[16,16,256]{2,1,0:T(8,128)(2,1)S(1)}, u32[]{:S(2)}, u32[]{:S(2)}) %collective-permute-start.11) | collective-permute-done | bytes 131104 | tf_op jit(solution)/shard_map/ppermute | solution.py:294
  40.4 0.0 collective-permute-done.13.got1
  40.5 4.7 %collective-permute-start.14 = (bf16[16,16,256]{2,1,0:T(8,128)(2,1)S(1)}, bf16[16,16,256]{2,1,0:T(8,128)(2,1)S(1)}, u32[]{:S(2)}, u32[]{:S(2)}) collective-permute-start(bf16[16,16,256]{2,1,0:T(8,128)(2,1)S(1)} %get-tuple-element.82), channel_id=1, source_target_pairs={{0,24},{4,228},{8,16},{12,236},{16,8},{20,244},{24,0},{28,252},{32... | collective-permute-start | bytes 393224 | tf_op jit(solution)/shard_map/ppermute | solution.py:294
  45.1 0.0 collective-permute-done.6.far
  45.1 0.7 %input_grad.1 = (f32[2,256,256]{2,1,0:T(8,128)S(1)}, bf16[2,256,256]{2,1,0:T(8,128)(2,1)S(1)}, bf16[2,256,256]{2,1,0:T(8,128)(2,1)S(1)}, bf16[2,256,256]{2,1,0:T(8,128)(2,1)S(1)}) custom-call(bf16[256,256]{1,0:T(8,128)(2,1)S(1)} %get-tuple-element.51.att, bf16[256,256]{1,0:T(8,128)(2,1)S(1)} %get-tuple-element.61.gq, ...), custom_call_target="tpu_custom_call" | custom-call | flops 540000000 | bytes 4000000 | tf_op jit(solution)/shard_map/input_grad/pallas_call | solution.py:279
  45.9 0.8 %collective-permute-start.7 = (bf16[2,256,256]{2,1,0:T(8,128)(2,1)S(1)}, bf16[2,256,256]{2,1,0:T(8,128)(2,1)S(1)}, u32[]{:S(2)}, u32[]{:S(2)}) collective-permute-start(bf16[2,256,256]{2,1,0:T(8,128)(2,1)S(1)} %get-tuple-element.67), channel_id=1, source_target_pairs={{0,1},{1,0},{2,3},{3,2},{4,5},{5,4},{6,7},{7,6},{8,9},{9,8},{10,11... | collective-permute-start | bytes 786440 | tf_op jit(solution)/shard_map/ppermute | solution.py:294
  46.6 2.5 %collective-permute-start.8 = (bf16[2,256,256]{2,1,0:T(8,128)(2,1)S(1)}, bf16[2,256,256]{2,1,0:T(8,128)(2,1)S(1)}, u32[]{:S(2)}, u32[]{:S(2)}) collective-permute-start(bf16[2,256,256]{2,1,0:T(8,128)(2,1)S(1)} %get-tuple-element.68), channel_id=1, source_target_pairs={{0,2},{1,3},{2,0},{3,1},{4,6},{5,7},{6,4},{7,5},{8,10},{9,11},{10,... | collective-permute-start | bytes 786440 | tf_op jit(solution)/shard_map/ppermute | solution.py:294
  49.1 0.7 %collective-permute-start.9 = (bf16[2,256,256]{2,1,0:T(8,128)(2,1)S(1)}, bf16[2,256,256]{2,1,0:T(8,128)(2,1)S(1)}, u32[]{:S(2)}, u32[]{:S(2)}) collective-permute-start(bf16[2,256,256]{2,1,0:T(8,128)(2,1)S(1)} %get-tuple-element.69), channel_id=1, source_target_pairs={{0,3},{1,2},{2,1},{3,0},{4,7},{5,6},{6,5},{7,4},{8,11},{9,10},{10,... | collective-permute-start | bytes 786440 | tf_op jit(solution)/shard_map/ppermute | solution.py:294
  49.8 0.0 collective-permute-done.14.got
  49.9 0.1 collective-permute-start.15
  50.0 3.4 %collective-permute-done.15.got = bf16[8,16,256]{2,1,0:T(8,128)(2,1)S(1)} collective-permute-done((bf16[8,16,256]{2,1,0:T(8,128)(2,1)S(1)}, bf16[8,16,256]{2,1,0:T(8,128)(2,1)S(1)}, u32[]{:S(2)}, u32[]{:S(2)}) %collective-permute-start.15) | collective-permute-done | bytes 65568 | tf_op jit(solution)/shard_map/ppermute | solution.py:294
  53.4 1.2 %collective-permute-start.16 = (bf16[4,16,256]{2,1,0:T(8,128)(2,1)S(1)}, bf16[4,16,256]{2,1,0:T(8,128)(2,1)S(1)}, u32[]{:S(2)}, u32[]{:S(2)}) collective-permute-start(bf16[4,16,256]{2,1,0:T(8,128)(2,1)S(1)} %get-tuple-element.86), channel_id=1, source_target_pairs={{0,160},{4,100},{8,168},{12,108},{16,176},{20,116},{24,184},{28,12... | collective-permute-start | bytes 98312 | tf_op jit(solution)/shard_map/ppermute | solution.py:294
  54.5 0.0 collective-permute-done.7.p1
  54.5 6.1 %collective-permute-done.8.p2 = bf16[2,256,256]{2,1,0:T(8,128)(2,1)S(1)} collective-permute-done((bf16[2,256,256]{2,1,0:T(8,128)(2,1)S(1)}, bf16[2,256,256]{2,1,0:T(8,128)(2,1)S(1)}, u32[]{:S(2)}, u32[]{:S(2)}) %collective-permute-start.8) | collective-permute-done | bytes 262176 | tf_op jit(solution)/shard_map/ppermute | solution.py:294
  60.6 3.2 %collective-permute-done.9.p3 = bf16[2,256,256]{2,1,0:T(8,128)(2,1)S(1)} collective-permute-done((bf16[2,256,256]{2,1,0:T(8,128)(2,1)S(1)}, bf16[2,256,256]{2,1,0:T(8,128)(2,1)S(1)}, u32[]{:S(2)}, u32[]{:S(2)}) %collective-permute-start.9) | collective-permute-done | bytes 262176 | tf_op jit(solution)/shard_map/ppermute | solution.py:294
  63.9 0.8 %mp_sum.1 = (bf16[256,256]{1,0:T(8,128)(2,1)}, bf16[256,256]{1,0:T(8,128)(2,1)}) custom-call(f32[2,256,256]{2,1,0:T(8,128)S(1)} %get-tuple-element.66.p0, bf16[2,256,256]{2,1,0:T(8,128)(2,1)S(1)} %collective-permute-done.7.p1, bf16[2,256,256]{2,1,0:T(8,128)(2,1)S(1)} %collective-permute-done.8.p2, bf16[2,256,256]{2,1,0:T(8,128)(2,1)S(1)} %collective-permute-done.9.p3), custom_call_target="tpu_custom_call" | custom-call | bytes 1000000 | tf_op jit(solution)/shard_map/mp_sum/pallas_call | solution.py:279
  64.6 0.0 collective-permute-done.16.got
  64.6 0.6 last_sum.1
  (3 shorter events, 0.1 us)
Async XLA Ops:
  0.6 8.6 %collective-permute-start.1 = (bf16[256,1024]{1,0:T(8,128)(2,1)}, bf16[256,1024]{1,0:T(8,128)(2,1)S(1)}, u32[]{:S(2)}, u32[]{:S(2)}) collective-permute-start(bf16[256,1024]{1,0:T(8,128)(2,1)} %act.1), channel_id=1, source_target_pairs={{0,4},{4,0},{8,12},{12,8},{16,20},{20,16},{24,28},{28,24},{32,36},... | collective-permute-start | bytes 1572872 | tf_op jit(solution)/shard_map/ppermute | solution.py:294
  4.0 10.7 %collective-permute-start = (bf16[256,1024]{1,0:T(8,128)(2,1)}, bf16[256,1024]{1,0:T(8,128)(2,1)S(1)}, u32[]{:S(2)}, u32[]{:S(2)}) collective-permute-start(bf16[256,1024]{1,0:T(8,128)(2,1)} %act.1), channel_id=1, source_target_pairs={{4,8},{8,4},{12,16},{16,12},{20,24},{24,20},{28,32},{32,28},{36,40... | collective-permute-start | bytes 1572872 | tf_op jit(solution)/shard_map/ppermute | solution.py:294
  5.9 10.9 %collective-permute-start.2 = (bf16[256,256]{1,0:T(8,128)(2,1)}, bf16[256,256]{1,0:T(8,128)(2,1)S(1)}, u32[]{:S(2)}, u32[]{:S(2)}) collective-permute-start(bf16[256,256]{1,0:T(8,128)(2,1)} %cot.1), channel_id=1, source_target_pairs={{0,1},{1,0},{2,3},{3,2},{4,5},{5,4},{6,7},{7,6},{8,9},{9,8},{10,11... | collective-permute-start | bytes 393224 | tf_op jit(solution)/shard_map/ppermute | solution.py:294
  6.6 10.1 %collective-permute-start.4 = (bf16[256,256]{1,0:T(8,128)(2,1)}, bf16[256,256]{1,0:T(8,128)(2,1)S(1)}, u32[]{:S(2)}, u32[]{:S(2)}) collective-permute-start(bf16[256,256]{1,0:T(8,128)(2,1)} %cot.1), channel_id=1, source_target_pairs={{0,3},{1,2},{2,1},{3,0},{4,7},{5,6},{6,5},{7,4},{8,11},{9,10},{10,... | collective-permute-start | bytes 393224 | tf_op jit(solution)/shard_map/ppermute | solution.py:294
  8.4 8.3 %collective-permute-start.3 = (bf16[256,256]{1,0:T(8,128)(2,1)}, bf16[256,256]{1,0:T(8,128)(2,1)S(1)}, u32[]{:S(2)}, u32[]{:S(2)}) collective-permute-start(bf16[256,256]{1,0:T(8,128)(2,1)} %cot.1), channel_id=1, source_target_pairs={{0,2},{1,3},{2,0},{3,1},{4,6},{5,7},{6,4},{7,5},{8,10},{9,11},{10,... | collective-permute-start | bytes 393224 | tf_op jit(solution)/shard_map/ppermute | solution.py:294
  20.8 3.1 %collective-permute-start.5 = (bf16[160,16,256]{2,1,0:T(8,128)(2,1)S(1)}, bf16[160,16,256]{2,1,0:T(8,128)(2,1)S(1)}, u32[]{:S(2)}, u32[]{:S(2)}) collective-permute-start(bf16[160,16,256]{2,1,0:T(8,128)(2,1)S(1)} %get-tuple-element.63), channel_id=1, source_target_pairs={{0,4},{4,0},{8,12},{12,8},{16,20},{20,16},{24,28},{28,24},{32,36},... | collective-permute-start | bytes 3932168 | tf_op jit(solution)/shard_map/ppermute | solution.py:294
  24.2 10.7 %collective-permute-start.10 = (bf16[32,16,256]{2,1,0:T(8,128)(2,1)S(1)}, bf16[32,16,256]{2,1,0:T(8,128)(2,1)S(1)}, u32[]{:S(2)}, u32[]{:S(2)}) collective-permute-start(bf16[32,16,256]{2,1,0:T(8,128)(2,1)S(1)} %get-tuple-element.74), channel_id=1, source_target_pairs={{0,8},{4,36},{8,0},{12,44},{16,24},{20,52},{24,16},{28,60},{32,40}... | collective-permute-start | bytes 786440 | tf_op jit(solution)/shard_map/ppermute | solution.py:294
  26.2 8.9 %collective-permute-start.12 = (bf16[32,16,256]{2,1,0:T(8,128)(2,1)S(1)}, bf16[32,16,256]{2,1,0:T(8,128)(2,1)S(1)}, u32[]{:S(2)}, u32[]{:S(2)}) collective-permute-start(bf16[32,16,256]{2,1,0:T(8,128)(2,1)S(1)} %get-tuple-element.78), channel_id=1, source_target_pairs={{0,224},{4,28},{8,232},{12,20},{16,240},{20,12},{24,248},{28,4},{3... | collective-permute-start | bytes 786440 | tf_op jit(solution)/shard_map/ppermute | solution.py:294
  29.3 15.8 %collective-permute-start.6 = (bf16[2,256,256]{2,1,0:T(8,128)(2,1)S(1)}, bf16[2,256,256]{2,1,0:T(8,128)(2,1)S(1)}, u32[]{:S(2)}, u32[]{:S(2)}) collective-permute-start(bf16[2,256,256]{2,1,0:T(8,128)(2,1)S(1)} %get-tuple-element.64), channel_id=1, source_target_pairs={{4,8},{8,4},{12,16},{16,12},{20,24},{24,20},{28,32},{32,28},{36,40... | collective-permute-start | bytes 786440 | tf_op jit(solution)/shard_map/ppermute | solution.py:294
  35.0 5.4 %collective-permute-start.11 = (bf16[16,16,256]{2,1,0:T(8,128)(2,1)S(1)}, bf16[16,16,256]{2,1,0:T(8,128)(2,1)S(1)}, u32[]{:S(2)}, u32[]{:S(2)}) collective-permute-start(bf16[16,16,256]{2,1,0:T(8,128)(2,1)S(1)} %get-tuple-element.76), channel_id=1, source_target_pairs={{0,224},{4,28},{8,232},{12,20},{16,240},{20,12},{24,248},{28,4},{3... | collective-permute-start | bytes 393224 | tf_op jit(solution)/shard_map/ppermute | solution.py:294
  35.2 5.2 %collective-permute-start.13 = (bf16[16,16,256]{2,1,0:T(8,128)(2,1)S(1)}, bf16[16,16,256]{2,1,0:T(8,128)(2,1)S(1)}, u32[]{:S(2)}, u32[]{:S(2)}) collective-permute-start(bf16[16,16,256]{2,1,0:T(8,128)(2,1)S(1)} %get-tuple-element.80), channel_id=1, source_target_pairs={{0,8},{4,36},{8,0},{12,44},{16,24},{20,52},{24,16},{28,60},{32,40}... | collective-permute-start | bytes 393224 | tf_op jit(solution)/shard_map/ppermute | solution.py:294
  40.5 9.3 %collective-permute-start.14 = (bf16[16,16,256]{2,1,0:T(8,128)(2,1)S(1)}, bf16[16,16,256]{2,1,0:T(8,128)(2,1)S(1)}, u32[]{:S(2)}, u32[]{:S(2)}) collective-permute-start(bf16[16,16,256]{2,1,0:T(8,128)(2,1)S(1)} %get-tuple-element.82), channel_id=1, source_target_pairs={{0,24},{4,228},{8,16},{12,236},{16,8},{20,244},{24,0},{28,252},{32... | collective-permute-start | bytes 393224 | tf_op jit(solution)/shard_map/ppermute | solution.py:294
  45.9 8.7 %collective-permute-start.7 = (bf16[2,256,256]{2,1,0:T(8,128)(2,1)S(1)}, bf16[2,256,256]{2,1,0:T(8,128)(2,1)S(1)}, u32[]{:S(2)}, u32[]{:S(2)}) collective-permute-start(bf16[2,256,256]{2,1,0:T(8,128)(2,1)S(1)} %get-tuple-element.67), channel_id=1, source_target_pairs={{0,1},{1,0},{2,3},{3,2},{4,5},{5,4},{6,7},{7,6},{8,9},{9,8},{10,11... | collective-permute-start | bytes 786440 | tf_op jit(solution)/shard_map/ppermute | solution.py:294
  46.6 14.0 %collective-permute-start.8 = (bf16[2,256,256]{2,1,0:T(8,128)(2,1)S(1)}, bf16[2,256,256]{2,1,0:T(8,128)(2,1)S(1)}, u32[]{:S(2)}, u32[]{:S(2)}) collective-permute-start(bf16[2,256,256]{2,1,0:T(8,128)(2,1)S(1)} %get-tuple-element.68), channel_id=1, source_target_pairs={{0,2},{1,3},{2,0},{3,1},{4,6},{5,7},{6,4},{7,5},{8,10},{9,11},{10,... | collective-permute-start | bytes 786440 | tf_op jit(solution)/shard_map/ppermute | solution.py:294
  49.1 14.8 %collective-permute-start.9 = (bf16[2,256,256]{2,1,0:T(8,128)(2,1)S(1)}, bf16[2,256,256]{2,1,0:T(8,128)(2,1)S(1)}, u32[]{:S(2)}, u32[]{:S(2)}) collective-permute-start(bf16[2,256,256]{2,1,0:T(8,128)(2,1)S(1)} %get-tuple-element.69), channel_id=1, source_target_pairs={{0,3},{1,2},{2,1},{3,0},{4,7},{5,6},{6,5},{7,4},{8,11},{9,10},{10,... | collective-permute-start | bytes 786440 | tf_op jit(solution)/shard_map/ppermute | solution.py:294
  49.9 3.5 %collective-permute-start.15 = (bf16[8,16,256]{2,1,0:T(8,128)(2,1)S(1)}, bf16[8,16,256]{2,1,0:T(8,128)(2,1)S(1)}, u32[]{:S(2)}, u32[]{:S(2)}) collective-permute-start(bf16[8,16,256]{2,1,0:T(8,128)(2,1)S(1)} %get-tuple-element.84), channel_id=1, source_target_pairs={{0,32},{4,12},{8,40},{12,4},{16,48},{20,28},{24,56},{28,20},{32,0}... | collective-permute-start | bytes 196616 | tf_op jit(solution)/shard_map/ppermute | solution.py:294
  53.4 11.3 %collective-permute-start.16 = (bf16[4,16,256]{2,1,0:T(8,128)(2,1)S(1)}, bf16[4,16,256]{2,1,0:T(8,128)(2,1)S(1)}, u32[]{:S(2)}, u32[]{:S(2)}) collective-permute-start(bf16[4,16,256]{2,1,0:T(8,128)(2,1)S(1)} %get-tuple-element.86), channel_id=1, source_target_pairs={{0,160},{4,100},{8,168},{12,108},{16,176},{20,116},{24,184},{28,12... | collective-permute-start | bytes 98312 | tf_op jit(solution)/shard_map/ppermute | solution.py:294

commit v6 on v5

--- a/solution.py
+++ b/solution.py
@@ -1,3 +1,5 @@
+import functools
+
 import jax
 import jax.numpy as jnp
 from jax import lax
@@ -12,7 +14,6 @@
 ROW = 256
 WIDTH = 256
 HEADS = WIDTH // HD
-LATE_FLOPS = 1_000_000_000
 KEYS = 3 * ROW
 LOG2E = 1.4426950408889634
 BF = jnp.bfloat16
@@ -73,12 +74,7 @@
     return z + 4 + (1 - 2 * (z % 2)) - 8 * (z // 4)
 
 
-def target_rows(z, y, core, stream):
-    if core == 0:
-        y_partners, z_partners = (y_pair, y_other), (z_other, z_pair, z_far_too)
-    else:
-        y_partners, z_partners = (y_other, y_pair), (z_pair, z_other, z_far)
-
+def target_rows(z, y, y_partners, z_partners):
     def reached(start, partners):
         places = [start]
         for partner in partners:
@@ -88,11 +84,15 @@
     ys, zs = reached(y, y_partners), reached(z, z_partners)
     rows = []
     for number in range(32):
-        s1, s2, s3, s4, s5 = ((number >> (4 - step)) & 1 for step in range(5))
-        first, second = (s1, s2) if stream == core else (s2, s1)
-        y_later, z_later = (s3, s4) if core == 0 else (s4, s3)
-        rows.append((zs[4 * second + 2 * z_later + s5], ys[2 * first + y_later]))
+        y1, z1, y2, z2, z3 = ((number >> (4 - bit)) & 1 for bit in range(5))
+        rows.append(zs[4 * z1 + 2 * z2 + z3] * 4 + ys[2 * y1 + y2])
     return rows
+
+
+PARTNERS = (
+    ((y_pair, y_other), (z_other, z_pair, z_far_too)),
+    ((y_other, y_pair), (z_pair, z_other, z_far)),
+)
 
 
 def columns(ref, x, step):
@@ -210,35 +210,23 @@
         dw_s[index] = (
             mm(act_t[...], grad[own]) + mm(far_t[...], grad[:ROW]) + mm(near_t[...], grad[2 * ROW :])
         )
-    for stream in range(2):
-        tables = [target_rows(z, y, which, stream) for which in (0, 1)]
-        for number in range(32):
-            first, second = ((zs * 4 + ys) * 32 for zs, ys in (table[number] for table in tables))
-            for c, out in ((1 - core, send_out), (core, keep_out)):
-                row = pl.multiple_of(jnp.where(c == 0, first, second) + c * 16, 16)
-                block = 64 * stream + 2 * number
-                out[block : block + 2] = dw_s[2 * stream : 2 * stream + 2, pl.ds(row, 16), :].astype(BF)
-
-
-def core_sum_kernel(kept, got, send0, keep0, send1, keep1):
-    for step, out in enumerate((keep0, send0, keep1, send1)):
-        part = slice(32 * step, 32 * (step + 1))
-        out[...] = (kept[part].astype(F32) + got[part].astype(F32)).astype(out.dtype)
-
-
-def halve_kernel(kept, got, send, keep):
-    half = send.shape[0]
-    for part, out in ((slice(0, half), keep), (slice(half, 2 * half), send)):
-        out[...] = (kept[part].astype(F32) + got[part].astype(F32)).astype(out.dtype)
-
-
-def join_kernel(kept0, got0, kept1, got1, send, keep):
-    for start, out in ((0, keep), (8, send)):
-        for path in range(4):
-            for stream, (kept, got) in enumerate(((kept0, got0), (kept1, got1))):
-                here = slice(start + 2 * path, start + 2 * path + 2)
-                there = slice(4 * path + 2 * stream, 4 * path + 2 * stream + 2)
-                out[there] = (kept[here].astype(F32) + got[here].astype(F32)).astype(out.dtype)
+    tables = [target_rows(z, y, *partners) for partners in PARTNERS]
+    for number in range(32):
+        first, second = (table[number] * 32 for table in tables)
+        for c, out in ((1 - core, send_out), (core, keep_out)):
+            row = pl.multiple_of(jnp.where(c == 0, first, second) + c * 16, 16)
+            out[4 * number : 4 * number + 4] = dw_s[:, pl.ds(row, 16), :].astype(BF)
+
+
+def share_kernel(count, *refs):
+    terms, outs = refs[:count], refs[count:]
+    size = outs[0].shape[0]
+    for place, out in enumerate(outs):
+        part = slice(size * place, size * (place + 1))
+        total = terms[0][part].astype(F32)
+        for term in terms[1:]:
+            total += term[part].astype(F32)
+        out[...] = total.astype(out.dtype)
 
 
 def input_kernel(att, gq, own, near, far, wq, wk, wv, wo, p0, p1, p2, p3):
@@ -367,49 +355,32 @@
         moved=8_000_000,
     )
 
-    def halve(kept, got, kept_as, flops=0):
-        half = (kept.shape[0] // 2,) + block
-        return call(halve_kernel, "halve", [(half, BF), (half, kept_as)], [kept, got], flops=flops)
-
-    def over_chips(value, core0, core1):
+    def share(name, terms, ways, kept_as):
+        part = (terms[0].shape[0] // ways,) + block
+        outs = [(part, kept_as)] + [(part, BF)] * (ways - 1)
+        return call(functools.partial(share_kernel, len(terms)), name, outs, terms)
+
+    def over_chips(value, y_step, z_step):
         def target(i):
             z, y, c = i // 8, i // 2 % 4, i % 2
-            return ((core0, core1)[c](z, y)) * 2 + c
+            y_partners, z_partners = PARTNERS[c]
+            y = y if y_step is None else y_partners[y_step](y)
+            z = z if z_step is None else z_partners[z_step](z)
+            return z * 8 + y * 2 + c
 
         return move(value, SPACE, target)
 
-    def along_y(partner):
-        return lambda z, y: z * 4 + partner(y)
-
-    def along_z(partner):
-        return lambda z, y: partner(z) * 4 + y
-
-    steps = (
-        ((along_y(y_pair), along_z(z_pair)), (along_z(z_other), along_y(y_other))),
-        ((along_z(z_other), along_y(y_other)), (along_y(y_pair), along_z(z_pair))),
-        (along_y(y_other), along_z(z_other)),
-        (along_z(z_pair), along_y(y_pair)),
-        (along_z(z_far_too), along_z(z_far)),
-    )
+    def four_ways(parts, step):
+        return [parts[0]] + [
+            over_chips(part, *partners)
+            for part, partners in zip(parts[1:], ((None, step), (step, None), (step, step)))
+        ]
+
     from_core = near_row(dw_send)
     grad_far = far_row(far)
-    send0, keep0, send1, keep1 = call(
-        core_sum_kernel, "core_sum", [((32,) + block, BF)] * 4, [dw_keep, from_core]
-    )
-    keeps = [keep0, keep1]
-    arrived = [over_chips(send, *step) for send, step in zip((send0, send1), steps[0])]
+    parts = four_ways(share("core_sum", [dw_keep, from_core], 4, BF), 0)
 
     piece = (2, ROW, WIDTH)
-    for stream, step in enumerate(steps[1]):
-        send, keeps[stream] = halve(keeps[stream], arrived[stream], F32)
-        arrived[stream] = over_chips(send, *step)
-    send, keep = call(
-        join_kernel,
-        "join",
-        [((16,) + block, BF), ((16,) + block, F32)],
-        [keeps[0], arrived[0], keeps[1], arrived[1]],
-    )
-    got = over_chips(send, *steps[2])
     pieces = call(
         input_kernel,
         "input_grad",
@@ -419,9 +390,9 @@
         moved=4_000_000,
     )
     outs = [pieces[0]] + [across(pieces[s], s) for s in (1, 2, 3)]
-    for step in steps[3:]:
-        send, keep = halve(keep, got, F32, flops=LATE_FLOPS)
-        got = over_chips(send, *step)
+    parts = four_ways(share("first_sum", parts, 4, F32), 1)
+    keep, send = share("second_sum", parts, 2, F32)
+    got = over_chips(send, None, 2)
     output, grad_input = call(mp_sum_kernel, "mp_sum", [(square, BF)] * 2, outs, keep=False)
     (dw,) = call(last_sum_kernel, "last_sum", [((4,) + block, F32)], [keep, got], keep=False)
     return output, grad_input, dw

time: 65.4 us -> 59.4 us (0.908)
  the two profiles are of different devices: /device:TPU:1 before, /device:TPU:6 now
where the time goes in v6:
time: 59.4 us; the launch traced here: 59.2 us
  starting transfers between devices  29.9 us (50%)
  waiting for transfers between devices  16.8 us (28%)
  Pallas kernels  11.7 us (20%)
  between operations  0.75 us (1%)
    ppermute x17, starting transfers between devices, move(): lax.ppermute(value, axis, [(i, target(i)) for i in range(count) if 0 <= t...  29.9 us
    ppermute x17, waiting for transfers between devices, move(): lax.ppermute(value, axis, [(i, target(i)) for i in range(count) if 0 <= t...  16.8 us
    pallas_call x9, Pallas kernels, call(): pl.pallas_call(kernel, out_shape=tuple(kept), in_specs=[pl.BlockSpec(memo...  11.7 us
  transfers between devices with their start and end apart: 17, of which 7 were waited for; matrix products, arithmetic and copies ran while one was open for 0% of the time, Pallas kernels for 12%

profile of v6, /device:TPU:6, one launch (start us, length us, event | category | flops | bytes accessed | tf_op | source)
XLA Modules:
  0.0 59.2 jit_solution(11482627381022076809)
XLA Ops:
  0.6 0.1 collective-permute-start.1
  0.7 0.7 %collective-permute-start = (bf16[256,1024]{1,0:T(8,128)(2,1)}, bf16[256,1024]{1,0:T(8,128)(2,1)S(1)}, u32[]{:S(2)}, u32[]{:S(2)}) collective-permute-start(bf16[256,1024]{1,0:T(8,128)(2,1)} %act.1), channel_id=1, source_target_pairs={{4,8},{8,4},{12,16},{16,12},{20,24},{24,20},{28,32},{32,28},{36,40... | collective-permute-start | bytes 1572872 | tf_op jit(solution)/shard_map/ppermute | solution.py:282
  1.4 0.9 %collective-permute-start.2 = (bf16[256,256]{1,0:T(8,128)(2,1)}, bf16[256,256]{1,0:T(8,128)(2,1)S(1)}, u32[]{:S(2)}, u32[]{:S(2)}) collective-permute-start(bf16[256,256]{1,0:T(8,128)(2,1)} %cot.1), channel_id=1, source_target_pairs={{0,1},{1,0},{2,3},{3,2},{4,5},{5,4},{6,7},{7,6},{8,9},{9,8},{10,11... | collective-permute-start | bytes 393224 | tf_op jit(solution)/shard_map/ppermute | solution.py:282
  2.4 1.5 %collective-permute-start.4 = (bf16[256,256]{1,0:T(8,128)(2,1)}, bf16[256,256]{1,0:T(8,128)(2,1)S(1)}, u32[]{:S(2)}, u32[]{:S(2)}) collective-permute-start(bf16[256,256]{1,0:T(8,128)(2,1)} %cot.1), channel_id=1, source_target_pairs={{0,3},{1,2},{2,1},{3,0},{4,7},{5,6},{6,5},{7,4},{8,11},{9,10},{10,... | collective-permute-start | bytes 393224 | tf_op jit(solution)/shard_map/ppermute | solution.py:282
  3.8 1.8 %collective-permute-start.3 = (bf16[256,256]{1,0:T(8,128)(2,1)}, bf16[256,256]{1,0:T(8,128)(2,1)S(1)}, u32[]{:S(2)}, u32[]{:S(2)}) collective-permute-start(bf16[256,256]{1,0:T(8,128)(2,1)} %cot.1), channel_id=1, source_target_pairs={{0,2},{1,3},{2,0},{3,1},{4,6},{5,7},{6,4},{7,5},{8,10},{9,11},{10,... | collective-permute-start | bytes 393224 | tf_op jit(solution)/shard_map/ppermute | solution.py:282
  5.6 0.0 collective-permute-done.1.a_near
  5.6 3.1 %own_part.1 = (bf16[1024,256]{1,0:T(8,128)(2,1)S(1)}, bf16[1024,256]{1,0:T(8,128)(2,1)S(1)}, bf16[1024,256]{1,0:T(8,128)(2,1)S(1)}, bf16[256,1024]{1,0:T(8,128)(...) custom-call(bf16[256,1024]{1,0:T(8,128)(2,1)} %act.1, ...), custom_call_target="tpu_custom_call" | custom-call | flops 600000000 | bytes 6000000 | tf_op jit(solution)/shard_map/own_part/pallas_call | solution.py:267
  8.7 0.0 collective-permute-done.a_far
  8.7 2.1 %forward.1 = (bf16[768,256]{1,0:T(8,128)(2,1)S(1)}, bf16[768,256]{1,0:T(8,128)(2,1)S(1)}, bf16[768,1024]{1,0:T(8,128)(2,1)S(1)}, bf16[256,256]{1,0:T(8,128)(2,1)S(1)}, bf16[1024,256]{1,0:T(8,128)(2,1)S(1)}) custom-call(bf16[256,1024]{1,0:T(8,128)(2,1)S(1)} %collective-permute-done.a_far, bf16[1024,256]{1,0:T(8,128)(2,1)S(1)} %get-tuple-element.41.wk, ...), custom_call_target="tpu_custom_call" | custom-call | flops 2000000000 | bytes 6000000 | tf_op jit(solution)/shard_map/forward/pallas_call | solution.py:267
  10.8 0.0 collective-permute-done.2.c1
  10.8 0.0 collective-permute-done.4.c3
  10.8 1.3 %collective-permute-done.3.c2 = bf16[256,256]{1,0:T(8,128)(2,1)S(1)} collective-permute-done((bf16[256,256]{1,0:T(8,128)(2,1)}, bf16[256,256]{1,0:T(8,128)(2,1)S(1)}, u32[]{:S(2)}, u32[]{:S(2)}) %collective-permute-start.3) | collective-permute-done | bytes 131104 | tf_op jit(solution)/shard_map/ppermute | solution.py:282
  12.1 4.1 %backward.1 = (bf16[256,256]{1,0:T(8,128)(2,1)S(1)}, bf16[2,256,256]{2,1,0:T(8,128)(2,1)S(1)}, f32[2,256,256]{2,1,0:T(8,128)S(1)}, bf16[160,16,256]{2,1,0:T(8,128)(2,1)S(1)}, bf16[128,16,256]{2,1,0:T(8,128)(2,1)S(1)}) custom-call(bf16[768,256]{1,0:T(8,128)(2,1)S(1)} %get-tuple-element.48.keys, bf16[768,256]{1,0:T(8,128)(2,1)S(1)} %get-tuple-element.49.values, ...), custom_call_target="tpu_custom_call" | custom-call | flops 3000000000 | bytes 8000000 | tf_op jit(solution)/shard_map/backward/pallas_call | solution.py:267
  16.1 2.3 %collective-permute-start.5 = (bf16[160,16,256]{2,1,0:T(8,128)(2,1)S(1)}, bf16[160,16,256]{2,1,0:T(8,128)(2,1)S(1)}, u32[]{:S(2)}, u32[]{:S(2)}) collective-permute-start(bf16[160,16,256]{2,1,0:T(8,128)(2,1)S(1)} %get-tuple-element.59), channel_id=1, source_target_pairs={{0,4},{4,0},{8,12},{12,8},{16,20},{20,16},{24,28},{28,24},{32,36},... | collective-permute-start | bytes 3932168 | tf_op jit(solution)/shard_map/ppermute | solution.py:282
  18.4 0.7 %collective-permute-start.6 = (bf16[2,256,256]{2,1,0:T(8,128)(2,1)S(1)}, bf16[2,256,256]{2,1,0:T(8,128)(2,1)S(1)}, u32[]{:S(2)}, u32[]{:S(2)}) collective-permute-start(bf16[2,256,256]{2,1,0:T(8,128)(2,1)S(1)} %get-tuple-element.60), channel_id=1, source_target_pairs={{4,8},{8,4},{12,16},{16,12},{20,24},{24,20},{28,32},{32,28},{36,40... | collective-permute-start | bytes 786440 | tf_op jit(solution)/shard_map/ppermute | solution.py:282
  19.1 2.0 %collective-permute-done.5.near.refs_1_ = bf16[160,16,256]{2,1,0:T(8,128)(2,1)S(1)} collective-permute-done((bf16[160,16,256]{2,1,0:T(8,128)(2,1)S(1)}, bf16[160,16,256]{2,1,0:T(8,128)(2,1)S(1)}, u32[]{:S(2)}, u32[]{:S(2)}) %collective-permute-start.5) | collective-permute-done | bytes 1310752 | tf_op jit(solution)/shard_map/ppermute | solution.py:282
  21.1 0.2 core_sum.1
  21.3 10.2 %collective-permute-start.10 = (bf16[32,16,256]{2,1,0:T(8,128)(2,1)S(1)}, bf16[32,16,256]{2,1,0:T(8,128)(2,1)S(1)}, u32[]{:S(2)}, u32[]{:S(2)}) collective-permute-start(bf16[32,16,256]{2,1,0:T(8,128)(2,1)S(1)} %get-tuple-element.70), channel_id=1, source_target_pairs={{0,224},{4,36},{8,232},{12,44},{16,240},{20,52},{24,248},{28,60},{... | collective-permute-start | bytes 786440 | tf_op jit(solution)/shard_map/ppermute | solution.py:282
  31.5 0.0 collective-permute-start.11
  31.5 1.6 %collective-permute-start.12 = (bf16[32,16,256]{2,1,0:T(8,128)(2,1)S(1)}, bf16[32,16,256]{2,1,0:T(8,128)(2,1)S(1)}, u32[]{:S(2)}, u32[]{:S(2)}) collective-permute-start(bf16[32,16,256]{2,1,0:T(8,128)(2,1)S(1)} %get-tuple-element.72), channel_id=1, source_target_pairs={{0,232},{4,60},{8,224},{12,52},{16,248},{20,44},{24,240},{28,36},{... | collective-permute-start | bytes 786440 | tf_op jit(solution)/shard_map/ppermute | solution.py:282
  33.1 0.0 collective-permute-done.6.far
  33.1 0.7 %input_grad.1 = (f32[2,256,256]{2,1,0:T(8,128)S(1)}, bf16[2,256,256]{2,1,0:T(8,128)(2,1)S(1)}, bf16[2,256,256]{2,1,0:T(8,128)(2,1)S(1)}, bf16[2,256,256]{2,1,0:T(8,128)(2,1)S(1)}) custom-call(bf16[256,256]{1,0:T(8,128)(2,1)S(1)} %get-tuple-element.47.att, bf16[256,256]{1,0:T(8,128)(2,1)S(1)} %get-tuple-element.57.gq, ...), custom_call_target="tpu_custom_call" | custom-call | flops 540000000 | bytes 4000000 | tf_op jit(solution)/shard_map/input_grad/pallas_call | solution.py:267
  33.8 0.9 %collective-permute-start.7 = (bf16[2,256,256]{2,1,0:T(8,128)(2,1)S(1)}, bf16[2,256,256]{2,1,0:T(8,128)(2,1)S(1)}, u32[]{:S(2)}, u32[]{:S(2)}) collective-permute-start(bf16[2,256,256]{2,1,0:T(8,128)(2,1)S(1)} %get-tuple-element.63), channel_id=1, source_target_pairs={{0,1},{1,0},{2,3},{3,2},{4,5},{5,4},{6,7},{7,6},{8,9},{9,8},{10,11... | collective-permute-start | bytes 786440 | tf_op jit(solution)/shard_map/ppermute | solution.py:282
  34.7 1.4 %collective-permute-start.8 = (bf16[2,256,256]{2,1,0:T(8,128)(2,1)S(1)}, bf16[2,256,256]{2,1,0:T(8,128)(2,1)S(1)}, u32[]{:S(2)}, u32[]{:S(2)}) collective-permute-start(bf16[2,256,256]{2,1,0:T(8,128)(2,1)S(1)} %get-tuple-element.64), channel_id=1, source_target_pairs={{0,2},{1,3},{2,0},{3,1},{4,6},{5,7},{6,4},{7,5},{8,10},{9,11},{10,... | collective-permute-start | bytes 786440 | tf_op jit(solution)/shard_map/ppermute | solution.py:282
  36.1 0.0 collective-permute-done.10.refs_1_
  36.1 2.5 %collective-permute-start.9 = (bf16[2,256,256]{2,1,0:T(8,128)(2,1)S(1)}, bf16[2,256,256]{2,1,0:T(8,128)(2,1)S(1)}, u32[]{:S(2)}, u32[]{:S(2)}) collective-permute-start(bf16[2,256,256]{2,1,0:T(8,128)(2,1)S(1)} %get-tuple-element.65), channel_id=1, source_target_pairs={{0,3},{1,2},{2,1},{3,0},{4,7},{5,6},{6,5},{7,4},{8,11},{9,10},{10,... | collective-permute-start | bytes 786440 | tf_op jit(solution)/shard_map/ppermute | solution.py:282
  38.6 2.1 %collective-permute-done.11.refs_2_ = bf16[32,16,256]{2,1,0:T(8,128)(2,1)S(1)} collective-permute-done((bf16[32,16,256]{2,1,0:T(8,128)(2,1)S(1)}, bf16[32,16,256]{2,1,0:T(8,128)(2,1)S(1)}, u32[]{:S(2)}, u32[]{:S(2)}) %collective-permute-start.11) | collective-permute-done | bytes 262176 | tf_op jit(solution)/shard_map/ppermute | solution.py:282
  40.7 0.0 collective-permute-done.12.refs_3_
  40.7 0.1 first_sum.1
  40.8 0.1 collective-permute-start.13
  40.9 0.1 collective-permute-start.14
  41.0 4.2 %collective-permute-done.13.refs_1_ = bf16[8,16,256]{2,1,0:T(8,128)(2,1)S(1)} collective-permute-done((bf16[8,16,256]{2,1,0:T(8,128)(2,1)S(1)}, bf16[8,16,256]{2,1,0:T(8,128)(2,1)S(1)}, u32[]{:S(2)}, u32[]{:S(2)}) %collective-permute-start.13) | collective-permute-done | bytes 65568 | tf_op jit(solution)/shard_map/ppermute | solution.py:282
  45.2 0.4 collective-permute-start.15
  45.6 0.9 %collective-permute-done.14.refs_2_ = bf16[8,16,256]{2,1,0:T(8,128)(2,1)S(1)} collective-permute-done((bf16[8,16,256]{2,1,0:T(8,128)(2,1)S(1)}, bf16[8,16,256]{2,1,0:T(8,128)(2,1)S(1)}, u32[]{:S(2)}, u32[]{:S(2)}) %collective-permute-start.14) | collective-permute-done | bytes 65568 | tf_op jit(solution)/shard_map/ppermute | solution.py:282
  46.5 5.1 %collective-permute-done.15.refs_3_ = bf16[8,16,256]{2,1,0:T(8,128)(2,1)S(1)} collective-permute-done((bf16[8,16,256]{2,1,0:T(8,128)(2,1)S(1)}, bf16[8,16,256]{2,1,0:T(8,128)(2,1)S(1)}, u32[]{:S(2)}, u32[]{:S(2)}) %collective-permute-start.15) | collective-permute-done | bytes 65568 | tf_op jit(solution)/shard_map/ppermute | solution.py:282
  51.6 4.9 %collective-permute-start.16 = (bf16[4,16,256]{2,1,0:T(8,128)(2,1)S(1)}, bf16[4,16,256]{2,1,0:T(8,128)(2,1)S(1)}, u32[]{:S(2)}, u32[]{:S(2)}) collective-permute-start(bf16[4,16,256]{2,1,0:T(8,128)(2,1)S(1)} %get-tuple-element.78), channel_id=1, source_target_pairs={{0,160},{4,100},{8,168},{12,108},{16,176},{20,116},{24,184},{28,12... | collective-permute-start | bytes 98312 | tf_op jit(solution)/shard_map/ppermute | solution.py:282
  56.4 0.0 collective-permute-done.7.p1
  56.5 0.0 collective-permute-done.8.p2
  56.5 0.0 collective-permute-done.9.p3
  56.5 0.8 %mp_sum.1 = (bf16[256,256]{1,0:T(8,128)(2,1)}, bf16[256,256]{1,0:T(8,128)(2,1)}) custom-call(f32[2,256,256]{2,1,0:T(8,128)S(1)} %get-tuple-element.62.p0, bf16[2,256,256]{2,1,0:T(8,128)(2,1)S(1)} %collective-permute-done.7.p1, bf16[2,256,256]{2,1,0:T(8,128)(2,1)S(1)} %collective-permute-done.8.p2, bf16[2,256,256]{2,1,0:T(8,128)(2,1)S(1)} %collective-permute-done.9.p3), custom_call_target="tpu_custom_call" | custom-call | bytes 1000000 | tf_op jit(solution)/shard_map/mp_sum/pallas_call | solution.py:267
  57.2 1.4 %collective-permute-done.16.got = bf16[4,16,256]{2,1,0:T(8,128)(2,1)S(1)} collective-permute-done((bf16[4,16,256]{2,1,0:T(8,128)(2,1)S(1)}, bf16[4,16,256]{2,1,0:T(8,128)(2,1)S(1)}, u32[]{:S(2)}, u32[]{:S(2)}) %collective-permute-start.16) | collective-permute-done | bytes 32800 | tf_op jit(solution)/shard_map/ppermute | solution.py:282
  58.6 0.6 %last_sum.1 = f32[4,16,256]{2,1,0:T(8,128)} custom-call(f32[4,16,256]{2,1,0:T(8,128)S(1)} %get-tuple-element.77.kept, bf16[4,16,256]{2,1,0:T(8,128)(2,1)S(1)} %collective-permute-done.16.got), custom_call_target="tpu_custom_call" | custom-call | bytes 1000000 | tf_op jit(solution)/shard_map/last_sum/pallas_call | solution.py:267
  (1 shorter events, 0.0 us)
Async XLA Ops:
  0.6 5.0 %collective-permute-start.1 = (bf16[256,1024]{1,0:T(8,128)(2,1)}, bf16[256,1024]{1,0:T(8,128)(2,1)S(1)}, u32[]{:S(2)}, u32[]{:S(2)}) collective-permute-start(bf16[256,1024]{1,0:T(8,128)(2,1)} %act.1), channel_id=1, source_target_pairs={{0,4},{4,0},{8,12},{12,8},{16,20},{20,16},{24,28},{28,24},{32,36},... | collective-permute-start | bytes 1572872 | tf_op jit(solution)/shard_map/ppermute | solution.py:282
  0.7 8.0 %collective-permute-start = (bf16[256,1024]{1,0:T(8,128)(2,1)}, bf16[256,1024]{1,0:T(8,128)(2,1)S(1)}, u32[]{:S(2)}, u32[]{:S(2)}) collective-permute-start(bf16[256,1024]{1,0:T(8,128)(2,1)} %act.1), channel_id=1, source_target_pairs={{4,8},{8,4},{12,16},{16,12},{20,24},{24,20},{28,32},{32,28},{36,40... | collective-permute-start | bytes 1572872 | tf_op jit(solution)/shard_map/ppermute | solution.py:282
  1.4 9.4 %collective-permute-start.2 = (bf16[256,256]{1,0:T(8,128)(2,1)}, bf16[256,256]{1,0:T(8,128)(2,1)S(1)}, u32[]{:S(2)}, u32[]{:S(2)}) collective-permute-start(bf16[256,256]{1,0:T(8,128)(2,1)} %cot.1), channel_id=1, source_target_pairs={{0,1},{1,0},{2,3},{3,2},{4,5},{5,4},{6,7},{7,6},{8,9},{9,8},{10,11... | collective-permute-start | bytes 393224 | tf_op jit(solution)/shard_map/ppermute | solution.py:282
  2.4 8.5 %collective-permute-start.4 = (bf16[256,256]{1,0:T(8,128)(2,1)}, bf16[256,256]{1,0:T(8,128)(2,1)S(1)}, u32[]{:S(2)}, u32[]{:S(2)}) collective-permute-start(bf16[256,256]{1,0:T(8,128)(2,1)} %cot.1), channel_id=1, source_target_pairs={{0,3},{1,2},{2,1},{3,0},{4,7},{5,6},{6,5},{7,4},{8,11},{9,10},{10,... | collective-permute-start | bytes 393224 | tf_op jit(solution)/shard_map/ppermute | solution.py:282
  3.8 8.2 %collective-permute-start.3 = (bf16[256,256]{1,0:T(8,128)(2,1)}, bf16[256,256]{1,0:T(8,128)(2,1)S(1)}, u32[]{:S(2)}, u32[]{:S(2)}) collective-permute-start(bf16[256,256]{1,0:T(8,128)(2,1)} %cot.1), channel_id=1, source_target_pairs={{0,2},{1,3},{2,0},{3,1},{4,6},{5,7},{6,4},{7,5},{8,10},{9,11},{10,... | collective-permute-start | bytes 393224 | tf_op jit(solution)/shard_map/ppermute | solution.py:282
  16.1 4.9 %collective-permute-start.5 = (bf16[160,16,256]{2,1,0:T(8,128)(2,1)S(1)}, bf16[160,16,256]{2,1,0:T(8,128)(2,1)S(1)}, u32[]{:S(2)}, u32[]{:S(2)}) collective-permute-start(bf16[160,16,256]{2,1,0:T(8,128)(2,1)S(1)} %get-tuple-element.59), channel_id=1, source_target_pairs={{0,4},{4,0},{8,12},{12,8},{16,20},{20,16},{24,28},{28,24},{32,36},... | collective-permute-start | bytes 3932168 | tf_op jit(solution)/shard_map/ppermute | solution.py:282
  18.4 14.7 %collective-permute-start.6 = (bf16[2,256,256]{2,1,0:T(8,128)(2,1)S(1)}, bf16[2,256,256]{2,1,0:T(8,128)(2,1)S(1)}, u32[]{:S(2)}, u32[]{:S(2)}) collective-permute-start(bf16[2,256,256]{2,1,0:T(8,128)(2,1)S(1)} %get-tuple-element.60), channel_id=1, source_target_pairs={{4,8},{8,4},{12,16},{16,12},{20,24},{24,20},{28,32},{32,28},{36,40... | collective-permute-start | bytes 786440 | tf_op jit(solution)/shard_map/ppermute | solution.py:282
  21.3 14.8 %collective-permute-start.10 = (bf16[32,16,256]{2,1,0:T(8,128)(2,1)S(1)}, bf16[32,16,256]{2,1,0:T(8,128)(2,1)S(1)}, u32[]{:S(2)}, u32[]{:S(2)}) collective-permute-start(bf16[32,16,256]{2,1,0:T(8,128)(2,1)S(1)} %get-tuple-element.70), channel_id=1, source_target_pairs={{0,224},{4,36},{8,232},{12,44},{16,240},{20,52},{24,248},{28,60},{... | collective-permute-start | bytes 786440 | tf_op jit(solution)/shard_map/ppermute | solution.py:282
  31.5 9.2 %collective-permute-start.11 = (bf16[32,16,256]{2,1,0:T(8,128)(2,1)S(1)}, bf16[32,16,256]{2,1,0:T(8,128)(2,1)S(1)}, u32[]{:S(2)}, u32[]{:S(2)}) collective-permute-start(bf16[32,16,256]{2,1,0:T(8,128)(2,1)S(1)} %get-tuple-element.71), channel_id=1, source_target_pairs={{0,8},{4,28},{8,0},{12,20},{16,24},{20,12},{24,16},{28,4},{32,40},... | collective-permute-start | bytes 786440 | tf_op jit(solution)/shard_map/ppermute | solution.py:282
  31.5 9.2 %collective-permute-start.12 = (bf16[32,16,256]{2,1,0:T(8,128)(2,1)S(1)}, bf16[32,16,256]{2,1,0:T(8,128)(2,1)S(1)}, u32[]{:S(2)}, u32[]{:S(2)}) collective-permute-start(bf16[32,16,256]{2,1,0:T(8,128)(2,1)S(1)} %get-tuple-element.72), channel_id=1, source_target_pairs={{0,232},{4,60},{8,224},{12,52},{16,248},{20,44},{24,240},{28,36},{... | collective-permute-start | bytes 786440 | tf_op jit(solution)/shard_map/ppermute | solution.py:282
  33.8 22.6 %collective-permute-start.7 = (bf16[2,256,256]{2,1,0:T(8,128)(2,1)S(1)}, bf16[2,256,256]{2,1,0:T(8,128)(2,1)S(1)}, u32[]{:S(2)}, u32[]{:S(2)}) collective-permute-start(bf16[2,256,256]{2,1,0:T(8,128)(2,1)S(1)} %get-tuple-element.63), channel_id=1, source_target_pairs={{0,1},{1,0},{2,3},{3,2},{4,5},{5,4},{6,7},{7,6},{8,9},{9,8},{10,11... | collective-permute-start | bytes 786440 | tf_op jit(solution)/shard_map/ppermute | solution.py:282
  34.7 21.7 %collective-permute-start.8 = (bf16[2,256,256]{2,1,0:T(8,128)(2,1)S(1)}, bf16[2,256,256]{2,1,0:T(8,128)(2,1)S(1)}, u32[]{:S(2)}, u32[]{:S(2)}) collective-permute-start(bf16[2,256,256]{2,1,0:T(8,128)(2,1)S(1)} %get-tuple-element.64), channel_id=1, source_target_pairs={{0,2},{1,3},{2,0},{3,1},{4,6},{5,7},{6,4},{7,5},{8,10},{9,11},{10,... | collective-permute-start | bytes 786440 | tf_op jit(solution)/shard_map/ppermute | solution.py:282
  36.1 20.3 %collective-permute-start.9 = (bf16[2,256,256]{2,1,0:T(8,128)(2,1)S(1)}, bf16[2,256,256]{2,1,0:T(8,128)(2,1)S(1)}, u32[]{:S(2)}, u32[]{:S(2)}) collective-permute-start(bf16[2,256,256]{2,1,0:T(8,128)(2,1)S(1)} %get-tuple-element.65), channel_id=1, source_target_pairs={{0,3},{1,2},{2,1},{3,0},{4,7},{5,6},{6,5},{7,4},{8,11},{9,10},{10,... | collective-permute-start | bytes 786440 | tf_op jit(solution)/shard_map/ppermute | solution.py:282
  40.8 4.4 %collective-permute-start.13 = (bf16[8,16,256]{2,1,0:T(8,128)(2,1)S(1)}, bf16[8,16,256]{2,1,0:T(8,128)(2,1)S(1)}, u32[]{:S(2)}, u32[]{:S(2)}) collective-permute-start(bf16[8,16,256]{2,1,0:T(8,128)(2,1)S(1)} %get-tuple-element.74), channel_id=1, source_target_pairs={{0,32},{4,228},{8,40},{12,236},{16,48},{20,244},{24,56},{28,252},{... | collective-permute-start | bytes 196616 | tf_op jit(solution)/shard_map/ppermute | solution.py:282
  40.9 5.6 %collective-permute-start.14 = (bf16[8,16,256]{2,1,0:T(8,128)(2,1)S(1)}, bf16[8,16,256]{2,1,0:T(8,128)(2,1)S(1)}, u32[]{:S(2)}, u32[]{:S(2)}) collective-permute-start(bf16[8,16,256]{2,1,0:T(8,128)(2,1)S(1)} %get-tuple-element.75), channel_id=1, source_target_pairs={{0,24},{4,12},{8,16},{12,4},{16,8},{20,28},{24,0},{28,20},{32,56},... | collective-permute-start | bytes 196616 | tf_op jit(solution)/shard_map/ppermute | solution.py:282
  45.2 6.4 %collective-permute-start.15 = (bf16[8,16,256]{2,1,0:T(8,128)(2,1)S(1)}, bf16[8,16,256]{2,1,0:T(8,128)(2,1)S(1)}, u32[]{:S(2)}, u32[]{:S(2)}) collective-permute-start(bf16[8,16,256]{2,1,0:T(8,128)(2,1)S(1)} %get-tuple-element.76), channel_id=1, source_target_pairs={{0,56},{4,236},{8,48},{12,228},{16,40},{20,252},{24,32},{28,244},{... | collective-permute-start | bytes 196616 | tf_op jit(solution)/shard_map/ppermute | solution.py:282
  51.6 7.0 %collective-permute-start.16 = (bf16[4,16,256]{2,1,0:T(8,128)(2,1)S(1)}, bf16[4,16,256]{2,1,0:T(8,128)(2,1)S(1)}, u32[]{:S(2)}, u32[]{:S(2)}) collective-permute-start(bf16[4,16,256]{2,1,0:T(8,128)(2,1)S(1)} %get-tuple-element.78), channel_id=1, source_target_pairs={{0,160},{4,100},{8,168},{12,108},{16,176},{20,116},{24,184},{28,12... | collective-permute-start | bytes 98312 | tf_op jit(solution)/shard_map/ppermute | solution.py:282

commit v7 on v6

--- a/solution.py
+++ b/solution.py
@@ -14,6 +14,7 @@
 ROW = 256
 WIDTH = 256
 HEADS = WIDTH // HD
+FIRST_FLOPS, SECOND_FLOPS = 4_000_000_000, 4_000_000_000
 KEYS = 3 * ROW
 LOG2E = 1.4426950408889634
 BF = jnp.bfloat16
@@ -229,30 +230,38 @@
         out[...] = total.astype(out.dtype)
 
 
-def input_kernel(att, gq, own, near, far, wq, wk, wv, wo, p0, p1, p2, p3):
-    x = places()[3]
+def mp_partner(core, x, step):
+    near, across = x ^ 1, 3 - x
+    if isinstance(core, int):
+        return (near, across)[(core + step) % 2]
+    return jnp.where(core == step, near, across)
+
+
+def input_kernel(att, gq, own, near, far, wq, wk, wv, wo, keep, send):
+    core, _, _, x = places()
     grads = []
     for part in range(2):
         from_near = near[128 + 16 * part : 144 + 16 * part].reshape(ROW, WIDTH)
         grads.append((own[part] + from_near.astype(F32) + far[part].astype(F32)).astype(BF))
     grad_key, grad_value = grads
-    for place, out in enumerate((p0, p1, p2, p3)):
-        block = pl.ds(pl.multiple_of((x ^ place) * WIDTH, WIDTH), WIDTH)
-        out[0] = mm(att[...], wo[:, block]).astype(out.dtype)
-        out[1] = (
-            mm(gq[...], wq[block, :], NT)
-            + mm(grad_key, wk[block, :], NT)
-            + mm(grad_value, wv[block, :], NT)
-        ).astype(out.dtype)
-
-
-def mp_sum_kernel(p0, p1, p2, p3, out, grad):
+    first, second = (mp_partner(core, x, step) for step in range(2))
+    for out, targets in ((keep, (x, second)), (send, (first, x ^ 2))):
+        for place, target in enumerate(targets):
+            block = pl.ds(pl.multiple_of(target * WIDTH, WIDTH), WIDTH)
+            out[2 * place] = mm(att[...], wo[:, block]).astype(out.dtype)
+            out[2 * place + 1] = (
+                mm(gq[...], wq[block, :], NT)
+                + mm(grad_key, wk[block, :], NT)
+                + mm(grad_value, wv[block, :], NT)
+            ).astype(out.dtype)
+
+
+def mp_sum_kernel(kept, got, out, grad):
     for part, ref in ((0, out), (1, grad)):
-        total = (p0[part] + p1[part].astype(F32)) + (p2[part].astype(F32) + p3[part].astype(F32))
-        ref[...] = total.astype(BF)
-
-
-def last_sum_kernel(kept, got, dw):
+        ref[...] = (kept[part] + got[part].astype(F32)).astype(BF)
+
+
+def last_sum_kernel(after, kept, got, dw):
     dw[...] = kept[...] + got[...].astype(F32)
 
 
@@ -355,10 +364,10 @@
         moved=8_000_000,
     )
 
-    def share(name, terms, ways, kept_as):
-        part = (terms[0].shape[0] // ways,) + block
+    def share(name, terms, ways, kept_as, flops=0):
+        part = (terms[0].shape[0] // ways,) + terms[0].shape[1:]
         outs = [(part, kept_as)] + [(part, BF)] * (ways - 1)
-        return call(functools.partial(share_kernel, len(terms)), name, outs, terms)
+        return call(functools.partial(share_kernel, len(terms)), name, outs, terms, flops=flops)
 
     def over_chips(value, y_step, z_step):
         def target(i):
@@ -380,21 +389,28 @@
     grad_far = far_row(far)
     parts = four_ways(share("core_sum", [dw_keep, from_core], 4, BF), 0)
 
-    piece = (2, ROW, WIDTH)
-    pieces = call(
+    def over_mp(value, step):
+        def target(i):
+            return i // 4 * 4 + mp_partner(i // 4 % 2, i % 4, step)
+
+        return move(value, SPACE + ("mp",), target)
+
+    mp_keep, mp_send = call(
         input_kernel,
         "input_grad",
-        [(piece, F32)] + [(piece, BF)] * 3,
+        [((4, ROW, WIDTH), F32), ((4, ROW, WIDTH), BF)],
         [att, gq, own, from_core, grad_far, wq, wk, wv, wo],
         flops=540_000_000,
         moved=4_000_000,
     )
-    outs = [pieces[0]] + [across(pieces[s], s) for s in (1, 2, 3)]
-    parts = four_ways(share("first_sum", parts, 4, F32), 1)
-    keep, send = share("second_sum", parts, 2, F32)
+    mp_keep, mp_send = share("mp_share", [mp_keep, over_mp(mp_send, 0)], 2, F32)
+    parts = four_ways(share("first_sum", parts, 4, F32, FIRST_FLOPS), 1)
+    keep, send = share("second_sum", parts, 2, F32, SECOND_FLOPS)
     got = over_chips(send, None, 2)
-    output, grad_input = call(mp_sum_kernel, "mp_sum", [(square, BF)] * 2, outs, keep=False)
-    (dw,) = call(last_sum_kernel, "last_sum", [((4,) + block, F32)], [keep, got], keep=False)
+    output, grad_input = call(
+        mp_sum_kernel, "mp_sum", [(square, BF)] * 2, [mp_keep, over_mp(mp_send, 1)], keep=False
+    )
+    (dw,) = call(last_sum_kernel, "last_sum", [((4,) + block, F32)], [keep, got], apart=(output,), keep=False)
     return output, grad_input, dw
 
 

time: 59.4 us -> 56.4 us (0.949); the launches traced: 59.2 us -> 55.5 us
  waiting for transfers between devices: 16.8 us -> 13.4 us
    ppermute x17 -> x16, waiting for transfers between devices: 16.8 us -> 13.4 us  [move(): lax.ppermute(value, axis, [(i, target(i)) for i in range(count) if 0 <= t...]
    ppermute x17 -> x16, starting transfers between devices: 29.9 us -> 29.6 us  [move(): lax.ppermute(value, axis, [(i, target(i)) for i in range(count) if 0 <= t...]
    pallas_call x9 -> x10, Pallas kernels: 11.7 us -> 11.8 us  [call(): pl.pallas_call(kernel, out_shape=tuple(kept), in_specs=[pl.BlockSpec(memo...]
  transfers between devices with their start and end apart: 17 -> 16, of which waited for: 7 -> 7; matrix products, arithmetic and copies ran while one was open for 0% -> 0% of each run, Pallas kernels for 12% -> 13%
where the time goes in v7:
time: 56.4 us; the launch traced here: 55.5 us
  starting transfers between devices  29.6 us (52%)
  waiting for transfers between devices  13.4 us (24%)
  Pallas kernels  11.8 us (21%)
  between operations  0.75 us (1%)
    ppermute x16, starting transfers between devices, move(): lax.ppermute(value, axis, [(i, target(i)) for i in range(count) if 0 <= t...  29.6 us
    ppermute x16, waiting for transfers between devices, move(): lax.ppermute(value, axis, [(i, target(i)) for i in range(count) if 0 <= t...  13.4 us
    pallas_call x10, Pallas kernels, call(): pl.pallas_call(kernel, out_shape=tuple(kept), in_specs=[pl.BlockSpec(memo...  11.8 us
  transfers between devices with their start and end apart: 16, of which 7 were waited for; matrix products, arithmetic and copies ran while one was open for 0% of the time, Pallas kernels for 13%

profile of v7, /device:TPU:6, one launch (start us, length us, event | category | flops | bytes accessed | tf_op | source)
XLA Modules:
  0.0 55.5 jit_solution(8623192215515264923)
XLA Ops:
  0.6 0.1 collective-permute-start.1
  0.7 0.7 %collective-permute-start = (bf16[256,1024]{1,0:T(8,128)(2,1)}, bf16[256,1024]{1,0:T(8,128)(2,1)S(1)}, u32[]{:S(2)}, u32[]{:S(2)}) collective-permute-start(bf16[256,1024]{1,0:T(8,128)(2,1)} %act.1), channel_id=1, source_target_pairs={{4,8},{8,4},{12,16},{16,12},{20,24},{24,20},{28,32},{32,28},{36,40... | collective-permute-start | bytes 1572872 | tf_op jit(solution)/shard_map/ppermute | solution.py:291
  1.4 0.9 %collective-permute-start.2 = (bf16[256,256]{1,0:T(8,128)(2,1)}, bf16[256,256]{1,0:T(8,128)(2,1)S(1)}, u32[]{:S(2)}, u32[]{:S(2)}) collective-permute-start(bf16[256,256]{1,0:T(8,128)(2,1)} %cot.1), channel_id=1, source_target_pairs={{0,1},{1,0},{2,3},{3,2},{4,5},{5,4},{6,7},{7,6},{8,9},{9,8},{10,11... | collective-permute-start | bytes 393224 | tf_op jit(solution)/shard_map/ppermute | solution.py:291
  2.4 1.5 %collective-permute-start.4 = (bf16[256,256]{1,0:T(8,128)(2,1)}, bf16[256,256]{1,0:T(8,128)(2,1)S(1)}, u32[]{:S(2)}, u32[]{:S(2)}) collective-permute-start(bf16[256,256]{1,0:T(8,128)(2,1)} %cot.1), channel_id=1, source_target_pairs={{0,3},{1,2},{2,1},{3,0},{4,7},{5,6},{6,5},{7,4},{8,11},{9,10},{10,... | collective-permute-start | bytes 393224 | tf_op jit(solution)/shard_map/ppermute | solution.py:291
  3.8 1.8 %collective-permute-start.3 = (bf16[256,256]{1,0:T(8,128)(2,1)}, bf16[256,256]{1,0:T(8,128)(2,1)S(1)}, u32[]{:S(2)}, u32[]{:S(2)}) collective-permute-start(bf16[256,256]{1,0:T(8,128)(2,1)} %cot.1), channel_id=1, source_target_pairs={{0,2},{1,3},{2,0},{3,1},{4,6},{5,7},{6,4},{7,5},{8,10},{9,11},{10,... | collective-permute-start | bytes 393224 | tf_op jit(solution)/shard_map/ppermute | solution.py:291
  5.6 0.0 collective-permute-done.1.a_near
  5.6 3.1 %own_part.1 = (bf16[1024,256]{1,0:T(8,128)(2,1)S(1)}, bf16[1024,256]{1,0:T(8,128)(2,1)S(1)}, bf16[1024,256]{1,0:T(8,128)(2,1)S(1)}, bf16[256,1024]{1,0:T(8,128)(...) custom-call(bf16[256,1024]{1,0:T(8,128)(2,1)} %act.1, ...), custom_call_target="tpu_custom_call" | custom-call | flops 600000000 | bytes 6000000 | tf_op jit(solution)/shard_map/own_part/pallas_call | solution.py:276
  8.7 0.0 collective-permute-done.a_far
  8.7 2.1 %forward.1 = (bf16[768,256]{1,0:T(8,128)(2,1)S(1)}, bf16[768,256]{1,0:T(8,128)(2,1)S(1)}, bf16[768,1024]{1,0:T(8,128)(2,1)S(1)}, bf16[256,256]{1,0:T(8,128)(2,1)S(1)}, bf16[1024,256]{1,0:T(8,128)(2,1)S(1)}) custom-call(bf16[256,1024]{1,0:T(8,128)(2,1)S(1)} %collective-permute-done.a_far, bf16[1024,256]{1,0:T(8,128)(2,1)S(1)} %get-tuple-element.41.wk, ...), custom_call_target="tpu_custom_call" | custom-call | flops 2000000000 | bytes 6000000 | tf_op jit(solution)/shard_map/forward/pallas_call | solution.py:276
  10.8 0.0 collective-permute-done.2.c1
  10.8 0.0 collective-permute-done.4.c3
  10.8 1.3 %collective-permute-done.3.c2 = bf16[256,256]{1,0:T(8,128)(2,1)S(1)} collective-permute-done((bf16[256,256]{1,0:T(8,128)(2,1)}, bf16[256,256]{1,0:T(8,128)(2,1)S(1)}, u32[]{:S(2)}, u32[]{:S(2)}) %collective-permute-start.3) | collective-permute-done | bytes 131104 | tf_op jit(solution)/shard_map/ppermute | solution.py:291
  12.1 4.1 %backward.1 = (bf16[256,256]{1,0:T(8,128)(2,1)S(1)}, bf16[2,256,256]{2,1,0:T(8,128)(2,1)S(1)}, f32[2,256,256]{2,1,0:T(8,128)S(1)}, bf16[160,16,256]{2,1,0:T(8,128)(2,1)S(1)}, bf16[128,16,256]{2,1,0:T(8,128)(2,1)S(1)}) custom-call(bf16[768,256]{1,0:T(8,128)(2,1)S(1)} %get-tuple-element.48.keys, bf16[768,256]{1,0:T(8,128)(2,1)S(1)} %get-tuple-element.49.values, ...), custom_call_target="tpu_custom_call" | custom-call | flops 3000000000 | bytes 8000000 | tf_op jit(solution)/shard_map/backward/pallas_call | solution.py:276
  16.1 2.3 %collective-permute-start.5 = (bf16[160,16,256]{2,1,0:T(8,128)(2,1)S(1)}, bf16[160,16,256]{2,1,0:T(8,128)(2,1)S(1)}, u32[]{:S(2)}, u32[]{:S(2)}) collective-permute-start(bf16[160,16,256]{2,1,0:T(8,128)(2,1)S(1)} %get-tuple-element.59), channel_id=1, source_target_pairs={{0,4},{4,0},{8,12},{12,8},{16,20},{20,16},{24,28},{28,24},{32,36},... | collective-permute-start | bytes 3932168 | tf_op jit(solution)/shard_map/ppermute | solution.py:291
  18.4 0.7 %collective-permute-start.6 = (bf16[2,256,256]{2,1,0:T(8,128)(2,1)S(1)}, bf16[2,256,256]{2,1,0:T(8,128)(2,1)S(1)}, u32[]{:S(2)}, u32[]{:S(2)}) collective-permute-start(bf16[2,256,256]{2,1,0:T(8,128)(2,1)S(1)} %get-tuple-element.60), channel_id=1, source_target_pairs={{4,8},{8,4},{12,16},{16,12},{20,24},{24,20},{28,32},{32,28},{36,40... | collective-permute-start | bytes 786440 | tf_op jit(solution)/shard_map/ppermute | solution.py:291
  19.1 2.0 %collective-permute-done.5.near.refs_1_ = bf16[160,16,256]{2,1,0:T(8,128)(2,1)S(1)} collective-permute-done((bf16[160,16,256]{2,1,0:T(8,128)(2,1)S(1)}, bf16[160,16,256]{2,1,0:T(8,128)(2,1)S(1)}, u32[]{:S(2)}, u32[]{:S(2)}) %collective-permute-start.5) | collective-permute-done | bytes 1310752 | tf_op jit(solution)/shard_map/ppermute | solution.py:291
  21.1 0.2 core_sum.1
  21.3 10.2 %collective-permute-start.9 = (bf16[32,16,256]{2,1,0:T(8,128)(2,1)S(1)}, bf16[32,16,256]{2,1,0:T(8,128)(2,1)S(1)}, u32[]{:S(2)}, u32[]{:S(2)}) collective-permute-start(bf16[32,16,256]{2,1,0:T(8,128)(2,1)S(1)} %get-tuple-element.70), channel_id=1, source_target_pairs={{0,224},{4,36},{8,232},{12,44},{16,240},{20,52},{24,248},{28,60},{... | collective-permute-start | bytes 786440 | tf_op jit(solution)/shard_map/ppermute | solution.py:291
  31.5 0.0 collective-permute-start.10
  31.5 1.6 %collective-permute-start.11 = (bf16[32,16,256]{2,1,0:T(8,128)(2,1)S(1)}, bf16[32,16,256]{2,1,0:T(8,128)(2,1)S(1)}, u32[]{:S(2)}, u32[]{:S(2)}) collective-permute-start(bf16[32,16,256]{2,1,0:T(8,128)(2,1)S(1)} %get-tuple-element.72), channel_id=1, source_target_pairs={{0,232},{4,60},{8,224},{12,52},{16,248},{20,44},{24,240},{28,36},{... | collective-permute-start | bytes 786440 | tf_op jit(solution)/shard_map/ppermute | solution.py:291
  33.1 0.0 collective-permute-done.6.far
  33.1 0.7 %input_grad.1 = (f32[4,256,256]{2,1,0:T(8,128)S(1)}, bf16[4,256,256]{2,1,0:T(8,128)(2,1)S(1)}) custom-call(bf16[256,256]{1,0:T(8,128)(2,1)S(1)} %get-tuple-element.47.att, bf16[256,256]{1,0:T(8,128)(2,1)S(1)} %get-tuple-element.57.gq, f32[2,256,256]{2,1,0:T(8,128)S(1)} %get-tuple-element.58.own, ...), custom_call_target="tpu_custom_call" | custom-call | flops 540000000 | bytes 4000000 | tf_op jit(solution)/shard_map/input_grad/pallas_call | solution.py:276
  33.8 0.9 %collective-permute-start.7 = (bf16[4,256,256]{2,1,0:T(8,128)(2,1)S(1)}, bf16[4,256,256]{2,1,0:T(8,128)(2,1)S(1)}, u32[]{:S(2)}, u32[]{:S(2)}) collective-permute-start(bf16[4,256,256]{2,1,0:T(8,128)(2,1)S(1)} %get-tuple-element.63), channel_id=1, source_target_pairs={{0,1},{1,0},{2,3},{3,2},{4,7},{5,6},{6,5},{7,4},{8,9},{9,8},{10,11... | collective-permute-start | bytes 1572872 | tf_op jit(solution)/shard_map/ppermute | solution.py:291
  34.7 1.1 %collective-permute-done.9.refs_1_ = bf16[32,16,256]{2,1,0:T(8,128)(2,1)S(1)} collective-permute-done((bf16[32,16,256]{2,1,0:T(8,128)(2,1)S(1)}, bf16[32,16,256]{2,1,0:T(8,128)(2,1)S(1)}, u32[]{:S(2)}, u32[]{:S(2)}) %collective-permute-start.9) | collective-permute-done | bytes 262176 | tf_op jit(solution)/shard_map/ppermute | solution.py:291
  35.9 4.8 %collective-permute-done.10.refs_2_ = bf16[32,16,256]{2,1,0:T(8,128)(2,1)S(1)} collective-permute-done((bf16[32,16,256]{2,1,0:T(8,128)(2,1)S(1)}, bf16[32,16,256]{2,1,0:T(8,128)(2,1)S(1)}, u32[]{:S(2)}, u32[]{:S(2)}) %collective-permute-start.10) | collective-permute-done | bytes 262176 | tf_op jit(solution)/shard_map/ppermute | solution.py:291
  40.7 0.0 collective-permute-done.11.refs_3_
  40.7 0.1 first_sum.1
  40.8 0.1 collective-permute-start.12
  40.9 0.1 collective-permute-start.13
  41.0 4.6 %collective-permute-start.14 = (bf16[8,16,256]{2,1,0:T(8,128)(2,1)S(1)}, bf16[8,16,256]{2,1,0:T(8,128)(2,1)S(1)}, u32[]{:S(2)}, u32[]{:S(2)}) collective-permute-start(bf16[8,16,256]{2,1,0:T(8,128)(2,1)S(1)} %get-tuple-element.76), channel_id=1, source_target_pairs={{0,56},{4,236},{8,48},{12,228},{16,40},{20,252},{24,32},{28,244},{... | collective-permute-start | bytes 196616 | tf_op jit(solution)/shard_map/ppermute | solution.py:291
  45.6 0.0 collective-permute-done.7.refs_1_
  45.6 0.1 mp_share.1
  45.7 0.8 %collective-permute-start.8 = (bf16[2,256,256]{2,1,0:T(8,128)(2,1)S(1)}, bf16[2,256,256]{2,1,0:T(8,128)(2,1)S(1)}, u32[]{:S(2)}, u32[]{:S(2)}) collective-permute-start(bf16[2,256,256]{2,1,0:T(8,128)(2,1)S(1)} %get-tuple-element.65), channel_id=1, source_target_pairs={{0,3},{1,2},{2,1},{3,0},{4,5},{5,4},{6,7},{7,6},{8,11},{9,10},{10,... | collective-permute-start | bytes 786440 | tf_op jit(solution)/shard_map/ppermute | solution.py:291
  46.6 0.0 collective-permute-done.12.refs_1_
  46.6 0.0 collective-permute-done.13.refs_2_
  46.6 1.3 %collective-permute-done.14.refs_3_ = bf16[8,16,256]{2,1,0:T(8,128)(2,1)S(1)} collective-permute-done((bf16[8,16,256]{2,1,0:T(8,128)(2,1)S(1)}, bf16[8,16,256]{2,1,0:T(8,128)(2,1)S(1)}, u32[]{:S(2)}, u32[]{:S(2)}) %collective-permute-start.14) | collective-permute-done | bytes 65568 | tf_op jit(solution)/shard_map/ppermute | solution.py:291
  47.9 3.4 %collective-permute-start.15 = (bf16[4,16,256]{2,1,0:T(8,128)(2,1)S(1)}, bf16[4,16,256]{2,1,0:T(8,128)(2,1)S(1)}, u32[]{:S(2)}, u32[]{:S(2)}) collective-permute-start(bf16[4,16,256]{2,1,0:T(8,128)(2,1)S(1)} %get-tuple-element.78), channel_id=1, source_target_pairs={{0,160},{4,100},{8,168},{12,108},{16,176},{20,116},{24,184},{28,12... | collective-permute-start | bytes 98312 | tf_op jit(solution)/shard_map/ppermute | solution.py:291
  51.3 2.1 %collective-permute-done.8.got = bf16[2,256,256]{2,1,0:T(8,128)(2,1)S(1)} collective-permute-done((bf16[2,256,256]{2,1,0:T(8,128)(2,1)S(1)}, bf16[2,256,256]{2,1,0:T(8,128)(2,1)S(1)}, u32[]{:S(2)}, u32[]{:S(2)}) %collective-permute-start.8) | collective-permute-done | bytes 262176 | tf_op jit(solution)/shard_map/ppermute | solution.py:291
  53.4 0.7 %mp_sum.1 = (bf16[256,256]{1,0:T(8,128)(2,1)}, bf16[256,256]{1,0:T(8,128)(2,1)}) custom-call(f32[2,256,256]{2,1,0:T(8,128)S(1)} %get-tuple-element.64.kept, bf16[2,256,256]{2,1,0:T(8,128)(2,1)S(1)} %collective-permute-done.8.got), custom_call_target="tpu_custom_call" | custom-call | bytes 1000000 | tf_op jit(solution)/shard_map/mp_sum/pallas_call | solution.py:276
  54.1 0.8 %collective-permute-done.15.got = bf16[4,16,256]{2,1,0:T(8,128)(2,1)S(1)} collective-permute-done((bf16[4,16,256]{2,1,0:T(8,128)(2,1)S(1)}, bf16[4,16,256]{2,1,0:T(8,128)(2,1)S(1)}, u32[]{:S(2)}, u32[]{:S(2)}) %collective-permute-start.15) | collective-permute-done | bytes 32800 | tf_op jit(solution)/shard_map/ppermute | solution.py:291
  54.9 0.6 %last_sum.1 = f32[4,16,256]{2,1,0:T(8,128)} custom-call(bf16[256,256]{1,0:T(8,128)(2,1)} %get-tuple-element.38.after, f32[4,16,256]{2,1,0:T(8,128)S(1)} %get-tuple-element.77.kept, bf16[4,16,256]{2,1,0:T(8,128)(2,1)S(1)} %collective-permute-done.15.got), custom_call_target="tpu_custom_call" | custom-call | bytes 1000000 | tf_op jit(solution)/shard_map/last_sum/pallas_call | solution.py:276
  (1 shorter events, 0.0 us)
Async XLA Ops:
  0.6 5.0 %collective-permute-start.1 = (bf16[256,1024]{1,0:T(8,128)(2,1)}, bf16[256,1024]{1,0:T(8,128)(2,1)S(1)}, u32[]{:S(2)}, u32[]{:S(2)}) collective-permute-start(bf16[256,1024]{1,0:T(8,128)(2,1)} %act.1), channel_id=1, source_target_pairs={{0,4},{4,0},{8,12},{12,8},{16,20},{20,16},{24,28},{28,24},{32,36},... | collective-permute-start | bytes 1572872 | tf_op jit(solution)/shard_map/ppermute | solution.py:291
  0.7 8.0 %collective-permute-start = (bf16[256,1024]{1,0:T(8,128)(2,1)}, bf16[256,1024]{1,0:T(8,128)(2,1)S(1)}, u32[]{:S(2)}, u32[]{:S(2)}) collective-permute-start(bf16[256,1024]{1,0:T(8,128)(2,1)} %act.1), channel_id=1, source_target_pairs={{4,8},{8,4},{12,16},{16,12},{20,24},{24,20},{28,32},{32,28},{36,40... | collective-permute-start | bytes 1572872 | tf_op jit(solution)/shard_map/ppermute | solution.py:291
  1.4 9.4 %collective-permute-start.2 = (bf16[256,256]{1,0:T(8,128)(2,1)}, bf16[256,256]{1,0:T(8,128)(2,1)S(1)}, u32[]{:S(2)}, u32[]{:S(2)}) collective-permute-start(bf16[256,256]{1,0:T(8,128)(2,1)} %cot.1), channel_id=1, source_target_pairs={{0,1},{1,0},{2,3},{3,2},{4,5},{5,4},{6,7},{7,6},{8,9},{9,8},{10,11... | collective-permute-start | bytes 393224 | tf_op jit(solution)/shard_map/ppermute | solution.py:291
  2.4 8.5 %collective-permute-start.4 = (bf16[256,256]{1,0:T(8,128)(2,1)}, bf16[256,256]{1,0:T(8,128)(2,1)S(1)}, u32[]{:S(2)}, u32[]{:S(2)}) collective-permute-start(bf16[256,256]{1,0:T(8,128)(2,1)} %cot.1), channel_id=1, source_target_pairs={{0,3},{1,2},{2,1},{3,0},{4,7},{5,6},{6,5},{7,4},{8,11},{9,10},{10,... | collective-permute-start | bytes 393224 | tf_op jit(solution)/shard_map/ppermute | solution.py:291
  3.8 8.2 %collective-permute-start.3 = (bf16[256,256]{1,0:T(8,128)(2,1)}, bf16[256,256]{1,0:T(8,128)(2,1)S(1)}, u32[]{:S(2)}, u32[]{:S(2)}) collective-permute-start(bf16[256,256]{1,0:T(8,128)(2,1)} %cot.1), channel_id=1, source_target_pairs={{0,2},{1,3},{2,0},{3,1},{4,6},{5,7},{6,4},{7,5},{8,10},{9,11},{10,... | collective-permute-start | bytes 393224 | tf_op jit(solution)/shard_map/ppermute | solution.py:291
  16.1 4.9 %collective-permute-start.5 = (bf16[160,16,256]{2,1,0:T(8,128)(2,1)S(1)}, bf16[160,16,256]{2,1,0:T(8,128)(2,1)S(1)}, u32[]{:S(2)}, u32[]{:S(2)}) collective-permute-start(bf16[160,16,256]{2,1,0:T(8,128)(2,1)S(1)} %get-tuple-element.59), channel_id=1, source_target_pairs={{0,4},{4,0},{8,12},{12,8},{16,20},{20,16},{24,28},{28,24},{32,36},... | collective-permute-start | bytes 3932168 | tf_op jit(solution)/shard_map/ppermute | solution.py:291
  18.4 14.7 %collective-permute-start.6 = (bf16[2,256,256]{2,1,0:T(8,128)(2,1)S(1)}, bf16[2,256,256]{2,1,0:T(8,128)(2,1)S(1)}, u32[]{:S(2)}, u32[]{:S(2)}) collective-permute-start(bf16[2,256,256]{2,1,0:T(8,128)(2,1)S(1)} %get-tuple-element.60), channel_id=1, source_target_pairs={{4,8},{8,4},{12,16},{16,12},{20,24},{24,20},{28,32},{32,28},{36,40... | collective-permute-start | bytes 786440 | tf_op jit(solution)/shard_map/ppermute | solution.py:291
  21.3 14.5 %collective-permute-start.9 = (bf16[32,16,256]{2,1,0:T(8,128)(2,1)S(1)}, bf16[32,16,256]{2,1,0:T(8,128)(2,1)S(1)}, u32[]{:S(2)}, u32[]{:S(2)}) collective-permute-start(bf16[32,16,256]{2,1,0:T(8,128)(2,1)S(1)} %get-tuple-element.70), channel_id=1, source_target_pairs={{0,224},{4,36},{8,232},{12,44},{16,240},{20,52},{24,248},{28,60},{... | collective-permute-start | bytes 786440 | tf_op jit(solution)/shard_map/ppermute | solution.py:291
  31.5 9.2 %collective-permute-start.10 = (bf16[32,16,256]{2,1,0:T(8,128)(2,1)S(1)}, bf16[32,16,256]{2,1,0:T(8,128)(2,1)S(1)}, u32[]{:S(2)}, u32[]{:S(2)}) collective-permute-start(bf16[32,16,256]{2,1,0:T(8,128)(2,1)S(1)} %get-tuple-element.71), channel_id=1, source_target_pairs={{0,8},{4,28},{8,0},{12,20},{16,24},{20,12},{24,16},{28,4},{32,40},... | collective-permute-start | bytes 786440 | tf_op jit(solution)/shard_map/ppermute | solution.py:291
  31.5 9.2 %collective-permute-start.11 = (bf16[32,16,256]{2,1,0:T(8,128)(2,1)S(1)}, bf16[32,16,256]{2,1,0:T(8,128)(2,1)S(1)}, u32[]{:S(2)}, u32[]{:S(2)}) collective-permute-start(bf16[32,16,256]{2,1,0:T(8,128)(2,1)S(1)} %get-tuple-element.72), channel_id=1, source_target_pairs={{0,232},{4,60},{8,224},{12,52},{16,248},{20,44},{24,240},{28,36},{... | collective-permute-start | bytes 786440 | tf_op jit(solution)/shard_map/ppermute | solution.py:291
  33.8 11.8 %collective-permute-start.7 = (bf16[4,256,256]{2,1,0:T(8,128)(2,1)S(1)}, bf16[4,256,256]{2,1,0:T(8,128)(2,1)S(1)}, u32[]{:S(2)}, u32[]{:S(2)}) collective-permute-start(bf16[4,256,256]{2,1,0:T(8,128)(2,1)S(1)} %get-tuple-element.63), channel_id=1, source_target_pairs={{0,1},{1,0},{2,3},{3,2},{4,7},{5,6},{6,5},{7,4},{8,9},{9,8},{10,11... | collective-permute-start | bytes 1572872 | tf_op jit(solution)/shard_map/ppermute | solution.py:291
  40.8 5.7 %collective-permute-start.12 = (bf16[8,16,256]{2,1,0:T(8,128)(2,1)S(1)}, bf16[8,16,256]{2,1,0:T(8,128)(2,1)S(1)}, u32[]{:S(2)}, u32[]{:S(2)}) collective-permute-start(bf16[8,16,256]{2,1,0:T(8,128)(2,1)S(1)} %get-tuple-element.74), channel_id=1, source_target_pairs={{0,32},{4,228},{8,40},{12,236},{16,48},{20,244},{24,56},{28,252},{... | collective-permute-start | bytes 196616 | tf_op jit(solution)/shard_map/ppermute | solution.py:291
  40.9 5.6 %collective-permute-start.13 = (bf16[8,16,256]{2,1,0:T(8,128)(2,1)S(1)}, bf16[8,16,256]{2,1,0:T(8,128)(2,1)S(1)}, u32[]{:S(2)}, u32[]{:S(2)}) collective-permute-start(bf16[8,16,256]{2,1,0:T(8,128)(2,1)S(1)} %get-tuple-element.75), channel_id=1, source_target_pairs={{0,24},{4,12},{8,16},{12,4},{16,8},{20,28},{24,0},{28,20},{32,56},... | collective-permute-start | bytes 196616 | tf_op jit(solution)/shard_map/ppermute | solution.py:291
  41.0 6.8 %collective-permute-start.14 = (bf16[8,16,256]{2,1,0:T(8,128)(2,1)S(1)}, bf16[8,16,256]{2,1,0:T(8,128)(2,1)S(1)}, u32[]{:S(2)}, u32[]{:S(2)}) collective-permute-start(bf16[8,16,256]{2,1,0:T(8,128)(2,1)S(1)} %get-tuple-element.76), channel_id=1, source_target_pairs={{0,56},{4,236},{8,48},{12,228},{16,40},{20,252},{24,32},{28,244},{... | collective-permute-start | bytes 196616 | tf_op jit(solution)/shard_map/ppermute | solution.py:291
  45.7 7.7 %collective-permute-start.8 = (bf16[2,256,256]{2,1,0:T(8,128)(2,1)S(1)}, bf16[2,256,256]{2,1,0:T(8,128)(2,1)S(1)}, u32[]{:S(2)}, u32[]{:S(2)}) collective-permute-start(bf16[2,256,256]{2,1,0:T(8,128)(2,1)S(1)} %get-tuple-element.65), channel_id=1, source_target_pairs={{0,3},{1,2},{2,1},{3,0},{4,5},{5,4},{6,7},{7,6},{8,11},{9,10},{10,... | collective-permute-start | bytes 786440 | tf_op jit(solution)/shard_map/ppermute | solution.py:291
  47.9 7.0 %collective-permute-start.15 = (bf16[4,16,256]{2,1,0:T(8,128)(2,1)S(1)}, bf16[4,16,256]{2,1,0:T(8,128)(2,1)S(1)}, u32[]{:S(2)}, u32[]{:S(2)}) collective-permute-start(bf16[4,16,256]{2,1,0:T(8,128)(2,1)S(1)} %get-tuple-element.78), channel_id=1, source_target_pairs={{0,160},{4,100},{8,168},{12,108},{16,176},{20,116},{24,184},{28,12... | collective-permute-start | bytes 98312 | tf_op jit(solution)/shard_map/ppermute | solution.py:291

commit v8 on v7

--- a/solution.py
+++ b/solution.py
@@ -96,8 +96,15 @@
 )
 
 
-def columns(ref, x, step):
-    return ref[:, pl.ds(pl.multiple_of((x ^ step) * WIDTH, WIDTH), WIDTH)]
+def mp_partner(core, x, step):
+    near, across = x ^ 1, 3 - x
+    if isinstance(core, int):
+        return (near, across)[(core + step) % 2]
+    return jnp.where(core == step, near, across)
+
+
+def columns(ref, place):
+    return ref[:, pl.ds(pl.multiple_of(place * WIDTH, WIDTH), WIDTH)]
 
 
 def head_lanes():
@@ -143,7 +150,7 @@
     copies[6].wait()
     cot_t[...] = cot_s[...].T
     copies[7].wait()
-    grad_out[...] = mm(cot_s[...], columns(wo, x, 0), NT)
+    grad_out[...] = mm(cot_s[...], columns(wo, x), NT)
 
 
 def forward_kernel(
@@ -178,8 +185,9 @@
 ):
     core, y, z, x = places()
     grad_att = grad_in[...]
-    for step, block in ((1, c1), (2, c2), (3, c3)):
-        grad_att += mm(block[...], columns(wo, x, step), NT)
+    blocks = ((mp_partner(core, x, 0), c1), (mp_partner(core, x, 1), c2), (x ^ 2, c3))
+    for place, block in blocks:
+        grad_att += mm(block[...], columns(wo, place), NT)
     stack_heads(grad_att.astype(BF), grad_s)
     for head in range(HEADS):
         part = slice(head * ROW, (head + 1) * ROW)
@@ -200,8 +208,8 @@
             rows = slice(2 * ROW + 16 * block, 2 * ROW + 16 * (block + 1))
             send_out[128 + 16 * part + block] = grad[rows].astype(BF)
 
-    for step, block_t in ((0, cot_t[...]), (1, c1[...].T), (2, c2[...].T), (3, c3[...].T)):
-        rows = pl.ds(pl.multiple_of((x ^ step) * WIDTH, WIDTH), WIDTH)
+    for place, block_t in ((x, cot_t[...]), *((place, block[...].T) for place, block in blocks)):
+        rows = pl.ds(pl.multiple_of(place * WIDTH, WIDTH), WIDTH)
         dw_s[3, rows, :] = mm(block_t, att[...])
     grad_key = grad_key.astype(BF)
     grad_value = grad_value.astype(BF)
@@ -228,13 +236,6 @@
         for term in terms[1:]:
             total += term[part].astype(F32)
         out[...] = total.astype(out.dtype)
-
-
-def mp_partner(core, x, step):
-    near, across = x ^ 1, 3 - x
-    if isinstance(core, int):
-        return (near, across)[(core + step) % 2]
-    return jnp.where(core == step, near, across)
 
 
 def input_kernel(att, gq, own, near, far, wq, wk, wv, wo, keep, send):
@@ -286,6 +287,21 @@
     )(*[pltpu.with_memory_space_constraint(a, pltpu.HBM) for a in apart], *on_chip(*arrays))
 
 
+def hold_kernel(after, value, out):
+    pass
+
+
+def hold(value, after):
+    return pl.pallas_call(
+        hold_kernel,
+        out_shape=pltpu.VMEM(value.shape, value.dtype),
+        in_specs=[pl.BlockSpec(memory_space=pltpu.VMEM)] * 2,
+        out_specs=pl.BlockSpec(memory_space=pltpu.VMEM),
+        input_output_aliases={1: 0},
+        name="hold",
+    )(*on_chip(after, value))
+
+
 def move(value, axis, target):
     count = lax.axis_size(axis)
     return lax.ppermute(
@@ -293,8 +309,11 @@
     )
 
 
-def across(value, step):
-    return move(value, "mp", lambda i: i ^ step)
+def over_mp(value, step):
+    def target(i):
+        return i // 4 * 4 + mp_partner(i // 4 % 2, i % 4, step)
+
+    return move(value, SPACE + ("mp",), target)
 
 
 def near_row(value):
@@ -307,7 +326,7 @@
 
 def body(activations, w_query, w_key, w_value, w_out, grad_output, neighbours, pad_mask):
     act_far = far_row(activations)
-    cots = [across(grad_output, s) for s in (1, 2, 3)]
+    cots = [over_mp(grad_output, 0), over_mp(grad_output, 1)]
     act_near = near_row(activations)
 
     square = (ROW, WIDTH)
@@ -330,6 +349,9 @@
         flops=600_000_000,
         moved=6_000_000,
     )
+
+    cots[1] = hold(cots[1], bias)
+    cots.append(over_mp(cots[1], 0))
 
     block = (16, WIDTH)
     keys, values, probs, att, far_t = call(
@@ -380,20 +402,12 @@
         return move(value, SPACE, target)
 
     def four_ways(parts, step):
-        return [parts[0]] + [
-            over_chips(part, *partners)
-            for part, partners in zip(parts[1:], ((None, step), (step, None), (step, step)))
-        ]
+        along_z, along_y = over_chips(parts[1], None, step), over_chips(parts[2], step, None)
+        return [parts[0], over_chips(parts[3], step, step), along_y, along_z]
 
     from_core = near_row(dw_send)
     grad_far = far_row(far)
     parts = four_ways(share("core_sum", [dw_keep, from_core], 4, BF), 0)
-
-    def over_mp(value, step):
-        def target(i):
-            return i // 4 * 4 + mp_partner(i // 4 % 2, i % 4, step)
-
-        return move(value, SPACE + ("mp",), target)
 
     mp_keep, mp_send = call(
         input_kernel,

time: 56.4 us -> 60.7 us (1.076)
  the two profiles are of different devices: /device:TPU:6 before, /device:TPU:32 now
where the time goes in v8:
time: 60.7 us; the launch traced here: 60.5 us
  starting transfers between devices  31 us (51%)
  Pallas kernels  12.9 us (21%)
  waiting for transfers between devices  10.9 us (18%)
  local copies, waits for them, and re-layouts  4.86 us (8%)
  between operations  0.77 us (1%)
    ppermute x16, starting transfers between devices, move(): lax.ppermute(value, axis, [(i, target(i)) for i in range(count) if 0 <= t...  31 us
    pallas_call x10, Pallas kernels, call(): pl.pallas_call(kernel, out_shape=tuple(kept), in_specs=[pl.BlockSpec(memo...  12.9 us
    ppermute x16, waiting for transfers between devices, move(): lax.ppermute(value, axis, [(i, target(i)) for i in range(count) if 0 <= t...  10.9 us
    unnamed x16, local copies, waits for them, and re-layouts  4.86 us
  transfers between devices with their start and end apart: 16, of which 7 were waited for; matrix products, arithmetic and copies ran while one was open for 0% of the time, Pallas kernels for 14%

profile of v8, /device:TPU:32, one launch (start us, length us, event | category | flops | bytes accessed | tf_op | source)
XLA Modules:
  0.0 60.5 jit_solution(13990359292232731381)
XLA Ops:
  0.6 0.1 collective-permute-start.1
  0.7 4.6 %collective-permute-start = (bf16[256,1024]{1,0:T(8,128)(2,1)}, bf16[256,1024]{1,0:T(8,128)(2,1)}, u32[]{:S(2)}, u32[]{:S(2)}) collective-permute-start(bf16[256,1024]{1,0:T(8,128)(2,1)} %act.1), channel_id=1, source_target_pairs={{4,8},{8,4},{12,16},{16,12},{20,24},{24,20},{28,32},{32,28},{36,40... | collective-permute-start | bytes 1572872 | tf_op jit(solution)/shard_map/ppermute | solution.py:307
  5.3 2.8 %collective-permute-start.3 = (bf16[256,256]{1,0:T(8,128)(2,1)}, bf16[256,256]{1,0:T(8,128)(2,1)S(1)}, u32[]{:S(2)}, u32[]{:S(2)}) collective-permute-start(bf16[256,256]{1,0:T(8,128)(2,1)} %cot.1), channel_id=1, source_target_pairs={{0,3},{1,2},{2,1},{3,0},{4,5},{5,4},{6,7},{7,6},{8,11},{9,10},{10,... | collective-permute-start | bytes 393224 | tf_op jit(solution)/shard_map/ppermute | solution.py:307
  8.1 0.2 collective-permute-start.2
  8.4 0.0 collective-permute-done.1.a_near
  8.4 3.1 %own_part.1 = (bf16[1024,256]{1,0:T(8,128)(2,1)S(1)}, bf16[1024,256]{1,0:T(8,128)(2,1)S(1)}, bf16[1024,256]{1,0:T(8,128)(2,1)S(1)}, bf16[256,1024]{1,0:T(8,128)(...) custom-call(bf16[256,1024]{1,0:T(8,128)(2,1)} %act.1, ...), custom_call_target="tpu_custom_call" | custom-call | flops 600000000 | bytes 6000000 | tf_op jit(solution)/shard_map/own_part/pallas_call | solution.py:277
  11.5 0.0 copy-start
  11.5 0.8 %copy-done = bf16[1024,256]{1,0:T(8,128)(2,1)} copy-done((bf16[1024,256]{1,0:T(8,128)(2,1)}, bf16[1024,256]{1,0:T(8,128)(2,1)S(1)}, u32[]{:S(2)}) %copy-start) | copy-done | bytes 524312
  12.3 0.0 copy-start.2
  12.3 0.7 %copy-done.2 = f32[256,256]{1,0:T(8,128)} copy-done((f32[256,256]{1,0:T(8,128)}, f32[256,256]{1,0:T(8,128)S(1)}, u32[]{:S(2)}) %copy-start.2) | copy-done | bytes 262168
  13.0 0.0 copy-start.4
  13.0 0.7 %copy-done.4 = bf16[512,256]{1,0:T(8,128)(2,1)} copy-done((bf16[512,256]{1,0:T(8,128)(2,1)}, bf16[512,256]{1,0:T(8,128)(2,1)S(1)}, u32[]{:S(2)}) %copy-start.4) | copy-done | bytes 262168
  13.7 0.0 copy-start.6
  13.7 0.7 %copy-done.6 = bf16[512,256]{1,0:T(8,128)(2,1)} copy-done((bf16[512,256]{1,0:T(8,128)(2,1)}, bf16[512,256]{1,0:T(8,128)(2,1)S(1)}, u32[]{:S(2)}) %copy-start.6) | copy-done | bytes 262168
  14.4 0.0 collective-permute-done.3.value
  14.4 1.8 %collective-permute-start.4 = (bf16[256,256]{1,0:T(8,128)(2,1)S(1)}, bf16[256,256]{1,0:T(8,128)(2,1)S(1)}, u32[]{:S(2)}, u32[]{:S(2)}) collective-permute-start(bf16[256,256]{1,0:T(8,128)(2,1)S(1)} %hold.1.c2), channel_id=1, source_target_pairs={{0,1},{1,0},{2,3},{3,2},{4,7},{5,6},{6,5},{7,4},{8,9},{9,8},{10,11... | collective-permute-start | bytes 393224 | tf_op jit(solution)/shard_map/ppermute | solution.py:307
  16.2 0.0 collective-permute-done.a_far
  16.2 0.0 copy-start.5
  16.2 0.9 %copy-done.5 = bf16[512,256]{1,0:T(8,128)(2,1)S(1)} copy-done((bf16[512,256]{1,0:T(8,128)(2,1)S(1)}, bf16[512,256]{1,0:T(8,128)(2,1)}, u32[]{:S(2)}) %copy-start.5) | copy-done | bytes 262168
  17.2 0.0 copy-start.7
  17.2 0.9 %copy-done.7 = bf16[512,256]{1,0:T(8,128)(2,1)S(1)} copy-done((bf16[512,256]{1,0:T(8,128)(2,1)S(1)}, bf16[512,256]{1,0:T(8,128)(2,1)}, u32[]{:S(2)}) %copy-start.7) | copy-done | bytes 262168
  18.1 0.0 copy-start.1
  18.1 0.0 copy-start.3
  18.1 3.2 %forward.1 = (bf16[768,256]{1,0:T(8,128)(2,1)S(1)}, bf16[768,256]{1,0:T(8,128)(2,1)S(1)}, bf16[768,1024]{1,0:T(8,128)(2,1)S(1)}, bf16[256,256]{1,0:T(8,128)(2,1)S(1)}, bf16[1024,256]{1,0:T(8,128)(2,1)S(1)}) custom-call(bf16[256,1024]{1,0:T(8,128)(2,1)} %collective-permute-done.a_far, bf16[1024,256]{1,0:T(8,128)(2,1)S(1)} %get-tuple-element.41.wk, ...), custom_call_target="tpu_custom_call" | custom-call | flops 2000000000 | bytes 6000000 | tf_op jit(solution)/shard_map/forward/pallas_call | solution.py:277
  21.3 0.0 collective-permute-done.2.c1
  21.4 0.0 collective-permute-done.4.c3
  21.4 0.0 copy-done.1
  21.4 0.0 copy-done.3
  21.4 4.1 %backward.1 = (bf16[256,256]{1,0:T(8,128)(2,1)S(1)}, bf16[2,256,256]{2,1,0:T(8,128)(2,1)S(1)}, f32[2,256,256]{2,1,0:T(8,128)S(1)}, bf16[160,16,256]{2,1,0:T(8,128)(2,1)S(1)}, bf16[128,16,256]{2,1,0:T(8,128)(2,1)S(1)}) custom-call(bf16[768,256]{1,0:T(8,128)(2,1)S(1)} %get-tuple-element.48.keys, bf16[768,256]{1,0:T(8,128)(2,1)S(1)} %get-tuple-element.49.values, ...), custom_call_target="tpu_custom_call" | custom-call | flops 3000000000 | bytes 8000000 | tf_op jit(solution)/shard_map/backward/pallas_call | solution.py:277
  25.5 0.1 collective-permute-start.5
  25.6 2.7 %collective-permute-start.6 = (bf16[2,256,256]{2,1,0:T(8,128)(2,1)S(1)}, bf16[2,256,256]{2,1,0:T(8,128)(2,1)S(1)}, u32[]{:S(2)}, u32[]{:S(2)}) collective-permute-start(bf16[2,256,256]{2,1,0:T(8,128)(2,1)S(1)} %get-tuple-element.60), channel_id=1, source_target_pairs={{4,8},{8,4},{12,16},{16,12},{20,24},{24,20},{28,32},{32,28},{36,40... | collective-permute-start | bytes 786440 | tf_op jit(solution)/shard_map/ppermute | solution.py:307
  28.3 0.3 collective-permute-done.5.near.refs_1_
  28.6 0.2 core_sum.1
  28.8 2.5 %collective-permute-start.9 = (bf16[32,16,256]{2,1,0:T(8,128)(2,1)S(1)}, bf16[32,16,256]{2,1,0:T(8,128)(2,1)S(1)}, u32[]{:S(2)}, u32[]{:S(2)}) collective-permute-start(bf16[32,16,256]{2,1,0:T(8,128)(2,1)S(1)} %get-tuple-element.70), channel_id=1, source_target_pairs={{0,232},{4,60},{8,224},{12,52},{16,248},{20,44},{24,240},{28,36},{... | collective-permute-start | bytes 786440 | tf_op jit(solution)/shard_map/ppermute | solution.py:307
  31.3 1.0 %collective-permute-start.10 = (bf16[32,16,256]{2,1,0:T(8,128)(2,1)S(1)}, bf16[32,16,256]{2,1,0:T(8,128)(2,1)S(1)}, u32[]{:S(2)}, u32[]{:S(2)}) collective-permute-start(bf16[32,16,256]{2,1,0:T(8,128)(2,1)S(1)} %get-tuple-element.71), channel_id=1, source_target_pairs={{0,8},{4,28},{8,0},{12,20},{16,24},{20,12},{24,16},{28,4},{32,40},... | collective-permute-start | bytes 786440 | tf_op jit(solution)/shard_map/ppermute | solution.py:307
  32.3 0.1 collective-permute-start.11
  32.4 3.0 %collective-permute-done.6.far = bf16[2,256,256]{2,1,0:T(8,128)(2,1)S(1)} collective-permute-done((bf16[2,256,256]{2,1,0:T(8,128)(2,1)S(1)}, bf16[2,256,256]{2,1,0:T(8,128)(2,1)S(1)}, u32[]{:S(2)}, u32[]{:S(2)}) %collective-permute-start.6) | collective-permute-done | bytes 262176 | tf_op jit(solution)/shard_map/ppermute | solution.py:307
  35.4 0.7 %input_grad.1 = (f32[4,256,256]{2,1,0:T(8,128)S(1)}, bf16[4,256,256]{2,1,0:T(8,128)(2,1)S(1)}) custom-call(bf16[256,256]{1,0:T(8,128)(2,1)S(1)} %get-tuple-element.47.att, bf16[256,256]{1,0:T(8,128)(2,1)S(1)} %get-tuple-element.57.gq, f32[2,256,256]{2,1,0:T(8,128)S(1)} %get-tuple-element.58.own, ...), custom_call_target="tpu_custom_call" | custom-call | flops 540000000 | bytes 4000000 | tf_op jit(solution)/shard_map/input_grad/pallas_call | solution.py:277
  36.1 0.3 collective-permute-start.7
  36.4 0.0 collective-permute-done.9.refs_1_
  36.4 3.1 %collective-permute-done.10.refs_2_ = bf16[32,16,256]{2,1,0:T(8,128)(2,1)S(1)} collective-permute-done((bf16[32,16,256]{2,1,0:T(8,128)(2,1)S(1)}, bf16[32,16,256]{2,1,0:T(8,128)(2,1)S(1)}, u32[]{:S(2)}, u32[]{:S(2)}) %collective-permute-start.10) | collective-permute-done | bytes 262176 | tf_op jit(solution)/shard_map/ppermute | solution.py:307
  39.5 0.7 %collective-permute-done.11.refs_3_ = bf16[32,16,256]{2,1,0:T(8,128)(2,1)S(1)} collective-permute-done((bf16[32,16,256]{2,1,0:T(8,128)(2,1)S(1)}, bf16[32,16,256]{2,1,0:T(8,128)(2,1)S(1)}, u32[]{:S(2)}, u32[]{:S(2)}) %collective-permute-start.11) | collective-permute-done | bytes 262176 | tf_op jit(solution)/shard_map/ppermute | solution.py:307
  40.2 0.1 first_sum.1
  40.4 4.4 %collective-permute-start.12 = (bf16[8,16,256]{2,1,0:T(8,128)(2,1)S(1)}, bf16[8,16,256]{2,1,0:T(8,128)(2,1)S(1)}, u32[]{:S(2)}, u32[]{:S(2)}) collective-permute-start(bf16[8,16,256]{2,1,0:T(8,128)(2,1)S(1)} %get-tuple-element.74), channel_id=1, source_target_pairs={{0,56},{4,236},{8,48},{12,228},{16,40},{20,252},{24,32},{28,244},{... | collective-permute-start | bytes 196616 | tf_op jit(solution)/shard_map/ppermute | solution.py:307
  44.8 2.9 %collective-permute-start.13 = (bf16[8,16,256]{2,1,0:T(8,128)(2,1)S(1)}, bf16[8,16,256]{2,1,0:T(8,128)(2,1)S(1)}, u32[]{:S(2)}, u32[]{:S(2)}) collective-permute-start(bf16[8,16,256]{2,1,0:T(8,128)(2,1)S(1)} %get-tuple-element.75), channel_id=1, source_target_pairs={{0,24},{4,12},{8,16},{12,4},{16,8},{20,28},{24,0},{28,20},{32,56},... | collective-permute-start | bytes 196616 | tf_op jit(solution)/shard_map/ppermute | solution.py:307
  47.7 0.0 collective-permute-start.14
  47.7 0.0 collective-permute-done.7.refs_1_
  47.7 0.1 mp_share.1
  47.8 1.8 %collective-permute-start.8 = (bf16[2,256,256]{2,1,0:T(8,128)(2,1)S(1)}, bf16[2,256,256]{2,1,0:T(8,128)(2,1)S(1)}, u32[]{:S(2)}, u32[]{:S(2)}) collective-permute-start(bf16[2,256,256]{2,1,0:T(8,128)(2,1)S(1)} %get-tuple-element.65), channel_id=1, source_target_pairs={{0,3},{1,2},{2,1},{3,0},{4,5},{5,4},{6,7},{7,6},{8,11},{9,10},{10,... | collective-permute-start | bytes 786440 | tf_op jit(solution)/shard_map/ppermute | solution.py:307
  49.7 0.0 collective-permute-done.12.refs_1_
  49.7 0.6 collective-permute-done.13.refs_2_
  50.3 1.7 %collective-permute-done.14.refs_3_ = bf16[8,16,256]{2,1,0:T(8,128)(2,1)S(1)} collective-permute-done((bf16[8,16,256]{2,1,0:T(8,128)(2,1)S(1)}, bf16[8,16,256]{2,1,0:T(8,128)(2,1)S(1)}, u32[]{:S(2)}, u32[]{:S(2)}) %collective-permute-start.14) | collective-permute-done | bytes 65568 | tf_op jit(solution)/shard_map/ppermute | solution.py:307
  52.0 5.6 %collective-permute-start.15 = (bf16[4,16,256]{2,1,0:T(8,128)(2,1)S(1)}, bf16[4,16,256]{2,1,0:T(8,128)(2,1)S(1)}, u32[]{:S(2)}, u32[]{:S(2)}) collective-permute-start(bf16[4,16,256]{2,1,0:T(8,128)(2,1)S(1)} %get-tuple-element.78), channel_id=1, source_target_pairs={{0,160},{4,100},{8,168},{12,108},{16,176},{20,116},{24,184},{28,12... | collective-permute-start | bytes 98312 | tf_op jit(solution)/shard_map/ppermute | solution.py:307
  57.6 0.0 collective-permute-done.8.got
  57.6 0.7 %mp_sum.1 = (bf16[256,256]{1,0:T(8,128)(2,1)}, bf16[256,256]{1,0:T(8,128)(2,1)}) custom-call(f32[2,256,256]{2,1,0:T(8,128)S(1)} %get-tuple-element.64.kept, bf16[2,256,256]{2,1,0:T(8,128)(2,1)S(1)} %collective-permute-done.8.got), custom_call_target="tpu_custom_call" | custom-call | bytes 1000000 | tf_op jit(solution)/shard_map/mp_sum/pallas_call | solution.py:277
  58.3 1.5 %collective-permute-done.15.got = bf16[4,16,256]{2,1,0:T(8,128)(2,1)S(1)} collective-permute-done((bf16[4,16,256]{2,1,0:T(8,128)(2,1)S(1)}, bf16[4,16,256]{2,1,0:T(8,128)(2,1)S(1)}, u32[]{:S(2)}, u32[]{:S(2)}) %collective-permute-start.15) | collective-permute-done | bytes 32800 | tf_op jit(solution)/shard_map/ppermute | solution.py:307
  59.8 0.6 %last_sum.1 = f32[4,16,256]{2,1,0:T(8,128)} custom-call(bf16[256,256]{1,0:T(8,128)(2,1)} %get-tuple-element.38.after, f32[4,16,256]{2,1,0:T(8,128)S(1)} %get-tuple-element.77.kept, bf16[4,16,256]{2,1,0:T(8,128)(2,1)S(1)} %collective-permute-done.15.got), custom_call_target="tpu_custom_call" | custom-call | bytes 1000000 | tf_op jit(solution)/shard_map/last_sum/pallas_call | solution.py:277
  (2 shorter events, 0.0 us)
Async XLA Ops:
  0.6 7.7 %collective-permute-start.1 = (bf16[256,1024]{1,0:T(8,128)(2,1)}, bf16[256,1024]{1,0:T(8,128)(2,1)S(1)}, u32[]{:S(2)}, u32[]{:S(2)}) collective-permute-start(bf16[256,1024]{1,0:T(8,128)(2,1)} %act.1), channel_id=1, source_target_pairs={{0,4},{4,0},{8,12},{12,8},{16,20},{20,16},{24,28},{28,24},{32,36},... | collective-permute-start | bytes 1572872 | tf_op jit(solution)/shard_map/ppermute | solution.py:307
  0.7 15.5 %collective-permute-start = (bf16[256,1024]{1,0:T(8,128)(2,1)}, bf16[256,1024]{1,0:T(8,128)(2,1)}, u32[]{:S(2)}, u32[]{:S(2)}) collective-permute-start(bf16[256,1024]{1,0:T(8,128)(2,1)} %act.1), channel_id=1, source_target_pairs={{4,8},{8,4},{12,16},{16,12},{20,24},{24,20},{28,32},{32,28},{36,40... | collective-permute-start | bytes 1572872 | tf_op jit(solution)/shard_map/ppermute | solution.py:307
  5.3 9.1 %collective-permute-start.3 = (bf16[256,256]{1,0:T(8,128)(2,1)}, bf16[256,256]{1,0:T(8,128)(2,1)S(1)}, u32[]{:S(2)}, u32[]{:S(2)}) collective-permute-start(bf16[256,256]{1,0:T(8,128)(2,1)} %cot.1), channel_id=1, source_target_pairs={{0,3},{1,2},{2,1},{3,0},{4,5},{5,4},{6,7},{7,6},{8,11},{9,10},{10,... | collective-permute-start | bytes 393224 | tf_op jit(solution)/shard_map/ppermute | solution.py:307
  8.1 13.2 %collective-permute-start.2 = (bf16[256,256]{1,0:T(8,128)(2,1)}, bf16[256,256]{1,0:T(8,128)(2,1)S(1)}, u32[]{:S(2)}, u32[]{:S(2)}) collective-permute-start(bf16[256,256]{1,0:T(8,128)(2,1)} %cot.1), channel_id=1, source_target_pairs={{0,1},{1,0},{2,3},{3,2},{4,7},{5,6},{6,5},{7,4},{8,9},{9,8},{10,11... | collective-permute-start | bytes 393224 | tf_op jit(solution)/shard_map/ppermute | solution.py:307
  11.5 0.8 %copy-start = (bf16[1024,256]{1,0:T(8,128)(2,1)}, bf16[1024,256]{1,0:T(8,128)(2,1)S(1)}, u32[]{:S(2)}) copy-start(bf16[1024,256]{1,0:T(8,128)(2,1)S(1)} %get-tuple-element.52.near_t) | copy-start | bytes 1572868
  12.3 0.7 %copy-start.2 = (f32[256,256]{1,0:T(8,128)}, f32[256,256]{1,0:T(8,128)S(1)}, u32[]{:S(2)}) copy-start(f32[256,256]{1,0:T(8,128)S(1)} %get-tuple-element.55.grad_in) | copy-start | bytes 786436
  13.0 0.7 %copy-start.4 = (bf16[512,256]{1,0:T(8,128)(2,1)}, bf16[512,256]{1,0:T(8,128)(2,1)S(1)}, u32[]{:S(2)}) copy-start(bf16[512,256]{1,0:T(8,128)(2,1)S(1)} %get-tuple-element.44.keys_in) | copy-start | bytes 786436
  13.7 0.7 %copy-start.6 = (bf16[512,256]{1,0:T(8,128)(2,1)}, bf16[512,256]{1,0:T(8,128)(2,1)S(1)}, u32[]{:S(2)}) copy-start(bf16[512,256]{1,0:T(8,128)(2,1)S(1)} %get-tuple-element.45.values_in) | copy-start | bytes 786436
  14.4 6.9 %collective-permute-start.4 = (bf16[256,256]{1,0:T(8,128)(2,1)S(1)}, bf16[256,256]{1,0:T(8,128)(2,1)S(1)}, u32[]{:S(2)}, u32[]{:S(2)}) collective-permute-start(bf16[256,256]{1,0:T(8,128)(2,1)S(1)} %hold.1.c2), channel_id=1, source_target_pairs={{0,1},{1,0},{2,3},{3,2},{4,7},{5,6},{6,5},{7,4},{8,9},{9,8},{10,11... | collective-permute-start | bytes 393224 | tf_op jit(solution)/shard_map/ppermute | solution.py:307
  16.2 1.0 %copy-start.5 = (bf16[512,256]{1,0:T(8,128)(2,1)S(1)}, bf16[512,256]{1,0:T(8,128)(2,1)}, u32[]{:S(2)}) copy-start(bf16[512,256]{1,0:T(8,128)(2,1)} %copy-done.4) | copy-start | bytes 786436
  17.2 0.9 %copy-start.7 = (bf16[512,256]{1,0:T(8,128)(2,1)S(1)}, bf16[512,256]{1,0:T(8,128)(2,1)}, u32[]{:S(2)}) copy-start(bf16[512,256]{1,0:T(8,128)(2,1)} %copy-done.6) | copy-start | bytes 786436
  18.1 3.2 %copy-start.1 = (bf16[1024,256]{1,0:T(8,128)(2,1)S(1)}, bf16[1024,256]{1,0:T(8,128)(2,1)}, u32[]{:S(2)}) copy-start(bf16[1024,256]{1,0:T(8,128)(2,1)} %copy-done) | copy-start | bytes 1572868
  18.1 3.2 %copy-start.3 = (f32[256,256]{1,0:T(8,128)S(1)}, f32[256,256]{1,0:T(8,128)}, u32[]{:S(2)}) copy-start(f32[256,256]{1,0:T(8,128)} %copy-done.2) | copy-start | bytes 786436
  25.5 3.1 %collective-permute-start.5 = (bf16[160,16,256]{2,1,0:T(8,128)(2,1)S(1)}, bf16[160,16,256]{2,1,0:T(8,128)(2,1)S(1)}, u32[]{:S(2)}, u32[]{:S(2)}) collective-permute-start(bf16[160,16,256]{2,1,0:T(8,128)(2,1)S(1)} %get-tuple-element.59), channel_id=1, source_target_pairs={{0,4},{4,0},{8,12},{12,8},{16,20},{20,16},{24,28},{28,24},{32,36},... | collective-permute-start | bytes 3932168 | tf_op jit(solution)/shard_map/ppermute | solution.py:307
  25.6 9.8 %collective-permute-start.6 = (bf16[2,256,256]{2,1,0:T(8,128)(2,1)S(1)}, bf16[2,256,256]{2,1,0:T(8,128)(2,1)S(1)}, u32[]{:S(2)}, u32[]{:S(2)}) collective-permute-start(bf16[2,256,256]{2,1,0:T(8,128)(2,1)S(1)} %get-tuple-element.60), channel_id=1, source_target_pairs={{4,8},{8,4},{12,16},{16,12},{20,24},{24,20},{28,32},{32,28},{36,40... | collective-permute-start | bytes 786440 | tf_op jit(solution)/shard_map/ppermute | solution.py:307
  28.8 7.6 %collective-permute-start.9 = (bf16[32,16,256]{2,1,0:T(8,128)(2,1)S(1)}, bf16[32,16,256]{2,1,0:T(8,128)(2,1)S(1)}, u32[]{:S(2)}, u32[]{:S(2)}) collective-permute-start(bf16[32,16,256]{2,1,0:T(8,128)(2,1)S(1)} %get-tuple-element.70), channel_id=1, source_target_pairs={{0,232},{4,60},{8,224},{12,52},{16,248},{20,44},{24,240},{28,36},{... | collective-permute-start | bytes 786440 | tf_op jit(solution)/shard_map/ppermute | solution.py:307
  31.3 8.2 %collective-permute-start.10 = (bf16[32,16,256]{2,1,0:T(8,128)(2,1)S(1)}, bf16[32,16,256]{2,1,0:T(8,128)(2,1)S(1)}, u32[]{:S(2)}, u32[]{:S(2)}) collective-permute-start(bf16[32,16,256]{2,1,0:T(8,128)(2,1)S(1)} %get-tuple-element.71), channel_id=1, source_target_pairs={{0,8},{4,28},{8,0},{12,20},{16,24},{20,12},{24,16},{28,4},{32,40},... | collective-permute-start | bytes 786440 | tf_op jit(solution)/shard_map/ppermute | solution.py:307
  32.3 7.9 %collective-permute-start.11 = (bf16[32,16,256]{2,1,0:T(8,128)(2,1)S(1)}, bf16[32,16,256]{2,1,0:T(8,128)(2,1)S(1)}, u32[]{:S(2)}, u32[]{:S(2)}) collective-permute-start(bf16[32,16,256]{2,1,0:T(8,128)(2,1)S(1)} %get-tuple-element.72), channel_id=1, source_target_pairs={{0,224},{4,36},{8,232},{12,44},{16,240},{20,52},{24,248},{28,60},{... | collective-permute-start | bytes 786440 | tf_op jit(solution)/shard_map/ppermute | solution.py:307
  36.1 11.6 %collective-permute-start.7 = (bf16[4,256,256]{2,1,0:T(8,128)(2,1)S(1)}, bf16[4,256,256]{2,1,0:T(8,128)(2,1)S(1)}, u32[]{:S(2)}, u32[]{:S(2)}) collective-permute-start(bf16[4,256,256]{2,1,0:T(8,128)(2,1)S(1)} %get-tuple-element.63), channel_id=1, source_target_pairs={{0,1},{1,0},{2,3},{3,2},{4,7},{5,6},{6,5},{7,4},{8,9},{9,8},{10,11... | collective-permute-start | bytes 1572872 | tf_op jit(solution)/shard_map/ppermute | solution.py:307
  40.4 9.3 %collective-permute-start.12 = (bf16[8,16,256]{2,1,0:T(8,128)(2,1)S(1)}, bf16[8,16,256]{2,1,0:T(8,128)(2,1)S(1)}, u32[]{:S(2)}, u32[]{:S(2)}) collective-permute-start(bf16[8,16,256]{2,1,0:T(8,128)(2,1)S(1)} %get-tuple-element.74), channel_id=1, source_target_pairs={{0,56},{4,236},{8,48},{12,228},{16,40},{20,252},{24,32},{28,244},{... | collective-permute-start | bytes 196616 | tf_op jit(solution)/shard_map/ppermute | solution.py:307
  44.8 5.5 %collective-permute-start.13 = (bf16[8,16,256]{2,1,0:T(8,128)(2,1)S(1)}, bf16[8,16,256]{2,1,0:T(8,128)(2,1)S(1)}, u32[]{:S(2)}, u32[]{:S(2)}) collective-permute-start(bf16[8,16,256]{2,1,0:T(8,128)(2,1)S(1)} %get-tuple-element.75), channel_id=1, source_target_pairs={{0,24},{4,12},{8,16},{12,4},{16,8},{20,28},{24,0},{28,20},{32,56},... | collective-permute-start | bytes 196616 | tf_op jit(solution)/shard_map/ppermute | solution.py:307
  47.7 4.3 %collective-permute-start.14 = (bf16[8,16,256]{2,1,0:T(8,128)(2,1)S(1)}, bf16[8,16,256]{2,1,0:T(8,128)(2,1)S(1)}, u32[]{:S(2)}, u32[]{:S(2)}) collective-permute-start(bf16[8,16,256]{2,1,0:T(8,128)(2,1)S(1)} %get-tuple-element.76), channel_id=1, source_target_pairs={{0,32},{4,228},{8,40},{12,236},{16,48},{20,244},{24,56},{28,252},{... | collective-permute-start | bytes 196616 | tf_op jit(solution)/shard_map/ppermute | solution.py:307
  47.8 9.8 %collective-permute-start.8 = (bf16[2,256,256]{2,1,0:T(8,128)(2,1)S(1)}, bf16[2,256,256]{2,1,0:T(8,128)(2,1)S(1)}, u32[]{:S(2)}, u32[]{:S(2)}) collective-permute-start(bf16[2,256,256]{2,1,0:T(8,128)(2,1)S(1)} %get-tuple-element.65), channel_id=1, source_target_pairs={{0,3},{1,2},{2,1},{3,0},{4,5},{5,4},{6,7},{7,6},{8,11},{9,10},{10,... | collective-permute-start | bytes 786440 | tf_op jit(solution)/shard_map/ppermute | solution.py:307
  52.0 7.8 %collective-permute-start.15 = (bf16[4,16,256]{2,1,0:T(8,128)(2,1)S(1)}, bf16[4,16,256]{2,1,0:T(8,128)(2,1)S(1)}, u32[]{:S(2)}, u32[]{:S(2)}) collective-permute-start(bf16[4,16,256]{2,1,0:T(8,128)(2,1)S(1)} %get-tuple-element.78), channel_id=1, source_target_pairs={{0,160},{4,100},{8,168},{12,108},{16,176},{20,116},{24,184},{28,12... | collective-permute-start | bytes 98312 | tf_op jit(solution)/shard_map/ppermute | solution.py:307

commit v9 on v8

--- a/solution.py
+++ b/solution.py
@@ -298,6 +298,7 @@
         in_specs=[pl.BlockSpec(memory_space=pltpu.VMEM)] * 2,
         out_specs=pl.BlockSpec(memory_space=pltpu.VMEM),
         input_output_aliases={1: 0},
+        compiler_params=pltpu.CompilerParams(vmem_limit_bytes=1024 * 1024),
         name="hold",
     )(*on_chip(after, value))
 

time: 60.7 us -> 57.1 us (0.941)
  the two profiles are of different devices: /device:TPU:32 before, /device:TPU:192 now
where the time goes in v9:
time: 57.1 us; the launch traced here: 57 us
  starting transfers between devices  28.2 us (49%)
  waiting for transfers between devices  16.2 us (28%)
  Pallas kernels  11.8 us (21%)
  between operations  0.77 us (1%)
    ppermute x16, starting transfers between devices, move(): lax.ppermute(value, axis, [(i, target(i)) for i in range(count) if 0 <= t...  28.2 us
    ppermute x16, waiting for transfers between devices, move(): lax.ppermute(value, axis, [(i, target(i)) for i in range(count) if 0 <= t...  16.2 us
    pallas_call x10, Pallas kernels, call(): pl.pallas_call(kernel, out_shape=tuple(kept), in_specs=[pl.BlockSpec(memo...  11.8 us
  transfers between devices with their start and end apart: 16, of which 6 were waited for; matrix products, arithmetic and copies ran while one was open for 0% of the time, Pallas kernels for 12%

profile of v9, /device:TPU:192, one launch (start us, length us, event | category | flops | bytes accessed | tf_op | source)
XLA Modules:
  0.0 57.0 jit_solution(2267617781631671173)
XLA Ops:
  0.6 0.1 collective-permute-start.1
  0.7 5.5 %collective-permute-start = (bf16[256,1024]{1,0:T(8,128)(2,1)}, bf16[256,1024]{1,0:T(8,128)(2,1)S(1)}, u32[]{:S(2)}, u32[]{:S(2)}) collective-permute-start(bf16[256,1024]{1,0:T(8,128)(2,1)} %act.1), channel_id=1, source_target_pairs={{4,8},{8,4},{12,16},{16,12},{20,24},{24,20},{28,32},{32,28},{36,40... | collective-permute-start | bytes 1572872 | tf_op jit(solution)/shard_map/ppermute | solution.py:308
  6.2 2.8 %collective-permute-start.3 = (bf16[256,256]{1,0:T(8,128)(2,1)}, bf16[256,256]{1,0:T(8,128)(2,1)S(1)}, u32[]{:S(2)}, u32[]{:S(2)}) collective-permute-start(bf16[256,256]{1,0:T(8,128)(2,1)} %cot.1), channel_id=1, source_target_pairs={{0,3},{1,2},{2,1},{3,0},{4,5},{5,4},{6,7},{7,6},{8,11},{9,10},{10,... | collective-permute-start | bytes 393224 | tf_op jit(solution)/shard_map/ppermute | solution.py:308
  9.0 0.2 collective-permute-start.2
  9.3 0.0 collective-permute-done.1.a_near
  9.3 3.1 %own_part.1 = (bf16[1024,256]{1,0:T(8,128)(2,1)S(1)}, bf16[1024,256]{1,0:T(8,128)(2,1)S(1)}, bf16[1024,256]{1,0:T(8,128)(2,1)S(1)}, bf16[256,1024]{1,0:T(8,128)(...) custom-call(bf16[256,1024]{1,0:T(8,128)(2,1)} %act.1, ...), custom_call_target="tpu_custom_call" | custom-call | flops 600000000 | bytes 6000000 | tf_op jit(solution)/shard_map/own_part/pallas_call | solution.py:277
  12.4 0.3 collective-permute-done.3.value
  12.7 1.6 %collective-permute-start.4 = (bf16[256,256]{1,0:T(8,128)(2,1)S(1)}, bf16[256,256]{1,0:T(8,128)(2,1)S(1)}, u32[]{:S(2)}, u32[]{:S(2)}) collective-permute-start(bf16[256,256]{1,0:T(8,128)(2,1)S(1)} %hold.1.c2), channel_id=1, source_target_pairs={{0,1},{1,0},{2,3},{3,2},{4,7},{5,6},{6,5},{7,4},{8,9},{9,8},{10,11... | collective-permute-start | bytes 393224 | tf_op jit(solution)/shard_map/ppermute | solution.py:308
  14.3 0.0 collective-permute-done.a_far
  14.3 2.1 %forward.1 = (bf16[768,256]{1,0:T(8,128)(2,1)S(1)}, bf16[768,256]{1,0:T(8,128)(2,1)S(1)}, bf16[768,1024]{1,0:T(8,128)(2,1)S(1)}, bf16[256,256]{1,0:T(8,128)(2,1)S(1)}, bf16[1024,256]{1,0:T(8,128)(2,1)S(1)}) custom-call(bf16[256,1024]{1,0:T(8,128)(2,1)S(1)} %collective-permute-done.a_far, bf16[1024,256]{1,0:T(8,128)(2,1)S(1)} %get-tuple-element.41.wk, ...), custom_call_target="tpu_custom_call" | custom-call | flops 2000000000 | bytes 6000000 | tf_op jit(solution)/shard_map/forward/pallas_call | solution.py:277
  16.4 0.0 collective-permute-done.2.c1
  16.4 1.3 %collective-permute-done.4.c3 = bf16[256,256]{1,0:T(8,128)(2,1)S(1)} collective-permute-done((bf16[256,256]{1,0:T(8,128)(2,1)S(1)}, bf16[256,256]{1,0:T(8,128)(2,1)S(1)}, u32[]{:S(2)}, u32[]{:S(2)}) %collective-permute-start.4) | collective-permute-done | bytes 131104 | tf_op jit(solution)/shard_map/ppermute | solution.py:308
  17.6 4.1 %backward.1 = (bf16[256,256]{1,0:T(8,128)(2,1)S(1)}, bf16[2,256,256]{2,1,0:T(8,128)(2,1)S(1)}, f32[2,256,256]{2,1,0:T(8,128)S(1)}, bf16[160,16,256]{2,1,0:T(8,128)(2,1)S(1)}, bf16[128,16,256]{2,1,0:T(8,128)(2,1)S(1)}) custom-call(bf16[768,256]{1,0:T(8,128)(2,1)S(1)} %get-tuple-element.48.keys, bf16[768,256]{1,0:T(8,128)(2,1)S(1)} %get-tuple-element.49.values, ...), custom_call_target="tpu_custom_call" | custom-call | flops 3000000000 | bytes 8000000 | tf_op jit(solution)/shard_map/backward/pallas_call | solution.py:277
  21.7 0.1 collective-permute-start.5
  21.8 3.9 %collective-permute-start.6 = (bf16[2,256,256]{2,1,0:T(8,128)(2,1)S(1)}, bf16[2,256,256]{2,1,0:T(8,128)(2,1)S(1)}, u32[]{:S(2)}, u32[]{:S(2)}) collective-permute-start(bf16[2,256,256]{2,1,0:T(8,128)(2,1)S(1)} %get-tuple-element.60), channel_id=1, source_target_pairs={{4,8},{8,4},{12,16},{16,12},{20,24},{24,20},{28,32},{32,28},{36,40... | collective-permute-start | bytes 786440 | tf_op jit(solution)/shard_map/ppermute | solution.py:308
  25.7 0.0 collective-permute-done.5.near.refs_1_
  25.8 0.2 core_sum.1
  26.0 0.6 %collective-permute-start.9 = (bf16[32,16,256]{2,1,0:T(8,128)(2,1)S(1)}, bf16[32,16,256]{2,1,0:T(8,128)(2,1)S(1)}, u32[]{:S(2)}, u32[]{:S(2)}) collective-permute-start(bf16[32,16,256]{2,1,0:T(8,128)(2,1)S(1)} %get-tuple-element.70), channel_id=1, source_target_pairs={{0,232},{4,60},{8,224},{12,52},{16,248},{20,44},{24,240},{28,36},{... | collective-permute-start | bytes 786440 | tf_op jit(solution)/shard_map/ppermute | solution.py:308
  26.6 2.0 %collective-permute-start.10 = (bf16[32,16,256]{2,1,0:T(8,128)(2,1)S(1)}, bf16[32,16,256]{2,1,0:T(8,128)(2,1)S(1)}, u32[]{:S(2)}, u32[]{:S(2)}) collective-permute-start(bf16[32,16,256]{2,1,0:T(8,128)(2,1)S(1)} %get-tuple-element.71), channel_id=1, source_target_pairs={{0,8},{4,28},{8,0},{12,20},{16,24},{20,12},{24,16},{28,4},{32,40},... | collective-permute-start | bytes 786440 | tf_op jit(solution)/shard_map/ppermute | solution.py:308
  28.6 1.0 %collective-permute-start.11 = (bf16[32,16,256]{2,1,0:T(8,128)(2,1)S(1)}, bf16[32,16,256]{2,1,0:T(8,128)(2,1)S(1)}, u32[]{:S(2)}, u32[]{:S(2)}) collective-permute-start(bf16[32,16,256]{2,1,0:T(8,128)(2,1)S(1)} %get-tuple-element.72), channel_id=1, source_target_pairs={{0,224},{4,36},{8,232},{12,44},{16,240},{20,52},{24,248},{28,60},{... | collective-permute-start | bytes 786440 | tf_op jit(solution)/shard_map/ppermute | solution.py:308
  29.6 5.5 %collective-permute-done.6.far = bf16[2,256,256]{2,1,0:T(8,128)(2,1)S(1)} collective-permute-done((bf16[2,256,256]{2,1,0:T(8,128)(2,1)S(1)}, bf16[2,256,256]{2,1,0:T(8,128)(2,1)S(1)}, u32[]{:S(2)}, u32[]{:S(2)}) %collective-permute-start.6) | collective-permute-done | bytes 262176 | tf_op jit(solution)/shard_map/ppermute | solution.py:308
  35.1 0.7 %input_grad.1 = (f32[4,256,256]{2,1,0:T(8,128)S(1)}, bf16[4,256,256]{2,1,0:T(8,128)(2,1)S(1)}) custom-call(bf16[256,256]{1,0:T(8,128)(2,1)S(1)} %get-tuple-element.47.att, bf16[256,256]{1,0:T(8,128)(2,1)S(1)} %get-tuple-element.57.gq, f32[2,256,256]{2,1,0:T(8,128)S(1)} %get-tuple-element.58.own, ...), custom_call_target="tpu_custom_call" | custom-call | flops 540000000 | bytes 4000000 | tf_op jit(solution)/shard_map/input_grad/pallas_call | solution.py:277
  35.9 1.6 %collective-permute-start.7 = (bf16[4,256,256]{2,1,0:T(8,128)(2,1)S(1)}, bf16[4,256,256]{2,1,0:T(8,128)(2,1)S(1)}, u32[]{:S(2)}, u32[]{:S(2)}) collective-permute-start(bf16[4,256,256]{2,1,0:T(8,128)(2,1)S(1)} %get-tuple-element.63), channel_id=1, source_target_pairs={{0,1},{1,0},{2,3},{3,2},{4,7},{5,6},{6,5},{7,4},{8,9},{9,8},{10,11... | collective-permute-start | bytes 1572872 | tf_op jit(solution)/shard_map/ppermute | solution.py:308
  37.5 0.0 collective-permute-done.9.refs_1_
  37.5 0.0 collective-permute-done.10.refs_2_
  37.5 0.0 collective-permute-done.11.refs_3_
  37.5 0.1 first_sum.1
  37.6 0.1 collective-permute-start.12
  37.8 2.2 %collective-permute-start.13 = (bf16[8,16,256]{2,1,0:T(8,128)(2,1)S(1)}, bf16[8,16,256]{2,1,0:T(8,128)(2,1)S(1)}, u32[]{:S(2)}, u32[]{:S(2)}) collective-permute-start(bf16[8,16,256]{2,1,0:T(8,128)(2,1)S(1)} %get-tuple-element.75), channel_id=1, source_target_pairs={{0,24},{4,12},{8,16},{12,4},{16,8},{20,28},{24,0},{28,20},{32,56},... | collective-permute-start | bytes 196616 | tf_op jit(solution)/shard_map/ppermute | solution.py:308
  40.0 2.5 %collective-permute-start.14 = (bf16[8,16,256]{2,1,0:T(8,128)(2,1)S(1)}, bf16[8,16,256]{2,1,0:T(8,128)(2,1)S(1)}, u32[]{:S(2)}, u32[]{:S(2)}) collective-permute-start(bf16[8,16,256]{2,1,0:T(8,128)(2,1)S(1)} %get-tuple-element.76), channel_id=1, source_target_pairs={{0,32},{4,228},{8,40},{12,236},{16,48},{20,244},{24,56},{28,252},{... | collective-permute-start | bytes 196616 | tf_op jit(solution)/shard_map/ppermute | solution.py:308
  42.4 2.9 %collective-permute-done.7.refs_1_ = bf16[4,256,256]{2,1,0:T(8,128)(2,1)S(1)} collective-permute-done((bf16[4,256,256]{2,1,0:T(8,128)(2,1)S(1)}, bf16[4,256,256]{2,1,0:T(8,128)(2,1)S(1)}, u32[]{:S(2)}, u32[]{:S(2)}) %collective-permute-start.7) | collective-permute-done | bytes 524320 | tf_op jit(solution)/shard_map/ppermute | solution.py:308
  45.3 0.1 mp_share.1
  45.4 3.9 %collective-permute-start.8 = (bf16[2,256,256]{2,1,0:T(8,128)(2,1)S(1)}, bf16[2,256,256]{2,1,0:T(8,128)(2,1)S(1)}, u32[]{:S(2)}, u32[]{:S(2)}) collective-permute-start(bf16[2,256,256]{2,1,0:T(8,128)(2,1)S(1)} %get-tuple-element.65), channel_id=1, source_target_pairs={{0,3},{1,2},{2,1},{3,0},{4,5},{5,4},{6,7},{7,6},{8,11},{9,10},{10,... | collective-permute-start | bytes 786440 | tf_op jit(solution)/shard_map/ppermute | solution.py:308
  49.3 0.0 collective-permute-done.12.refs_1_
  49.3 0.0 collective-permute-done.13.refs_2_
  49.3 0.0 collective-permute-done.14.refs_3_
  49.3 0.1 collective-permute-start.15
  49.4 4.2 %collective-permute-done.8.got = bf16[2,256,256]{2,1,0:T(8,128)(2,1)S(1)} collective-permute-done((bf16[2,256,256]{2,1,0:T(8,128)(2,1)S(1)}, bf16[2,256,256]{2,1,0:T(8,128)(2,1)S(1)}, u32[]{:S(2)}, u32[]{:S(2)}) %collective-permute-start.8) | collective-permute-done | bytes 262176 | tf_op jit(solution)/shard_map/ppermute | solution.py:308
  53.6 0.7 %mp_sum.1 = (bf16[256,256]{1,0:T(8,128)(2,1)}, bf16[256,256]{1,0:T(8,128)(2,1)}) custom-call(f32[2,256,256]{2,1,0:T(8,128)S(1)} %get-tuple-element.64.kept, bf16[2,256,256]{2,1,0:T(8,128)(2,1)S(1)} %collective-permute-done.8.got), custom_call_target="tpu_custom_call" | custom-call | bytes 1000000 | tf_op jit(solution)/shard_map/mp_sum/pallas_call | solution.py:277
  54.4 2.0 %collective-permute-done.15.got = bf16[4,16,256]{2,1,0:T(8,128)(2,1)S(1)} collective-permute-done((bf16[4,16,256]{2,1,0:T(8,128)(2,1)S(1)}, bf16[4,16,256]{2,1,0:T(8,128)(2,1)S(1)}, u32[]{:S(2)}, u32[]{:S(2)}) %collective-permute-start.15) | collective-permute-done | bytes 32800 | tf_op jit(solution)/shard_map/ppermute | solution.py:308
  56.3 0.6 %last_sum.1 = f32[4,16,256]{2,1,0:T(8,128)} custom-call(bf16[256,256]{1,0:T(8,128)(2,1)} %get-tuple-element.38.after, f32[4,16,256]{2,1,0:T(8,128)S(1)} %get-tuple-element.77.kept, bf16[4,16,256]{2,1,0:T(8,128)(2,1)S(1)} %collective-permute-done.15.got), custom_call_target="tpu_custom_call" | custom-call | bytes 1000000 | tf_op jit(solution)/shard_map/last_sum/pallas_call | solution.py:277
  (2 shorter events, 0.0 us)
Async XLA Ops:
  0.6 8.6 %collective-permute-start.1 = (bf16[256,1024]{1,0:T(8,128)(2,1)}, bf16[256,1024]{1,0:T(8,128)(2,1)S(1)}, u32[]{:S(2)}, u32[]{:S(2)}) collective-permute-start(bf16[256,1024]{1,0:T(8,128)(2,1)} %act.1), channel_id=1, source_target_pairs={{0,4},{4,0},{8,12},{12,8},{16,20},{20,16},{24,28},{28,24},{32,36},... | collective-permute-start | bytes 1572872 | tf_op jit(solution)/shard_map/ppermute | solution.py:308
  0.7 13.5 %collective-permute-start = (bf16[256,1024]{1,0:T(8,128)(2,1)}, bf16[256,1024]{1,0:T(8,128)(2,1)S(1)}, u32[]{:S(2)}, u32[]{:S(2)}) collective-permute-start(bf16[256,1024]{1,0:T(8,128)(2,1)} %act.1), channel_id=1, source_target_pairs={{4,8},{8,4},{12,16},{16,12},{20,24},{24,20},{28,32},{32,28},{36,40... | collective-permute-start | bytes 1572872 | tf_op jit(solution)/shard_map/ppermute | solution.py:308
  6.2 6.5 %collective-permute-start.3 = (bf16[256,256]{1,0:T(8,128)(2,1)}, bf16[256,256]{1,0:T(8,128)(2,1)S(1)}, u32[]{:S(2)}, u32[]{:S(2)}) collective-permute-start(bf16[256,256]{1,0:T(8,128)(2,1)} %cot.1), channel_id=1, source_target_pairs={{0,3},{1,2},{2,1},{3,0},{4,5},{5,4},{6,7},{7,6},{8,11},{9,10},{10,... | collective-permute-start | bytes 393224 | tf_op jit(solution)/shard_map/ppermute | solution.py:308
  9.0 7.3 %collective-permute-start.2 = (bf16[256,256]{1,0:T(8,128)(2,1)}, bf16[256,256]{1,0:T(8,128)(2,1)S(1)}, u32[]{:S(2)}, u32[]{:S(2)}) collective-permute-start(bf16[256,256]{1,0:T(8,128)(2,1)} %cot.1), channel_id=1, source_target_pairs={{0,1},{1,0},{2,3},{3,2},{4,7},{5,6},{6,5},{7,4},{8,9},{9,8},{10,11... | collective-permute-start | bytes 393224 | tf_op jit(solution)/shard_map/ppermute | solution.py:308
  12.7 5.0 %collective-permute-start.4 = (bf16[256,256]{1,0:T(8,128)(2,1)S(1)}, bf16[256,256]{1,0:T(8,128)(2,1)S(1)}, u32[]{:S(2)}, u32[]{:S(2)}) collective-permute-start(bf16[256,256]{1,0:T(8,128)(2,1)S(1)} %hold.1.c2), channel_id=1, source_target_pairs={{0,1},{1,0},{2,3},{3,2},{4,7},{5,6},{6,5},{7,4},{8,9},{9,8},{10,11... | collective-permute-start | bytes 393224 | tf_op jit(solution)/shard_map/ppermute | solution.py:308
  21.7 4.0 %collective-permute-start.5 = (bf16[160,16,256]{2,1,0:T(8,128)(2,1)S(1)}, bf16[160,16,256]{2,1,0:T(8,128)(2,1)S(1)}, u32[]{:S(2)}, u32[]{:S(2)}) collective-permute-start(bf16[160,16,256]{2,1,0:T(8,128)(2,1)S(1)} %get-tuple-element.59), channel_id=1, source_target_pairs={{0,4},{4,0},{8,12},{12,8},{16,20},{20,16},{24,28},{28,24},{32,36},... | collective-permute-start | bytes 3932168 | tf_op jit(solution)/shard_map/ppermute | solution.py:308
  21.8 13.3 %collective-permute-start.6 = (bf16[2,256,256]{2,1,0:T(8,128)(2,1)S(1)}, bf16[2,256,256]{2,1,0:T(8,128)(2,1)S(1)}, u32[]{:S(2)}, u32[]{:S(2)}) collective-permute-start(bf16[2,256,256]{2,1,0:T(8,128)(2,1)S(1)} %get-tuple-element.60), channel_id=1, source_target_pairs={{4,8},{8,4},{12,16},{16,12},{20,24},{24,20},{28,32},{32,28},{36,40... | collective-permute-start | bytes 786440 | tf_op jit(solution)/shard_map/ppermute | solution.py:308
  26.0 11.5 %collective-permute-start.9 = (bf16[32,16,256]{2,1,0:T(8,128)(2,1)S(1)}, bf16[32,16,256]{2,1,0:T(8,128)(2,1)S(1)}, u32[]{:S(2)}, u32[]{:S(2)}) collective-permute-start(bf16[32,16,256]{2,1,0:T(8,128)(2,1)S(1)} %get-tuple-element.70), channel_id=1, source_target_pairs={{0,232},{4,60},{8,224},{12,52},{16,248},{20,44},{24,240},{28,36},{... | collective-permute-start | bytes 786440 | tf_op jit(solution)/shard_map/ppermute | solution.py:308
  26.6 10.9 %collective-permute-start.10 = (bf16[32,16,256]{2,1,0:T(8,128)(2,1)S(1)}, bf16[32,16,256]{2,1,0:T(8,128)(2,1)S(1)}, u32[]{:S(2)}, u32[]{:S(2)}) collective-permute-start(bf16[32,16,256]{2,1,0:T(8,128)(2,1)S(1)} %get-tuple-element.71), channel_id=1, source_target_pairs={{0,8},{4,28},{8,0},{12,20},{16,24},{20,12},{24,16},{28,4},{32,40},... | collective-permute-start | bytes 786440 | tf_op jit(solution)/shard_map/ppermute | solution.py:308
  28.6 8.9 %collective-permute-start.11 = (bf16[32,16,256]{2,1,0:T(8,128)(2,1)S(1)}, bf16[32,16,256]{2,1,0:T(8,128)(2,1)S(1)}, u32[]{:S(2)}, u32[]{:S(2)}) collective-permute-start(bf16[32,16,256]{2,1,0:T(8,128)(2,1)S(1)} %get-tuple-element.72), channel_id=1, source_target_pairs={{0,224},{4,36},{8,232},{12,44},{16,240},{20,52},{24,248},{28,60},{... | collective-permute-start | bytes 786440 | tf_op jit(solution)/shard_map/ppermute | solution.py:308
  35.9 9.5 %collective-permute-start.7 = (bf16[4,256,256]{2,1,0:T(8,128)(2,1)S(1)}, bf16[4,256,256]{2,1,0:T(8,128)(2,1)S(1)}, u32[]{:S(2)}, u32[]{:S(2)}) collective-permute-start(bf16[4,256,256]{2,1,0:T(8,128)(2,1)S(1)} %get-tuple-element.63), channel_id=1, source_target_pairs={{0,1},{1,0},{2,3},{3,2},{4,7},{5,6},{6,5},{7,4},{8,9},{9,8},{10,11... | collective-permute-start | bytes 1572872 | tf_op jit(solution)/shard_map/ppermute | solution.py:308
  37.6 11.6 %collective-permute-start.12 = (bf16[8,16,256]{2,1,0:T(8,128)(2,1)S(1)}, bf16[8,16,256]{2,1,0:T(8,128)(2,1)S(1)}, u32[]{:S(2)}, u32[]{:S(2)}) collective-permute-start(bf16[8,16,256]{2,1,0:T(8,128)(2,1)S(1)} %get-tuple-element.74), channel_id=1, source_target_pairs={{0,56},{4,236},{8,48},{12,228},{16,40},{20,252},{24,32},{28,244},{... | collective-permute-start | bytes 196616 | tf_op jit(solution)/shard_map/ppermute | solution.py:308
  37.8 11.5 %collective-permute-start.13 = (bf16[8,16,256]{2,1,0:T(8,128)(2,1)S(1)}, bf16[8,16,256]{2,1,0:T(8,128)(2,1)S(1)}, u32[]{:S(2)}, u32[]{:S(2)}) collective-permute-start(bf16[8,16,256]{2,1,0:T(8,128)(2,1)S(1)} %get-tuple-element.75), channel_id=1, source_target_pairs={{0,24},{4,12},{8,16},{12,4},{16,8},{20,28},{24,0},{28,20},{32,56},... | collective-permute-start | bytes 196616 | tf_op jit(solution)/shard_map/ppermute | solution.py:308
  40.0 9.3 %collective-permute-start.14 = (bf16[8,16,256]{2,1,0:T(8,128)(2,1)S(1)}, bf16[8,16,256]{2,1,0:T(8,128)(2,1)S(1)}, u32[]{:S(2)}, u32[]{:S(2)}) collective-permute-start(bf16[8,16,256]{2,1,0:T(8,128)(2,1)S(1)} %get-tuple-element.76), channel_id=1, source_target_pairs={{0,32},{4,228},{8,40},{12,236},{16,48},{20,244},{24,56},{28,252},{... | collective-permute-start | bytes 196616 | tf_op jit(solution)/shard_map/ppermute | solution.py:308
  45.4 8.2 %collective-permute-start.8 = (bf16[2,256,256]{2,1,0:T(8,128)(2,1)S(1)}, bf16[2,256,256]{2,1,0:T(8,128)(2,1)S(1)}, u32[]{:S(2)}, u32[]{:S(2)}) collective-permute-start(bf16[2,256,256]{2,1,0:T(8,128)(2,1)S(1)} %get-tuple-element.65), channel_id=1, source_target_pairs={{0,3},{1,2},{2,1},{3,0},{4,5},{5,4},{6,7},{7,6},{8,11},{9,10},{10,... | collective-permute-start | bytes 786440 | tf_op jit(solution)/shard_map/ppermute | solution.py:308
  49.3 7.0 %collective-permute-start.15 = (bf16[4,16,256]{2,1,0:T(8,128)(2,1)S(1)}, bf16[4,16,256]{2,1,0:T(8,128)(2,1)S(1)}, u32[]{:S(2)}, u32[]{:S(2)}) collective-permute-start(bf16[4,16,256]{2,1,0:T(8,128)(2,1)S(1)} %get-tuple-element.78), channel_id=1, source_target_pairs={{0,160},{4,100},{8,168},{12,108},{16,176},{20,116},{24,184},{28,12... | collective-permute-start | bytes 98312 | tf_op jit(solution)/shard_map/ppermute | solution.py:308

commit v10 on v8

--- a/solution.py
+++ b/solution.py
@@ -179,13 +179,13 @@
 
 
 def backward_kernel(
-    keys, values, probs_in, att, far_t, near_t, wo, query, act_t, grad_in, cot_t, c1, c2, c3,
+    keys, values, probs_in, att, far_t, near_t, wo, query, act_t, grad_in, cot_t, c2, c1, c3,
     gq_out, far_out, own_out, send_out, keep_out,
     grad_s, scores_s, scores_t, dw_s,
 ):
     core, y, z, x = places()
     grad_att = grad_in[...]
-    blocks = ((mp_partner(core, x, 0), c1), (mp_partner(core, x, 1), c2), (x ^ 2, c3))
+    blocks = ((x ^ 2, c2), (x ^ 1, c1), (x ^ 3, c3))
     for place, block in blocks:
         grad_att += mm(block[...], columns(wo, place), NT)
     stack_heads(grad_att.astype(BF), grad_s)
@@ -287,21 +287,6 @@
     )(*[pltpu.with_memory_space_constraint(a, pltpu.HBM) for a in apart], *on_chip(*arrays))
 
 
-def hold_kernel(after, value, out):
-    pass
-
-
-def hold(value, after):
-    return pl.pallas_call(
-        hold_kernel,
-        out_shape=pltpu.VMEM(value.shape, value.dtype),
-        in_specs=[pl.BlockSpec(memory_space=pltpu.VMEM)] * 2,
-        out_specs=pl.BlockSpec(memory_space=pltpu.VMEM),
-        input_output_aliases={1: 0},
-        name="hold",
-    )(*on_chip(after, value))
-
-
 def move(value, axis, target):
     count = lax.axis_size(axis)
     return lax.ppermute(
@@ -326,7 +311,7 @@
 
 def body(activations, w_query, w_key, w_value, w_out, grad_output, neighbours, pad_mask):
     act_far = far_row(activations)
-    cots = [over_mp(grad_output, 0), over_mp(grad_output, 1)]
+    cots = [move(grad_output, "mp", lambda i, step=step: i ^ step) for step in (2, 1, 3)]
     act_near = near_row(activations)
 
     square = (ROW, WIDTH)
@@ -349,9 +334,6 @@
         flops=600_000_000,
         moved=6_000_000,
     )
-
-    cots[1] = hold(cots[1], bias)
-    cots.append(over_mp(cots[1], 0))
 
     block = (16, WIDTH)
     keys, values, probs, att, far_t = call(

time: 60.7 us -> 57.5 us (0.947)
  local copies, waits for them, and re-layouts: 4.86 us -> 0 us
  starting transfers between devices: 31 us -> 34.3 us
  Pallas kernels: 12.9 us -> 11.8 us
    unnamed x16 -> x0, local copies, waits for them, and re-layouts: 4.86 us -> none
    ppermute x16, starting transfers between devices: 31 us -> 34.3 us  [move(): lax.ppermute(value, axis, [(i, target(i)) for i in range(count) if 0 <= t...]
    pallas_call x10, Pallas kernels: 12.9 us -> 11.8 us  [call(): pl.pallas_call(kernel, out_shape=tuple(kept), in_specs=[pl.BlockSpec(memo...]
  transfers between devices with their start and end apart: 16 -> 16, of which waited for: 7 -> 6; matrix products, arithmetic and copies ran while one was open for 0% -> 0% of each run, Pallas kernels for 14% -> 12%
where the time goes in v10:
time: 57.5 us; the launch traced here: 57.3 us
  starting transfers between devices  34.3 us (60%)
  Pallas kernels  11.8 us (21%)
  waiting for transfers between devices  10.4 us (18%)
  between operations  0.76 us (1%)
    ppermute x16, starting transfers between devices, move(): lax.ppermute(value, axis, [(i, target(i)) for i in range(count) if 0 <= t...  34.3 us
    pallas_call x10, Pallas kernels, call(): pl.pallas_call(kernel, out_shape=tuple(kept), in_specs=[pl.BlockSpec(memo...  11.8 us
    ppermute x16, waiting for transfers between devices, move(): lax.ppermute(value, axis, [(i, target(i)) for i in range(count) if 0 <= t...  10.4 us
  transfers between devices with their start and end apart: 16, of which 6 were waited for; matrix products, arithmetic and copies ran while one was open for 0% of the time, Pallas kernels for 12%

profile of v10, /device:TPU:32, one launch (start us, length us, event | category | flops | bytes accessed | tf_op | source)
XLA Modules:
  0.0 57.3 jit_solution(7846956038685988690)
XLA Ops:
  0.6 0.1 collective-permute-start.1
  0.7 4.6 %collective-permute-start = (bf16[256,1024]{1,0:T(8,128)(2,1)}, bf16[256,1024]{1,0:T(8,128)(2,1)S(1)}, u32[]{:S(2)}, u32[]{:S(2)}) collective-permute-start(bf16[256,1024]{1,0:T(8,128)(2,1)} %act.1), channel_id=1, source_target_pairs={{4,8},{8,4},{12,16},{16,12},{20,24},{24,20},{28,32},{32,28},{36,40... | collective-permute-start | bytes 1572872 | tf_op jit(solution)/shard_map/ppermute | solution.py:292
  5.3 3.1 %collective-permute-start.2 = (bf16[256,256]{1,0:T(8,128)(2,1)}, bf16[256,256]{1,0:T(8,128)(2,1)S(1)}, u32[]{:S(2)}, u32[]{:S(2)}) collective-permute-start(bf16[256,256]{1,0:T(8,128)(2,1)} %cot.1), channel_id=1, source_target_pairs={{0,2},{1,3},{2,0},{3,1},{4,6},{5,7},{6,4},{7,5},{8,10},{9,11},{10,... | collective-permute-start | bytes 393224 | tf_op jit(solution)/shard_map/ppermute | solution.py:292
  8.4 1.1 %collective-permute-start.4 = (bf16[256,256]{1,0:T(8,128)(2,1)}, bf16[256,256]{1,0:T(8,128)(2,1)S(1)}, u32[]{:S(2)}, u32[]{:S(2)}) collective-permute-start(bf16[256,256]{1,0:T(8,128)(2,1)} %cot.1), channel_id=1, source_target_pairs={{0,3},{1,2},{2,1},{3,0},{4,7},{5,6},{6,5},{7,4},{8,11},{9,10},{10,... | collective-permute-start | bytes 393224 | tf_op jit(solution)/shard_map/ppermute | solution.py:292
  9.5 0.0 collective-permute-start.3
  9.6 0.0 collective-permute-done.1.a_near
  9.6 3.1 %own_part.1 = (bf16[1024,256]{1,0:T(8,128)(2,1)S(1)}, bf16[1024,256]{1,0:T(8,128)(2,1)S(1)}, bf16[1024,256]{1,0:T(8,128)(2,1)S(1)}, bf16[256,1024]{1,0:T(8,128)(...) custom-call(bf16[256,1024]{1,0:T(8,128)(2,1)} %act.1, ...), custom_call_target="tpu_custom_call" | custom-call | flops 600000000 | bytes 6000000 | tf_op jit(solution)/shard_map/own_part/pallas_call | solution.py:277
  12.6 0.9 %collective-permute-done.a_far = bf16[256,1024]{1,0:T(8,128)(2,1)S(1)} collective-permute-done((bf16[256,1024]{1,0:T(8,128)(2,1)}, bf16[256,1024]{1,0:T(8,128)(2,1)S(1)}, u32[]{:S(2)}, u32[]{:S(2)}) %collective-permute-start) | collective-permute-done | bytes 524320 | tf_op jit(solution)/shard_map/ppermute | solution.py:292
  13.6 2.1 %forward.1 = (bf16[768,256]{1,0:T(8,128)(2,1)S(1)}, bf16[768,256]{1,0:T(8,128)(2,1)S(1)}, bf16[768,1024]{1,0:T(8,128)(2,1)S(1)}, bf16[256,256]{1,0:T(8,128)(2,1)S(1)}, bf16[1024,256]{1,0:T(8,128)(2,1)S(1)}) custom-call(bf16[256,1024]{1,0:T(8,128)(2,1)S(1)} %collective-permute-done.a_far, bf16[1024,256]{1,0:T(8,128)(2,1)S(1)} %get-tuple-element.41.wk, ...), custom_call_target="tpu_custom_call" | custom-call | flops 2000000000 | bytes 6000000 | tf_op jit(solution)/shard_map/forward/pallas_call | solution.py:277
  15.6 0.0 collective-permute-done.2.c2
  15.6 0.0 collective-permute-done.4.c3
  15.7 0.0 collective-permute-done.3.c1
  15.7 4.1 %backward.1 = (bf16[256,256]{1,0:T(8,128)(2,1)S(1)}, bf16[2,256,256]{2,1,0:T(8,128)(2,1)S(1)}, f32[2,256,256]{2,1,0:T(8,128)S(1)}, bf16[160,16,256]{2,1,0:T(8,128)(2,1)S(1)}, bf16[128,16,256]{2,1,0:T(8,128)(2,1)S(1)}) custom-call(bf16[768,256]{1,0:T(8,128)(2,1)S(1)} %get-tuple-element.48.keys, bf16[768,256]{1,0:T(8,128)(2,1)S(1)} %get-tuple-element.49.values, ...), custom_call_target="tpu_custom_call" | custom-call | flops 3000000000 | bytes 8000000 | tf_op jit(solution)/shard_map/backward/pallas_call | solution.py:277
  19.7 0.1 collective-permute-start.5
  19.8 4.6 %collective-permute-start.6 = (bf16[2,256,256]{2,1,0:T(8,128)(2,1)S(1)}, bf16[2,256,256]{2,1,0:T(8,128)(2,1)S(1)}, u32[]{:S(2)}, u32[]{:S(2)}) collective-permute-start(bf16[2,256,256]{2,1,0:T(8,128)(2,1)S(1)} %get-tuple-element.60), channel_id=1, source_target_pairs={{4,8},{8,4},{12,16},{16,12},{20,24},{24,20},{28,32},{32,28},{36,40... | collective-permute-start | bytes 786440 | tf_op jit(solution)/shard_map/ppermute | solution.py:292
  24.4 0.0 collective-permute-done.5.near.refs_1_
  24.4 0.2 core_sum.1
  24.7 0.9 %collective-permute-start.9 = (bf16[32,16,256]{2,1,0:T(8,128)(2,1)S(1)}, bf16[32,16,256]{2,1,0:T(8,128)(2,1)S(1)}, u32[]{:S(2)}, u32[]{:S(2)}) collective-permute-start(bf16[32,16,256]{2,1,0:T(8,128)(2,1)S(1)} %get-tuple-element.70), channel_id=1, source_target_pairs={{0,232},{4,60},{8,224},{12,52},{16,248},{20,44},{24,240},{28,36},{... | collective-permute-start | bytes 786440 | tf_op jit(solution)/shard_map/ppermute | solution.py:292
  25.6 2.6 %collective-permute-start.10 = (bf16[32,16,256]{2,1,0:T(8,128)(2,1)S(1)}, bf16[32,16,256]{2,1,0:T(8,128)(2,1)S(1)}, u32[]{:S(2)}, u32[]{:S(2)}) collective-permute-start(bf16[32,16,256]{2,1,0:T(8,128)(2,1)S(1)} %get-tuple-element.71), channel_id=1, source_target_pairs={{0,8},{4,28},{8,0},{12,20},{16,24},{20,12},{24,16},{28,4},{32,40},... | collective-permute-start | bytes 786440 | tf_op jit(solution)/shard_map/ppermute | solution.py:292
  28.1 0.1 collective-permute-start.11
  28.3 1.9 %collective-permute-done.6.far = bf16[2,256,256]{2,1,0:T(8,128)(2,1)S(1)} collective-permute-done((bf16[2,256,256]{2,1,0:T(8,128)(2,1)S(1)}, bf16[2,256,256]{2,1,0:T(8,128)(2,1)S(1)}, u32[]{:S(2)}, u32[]{:S(2)}) %collective-permute-start.6) | collective-permute-done | bytes 262176 | tf_op jit(solution)/shard_map/ppermute | solution.py:292
  30.1 0.7 %input_grad.1 = (f32[4,256,256]{2,1,0:T(8,128)S(1)}, bf16[4,256,256]{2,1,0:T(8,128)(2,1)S(1)}) custom-call(bf16[256,256]{1,0:T(8,128)(2,1)S(1)} %get-tuple-element.47.att, bf16[256,256]{1,0:T(8,128)(2,1)S(1)} %get-tuple-element.57.gq, f32[2,256,256]{2,1,0:T(8,128)S(1)} %get-tuple-element.58.own, ...), custom_call_target="tpu_custom_call" | custom-call | flops 540000000 | bytes 4000000 | tf_op jit(solution)/shard_map/input_grad/pallas_call | solution.py:277
  30.9 1.6 %collective-permute-start.7 = (bf16[4,256,256]{2,1,0:T(8,128)(2,1)S(1)}, bf16[4,256,256]{2,1,0:T(8,128)(2,1)S(1)}, u32[]{:S(2)}, u32[]{:S(2)}) collective-permute-start(bf16[4,256,256]{2,1,0:T(8,128)(2,1)S(1)} %get-tuple-element.63), channel_id=1, source_target_pairs={{0,1},{1,0},{2,3},{3,2},{4,7},{5,6},{6,5},{7,4},{8,9},{9,8},{10,11... | collective-permute-start | bytes 1572872 | tf_op jit(solution)/shard_map/ppermute | solution.py:292
  32.4 0.0 collective-permute-done.9.refs_1_
  32.4 2.4 %collective-permute-done.10.refs_2_ = bf16[32,16,256]{2,1,0:T(8,128)(2,1)S(1)} collective-permute-done((bf16[32,16,256]{2,1,0:T(8,128)(2,1)S(1)}, bf16[32,16,256]{2,1,0:T(8,128)(2,1)S(1)}, u32[]{:S(2)}, u32[]{:S(2)}) %collective-permute-start.10) | collective-permute-done | bytes 262176 | tf_op jit(solution)/shard_map/ppermute | solution.py:292
  34.8 2.4 %collective-permute-done.11.refs_3_ = bf16[32,16,256]{2,1,0:T(8,128)(2,1)S(1)} collective-permute-done((bf16[32,16,256]{2,1,0:T(8,128)(2,1)S(1)}, bf16[32,16,256]{2,1,0:T(8,128)(2,1)S(1)}, u32[]{:S(2)}, u32[]{:S(2)}) %collective-permute-start.11) | collective-permute-done | bytes 262176 | tf_op jit(solution)/shard_map/ppermute | solution.py:292
  37.2 0.1 first_sum.1
  37.4 1.8 %collective-permute-start.12 = (bf16[8,16,256]{2,1,0:T(8,128)(2,1)S(1)}, bf16[8,16,256]{2,1,0:T(8,128)(2,1)S(1)}, u32[]{:S(2)}, u32[]{:S(2)}) collective-permute-start(bf16[8,16,256]{2,1,0:T(8,128)(2,1)S(1)} %get-tuple-element.74), channel_id=1, source_target_pairs={{0,56},{4,236},{8,48},{12,228},{16,40},{20,252},{24,32},{28,244},{... | collective-permute-start | bytes 196616 | tf_op jit(solution)/shard_map/ppermute | solution.py:292
  39.1 4.4 %collective-permute-start.13 = (bf16[8,16,256]{2,1,0:T(8,128)(2,1)S(1)}, bf16[8,16,256]{2,1,0:T(8,128)(2,1)S(1)}, u32[]{:S(2)}, u32[]{:S(2)}) collective-permute-start(bf16[8,16,256]{2,1,0:T(8,128)(2,1)S(1)} %get-tuple-element.75), channel_id=1, source_target_pairs={{0,24},{4,12},{8,16},{12,4},{16,8},{20,28},{24,0},{28,20},{32,56},... | collective-permute-start | bytes 196616 | tf_op jit(solution)/shard_map/ppermute | solution.py:292
  43.6 0.0 collective-permute-start.14
  43.6 0.0 collective-permute-done.7.refs_1_
  43.6 0.1 mp_share.1
  43.7 2.9 %collective-permute-start.8 = (bf16[2,256,256]{2,1,0:T(8,128)(2,1)S(1)}, bf16[2,256,256]{2,1,0:T(8,128)(2,1)S(1)}, u32[]{:S(2)}, u32[]{:S(2)}) collective-permute-start(bf16[2,256,256]{2,1,0:T(8,128)(2,1)S(1)} %get-tuple-element.65), channel_id=1, source_target_pairs={{0,3},{1,2},{2,1},{3,0},{4,5},{5,4},{6,7},{7,6},{8,11},{9,10},{10,... | collective-permute-start | bytes 786440 | tf_op jit(solution)/shard_map/ppermute | solution.py:292
  46.5 0.0 collective-permute-done.12.refs_1_
  46.5 0.0 collective-permute-done.13.refs_2_
  46.5 1.3 %collective-permute-done.14.refs_3_ = bf16[8,16,256]{2,1,0:T(8,128)(2,1)S(1)} collective-permute-done((bf16[8,16,256]{2,1,0:T(8,128)(2,1)S(1)}, bf16[8,16,256]{2,1,0:T(8,128)(2,1)S(1)}, u32[]{:S(2)}, u32[]{:S(2)}) %collective-permute-start.14) | collective-permute-done | bytes 65568 | tf_op jit(solution)/shard_map/ppermute | solution.py:292
  47.9 6.6 %collective-permute-start.15 = (bf16[4,16,256]{2,1,0:T(8,128)(2,1)S(1)}, bf16[4,16,256]{2,1,0:T(8,128)(2,1)S(1)}, u32[]{:S(2)}, u32[]{:S(2)}) collective-permute-start(bf16[4,16,256]{2,1,0:T(8,128)(2,1)S(1)} %get-tuple-element.78), channel_id=1, source_target_pairs={{0,160},{4,100},{8,168},{12,108},{16,176},{20,116},{24,184},{28,12... | collective-permute-start | bytes 98312 | tf_op jit(solution)/shard_map/ppermute | solution.py:292
  54.5 0.0 collective-permute-done.8.got
  54.5 0.7 %mp_sum.1 = (bf16[256,256]{1,0:T(8,128)(2,1)}, bf16[256,256]{1,0:T(8,128)(2,1)}) custom-call(f32[2,256,256]{2,1,0:T(8,128)S(1)} %get-tuple-element.64.kept, bf16[2,256,256]{2,1,0:T(8,128)(2,1)S(1)} %collective-permute-done.8.got), custom_call_target="tpu_custom_call" | custom-call | bytes 1000000 | tf_op jit(solution)/shard_map/mp_sum/pallas_call | solution.py:277
  55.2 1.5 %collective-permute-done.15.got = bf16[4,16,256]{2,1,0:T(8,128)(2,1)S(1)} collective-permute-done((bf16[4,16,256]{2,1,0:T(8,128)(2,1)S(1)}, bf16[4,16,256]{2,1,0:T(8,128)(2,1)S(1)}, u32[]{:S(2)}, u32[]{:S(2)}) %collective-permute-start.15) | collective-permute-done | bytes 32800 | tf_op jit(solution)/shard_map/ppermute | solution.py:292
  56.7 0.6 %last_sum.1 = f32[4,16,256]{2,1,0:T(8,128)} custom-call(bf16[256,256]{1,0:T(8,128)(2,1)} %get-tuple-element.38.after, f32[4,16,256]{2,1,0:T(8,128)S(1)} %get-tuple-element.77.kept, bf16[4,16,256]{2,1,0:T(8,128)(2,1)S(1)} %collective-permute-done.15.got), custom_call_target="tpu_custom_call" | custom-call | bytes 1000000 | tf_op jit(solution)/shard_map/last_sum/pallas_call | solution.py:277
  (1 shorter events, 0.0 us)
Async XLA Ops:
  0.6 8.9 %collective-permute-start.1 = (bf16[256,1024]{1,0:T(8,128)(2,1)}, bf16[256,1024]{1,0:T(8,128)(2,1)S(1)}, u32[]{:S(2)}, u32[]{:S(2)}) collective-permute-start(bf16[256,1024]{1,0:T(8,128)(2,1)} %act.1), channel_id=1, source_target_pairs={{0,4},{4,0},{8,12},{12,8},{16,20},{20,16},{24,28},{28,24},{32,36},... | collective-permute-start | bytes 1572872 | tf_op jit(solution)/shard_map/ppermute | solution.py:292
  0.7 12.8 %collective-permute-start = (bf16[256,1024]{1,0:T(8,128)(2,1)}, bf16[256,1024]{1,0:T(8,128)(2,1)S(1)}, u32[]{:S(2)}, u32[]{:S(2)}) collective-permute-start(bf16[256,1024]{1,0:T(8,128)(2,1)} %act.1), channel_id=1, source_target_pairs={{4,8},{8,4},{12,16},{16,12},{20,24},{24,20},{28,32},{32,28},{36,40... | collective-permute-start | bytes 1572872 | tf_op jit(solution)/shard_map/ppermute | solution.py:292
  5.3 10.3 %collective-permute-start.2 = (bf16[256,256]{1,0:T(8,128)(2,1)}, bf16[256,256]{1,0:T(8,128)(2,1)S(1)}, u32[]{:S(2)}, u32[]{:S(2)}) collective-permute-start(bf16[256,256]{1,0:T(8,128)(2,1)} %cot.1), channel_id=1, source_target_pairs={{0,2},{1,3},{2,0},{3,1},{4,6},{5,7},{6,4},{7,5},{8,10},{9,11},{10,... | collective-permute-start | bytes 393224 | tf_op jit(solution)/shard_map/ppermute | solution.py:292
  8.4 7.2 %collective-permute-start.4 = (bf16[256,256]{1,0:T(8,128)(2,1)}, bf16[256,256]{1,0:T(8,128)(2,1)S(1)}, u32[]{:S(2)}, u32[]{:S(2)}) collective-permute-start(bf16[256,256]{1,0:T(8,128)(2,1)} %cot.1), channel_id=1, source_target_pairs={{0,3},{1,2},{2,1},{3,0},{4,7},{5,6},{6,5},{7,4},{8,11},{9,10},{10,... | collective-permute-start | bytes 393224 | tf_op jit(solution)/shard_map/ppermute | solution.py:292
  9.5 6.1 %collective-permute-start.3 = (bf16[256,256]{1,0:T(8,128)(2,1)}, bf16[256,256]{1,0:T(8,128)(2,1)S(1)}, u32[]{:S(2)}, u32[]{:S(2)}) collective-permute-start(bf16[256,256]{1,0:T(8,128)(2,1)} %cot.1), channel_id=1, source_target_pairs={{0,1},{1,0},{2,3},{3,2},{4,5},{5,4},{6,7},{7,6},{8,9},{9,8},{10,11... | collective-permute-start | bytes 393224 | tf_op jit(solution)/shard_map/ppermute | solution.py:292
  19.7 4.7 %collective-permute-start.5 = (bf16[160,16,256]{2,1,0:T(8,128)(2,1)S(1)}, bf16[160,16,256]{2,1,0:T(8,128)(2,1)S(1)}, u32[]{:S(2)}, u32[]{:S(2)}) collective-permute-start(bf16[160,16,256]{2,1,0:T(8,128)(2,1)S(1)} %get-tuple-element.59), channel_id=1, source_target_pairs={{0,4},{4,0},{8,12},{12,8},{16,20},{20,16},{24,28},{28,24},{32,36},... | collective-permute-start | bytes 3932168 | tf_op jit(solution)/shard_map/ppermute | solution.py:292
  19.8 10.3 %collective-permute-start.6 = (bf16[2,256,256]{2,1,0:T(8,128)(2,1)S(1)}, bf16[2,256,256]{2,1,0:T(8,128)(2,1)S(1)}, u32[]{:S(2)}, u32[]{:S(2)}) collective-permute-start(bf16[2,256,256]{2,1,0:T(8,128)(2,1)S(1)} %get-tuple-element.60), channel_id=1, source_target_pairs={{4,8},{8,4},{12,16},{16,12},{20,24},{24,20},{28,32},{32,28},{36,40... | collective-permute-start | bytes 786440 | tf_op jit(solution)/shard_map/ppermute | solution.py:292
  24.7 7.8 %collective-permute-start.9 = (bf16[32,16,256]{2,1,0:T(8,128)(2,1)S(1)}, bf16[32,16,256]{2,1,0:T(8,128)(2,1)S(1)}, u32[]{:S(2)}, u32[]{:S(2)}) collective-permute-start(bf16[32,16,256]{2,1,0:T(8,128)(2,1)S(1)} %get-tuple-element.70), channel_id=1, source_target_pairs={{0,232},{4,60},{8,224},{12,52},{16,248},{20,44},{24,240},{28,36},{... | collective-permute-start | bytes 786440 | tf_op jit(solution)/shard_map/ppermute | solution.py:292
  25.6 9.3 %collective-permute-start.10 = (bf16[32,16,256]{2,1,0:T(8,128)(2,1)S(1)}, bf16[32,16,256]{2,1,0:T(8,128)(2,1)S(1)}, u32[]{:S(2)}, u32[]{:S(2)}) collective-permute-start(bf16[32,16,256]{2,1,0:T(8,128)(2,1)S(1)} %get-tuple-element.71), channel_id=1, source_target_pairs={{0,8},{4,28},{8,0},{12,20},{16,24},{20,12},{24,16},{28,4},{32,40},... | collective-permute-start | bytes 786440 | tf_op jit(solution)/shard_map/ppermute | solution.py:292
  28.1 9.1 %collective-permute-start.11 = (bf16[32,16,256]{2,1,0:T(8,128)(2,1)S(1)}, bf16[32,16,256]{2,1,0:T(8,128)(2,1)S(1)}, u32[]{:S(2)}, u32[]{:S(2)}) collective-permute-start(bf16[32,16,256]{2,1,0:T(8,128)(2,1)S(1)} %get-tuple-element.72), channel_id=1, source_target_pairs={{0,224},{4,36},{8,232},{12,44},{16,240},{20,52},{24,248},{28,60},{... | collective-permute-start | bytes 786440 | tf_op jit(solution)/shard_map/ppermute | solution.py:292
  30.9 12.7 %collective-permute-start.7 = (bf16[4,256,256]{2,1,0:T(8,128)(2,1)S(1)}, bf16[4,256,256]{2,1,0:T(8,128)(2,1)S(1)}, u32[]{:S(2)}, u32[]{:S(2)}) collective-permute-start(bf16[4,256,256]{2,1,0:T(8,128)(2,1)S(1)} %get-tuple-element.63), channel_id=1, source_target_pairs={{0,1},{1,0},{2,3},{3,2},{4,7},{5,6},{6,5},{7,4},{8,9},{9,8},{10,11... | collective-permute-start | bytes 1572872 | tf_op jit(solution)/shard_map/ppermute | solution.py:292
  37.4 9.2 %collective-permute-start.12 = (bf16[8,16,256]{2,1,0:T(8,128)(2,1)S(1)}, bf16[8,16,256]{2,1,0:T(8,128)(2,1)S(1)}, u32[]{:S(2)}, u32[]{:S(2)}) collective-permute-start(bf16[8,16,256]{2,1,0:T(8,128)(2,1)S(1)} %get-tuple-element.74), channel_id=1, source_target_pairs={{0,56},{4,236},{8,48},{12,228},{16,40},{20,252},{24,32},{28,244},{... | collective-permute-start | bytes 196616 | tf_op jit(solution)/shard_map/ppermute | solution.py:292
  39.1 7.4 %collective-permute-start.13 = (bf16[8,16,256]{2,1,0:T(8,128)(2,1)S(1)}, bf16[8,16,256]{2,1,0:T(8,128)(2,1)S(1)}, u32[]{:S(2)}, u32[]{:S(2)}) collective-permute-start(bf16[8,16,256]{2,1,0:T(8,128)(2,1)S(1)} %get-tuple-element.75), channel_id=1, source_target_pairs={{0,24},{4,12},{8,16},{12,4},{16,8},{20,28},{24,0},{28,20},{32,56},... | collective-permute-start | bytes 196616 | tf_op jit(solution)/shard_map/ppermute | solution.py:292
  43.6 4.3 %collective-permute-start.14 = (bf16[8,16,256]{2,1,0:T(8,128)(2,1)S(1)}, bf16[8,16,256]{2,1,0:T(8,128)(2,1)S(1)}, u32[]{:S(2)}, u32[]{:S(2)}) collective-permute-start(bf16[8,16,256]{2,1,0:T(8,128)(2,1)S(1)} %get-tuple-element.76), channel_id=1, source_target_pairs={{0,32},{4,228},{8,40},{12,236},{16,48},{20,244},{24,56},{28,252},{... | collective-permute-start | bytes 196616 | tf_op jit(solution)/shard_map/ppermute | solution.py:292
  43.7 10.8 %collective-permute-start.8 = (bf16[2,256,256]{2,1,0:T(8,128)(2,1)S(1)}, bf16[2,256,256]{2,1,0:T(8,128)(2,1)S(1)}, u32[]{:S(2)}, u32[]{:S(2)}) collective-permute-start(bf16[2,256,256]{2,1,0:T(8,128)(2,1)S(1)} %get-tuple-element.65), channel_id=1, source_target_pairs={{0,3},{1,2},{2,1},{3,0},{4,5},{5,4},{6,7},{7,6},{8,11},{9,10},{10,... | collective-permute-start | bytes 786440 | tf_op jit(solution)/shard_map/ppermute | solution.py:292
  47.9 8.8 %collective-permute-start.15 = (bf16[4,16,256]{2,1,0:T(8,128)(2,1)S(1)}, bf16[4,16,256]{2,1,0:T(8,128)(2,1)S(1)}, u32[]{:S(2)}, u32[]{:S(2)}) collective-permute-start(bf16[4,16,256]{2,1,0:T(8,128)(2,1)S(1)} %get-tuple-element.78), channel_id=1, source_target_pairs={{0,160},{4,100},{8,168},{12,108},{16,176},{20,116},{24,184},{28,12... | collective-permute-start | bytes 98312 | tf_op jit(solution)/shard_map/ppermute | solution.py:292

commit v11 on v10

--- a/solution.py
+++ b/solution.py
@@ -91,8 +91,8 @@
 
 
 PARTNERS = (
+    ((y_other, y_pair), (z_pair, z_other, z_far)),
     ((y_pair, y_other), (z_other, z_pair, z_far_too)),
-    ((y_other, y_pair), (z_pair, z_other, z_far)),
 )
 
 
@@ -306,7 +306,7 @@
 
 
 def far_row(value):
-    return move(value, SPACE, lambda i: i + 1 if i % 2 else i - 1)
+    return move(value, SPACE, lambda i: (i + 1 if i % 2 else i - 1) % 64)
 
 
 def body(activations, w_query, w_key, w_value, w_out, grad_output, neighbours, pad_mask):

time: 57.5 us -> 55.6 us (0.967)
  the two profiles are of different devices: /device:TPU:32 before, /device:TPU:6 now
where the time goes in v11:
time: 55.6 us; the launch traced here: 55 us
  starting transfers between devices  28.8 us (52%)
  waiting for transfers between devices  13.6 us (24%)
  Pallas kernels  11.8 us (21%)
  between operations  0.75 us (1%)
    ppermute x16, starting transfers between devices, move(): lax.ppermute(value, axis, [(i, target(i)) for i in range(count) if 0 <= t...  28.8 us
    ppermute x16, waiting for transfers between devices, move(): lax.ppermute(value, axis, [(i, target(i)) for i in range(count) if 0 <= t...  13.6 us
    pallas_call x10, Pallas kernels, call(): pl.pallas_call(kernel, out_shape=tuple(kept), in_specs=[pl.BlockSpec(memo...  11.8 us
  transfers between devices with their start and end apart: 16, of which 8 were waited for; matrix products, arithmetic and copies ran while one was open for 0% of the time, Pallas kernels for 13%

profile of v11, /device:TPU:6, one launch (start us, length us, event | category | flops | bytes accessed | tf_op | source)
XLA Modules:
  0.0 55.0 jit_solution(11702785148628347495)
XLA Ops:
  0.6 0.1 collective-permute-start.1
  0.7 8.4 %collective-permute-start = (bf16[256,1024]{1,0:T(8,128)(2,1)}, bf16[256,1024]{1,0:T(8,128)(2,1)S(1)}, u32[]{:S(2)}, u32[]{:S(2)}) collective-permute-start(bf16[256,1024]{1,0:T(8,128)(2,1)} %act.1), channel_id=1, source_target_pairs={{0,252},{4,8},{8,4},{12,16},{16,12},{20,24},{24,20},{28,32},{32,28... | collective-permute-start | bytes 1572872 | tf_op jit(solution)/shard_map/ppermute | solution.py:292
  9.1 1.4 %collective-permute-start.2 = (bf16[256,256]{1,0:T(8,128)(2,1)}, bf16[256,256]{1,0:T(8,128)(2,1)S(1)}, u32[]{:S(2)}, u32[]{:S(2)}) collective-permute-start(bf16[256,256]{1,0:T(8,128)(2,1)} %cot.1), channel_id=1, source_target_pairs={{0,2},{1,3},{2,0},{3,1},{4,6},{5,7},{6,4},{7,5},{8,10},{9,11},{10,... | collective-permute-start | bytes 393224 | tf_op jit(solution)/shard_map/ppermute | solution.py:292
  10.5 2.1 %collective-permute-start.4 = (bf16[256,256]{1,0:T(8,128)(2,1)}, bf16[256,256]{1,0:T(8,128)(2,1)S(1)}, u32[]{:S(2)}, u32[]{:S(2)}) collective-permute-start(bf16[256,256]{1,0:T(8,128)(2,1)} %cot.1), channel_id=1, source_target_pairs={{0,3},{1,2},{2,1},{3,0},{4,7},{5,6},{6,5},{7,4},{8,11},{9,10},{10,... | collective-permute-start | bytes 393224 | tf_op jit(solution)/shard_map/ppermute | solution.py:292
  12.6 0.0 collective-permute-start.3
  12.6 0.0 collective-permute-done.1.a_near
  12.7 3.1 %own_part.1 = (bf16[1024,256]{1,0:T(8,128)(2,1)S(1)}, bf16[1024,256]{1,0:T(8,128)(2,1)S(1)}, bf16[1024,256]{1,0:T(8,128)(2,1)S(1)}, bf16[256,1024]{1,0:T(8,128)(...) custom-call(bf16[256,1024]{1,0:T(8,128)(2,1)} %act.1, ...), custom_call_target="tpu_custom_call" | custom-call | flops 600000000 | bytes 6000000 | tf_op jit(solution)/shard_map/own_part/pallas_call | solution.py:277
  15.7 0.5 collective-permute-done.a_far
  16.2 2.1 %forward.1 = (bf16[768,256]{1,0:T(8,128)(2,1)S(1)}, bf16[768,256]{1,0:T(8,128)(2,1)S(1)}, bf16[768,1024]{1,0:T(8,128)(2,1)S(1)}, bf16[256,256]{1,0:T(8,128)(2,1)S(1)}, bf16[1024,256]{1,0:T(8,128)(2,1)S(1)}) custom-call(bf16[256,1024]{1,0:T(8,128)(2,1)S(1)} %collective-permute-done.a_far, bf16[1024,256]{1,0:T(8,128)(2,1)S(1)} %get-tuple-element.41.wk, ...), custom_call_target="tpu_custom_call" | custom-call | flops 2000000000 | bytes 6000000 | tf_op jit(solution)/shard_map/forward/pallas_call | solution.py:277
  18.3 0.0 collective-permute-done.2.c2
  18.3 0.0 collective-permute-done.4.c3
  18.3 0.0 collective-permute-done.3.c1
  18.3 4.1 %backward.1 = (bf16[256,256]{1,0:T(8,128)(2,1)S(1)}, bf16[2,256,256]{2,1,0:T(8,128)(2,1)S(1)}, f32[2,256,256]{2,1,0:T(8,128)S(1)}, bf16[160,16,256]{2,1,0:T(8,128)(2,1)S(1)}, bf16[128,16,256]{2,1,0:T(8,128)(2,1)S(1)}) custom-call(bf16[768,256]{1,0:T(8,128)(2,1)S(1)} %get-tuple-element.48.keys, bf16[768,256]{1,0:T(8,128)(2,1)S(1)} %get-tuple-element.49.values, ...), custom_call_target="tpu_custom_call" | custom-call | flops 3000000000 | bytes 8000000 | tf_op jit(solution)/shard_map/backward/pallas_call | solution.py:277
  22.4 0.1 collective-permute-start.5
  22.5 5.1 %collective-permute-start.6 = (bf16[2,256,256]{2,1,0:T(8,128)(2,1)S(1)}, bf16[2,256,256]{2,1,0:T(8,128)(2,1)S(1)}, u32[]{:S(2)}, u32[]{:S(2)}) collective-permute-start(bf16[2,256,256]{2,1,0:T(8,128)(2,1)S(1)} %get-tuple-element.60), channel_id=1, source_target_pairs={{0,252},{4,8},{8,4},{12,16},{16,12},{20,24},{24,20},{28,32},{32,28... | collective-permute-start | bytes 786440 | tf_op jit(solution)/shard_map/ppermute | solution.py:292
  27.7 0.0 collective-permute-done.5.near.refs_1_
  27.7 0.2 core_sum.1
  27.9 0.1 collective-permute-start.9
  28.0 0.3 collective-permute-start.10
  28.3 4.4 %collective-permute-start.11 = (bf16[32,16,256]{2,1,0:T(8,128)(2,1)S(1)}, bf16[32,16,256]{2,1,0:T(8,128)(2,1)S(1)}, u32[]{:S(2)}, u32[]{:S(2)}) collective-permute-start(bf16[32,16,256]{2,1,0:T(8,128)(2,1)S(1)} %get-tuple-element.72), channel_id=1, source_target_pairs={{0,32},{4,228},{8,40},{12,236},{16,48},{20,244},{24,56},{28,252},{... | collective-permute-start | bytes 786440 | tf_op jit(solution)/shard_map/ppermute | solution.py:292
  32.7 1.7 %collective-permute-done.6.far = bf16[2,256,256]{2,1,0:T(8,128)(2,1)S(1)} collective-permute-done((bf16[2,256,256]{2,1,0:T(8,128)(2,1)S(1)}, bf16[2,256,256]{2,1,0:T(8,128)(2,1)S(1)}, u32[]{:S(2)}, u32[]{:S(2)}) %collective-permute-start.6) | collective-permute-done | bytes 262176 | tf_op jit(solution)/shard_map/ppermute | solution.py:292
  34.4 0.7 %input_grad.1 = (f32[4,256,256]{2,1,0:T(8,128)S(1)}, bf16[4,256,256]{2,1,0:T(8,128)(2,1)S(1)}) custom-call(bf16[256,256]{1,0:T(8,128)(2,1)S(1)} %get-tuple-element.47.att, bf16[256,256]{1,0:T(8,128)(2,1)S(1)} %get-tuple-element.57.gq, f32[2,256,256]{2,1,0:T(8,128)S(1)} %get-tuple-element.58.own, ...), custom_call_target="tpu_custom_call" | custom-call | flops 540000000 | bytes 4000000 | tf_op jit(solution)/shard_map/input_grad/pallas_call | solution.py:277
  35.2 0.9 %collective-permute-start.7 = (bf16[4,256,256]{2,1,0:T(8,128)(2,1)S(1)}, bf16[4,256,256]{2,1,0:T(8,128)(2,1)S(1)}, u32[]{:S(2)}, u32[]{:S(2)}) collective-permute-start(bf16[4,256,256]{2,1,0:T(8,128)(2,1)S(1)} %get-tuple-element.63), channel_id=1, source_target_pairs={{0,1},{1,0},{2,3},{3,2},{4,7},{5,6},{6,5},{7,4},{8,9},{9,8},{10,11... | collective-permute-start | bytes 1572872 | tf_op jit(solution)/shard_map/ppermute | solution.py:292
  36.1 0.5 collective-permute-done.9.refs_1_
  36.6 2.1 %collective-permute-done.10.refs_2_ = bf16[32,16,256]{2,1,0:T(8,128)(2,1)S(1)} collective-permute-done((bf16[32,16,256]{2,1,0:T(8,128)(2,1)S(1)}, bf16[32,16,256]{2,1,0:T(8,128)(2,1)S(1)}, u32[]{:S(2)}, u32[]{:S(2)}) %collective-permute-start.10) | collective-permute-done | bytes 262176 | tf_op jit(solution)/shard_map/ppermute | solution.py:292
  38.7 0.0 collective-permute-done.11.refs_3_
  38.7 0.1 first_sum.1
  38.8 0.1 collective-permute-start.12
  38.9 4.1 %collective-permute-start.13 = (bf16[8,16,256]{2,1,0:T(8,128)(2,1)S(1)}, bf16[8,16,256]{2,1,0:T(8,128)(2,1)S(1)}, u32[]{:S(2)}, u32[]{:S(2)}) collective-permute-start(bf16[8,16,256]{2,1,0:T(8,128)(2,1)S(1)} %get-tuple-element.75), channel_id=1, source_target_pairs={{0,8},{4,28},{8,0},{12,20},{16,24},{20,12},{24,16},{28,4},{32,40},... | collective-permute-start | bytes 196616 | tf_op jit(solution)/shard_map/ppermute | solution.py:292
  43.0 0.6 %collective-permute-start.14 = (bf16[8,16,256]{2,1,0:T(8,128)(2,1)S(1)}, bf16[8,16,256]{2,1,0:T(8,128)(2,1)S(1)}, u32[]{:S(2)}, u32[]{:S(2)}) collective-permute-start(bf16[8,16,256]{2,1,0:T(8,128)(2,1)S(1)} %get-tuple-element.76), channel_id=1, source_target_pairs={{0,224},{4,36},{8,232},{12,44},{16,240},{20,52},{24,248},{28,60},{... | collective-permute-start | bytes 196616 | tf_op jit(solution)/shard_map/ppermute | solution.py:292
  43.6 2.1 %collective-permute-done.7.refs_1_ = bf16[4,256,256]{2,1,0:T(8,128)(2,1)S(1)} collective-permute-done((bf16[4,256,256]{2,1,0:T(8,128)(2,1)S(1)}, bf16[4,256,256]{2,1,0:T(8,128)(2,1)S(1)}, u32[]{:S(2)}, u32[]{:S(2)}) %collective-permute-start.7) | collective-permute-done | bytes 524320 | tf_op jit(solution)/shard_map/ppermute | solution.py:292
  45.7 0.1 mp_share.1
  45.8 0.6 %collective-permute-start.8 = (bf16[2,256,256]{2,1,0:T(8,128)(2,1)S(1)}, bf16[2,256,256]{2,1,0:T(8,128)(2,1)S(1)}, u32[]{:S(2)}, u32[]{:S(2)}) collective-permute-start(bf16[2,256,256]{2,1,0:T(8,128)(2,1)S(1)} %get-tuple-element.65), channel_id=1, source_target_pairs={{0,3},{1,2},{2,1},{3,0},{4,5},{5,4},{6,7},{7,6},{8,11},{9,10},{10,... | collective-permute-start | bytes 786440 | tf_op jit(solution)/shard_map/ppermute | solution.py:292
  46.3 0.0 collective-permute-done.12.refs_1_
  46.3 0.0 collective-permute-done.13.refs_2_
  46.3 2.2 %collective-permute-done.14.refs_3_ = bf16[8,16,256]{2,1,0:T(8,128)(2,1)S(1)} collective-permute-done((bf16[8,16,256]{2,1,0:T(8,128)(2,1)S(1)}, bf16[8,16,256]{2,1,0:T(8,128)(2,1)S(1)}, u32[]{:S(2)}, u32[]{:S(2)}) %collective-permute-start.14) | collective-permute-done | bytes 65568 | tf_op jit(solution)/shard_map/ppermute | solution.py:292
  48.5 0.6 %collective-permute-start.15 = (bf16[4,16,256]{2,1,0:T(8,128)(2,1)S(1)}, bf16[4,16,256]{2,1,0:T(8,128)(2,1)S(1)}, u32[]{:S(2)}, u32[]{:S(2)}) collective-permute-start(bf16[4,16,256]{2,1,0:T(8,128)(2,1)S(1)} %get-tuple-element.78), channel_id=1, source_target_pairs={{0,96},{4,164},{8,104},{12,172},{16,112},{20,180},{24,120},{28,188... | collective-permute-start | bytes 98312 | tf_op jit(solution)/shard_map/ppermute | solution.py:292
  49.1 4.3 %collective-permute-done.8.got = bf16[2,256,256]{2,1,0:T(8,128)(2,1)S(1)} collective-permute-done((bf16[2,256,256]{2,1,0:T(8,128)(2,1)S(1)}, bf16[2,256,256]{2,1,0:T(8,128)(2,1)S(1)}, u32[]{:S(2)}, u32[]{:S(2)}) %collective-permute-start.8) | collective-permute-done | bytes 262176 | tf_op jit(solution)/shard_map/ppermute | solution.py:292
  53.4 0.7 %mp_sum.1 = (bf16[256,256]{1,0:T(8,128)(2,1)}, bf16[256,256]{1,0:T(8,128)(2,1)}) custom-call(f32[2,256,256]{2,1,0:T(8,128)S(1)} %get-tuple-element.64.kept, bf16[2,256,256]{2,1,0:T(8,128)(2,1)S(1)} %collective-permute-done.8.got), custom_call_target="tpu_custom_call" | custom-call | bytes 1000000 | tf_op jit(solution)/shard_map/mp_sum/pallas_call | solution.py:277
  54.2 0.2 collective-permute-done.15.got
  54.3 0.6 %last_sum.1 = f32[4,16,256]{2,1,0:T(8,128)} custom-call(bf16[256,256]{1,0:T(8,128)(2,1)} %get-tuple-element.38.after, f32[4,16,256]{2,1,0:T(8,128)S(1)} %get-tuple-element.77.kept, bf16[4,16,256]{2,1,0:T(8,128)(2,1)S(1)} %collective-permute-done.15.got), custom_call_target="tpu_custom_call" | custom-call | bytes 1000000 | tf_op jit(solution)/shard_map/last_sum/pallas_call | solution.py:277
  (1 shorter events, 0.0 us)
Async XLA Ops:
  0.6 12.0 %collective-permute-start.1 = (bf16[256,1024]{1,0:T(8,128)(2,1)}, bf16[256,1024]{1,0:T(8,128)(2,1)S(1)}, u32[]{:S(2)}, u32[]{:S(2)}) collective-permute-start(bf16[256,1024]{1,0:T(8,128)(2,1)} %act.1), channel_id=1, source_target_pairs={{0,4},{4,0},{8,12},{12,8},{16,20},{20,16},{24,28},{28,24},{32,36},... | collective-permute-start | bytes 1572872 | tf_op jit(solution)/shard_map/ppermute | solution.py:292
  0.7 15.5 %collective-permute-start = (bf16[256,1024]{1,0:T(8,128)(2,1)}, bf16[256,1024]{1,0:T(8,128)(2,1)S(1)}, u32[]{:S(2)}, u32[]{:S(2)}) collective-permute-start(bf16[256,1024]{1,0:T(8,128)(2,1)} %act.1), channel_id=1, source_target_pairs={{0,252},{4,8},{8,4},{12,16},{16,12},{20,24},{24,20},{28,32},{32,28... | collective-permute-start | bytes 1572872 | tf_op jit(solution)/shard_map/ppermute | solution.py:292
  9.1 9.2 %collective-permute-start.2 = (bf16[256,256]{1,0:T(8,128)(2,1)}, bf16[256,256]{1,0:T(8,128)(2,1)S(1)}, u32[]{:S(2)}, u32[]{:S(2)}) collective-permute-start(bf16[256,256]{1,0:T(8,128)(2,1)} %cot.1), channel_id=1, source_target_pairs={{0,2},{1,3},{2,0},{3,1},{4,6},{5,7},{6,4},{7,5},{8,10},{9,11},{10,... | collective-permute-start | bytes 393224 | tf_op jit(solution)/shard_map/ppermute | solution.py:292
  10.5 7.8 %collective-permute-start.4 = (bf16[256,256]{1,0:T(8,128)(2,1)}, bf16[256,256]{1,0:T(8,128)(2,1)S(1)}, u32[]{:S(2)}, u32[]{:S(2)}) collective-permute-start(bf16[256,256]{1,0:T(8,128)(2,1)} %cot.1), channel_id=1, source_target_pairs={{0,3},{1,2},{2,1},{3,0},{4,7},{5,6},{6,5},{7,4},{8,11},{9,10},{10,... | collective-permute-start | bytes 393224 | tf_op jit(solution)/shard_map/ppermute | solution.py:292
  12.6 5.7 %collective-permute-start.3 = (bf16[256,256]{1,0:T(8,128)(2,1)}, bf16[256,256]{1,0:T(8,128)(2,1)S(1)}, u32[]{:S(2)}, u32[]{:S(2)}) collective-permute-start(bf16[256,256]{1,0:T(8,128)(2,1)} %cot.1), channel_id=1, source_target_pairs={{0,1},{1,0},{2,3},{3,2},{4,5},{5,4},{6,7},{7,6},{8,9},{9,8},{10,11... | collective-permute-start | bytes 393224 | tf_op jit(solution)/shard_map/ppermute | solution.py:292
  22.4 5.3 %collective-permute-start.5 = (bf16[160,16,256]{2,1,0:T(8,128)(2,1)S(1)}, bf16[160,16,256]{2,1,0:T(8,128)(2,1)S(1)}, u32[]{:S(2)}, u32[]{:S(2)}) collective-permute-start(bf16[160,16,256]{2,1,0:T(8,128)(2,1)S(1)} %get-tuple-element.59), channel_id=1, source_target_pairs={{0,4},{4,0},{8,12},{12,8},{16,20},{20,16},{24,28},{28,24},{32,36},... | collective-permute-start | bytes 3932168 | tf_op jit(solution)/shard_map/ppermute | solution.py:292
  22.5 11.9 %collective-permute-start.6 = (bf16[2,256,256]{2,1,0:T(8,128)(2,1)S(1)}, bf16[2,256,256]{2,1,0:T(8,128)(2,1)S(1)}, u32[]{:S(2)}, u32[]{:S(2)}) collective-permute-start(bf16[2,256,256]{2,1,0:T(8,128)(2,1)S(1)} %get-tuple-element.60), channel_id=1, source_target_pairs={{0,252},{4,8},{8,4},{12,16},{16,12},{20,24},{24,20},{28,32},{32,28... | collective-permute-start | bytes 786440 | tf_op jit(solution)/shard_map/ppermute | solution.py:292
  27.9 8.7 %collective-permute-start.9 = (bf16[32,16,256]{2,1,0:T(8,128)(2,1)S(1)}, bf16[32,16,256]{2,1,0:T(8,128)(2,1)S(1)}, u32[]{:S(2)}, u32[]{:S(2)}) collective-permute-start(bf16[32,16,256]{2,1,0:T(8,128)(2,1)S(1)} %get-tuple-element.70), channel_id=1, source_target_pairs={{0,56},{4,236},{8,48},{12,228},{16,40},{20,252},{24,32},{28,244},{... | collective-permute-start | bytes 786440 | tf_op jit(solution)/shard_map/ppermute | solution.py:292
  28.0 10.7 %collective-permute-start.10 = (bf16[32,16,256]{2,1,0:T(8,128)(2,1)S(1)}, bf16[32,16,256]{2,1,0:T(8,128)(2,1)S(1)}, u32[]{:S(2)}, u32[]{:S(2)}) collective-permute-start(bf16[32,16,256]{2,1,0:T(8,128)(2,1)S(1)} %get-tuple-element.71), channel_id=1, source_target_pairs={{0,24},{4,12},{8,16},{12,4},{16,8},{20,28},{24,0},{28,20},{32,56},... | collective-permute-start | bytes 786440 | tf_op jit(solution)/shard_map/ppermute | solution.py:292
  28.3 10.4 %collective-permute-start.11 = (bf16[32,16,256]{2,1,0:T(8,128)(2,1)S(1)}, bf16[32,16,256]{2,1,0:T(8,128)(2,1)S(1)}, u32[]{:S(2)}, u32[]{:S(2)}) collective-permute-start(bf16[32,16,256]{2,1,0:T(8,128)(2,1)S(1)} %get-tuple-element.72), channel_id=1, source_target_pairs={{0,32},{4,228},{8,40},{12,236},{16,48},{20,244},{24,56},{28,252},{... | collective-permute-start | bytes 786440 | tf_op jit(solution)/shard_map/ppermute | solution.py:292
  35.2 10.5 %collective-permute-start.7 = (bf16[4,256,256]{2,1,0:T(8,128)(2,1)S(1)}, bf16[4,256,256]{2,1,0:T(8,128)(2,1)S(1)}, u32[]{:S(2)}, u32[]{:S(2)}) collective-permute-start(bf16[4,256,256]{2,1,0:T(8,128)(2,1)S(1)} %get-tuple-element.63), channel_id=1, source_target_pairs={{0,1},{1,0},{2,3},{3,2},{4,7},{5,6},{6,5},{7,4},{8,9},{9,8},{10,11... | collective-permute-start | bytes 1572872 | tf_op jit(solution)/shard_map/ppermute | solution.py:292
  38.8 7.5 %collective-permute-start.12 = (bf16[8,16,256]{2,1,0:T(8,128)(2,1)S(1)}, bf16[8,16,256]{2,1,0:T(8,128)(2,1)S(1)}, u32[]{:S(2)}, u32[]{:S(2)}) collective-permute-start(bf16[8,16,256]{2,1,0:T(8,128)(2,1)S(1)} %get-tuple-element.74), channel_id=1, source_target_pairs={{0,232},{4,60},{8,224},{12,52},{16,248},{20,44},{24,240},{28,36},{... | collective-permute-start | bytes 196616 | tf_op jit(solution)/shard_map/ppermute | solution.py:292
  38.9 7.4 %collective-permute-start.13 = (bf16[8,16,256]{2,1,0:T(8,128)(2,1)S(1)}, bf16[8,16,256]{2,1,0:T(8,128)(2,1)S(1)}, u32[]{:S(2)}, u32[]{:S(2)}) collective-permute-start(bf16[8,16,256]{2,1,0:T(8,128)(2,1)S(1)} %get-tuple-element.75), channel_id=1, source_target_pairs={{0,8},{4,28},{8,0},{12,20},{16,24},{20,12},{24,16},{28,4},{32,40},... | collective-permute-start | bytes 196616 | tf_op jit(solution)/shard_map/ppermute | solution.py:292
  43.0 5.5 %collective-permute-start.14 = (bf16[8,16,256]{2,1,0:T(8,128)(2,1)S(1)}, bf16[8,16,256]{2,1,0:T(8,128)(2,1)S(1)}, u32[]{:S(2)}, u32[]{:S(2)}) collective-permute-start(bf16[8,16,256]{2,1,0:T(8,128)(2,1)S(1)} %get-tuple-element.76), channel_id=1, source_target_pairs={{0,224},{4,36},{8,232},{12,44},{16,240},{20,52},{24,248},{28,60},{... | collective-permute-start | bytes 196616 | tf_op jit(solution)/shard_map/ppermute | solution.py:292
  45.8 7.7 %collective-permute-start.8 = (bf16[2,256,256]{2,1,0:T(8,128)(2,1)S(1)}, bf16[2,256,256]{2,1,0:T(8,128)(2,1)S(1)}, u32[]{:S(2)}, u32[]{:S(2)}) collective-permute-start(bf16[2,256,256]{2,1,0:T(8,128)(2,1)S(1)} %get-tuple-element.65), channel_id=1, source_target_pairs={{0,3},{1,2},{2,1},{3,0},{4,5},{5,4},{6,7},{7,6},{8,11},{9,10},{10,... | collective-permute-start | bytes 786440 | tf_op jit(solution)/shard_map/ppermute | solution.py:292
  48.5 5.8 %collective-permute-start.15 = (bf16[4,16,256]{2,1,0:T(8,128)(2,1)S(1)}, bf16[4,16,256]{2,1,0:T(8,128)(2,1)S(1)}, u32[]{:S(2)}, u32[]{:S(2)}) collective-permute-start(bf16[4,16,256]{2,1,0:T(8,128)(2,1)S(1)} %get-tuple-element.78), channel_id=1, source_target_pairs={{0,96},{4,164},{8,104},{12,172},{16,112},{20,180},{24,120},{28,188... | collective-permute-start | bytes 98312 | tf_op jit(solution)/shard_map/ppermute | solution.py:292

commit v12 on v11

--- a/solution.py
+++ b/solution.py
@@ -306,7 +306,7 @@
 
 
 def far_row(value):
-    return move(value, SPACE, lambda i: (i + 1 if i % 2 else i - 1) % 64)
+    return move(value, SPACE, lambda i: i if i in (0, 63) else (i + 1 if i % 2 else i - 1))
 
 
 def body(activations, w_query, w_key, w_value, w_out, grad_output, neighbours, pad_mask):

time: 55.6 us -> 56.6 us (1.018)
  waiting for transfers between devices: 13.6 us -> 16.6 us
  starting transfers between devices: 28.8 us -> 27.3 us
    ppermute x16, waiting for transfers between devices: 13.6 us -> 16.6 us  [move(): lax.ppermute(value, axis, [(i, target(i)) for i in range(count) if 0 <= t...]
    ppermute x16, starting transfers between devices: 28.8 us -> 27.3 us  [move(): lax.ppermute(value, axis, [(i, target(i)) for i in range(count) if 0 <= t...]
where the time goes in v12:
time: 56.6 us; the launch traced here: 56.4 us
  starting transfers between devices  27.3 us (48%)
  waiting for transfers between devices  16.6 us (29%)
  Pallas kernels  11.8 us (21%)
  between operations  0.72 us (1%)
    ppermute x16, starting transfers between devices, move(): lax.ppermute(value, axis, [(i, target(i)) for i in range(count) if 0 <= t...  27.3 us
    ppermute x16, waiting for transfers between devices, move(): lax.ppermute(value, axis, [(i, target(i)) for i in range(count) if 0 <= t...  16.6 us
    pallas_call x10, Pallas kernels, call(): pl.pallas_call(kernel, out_shape=tuple(kept), in_specs=[pl.BlockSpec(memo...  11.8 us
  transfers between devices with their start and end apart: 16, of which 8 were waited for; matrix products, arithmetic and copies ran while one was open for 0% of the time, Pallas kernels for 13%

profile of v12, /device:TPU:6, one launch (start us, length us, event | category | flops | bytes accessed | tf_op | source)
XLA Modules:
  0.0 56.4 jit_solution(18383212955629557138)
XLA Ops:
  0.6 0.1 collective-permute-start.1
  0.7 1.7 %collective-permute-start = (bf16[256,1024]{1,0:T(8,128)(2,1)}, bf16[256,1024]{1,0:T(8,128)(2,1)S(1)}, u32[]{:S(2)}, u32[]{:S(2)}) collective-permute-start(bf16[256,1024]{1,0:T(8,128)(2,1)} %act.1), channel_id=1, source_target_pairs={{0,0},{4,8},{8,4},{12,16},{16,12},{20,24},{24,20},{28,32},{32,28},... | collective-permute-start | bytes 1572872 | tf_op jit(solution)/shard_map/ppermute | solution.py:292
  2.4 1.4 %collective-permute-start.2 = (bf16[256,256]{1,0:T(8,128)(2,1)}, bf16[256,256]{1,0:T(8,128)(2,1)S(1)}, u32[]{:S(2)}, u32[]{:S(2)}) collective-permute-start(bf16[256,256]{1,0:T(8,128)(2,1)} %cot.1), channel_id=1, source_target_pairs={{0,2},{1,3},{2,0},{3,1},{4,6},{5,7},{6,4},{7,5},{8,10},{9,11},{10,... | collective-permute-start | bytes 393224 | tf_op jit(solution)/shard_map/ppermute | solution.py:292
  3.8 2.1 %collective-permute-start.4 = (bf16[256,256]{1,0:T(8,128)(2,1)}, bf16[256,256]{1,0:T(8,128)(2,1)S(1)}, u32[]{:S(2)}, u32[]{:S(2)}) collective-permute-start(bf16[256,256]{1,0:T(8,128)(2,1)} %cot.1), channel_id=1, source_target_pairs={{0,3},{1,2},{2,1},{3,0},{4,7},{5,6},{6,5},{7,4},{8,11},{9,10},{10,... | collective-permute-start | bytes 393224 | tf_op jit(solution)/shard_map/ppermute | solution.py:292
  5.9 0.0 collective-permute-start.3
  5.9 0.0 collective-permute-done.1.a_near
  5.9 3.1 %own_part.1 = (bf16[1024,256]{1,0:T(8,128)(2,1)S(1)}, bf16[1024,256]{1,0:T(8,128)(2,1)S(1)}, bf16[1024,256]{1,0:T(8,128)(2,1)S(1)}, bf16[256,1024]{1,0:T(8,128)(...) custom-call(bf16[256,1024]{1,0:T(8,128)(2,1)} %act.1, ...), custom_call_target="tpu_custom_call" | custom-call | flops 600000000 | bytes 6000000 | tf_op jit(solution)/shard_map/own_part/pallas_call | solution.py:277
  9.0 0.0 collective-permute-done.a_far
  9.0 2.1 %forward.1 = (bf16[768,256]{1,0:T(8,128)(2,1)S(1)}, bf16[768,256]{1,0:T(8,128)(2,1)S(1)}, bf16[768,1024]{1,0:T(8,128)(2,1)S(1)}, bf16[256,256]{1,0:T(8,128)(2,1)S(1)}, bf16[1024,256]{1,0:T(8,128)(2,1)S(1)}) custom-call(bf16[256,1024]{1,0:T(8,128)(2,1)S(1)} %collective-permute-done.a_far, bf16[1024,256]{1,0:T(8,128)(2,1)S(1)} %get-tuple-element.41.wk, ...), custom_call_target="tpu_custom_call" | custom-call | flops 2000000000 | bytes 6000000 | tf_op jit(solution)/shard_map/forward/pallas_call | solution.py:277
  11.1 0.0 collective-permute-done.2.c2
  11.1 2.1 %collective-permute-done.4.c3 = bf16[256,256]{1,0:T(8,128)(2,1)S(1)} collective-permute-done((bf16[256,256]{1,0:T(8,128)(2,1)}, bf16[256,256]{1,0:T(8,128)(2,1)S(1)}, u32[]{:S(2)}, u32[]{:S(2)}) %collective-permute-start.4) | collective-permute-done | bytes 131104 | tf_op jit(solution)/shard_map/ppermute | solution.py:292
  13.3 0.0 collective-permute-done.3.c1
  13.3 4.1 %backward.1 = (bf16[256,256]{1,0:T(8,128)(2,1)S(1)}, bf16[2,256,256]{2,1,0:T(8,128)(2,1)S(1)}, f32[2,256,256]{2,1,0:T(8,128)S(1)}, bf16[160,16,256]{2,1,0:T(8,128)(2,1)S(1)}, bf16[128,16,256]{2,1,0:T(8,128)(2,1)S(1)}) custom-call(bf16[768,256]{1,0:T(8,128)(2,1)S(1)} %get-tuple-element.48.keys, bf16[768,256]{1,0:T(8,128)(2,1)S(1)} %get-tuple-element.49.values, ...), custom_call_target="tpu_custom_call" | custom-call | flops 3000000000 | bytes 8000000 | tf_op jit(solution)/shard_map/backward/pallas_call | solution.py:277
  17.3 1.2 %collective-permute-start.5 = (bf16[160,16,256]{2,1,0:T(8,128)(2,1)S(1)}, bf16[160,16,256]{2,1,0:T(8,128)(2,1)S(1)}, u32[]{:S(2)}, u32[]{:S(2)}) collective-permute-start(bf16[160,16,256]{2,1,0:T(8,128)(2,1)S(1)} %get-tuple-element.59), channel_id=1, source_target_pairs={{0,4},{4,0},{8,12},{12,8},{16,20},{20,16},{24,28},{28,24},{32,36},... | collective-permute-start | bytes 3932168 | tf_op jit(solution)/shard_map/ppermute | solution.py:292
  18.5 0.7 %collective-permute-start.6 = (bf16[2,256,256]{2,1,0:T(8,128)(2,1)S(1)}, bf16[2,256,256]{2,1,0:T(8,128)(2,1)S(1)}, u32[]{:S(2)}, u32[]{:S(2)}) collective-permute-start(bf16[2,256,256]{2,1,0:T(8,128)(2,1)S(1)} %get-tuple-element.60), channel_id=1, source_target_pairs={{0,0},{4,8},{8,4},{12,16},{16,12},{20,24},{24,20},{28,32},{32,28},... | collective-permute-start | bytes 786440 | tf_op jit(solution)/shard_map/ppermute | solution.py:292
  19.2 2.0 %collective-permute-done.5.near.refs_1_ = bf16[160,16,256]{2,1,0:T(8,128)(2,1)S(1)} collective-permute-done((bf16[160,16,256]{2,1,0:T(8,128)(2,1)S(1)}, bf16[160,16,256]{2,1,0:T(8,128)(2,1)S(1)}, u32[]{:S(2)}, u32[]{:S(2)}) %collective-permute-start.5) | collective-permute-done | bytes 1310752 | tf_op jit(solution)/shard_map/ppermute | solution.py:292
  21.2 0.2 core_sum.1
  21.4 6.3 %collective-permute-start.9 = (bf16[32,16,256]{2,1,0:T(8,128)(2,1)S(1)}, bf16[32,16,256]{2,1,0:T(8,128)(2,1)S(1)}, u32[]{:S(2)}, u32[]{:S(2)}) collective-permute-start(bf16[32,16,256]{2,1,0:T(8,128)(2,1)S(1)} %get-tuple-element.70), channel_id=1, source_target_pairs={{0,56},{4,236},{8,48},{12,228},{16,40},{20,252},{24,32},{28,244},{... | collective-permute-start | bytes 786440 | tf_op jit(solution)/shard_map/ppermute | solution.py:292
  27.7 1.7 %collective-permute-start.10 = (bf16[32,16,256]{2,1,0:T(8,128)(2,1)S(1)}, bf16[32,16,256]{2,1,0:T(8,128)(2,1)S(1)}, u32[]{:S(2)}, u32[]{:S(2)}) collective-permute-start(bf16[32,16,256]{2,1,0:T(8,128)(2,1)S(1)} %get-tuple-element.71), channel_id=1, source_target_pairs={{0,24},{4,12},{8,16},{12,4},{16,8},{20,28},{24,0},{28,20},{32,56},... | collective-permute-start | bytes 786440 | tf_op jit(solution)/shard_map/ppermute | solution.py:292
  29.4 0.0 collective-permute-start.11
  29.4 0.0 collective-permute-done.6.far
  29.4 0.7 %input_grad.1 = (f32[4,256,256]{2,1,0:T(8,128)S(1)}, bf16[4,256,256]{2,1,0:T(8,128)(2,1)S(1)}) custom-call(bf16[256,256]{1,0:T(8,128)(2,1)S(1)} %get-tuple-element.47.att, bf16[256,256]{1,0:T(8,128)(2,1)S(1)} %get-tuple-element.57.gq, f32[2,256,256]{2,1,0:T(8,128)S(1)} %get-tuple-element.58.own, ...), custom_call_target="tpu_custom_call" | custom-call | flops 540000000 | bytes 4000000 | tf_op jit(solution)/shard_map/input_grad/pallas_call | solution.py:277
  30.1 0.9 %collective-permute-start.7 = (bf16[4,256,256]{2,1,0:T(8,128)(2,1)S(1)}, bf16[4,256,256]{2,1,0:T(8,128)(2,1)S(1)}, u32[]{:S(2)}, u32[]{:S(2)}) collective-permute-start(bf16[4,256,256]{2,1,0:T(8,128)(2,1)S(1)} %get-tuple-element.63), channel_id=1, source_target_pairs={{0,1},{1,0},{2,3},{3,2},{4,7},{5,6},{6,5},{7,4},{8,9},{9,8},{10,11... | collective-permute-start | bytes 1572872 | tf_op jit(solution)/shard_map/ppermute | solution.py:292
  31.0 1.8 %collective-permute-done.9.refs_1_ = bf16[32,16,256]{2,1,0:T(8,128)(2,1)S(1)} collective-permute-done((bf16[32,16,256]{2,1,0:T(8,128)(2,1)S(1)}, bf16[32,16,256]{2,1,0:T(8,128)(2,1)S(1)}, u32[]{:S(2)}, u32[]{:S(2)}) %collective-permute-start.9) | collective-permute-done | bytes 262176 | tf_op jit(solution)/shard_map/ppermute | solution.py:292
  32.8 2.5 %collective-permute-done.10.refs_2_ = bf16[32,16,256]{2,1,0:T(8,128)(2,1)S(1)} collective-permute-done((bf16[32,16,256]{2,1,0:T(8,128)(2,1)S(1)}, bf16[32,16,256]{2,1,0:T(8,128)(2,1)S(1)}, u32[]{:S(2)}, u32[]{:S(2)}) %collective-permute-start.10) | collective-permute-done | bytes 262176 | tf_op jit(solution)/shard_map/ppermute | solution.py:292
  35.3 1.0 %collective-permute-done.11.refs_3_ = bf16[32,16,256]{2,1,0:T(8,128)(2,1)S(1)} collective-permute-done((bf16[32,16,256]{2,1,0:T(8,128)(2,1)S(1)}, bf16[32,16,256]{2,1,0:T(8,128)(2,1)S(1)}, u32[]{:S(2)}, u32[]{:S(2)}) %collective-permute-start.11) | collective-permute-done | bytes 262176 | tf_op jit(solution)/shard_map/ppermute | solution.py:292
  36.3 0.1 first_sum.1
  36.4 4.1 %collective-permute-start.12 = (bf16[8,16,256]{2,1,0:T(8,128)(2,1)S(1)}, bf16[8,16,256]{2,1,0:T(8,128)(2,1)S(1)}, u32[]{:S(2)}, u32[]{:S(2)}) collective-permute-start(bf16[8,16,256]{2,1,0:T(8,128)(2,1)S(1)} %get-tuple-element.74), channel_id=1, source_target_pairs={{0,232},{4,60},{8,224},{12,52},{16,248},{20,44},{24,240},{28,36},{... | collective-permute-start | bytes 196616 | tf_op jit(solution)/shard_map/ppermute | solution.py:292
  40.5 4.0 %collective-permute-start.13 = (bf16[8,16,256]{2,1,0:T(8,128)(2,1)S(1)}, bf16[8,16,256]{2,1,0:T(8,128)(2,1)S(1)}, u32[]{:S(2)}, u32[]{:S(2)}) collective-permute-start(bf16[8,16,256]{2,1,0:T(8,128)(2,1)S(1)} %get-tuple-element.75), channel_id=1, source_target_pairs={{0,8},{4,28},{8,0},{12,20},{16,24},{20,12},{24,16},{28,4},{32,40},... | collective-permute-start | bytes 196616 | tf_op jit(solution)/shard_map/ppermute | solution.py:292
  44.5 0.0 collective-permute-start.14
  44.5 0.0 collective-permute-done.7.refs_1_
  44.5 0.1 mp_share.1
  44.6 0.6 collective-permute-start.8
  45.2 0.0 collective-permute-done.12.refs_1_
  45.2 1.6 %collective-permute-done.13.refs_2_ = bf16[8,16,256]{2,1,0:T(8,128)(2,1)S(1)} collective-permute-done((bf16[8,16,256]{2,1,0:T(8,128)(2,1)S(1)}, bf16[8,16,256]{2,1,0:T(8,128)(2,1)S(1)}, u32[]{:S(2)}, u32[]{:S(2)}) %collective-permute-start.13) | collective-permute-done | bytes 65568 | tf_op jit(solution)/shard_map/ppermute | solution.py:292
  46.7 3.2 %collective-permute-done.14.refs_3_ = bf16[8,16,256]{2,1,0:T(8,128)(2,1)S(1)} collective-permute-done((bf16[8,16,256]{2,1,0:T(8,128)(2,1)S(1)}, bf16[8,16,256]{2,1,0:T(8,128)(2,1)S(1)}, u32[]{:S(2)}, u32[]{:S(2)}) %collective-permute-start.14) | collective-permute-done | bytes 65568 | tf_op jit(solution)/shard_map/ppermute | solution.py:292
  50.0 2.7 %collective-permute-start.15 = (bf16[4,16,256]{2,1,0:T(8,128)(2,1)S(1)}, bf16[4,16,256]{2,1,0:T(8,128)(2,1)S(1)}, u32[]{:S(2)}, u32[]{:S(2)}) collective-permute-start(bf16[4,16,256]{2,1,0:T(8,128)(2,1)S(1)} %get-tuple-element.78), channel_id=1, source_target_pairs={{0,96},{4,164},{8,104},{12,172},{16,112},{20,180},{24,120},{28,188... | collective-permute-start | bytes 98312 | tf_op jit(solution)/shard_map/ppermute | solution.py:292
  52.7 0.0 collective-permute-done.8.got
  52.7 0.7 %mp_sum.1 = (bf16[256,256]{1,0:T(8,128)(2,1)}, bf16[256,256]{1,0:T(8,128)(2,1)}) custom-call(f32[2,256,256]{2,1,0:T(8,128)S(1)} %get-tuple-element.64.kept, bf16[2,256,256]{2,1,0:T(8,128)(2,1)S(1)} %collective-permute-done.8.got), custom_call_target="tpu_custom_call" | custom-call | bytes 1000000 | tf_op jit(solution)/shard_map/mp_sum/pallas_call | solution.py:277
  53.5 2.3 %collective-permute-done.15.got = bf16[4,16,256]{2,1,0:T(8,128)(2,1)S(1)} collective-permute-done((bf16[4,16,256]{2,1,0:T(8,128)(2,1)S(1)}, bf16[4,16,256]{2,1,0:T(8,128)(2,1)S(1)}, u32[]{:S(2)}, u32[]{:S(2)}) %collective-permute-start.15) | collective-permute-done | bytes 32800 | tf_op jit(solution)/shard_map/ppermute | solution.py:292
  55.8 0.6 %last_sum.1 = f32[4,16,256]{2,1,0:T(8,128)} custom-call(bf16[256,256]{1,0:T(8,128)(2,1)} %get-tuple-element.38.after, f32[4,16,256]{2,1,0:T(8,128)S(1)} %get-tuple-element.77.kept, bf16[4,16,256]{2,1,0:T(8,128)(2,1)S(1)} %collective-permute-done.15.got), custom_call_target="tpu_custom_call" | custom-call | bytes 1000000 | tf_op jit(solution)/shard_map/last_sum/pallas_call | solution.py:277
  (1 shorter events, 0.0 us)
Async XLA Ops:
  0.6 5.3 %collective-permute-start.1 = (bf16[256,1024]{1,0:T(8,128)(2,1)}, bf16[256,1024]{1,0:T(8,128)(2,1)S(1)}, u32[]{:S(2)}, u32[]{:S(2)}) collective-permute-start(bf16[256,1024]{1,0:T(8,128)(2,1)} %act.1), channel_id=1, source_target_pairs={{0,4},{4,0},{8,12},{12,8},{16,20},{20,16},{24,28},{28,24},{32,36},... | collective-permute-start | bytes 1572872 | tf_op jit(solution)/shard_map/ppermute | solution.py:292
  0.7 8.3 %collective-permute-start = (bf16[256,1024]{1,0:T(8,128)(2,1)}, bf16[256,1024]{1,0:T(8,128)(2,1)S(1)}, u32[]{:S(2)}, u32[]{:S(2)}) collective-permute-start(bf16[256,1024]{1,0:T(8,128)(2,1)} %act.1), channel_id=1, source_target_pairs={{0,0},{4,8},{8,4},{12,16},{16,12},{20,24},{24,20},{28,32},{32,28},... | collective-permute-start | bytes 1572872 | tf_op jit(solution)/shard_map/ppermute | solution.py:292
  2.4 8.7 %collective-permute-start.2 = (bf16[256,256]{1,0:T(8,128)(2,1)}, bf16[256,256]{1,0:T(8,128)(2,1)S(1)}, u32[]{:S(2)}, u32[]{:S(2)}) collective-permute-start(bf16[256,256]{1,0:T(8,128)(2,1)} %cot.1), channel_id=1, source_target_pairs={{0,2},{1,3},{2,0},{3,1},{4,6},{5,7},{6,4},{7,5},{8,10},{9,11},{10,... | collective-permute-start | bytes 393224 | tf_op jit(solution)/shard_map/ppermute | solution.py:292
  3.8 9.4 %collective-permute-start.4 = (bf16[256,256]{1,0:T(8,128)(2,1)}, bf16[256,256]{1,0:T(8,128)(2,1)S(1)}, u32[]{:S(2)}, u32[]{:S(2)}) collective-permute-start(bf16[256,256]{1,0:T(8,128)(2,1)} %cot.1), channel_id=1, source_target_pairs={{0,3},{1,2},{2,1},{3,0},{4,7},{5,6},{6,5},{7,4},{8,11},{9,10},{10,... | collective-permute-start | bytes 393224 | tf_op jit(solution)/shard_map/ppermute | solution.py:292
  5.9 7.3 %collective-permute-start.3 = (bf16[256,256]{1,0:T(8,128)(2,1)}, bf16[256,256]{1,0:T(8,128)(2,1)S(1)}, u32[]{:S(2)}, u32[]{:S(2)}) collective-permute-start(bf16[256,256]{1,0:T(8,128)(2,1)} %cot.1), channel_id=1, source_target_pairs={{0,1},{1,0},{2,3},{3,2},{4,5},{5,4},{6,7},{7,6},{8,9},{9,8},{10,11... | collective-permute-start | bytes 393224 | tf_op jit(solution)/shard_map/ppermute | solution.py:292
  17.3 3.8 %collective-permute-start.5 = (bf16[160,16,256]{2,1,0:T(8,128)(2,1)S(1)}, bf16[160,16,256]{2,1,0:T(8,128)(2,1)S(1)}, u32[]{:S(2)}, u32[]{:S(2)}) collective-permute-start(bf16[160,16,256]{2,1,0:T(8,128)(2,1)S(1)} %get-tuple-element.59), channel_id=1, source_target_pairs={{0,4},{4,0},{8,12},{12,8},{16,20},{20,16},{24,28},{28,24},{32,36},... | collective-permute-start | bytes 3932168 | tf_op jit(solution)/shard_map/ppermute | solution.py:292
  18.5 10.8 %collective-permute-start.6 = (bf16[2,256,256]{2,1,0:T(8,128)(2,1)S(1)}, bf16[2,256,256]{2,1,0:T(8,128)(2,1)S(1)}, u32[]{:S(2)}, u32[]{:S(2)}) collective-permute-start(bf16[2,256,256]{2,1,0:T(8,128)(2,1)S(1)} %get-tuple-element.60), channel_id=1, source_target_pairs={{0,0},{4,8},{8,4},{12,16},{16,12},{20,24},{24,20},{28,32},{32,28},... | collective-permute-start | bytes 786440 | tf_op jit(solution)/shard_map/ppermute | solution.py:292
  21.4 11.4 %collective-permute-start.9 = (bf16[32,16,256]{2,1,0:T(8,128)(2,1)S(1)}, bf16[32,16,256]{2,1,0:T(8,128)(2,1)S(1)}, u32[]{:S(2)}, u32[]{:S(2)}) collective-permute-start(bf16[32,16,256]{2,1,0:T(8,128)(2,1)S(1)} %get-tuple-element.70), channel_id=1, source_target_pairs={{0,56},{4,236},{8,48},{12,228},{16,40},{20,252},{24,32},{28,244},{... | collective-permute-start | bytes 786440 | tf_op jit(solution)/shard_map/ppermute | solution.py:292
  27.7 7.6 %collective-permute-start.10 = (bf16[32,16,256]{2,1,0:T(8,128)(2,1)S(1)}, bf16[32,16,256]{2,1,0:T(8,128)(2,1)S(1)}, u32[]{:S(2)}, u32[]{:S(2)}) collective-permute-start(bf16[32,16,256]{2,1,0:T(8,128)(2,1)S(1)} %get-tuple-element.71), channel_id=1, source_target_pairs={{0,24},{4,12},{8,16},{12,4},{16,8},{20,28},{24,0},{28,20},{32,56},... | collective-permute-start | bytes 786440 | tf_op jit(solution)/shard_map/ppermute | solution.py:292
  29.4 7.0 %collective-permute-start.11 = (bf16[32,16,256]{2,1,0:T(8,128)(2,1)S(1)}, bf16[32,16,256]{2,1,0:T(8,128)(2,1)S(1)}, u32[]{:S(2)}, u32[]{:S(2)}) collective-permute-start(bf16[32,16,256]{2,1,0:T(8,128)(2,1)S(1)} %get-tuple-element.72), channel_id=1, source_target_pairs={{0,32},{4,228},{8,40},{12,236},{16,48},{20,244},{24,56},{28,252},{... | collective-permute-start | bytes 786440 | tf_op jit(solution)/shard_map/ppermute | solution.py:292
  30.1 14.4 %collective-permute-start.7 = (bf16[4,256,256]{2,1,0:T(8,128)(2,1)S(1)}, bf16[4,256,256]{2,1,0:T(8,128)(2,1)S(1)}, u32[]{:S(2)}, u32[]{:S(2)}) collective-permute-start(bf16[4,256,256]{2,1,0:T(8,128)(2,1)S(1)} %get-tuple-element.63), channel_id=1, source_target_pairs={{0,1},{1,0},{2,3},{3,2},{4,7},{5,6},{6,5},{7,4},{8,9},{9,8},{10,11... | collective-permute-start | bytes 1572872 | tf_op jit(solution)/shard_map/ppermute | solution.py:292
  36.4 8.7 %collective-permute-start.12 = (bf16[8,16,256]{2,1,0:T(8,128)(2,1)S(1)}, bf16[8,16,256]{2,1,0:T(8,128)(2,1)S(1)}, u32[]{:S(2)}, u32[]{:S(2)}) collective-permute-start(bf16[8,16,256]{2,1,0:T(8,128)(2,1)S(1)} %get-tuple-element.74), channel_id=1, source_target_pairs={{0,232},{4,60},{8,224},{12,52},{16,248},{20,44},{24,240},{28,36},{... | collective-permute-start | bytes 196616 | tf_op jit(solution)/shard_map/ppermute | solution.py:292
  40.5 6.2 %collective-permute-start.13 = (bf16[8,16,256]{2,1,0:T(8,128)(2,1)S(1)}, bf16[8,16,256]{2,1,0:T(8,128)(2,1)S(1)}, u32[]{:S(2)}, u32[]{:S(2)}) collective-permute-start(bf16[8,16,256]{2,1,0:T(8,128)(2,1)S(1)} %get-tuple-element.75), channel_id=1, source_target_pairs={{0,8},{4,28},{8,0},{12,20},{16,24},{20,12},{24,16},{28,4},{32,40},... | collective-permute-start | bytes 196616 | tf_op jit(solution)/shard_map/ppermute | solution.py:292
  44.5 5.5 %collective-permute-start.14 = (bf16[8,16,256]{2,1,0:T(8,128)(2,1)S(1)}, bf16[8,16,256]{2,1,0:T(8,128)(2,1)S(1)}, u32[]{:S(2)}, u32[]{:S(2)}) collective-permute-start(bf16[8,16,256]{2,1,0:T(8,128)(2,1)S(1)} %get-tuple-element.76), channel_id=1, source_target_pairs={{0,224},{4,36},{8,232},{12,44},{16,240},{20,52},{24,248},{28,60},{... | collective-permute-start | bytes 196616 | tf_op jit(solution)/shard_map/ppermute | solution.py:292
  44.6 8.1 %collective-permute-start.8 = (bf16[2,256,256]{2,1,0:T(8,128)(2,1)S(1)}, bf16[2,256,256]{2,1,0:T(8,128)(2,1)S(1)}, u32[]{:S(2)}, u32[]{:S(2)}) collective-permute-start(bf16[2,256,256]{2,1,0:T(8,128)(2,1)S(1)} %get-tuple-element.65), channel_id=1, source_target_pairs={{0,3},{1,2},{2,1},{3,0},{4,5},{5,4},{6,7},{7,6},{8,11},{9,10},{10,... | collective-permute-start | bytes 786440 | tf_op jit(solution)/shard_map/ppermute | solution.py:292
  50.0 5.8 %collective-permute-start.15 = (bf16[4,16,256]{2,1,0:T(8,128)(2,1)S(1)}, bf16[4,16,256]{2,1,0:T(8,128)(2,1)S(1)}, u32[]{:S(2)}, u32[]{:S(2)}) collective-permute-start(bf16[4,16,256]{2,1,0:T(8,128)(2,1)S(1)} %get-tuple-element.78), channel_id=1, source_target_pairs={{0,96},{4,164},{8,104},{12,172},{16,112},{20,180},{24,120},{28,188... | collective-permute-start | bytes 98312 | tf_op jit(solution)/shard_map/ppermute | solution.py:292

commit v13 on v12

--- a/solution.py
+++ b/solution.py
@@ -306,7 +306,13 @@
 
 
 def far_row(value):
-    return move(value, SPACE, lambda i: i if i in (0, 63) else (i + 1 if i % 2 else i - 1))
+    def target(i):
+        row, x = i // 4, i % 4
+        if row in (0, 63):
+            return row * 4 + (x ^ 1)
+        return (row + 1 if row % 2 else row - 1) * 4 + x
+
+    return move(value, SPACE + ("mp",), target)
 
 
 def body(activations, w_query, w_key, w_value, w_out, grad_output, neighbours, pad_mask):

time: 56.6 us -> 53.5 us (0.945)
  starting transfers between devices: 27.3 us -> 21 us
  waiting for transfers between devices: 16.6 us -> 19.9 us
    ppermute x16, starting transfers between devices: 27.3 us -> 21 us  [move(): lax.ppermute(value, axis, [(i, target(i)) for i in range(count) if 0 <= t...]
    ppermute x16, waiting for transfers between devices: 16.6 us -> 19.9 us  [move(): lax.ppermute(value, axis, [(i, target(i)) for i in range(count) if 0 <= t...]
  transfers between devices with their start and end apart: 16 -> 16, of which waited for: 8 -> 9; matrix products, arithmetic and copies ran while one was open for 0% -> 0% of each run, Pallas kernels for 13% -> 13%
where the time goes in v13:
time: 53.5 us; the launch traced here: 53.4 us
  starting transfers between devices  21 us (39%)
  waiting for transfers between devices  19.9 us (37%)
  Pallas kernels  11.8 us (22%)
  between operations  0.71 us (1%)
    ppermute x16, starting transfers between devices, move(): lax.ppermute(value, axis, [(i, target(i)) for i in range(count) if 0 <= t...  21 us
    ppermute x16, waiting for transfers between devices, move(): lax.ppermute(value, axis, [(i, target(i)) for i in range(count) if 0 <= t...  19.9 us
    pallas_call x10, Pallas kernels, call(): pl.pallas_call(kernel, out_shape=tuple(kept), in_specs=[pl.BlockSpec(memo...  11.8 us
  transfers between devices with their start and end apart: 16, of which 9 were waited for; matrix products, arithmetic and copies ran while one was open for 0% of the time, Pallas kernels for 13%

profile of v13, /device:TPU:6, one launch (start us, length us, event | category | flops | bytes accessed | tf_op | source)
XLA Modules:
  0.0 53.4 jit_solution(9813073129968673168)
XLA Ops:
  0.6 0.1 collective-permute-start.1
  0.7 0.9 %collective-permute-start = (bf16[256,1024]{1,0:T(8,128)(2,1)}, bf16[256,1024]{1,0:T(8,128)(2,1)S(1)}, u32[]{:S(2)}, u32[]{:S(2)}) collective-permute-start(bf16[256,1024]{1,0:T(8,128)(2,1)} %act.1), channel_id=1, source_target_pairs={{0,1},{1,0},{2,3},{3,2},{4,8},{5,9},{6,10},{7,11},{8,4},{9,5},{10,... | collective-permute-start | bytes 1572872 | tf_op jit(solution)/shard_map/ppermute | solution.py:292
  1.6 2.8 %collective-permute-start.2 = (bf16[256,256]{1,0:T(8,128)(2,1)}, bf16[256,256]{1,0:T(8,128)(2,1)S(1)}, u32[]{:S(2)}, u32[]{:S(2)}) collective-permute-start(bf16[256,256]{1,0:T(8,128)(2,1)} %cot.1), channel_id=1, source_target_pairs={{0,2},{1,3},{2,0},{3,1},{4,6},{5,7},{6,4},{7,5},{8,10},{9,11},{10,... | collective-permute-start | bytes 393224 | tf_op jit(solution)/shard_map/ppermute | solution.py:292
  4.5 1.0 %collective-permute-start.4 = (bf16[256,256]{1,0:T(8,128)(2,1)}, bf16[256,256]{1,0:T(8,128)(2,1)S(1)}, u32[]{:S(2)}, u32[]{:S(2)}) collective-permute-start(bf16[256,256]{1,0:T(8,128)(2,1)} %cot.1), channel_id=1, source_target_pairs={{0,3},{1,2},{2,1},{3,0},{4,7},{5,6},{6,5},{7,4},{8,11},{9,10},{10,... | collective-permute-start | bytes 393224 | tf_op jit(solution)/shard_map/ppermute | solution.py:292
  5.5 0.0 collective-permute-start.3
  5.5 0.0 collective-permute-done.1.a_near
  5.5 3.1 %own_part.1 = (bf16[1024,256]{1,0:T(8,128)(2,1)S(1)}, bf16[1024,256]{1,0:T(8,128)(2,1)S(1)}, bf16[1024,256]{1,0:T(8,128)(2,1)S(1)}, bf16[256,1024]{1,0:T(8,128)(...) custom-call(bf16[256,1024]{1,0:T(8,128)(2,1)} %act.1, ...), custom_call_target="tpu_custom_call" | custom-call | flops 600000000 | bytes 6000000 | tf_op jit(solution)/shard_map/own_part/pallas_call | solution.py:277
  8.6 4.4 %collective-permute-done.a_far = bf16[256,1024]{1,0:T(8,128)(2,1)S(1)} collective-permute-done((bf16[256,1024]{1,0:T(8,128)(2,1)}, bf16[256,1024]{1,0:T(8,128)(2,1)S(1)}, u32[]{:S(2)}, u32[]{:S(2)}) %collective-permute-start) | collective-permute-done | bytes 524320 | tf_op jit(solution)/shard_map/ppermute | solution.py:292
  13.0 2.1 %forward.1 = (bf16[768,256]{1,0:T(8,128)(2,1)S(1)}, bf16[768,256]{1,0:T(8,128)(2,1)S(1)}, bf16[768,1024]{1,0:T(8,128)(2,1)S(1)}, bf16[256,256]{1,0:T(8,128)(2,1)S(1)}, bf16[1024,256]{1,0:T(8,128)(2,1)S(1)}) custom-call(bf16[256,1024]{1,0:T(8,128)(2,1)S(1)} %collective-permute-done.a_far, bf16[1024,256]{1,0:T(8,128)(2,1)S(1)} %get-tuple-element.41.wk, ...), custom_call_target="tpu_custom_call" | custom-call | flops 2000000000 | bytes 6000000 | tf_op jit(solution)/shard_map/forward/pallas_call | solution.py:277
  15.1 1.0 %collective-permute-done.2.c2 = bf16[256,256]{1,0:T(8,128)(2,1)S(1)} collective-permute-done((bf16[256,256]{1,0:T(8,128)(2,1)}, bf16[256,256]{1,0:T(8,128)(2,1)S(1)}, u32[]{:S(2)}, u32[]{:S(2)}) %collective-permute-start.2) | collective-permute-done | bytes 131104 | tf_op jit(solution)/shard_map/ppermute | solution.py:292
  16.1 0.0 collective-permute-done.4.c3
  16.1 0.0 collective-permute-done.3.c1
  16.1 4.1 %backward.1 = (bf16[256,256]{1,0:T(8,128)(2,1)S(1)}, bf16[2,256,256]{2,1,0:T(8,128)(2,1)S(1)}, f32[2,256,256]{2,1,0:T(8,128)S(1)}, bf16[160,16,256]{2,1,0:T(8,128)(2,1)S(1)}, bf16[128,16,256]{2,1,0:T(8,128)(2,1)S(1)}) custom-call(bf16[768,256]{1,0:T(8,128)(2,1)S(1)} %get-tuple-element.48.keys, bf16[768,256]{1,0:T(8,128)(2,1)S(1)} %get-tuple-element.49.values, ...), custom_call_target="tpu_custom_call" | custom-call | flops 3000000000 | bytes 8000000 | tf_op jit(solution)/shard_map/backward/pallas_call | solution.py:277
  20.1 0.1 collective-permute-start.5
  20.2 0.7 %collective-permute-start.6 = (bf16[2,256,256]{2,1,0:T(8,128)(2,1)S(1)}, bf16[2,256,256]{2,1,0:T(8,128)(2,1)S(1)}, u32[]{:S(2)}, u32[]{:S(2)}) collective-permute-start(bf16[2,256,256]{2,1,0:T(8,128)(2,1)S(1)} %get-tuple-element.60), channel_id=1, source_target_pairs={{0,1},{1,0},{2,3},{3,2},{4,8},{5,9},{6,10},{7,11},{8,4},{9,5},{10,... | collective-permute-start | bytes 786440 | tf_op jit(solution)/shard_map/ppermute | solution.py:292
  20.9 2.4 %collective-permute-done.5.near.refs_1_ = bf16[160,16,256]{2,1,0:T(8,128)(2,1)S(1)} collective-permute-done((bf16[160,16,256]{2,1,0:T(8,128)(2,1)S(1)}, bf16[160,16,256]{2,1,0:T(8,128)(2,1)S(1)}, u32[]{:S(2)}, u32[]{:S(2)}) %collective-permute-start.5) | collective-permute-done | bytes 1310752 | tf_op jit(solution)/shard_map/ppermute | solution.py:292
  23.3 0.2 core_sum.1
  23.5 2.3 %collective-permute-start.9 = (bf16[32,16,256]{2,1,0:T(8,128)(2,1)S(1)}, bf16[32,16,256]{2,1,0:T(8,128)(2,1)S(1)}, u32[]{:S(2)}, u32[]{:S(2)}) collective-permute-start(bf16[32,16,256]{2,1,0:T(8,128)(2,1)S(1)} %get-tuple-element.70), channel_id=1, source_target_pairs={{0,56},{4,236},{8,48},{12,228},{16,40},{20,252},{24,32},{28,244},{... | collective-permute-start | bytes 786440 | tf_op jit(solution)/shard_map/ppermute | solution.py:292
  25.8 0.2 collective-permute-start.10
  26.0 2.3 %collective-permute-start.11 = (bf16[32,16,256]{2,1,0:T(8,128)(2,1)S(1)}, bf16[32,16,256]{2,1,0:T(8,128)(2,1)S(1)}, u32[]{:S(2)}, u32[]{:S(2)}) collective-permute-start(bf16[32,16,256]{2,1,0:T(8,128)(2,1)S(1)} %get-tuple-element.72), channel_id=1, source_target_pairs={{0,32},{4,228},{8,40},{12,236},{16,48},{20,244},{24,56},{28,252},{... | collective-permute-start | bytes 786440 | tf_op jit(solution)/shard_map/ppermute | solution.py:292
  28.3 0.0 collective-permute-done.6.far
  28.3 0.7 %input_grad.1 = (f32[4,256,256]{2,1,0:T(8,128)S(1)}, bf16[4,256,256]{2,1,0:T(8,128)(2,1)S(1)}) custom-call(bf16[256,256]{1,0:T(8,128)(2,1)S(1)} %get-tuple-element.47.att, bf16[256,256]{1,0:T(8,128)(2,1)S(1)} %get-tuple-element.57.gq, f32[2,256,256]{2,1,0:T(8,128)S(1)} %get-tuple-element.58.own, ...), custom_call_target="tpu_custom_call" | custom-call | flops 540000000 | bytes 4000000 | tf_op jit(solution)/shard_map/input_grad/pallas_call | solution.py:277
  29.0 0.7 %collective-permute-start.7 = (bf16[4,256,256]{2,1,0:T(8,128)(2,1)S(1)}, bf16[4,256,256]{2,1,0:T(8,128)(2,1)S(1)}, u32[]{:S(2)}, u32[]{:S(2)}) collective-permute-start(bf16[4,256,256]{2,1,0:T(8,128)(2,1)S(1)} %get-tuple-element.63), channel_id=1, source_target_pairs={{0,1},{1,0},{2,3},{3,2},{4,7},{5,6},{6,5},{7,4},{8,9},{9,8},{10,11... | collective-permute-start | bytes 1572872 | tf_op jit(solution)/shard_map/ppermute | solution.py:292
  29.7 2.5 %collective-permute-done.9.refs_1_ = bf16[32,16,256]{2,1,0:T(8,128)(2,1)S(1)} collective-permute-done((bf16[32,16,256]{2,1,0:T(8,128)(2,1)S(1)}, bf16[32,16,256]{2,1,0:T(8,128)(2,1)S(1)}, u32[]{:S(2)}, u32[]{:S(2)}) %collective-permute-start.9) | collective-permute-done | bytes 262176 | tf_op jit(solution)/shard_map/ppermute | solution.py:292
  32.2 2.7 %collective-permute-done.10.refs_2_ = bf16[32,16,256]{2,1,0:T(8,128)(2,1)S(1)} collective-permute-done((bf16[32,16,256]{2,1,0:T(8,128)(2,1)S(1)}, bf16[32,16,256]{2,1,0:T(8,128)(2,1)S(1)}, u32[]{:S(2)}, u32[]{:S(2)}) %collective-permute-start.10) | collective-permute-done | bytes 262176 | tf_op jit(solution)/shard_map/ppermute | solution.py:292
  34.9 0.0 collective-permute-done.11.refs_3_
  34.9 0.1 first_sum.1
  35.0 2.0 %collective-permute-start.12 = (bf16[8,16,256]{2,1,0:T(8,128)(2,1)S(1)}, bf16[8,16,256]{2,1,0:T(8,128)(2,1)S(1)}, u32[]{:S(2)}, u32[]{:S(2)}) collective-permute-start(bf16[8,16,256]{2,1,0:T(8,128)(2,1)S(1)} %get-tuple-element.74), channel_id=1, source_target_pairs={{0,232},{4,60},{8,224},{12,52},{16,248},{20,44},{24,240},{28,36},{... | collective-permute-start | bytes 196616 | tf_op jit(solution)/shard_map/ppermute | solution.py:292
  37.0 4.5 %collective-permute-start.13 = (bf16[8,16,256]{2,1,0:T(8,128)(2,1)S(1)}, bf16[8,16,256]{2,1,0:T(8,128)(2,1)S(1)}, u32[]{:S(2)}, u32[]{:S(2)}) collective-permute-start(bf16[8,16,256]{2,1,0:T(8,128)(2,1)S(1)} %get-tuple-element.75), channel_id=1, source_target_pairs={{0,8},{4,28},{8,0},{12,20},{16,24},{20,12},{24,16},{28,4},{32,40},... | collective-permute-start | bytes 196616 | tf_op jit(solution)/shard_map/ppermute | solution.py:292
  41.4 0.0 collective-permute-start.14
  41.4 0.0 collective-permute-done.7.refs_1_
  41.4 0.1 mp_share.1
  41.5 1.4 %collective-permute-start.8 = (bf16[2,256,256]{2,1,0:T(8,128)(2,1)S(1)}, bf16[2,256,256]{2,1,0:T(8,128)(2,1)S(1)}, u32[]{:S(2)}, u32[]{:S(2)}) collective-permute-start(bf16[2,256,256]{2,1,0:T(8,128)(2,1)S(1)} %get-tuple-element.65), channel_id=1, source_target_pairs={{0,3},{1,2},{2,1},{3,0},{4,5},{5,4},{6,7},{7,6},{8,11},{9,10},{10,... | collective-permute-start | bytes 786440 | tf_op jit(solution)/shard_map/ppermute | solution.py:292
  42.9 0.0 collective-permute-done.12.refs_1_
  42.9 0.8 %collective-permute-done.13.refs_2_ = bf16[8,16,256]{2,1,0:T(8,128)(2,1)S(1)} collective-permute-done((bf16[8,16,256]{2,1,0:T(8,128)(2,1)S(1)}, bf16[8,16,256]{2,1,0:T(8,128)(2,1)S(1)}, u32[]{:S(2)}, u32[]{:S(2)}) %collective-permute-start.13) | collective-permute-done | bytes 65568 | tf_op jit(solution)/shard_map/ppermute | solution.py:292
  43.7 3.2 %collective-permute-done.14.refs_3_ = bf16[8,16,256]{2,1,0:T(8,128)(2,1)S(1)} collective-permute-done((bf16[8,16,256]{2,1,0:T(8,128)(2,1)S(1)}, bf16[8,16,256]{2,1,0:T(8,128)(2,1)S(1)}, u32[]{:S(2)}, u32[]{:S(2)}) %collective-permute-start.14) | collective-permute-done | bytes 65568 | tf_op jit(solution)/shard_map/ppermute | solution.py:292
  47.0 2.2 %collective-permute-start.15 = (bf16[4,16,256]{2,1,0:T(8,128)(2,1)S(1)}, bf16[4,16,256]{2,1,0:T(8,128)(2,1)S(1)}, u32[]{:S(2)}, u32[]{:S(2)}) collective-permute-start(bf16[4,16,256]{2,1,0:T(8,128)(2,1)S(1)} %get-tuple-element.78), channel_id=1, source_target_pairs={{0,96},{4,164},{8,104},{12,172},{16,112},{20,180},{24,120},{28,188... | collective-permute-start | bytes 98312 | tf_op jit(solution)/shard_map/ppermute | solution.py:292
  49.1 0.1 collective-permute-done.8.got
  49.2 0.7 %mp_sum.1 = (bf16[256,256]{1,0:T(8,128)(2,1)}, bf16[256,256]{1,0:T(8,128)(2,1)}) custom-call(f32[2,256,256]{2,1,0:T(8,128)S(1)} %get-tuple-element.64.kept, bf16[2,256,256]{2,1,0:T(8,128)(2,1)S(1)} %collective-permute-done.8.got), custom_call_target="tpu_custom_call" | custom-call | bytes 1000000 | tf_op jit(solution)/shard_map/mp_sum/pallas_call | solution.py:277
  49.9 2.8 %collective-permute-done.15.got = bf16[4,16,256]{2,1,0:T(8,128)(2,1)S(1)} collective-permute-done((bf16[4,16,256]{2,1,0:T(8,128)(2,1)S(1)}, bf16[4,16,256]{2,1,0:T(8,128)(2,1)S(1)}, u32[]{:S(2)}, u32[]{:S(2)}) %collective-permute-start.15) | collective-permute-done | bytes 32800 | tf_op jit(solution)/shard_map/ppermute | solution.py:292
  52.8 0.6 %last_sum.1 = f32[4,16,256]{2,1,0:T(8,128)} custom-call(bf16[256,256]{1,0:T(8,128)(2,1)} %get-tuple-element.38.after, f32[4,16,256]{2,1,0:T(8,128)S(1)} %get-tuple-element.77.kept, bf16[4,16,256]{2,1,0:T(8,128)(2,1)S(1)} %collective-permute-done.15.got), custom_call_target="tpu_custom_call" | custom-call | bytes 1000000 | tf_op jit(solution)/shard_map/last_sum/pallas_call | solution.py:277
  (1 shorter events, 0.0 us)
Async XLA Ops:
  0.6 4.9 %collective-permute-start.1 = (bf16[256,1024]{1,0:T(8,128)(2,1)}, bf16[256,1024]{1,0:T(8,128)(2,1)S(1)}, u32[]{:S(2)}, u32[]{:S(2)}) collective-permute-start(bf16[256,1024]{1,0:T(8,128)(2,1)} %act.1), channel_id=1, source_target_pairs={{0,4},{4,0},{8,12},{12,8},{16,20},{20,16},{24,28},{28,24},{32,36},... | collective-permute-start | bytes 1572872 | tf_op jit(solution)/shard_map/ppermute | solution.py:292
  0.7 12.3 %collective-permute-start = (bf16[256,1024]{1,0:T(8,128)(2,1)}, bf16[256,1024]{1,0:T(8,128)(2,1)S(1)}, u32[]{:S(2)}, u32[]{:S(2)}) collective-permute-start(bf16[256,1024]{1,0:T(8,128)(2,1)} %act.1), channel_id=1, source_target_pairs={{0,1},{1,0},{2,3},{3,2},{4,8},{5,9},{6,10},{7,11},{8,4},{9,5},{10,... | collective-permute-start | bytes 1572872 | tf_op jit(solution)/shard_map/ppermute | solution.py:292
  1.6 14.4 %collective-permute-start.2 = (bf16[256,256]{1,0:T(8,128)(2,1)}, bf16[256,256]{1,0:T(8,128)(2,1)S(1)}, u32[]{:S(2)}, u32[]{:S(2)}) collective-permute-start(bf16[256,256]{1,0:T(8,128)(2,1)} %cot.1), channel_id=1, source_target_pairs={{0,2},{1,3},{2,0},{3,1},{4,6},{5,7},{6,4},{7,5},{8,10},{9,11},{10,... | collective-permute-start | bytes 393224 | tf_op jit(solution)/shard_map/ppermute | solution.py:292
  4.5 11.6 %collective-permute-start.4 = (bf16[256,256]{1,0:T(8,128)(2,1)}, bf16[256,256]{1,0:T(8,128)(2,1)S(1)}, u32[]{:S(2)}, u32[]{:S(2)}) collective-permute-start(bf16[256,256]{1,0:T(8,128)(2,1)} %cot.1), channel_id=1, source_target_pairs={{0,3},{1,2},{2,1},{3,0},{4,7},{5,6},{6,5},{7,4},{8,11},{9,10},{10,... | collective-permute-start | bytes 393224 | tf_op jit(solution)/shard_map/ppermute | solution.py:292
  5.5 10.6 %collective-permute-start.3 = (bf16[256,256]{1,0:T(8,128)(2,1)}, bf16[256,256]{1,0:T(8,128)(2,1)S(1)}, u32[]{:S(2)}, u32[]{:S(2)}) collective-permute-start(bf16[256,256]{1,0:T(8,128)(2,1)} %cot.1), channel_id=1, source_target_pairs={{0,1},{1,0},{2,3},{3,2},{4,5},{5,4},{6,7},{7,6},{8,9},{9,8},{10,11... | collective-permute-start | bytes 393224 | tf_op jit(solution)/shard_map/ppermute | solution.py:292
  20.1 3.1 %collective-permute-start.5 = (bf16[160,16,256]{2,1,0:T(8,128)(2,1)S(1)}, bf16[160,16,256]{2,1,0:T(8,128)(2,1)S(1)}, u32[]{:S(2)}, u32[]{:S(2)}) collective-permute-start(bf16[160,16,256]{2,1,0:T(8,128)(2,1)S(1)} %get-tuple-element.59), channel_id=1, source_target_pairs={{0,4},{4,0},{8,12},{12,8},{16,20},{20,16},{24,28},{28,24},{32,36},... | collective-permute-start | bytes 3932168 | tf_op jit(solution)/shard_map/ppermute | solution.py:292
  20.2 8.1 %collective-permute-start.6 = (bf16[2,256,256]{2,1,0:T(8,128)(2,1)S(1)}, bf16[2,256,256]{2,1,0:T(8,128)(2,1)S(1)}, u32[]{:S(2)}, u32[]{:S(2)}) collective-permute-start(bf16[2,256,256]{2,1,0:T(8,128)(2,1)S(1)} %get-tuple-element.60), channel_id=1, source_target_pairs={{0,1},{1,0},{2,3},{3,2},{4,8},{5,9},{6,10},{7,11},{8,4},{9,5},{10,... | collective-permute-start | bytes 786440 | tf_op jit(solution)/shard_map/ppermute | solution.py:292
  23.5 8.7 %collective-permute-start.9 = (bf16[32,16,256]{2,1,0:T(8,128)(2,1)S(1)}, bf16[32,16,256]{2,1,0:T(8,128)(2,1)S(1)}, u32[]{:S(2)}, u32[]{:S(2)}) collective-permute-start(bf16[32,16,256]{2,1,0:T(8,128)(2,1)S(1)} %get-tuple-element.70), channel_id=1, source_target_pairs={{0,56},{4,236},{8,48},{12,228},{16,40},{20,252},{24,32},{28,244},{... | collective-permute-start | bytes 786440 | tf_op jit(solution)/shard_map/ppermute | solution.py:292
  25.8 9.1 %collective-permute-start.10 = (bf16[32,16,256]{2,1,0:T(8,128)(2,1)S(1)}, bf16[32,16,256]{2,1,0:T(8,128)(2,1)S(1)}, u32[]{:S(2)}, u32[]{:S(2)}) collective-permute-start(bf16[32,16,256]{2,1,0:T(8,128)(2,1)S(1)} %get-tuple-element.71), channel_id=1, source_target_pairs={{0,24},{4,12},{8,16},{12,4},{16,8},{20,28},{24,0},{28,20},{32,56},... | collective-permute-start | bytes 786440 | tf_op jit(solution)/shard_map/ppermute | solution.py:292
  26.0 8.9 %collective-permute-start.11 = (bf16[32,16,256]{2,1,0:T(8,128)(2,1)S(1)}, bf16[32,16,256]{2,1,0:T(8,128)(2,1)S(1)}, u32[]{:S(2)}, u32[]{:S(2)}) collective-permute-start(bf16[32,16,256]{2,1,0:T(8,128)(2,1)S(1)} %get-tuple-element.72), channel_id=1, source_target_pairs={{0,32},{4,228},{8,40},{12,236},{16,48},{20,244},{24,56},{28,252},{... | collective-permute-start | bytes 786440 | tf_op jit(solution)/shard_map/ppermute | solution.py:292
  29.0 12.4 %collective-permute-start.7 = (bf16[4,256,256]{2,1,0:T(8,128)(2,1)S(1)}, bf16[4,256,256]{2,1,0:T(8,128)(2,1)S(1)}, u32[]{:S(2)}, u32[]{:S(2)}) collective-permute-start(bf16[4,256,256]{2,1,0:T(8,128)(2,1)S(1)} %get-tuple-element.63), channel_id=1, source_target_pairs={{0,1},{1,0},{2,3},{3,2},{4,7},{5,6},{6,5},{7,4},{8,9},{9,8},{10,11... | collective-permute-start | bytes 1572872 | tf_op jit(solution)/shard_map/ppermute | solution.py:292
  35.0 7.9 %collective-permute-start.12 = (bf16[8,16,256]{2,1,0:T(8,128)(2,1)S(1)}, bf16[8,16,256]{2,1,0:T(8,128)(2,1)S(1)}, u32[]{:S(2)}, u32[]{:S(2)}) collective-permute-start(bf16[8,16,256]{2,1,0:T(8,128)(2,1)S(1)} %get-tuple-element.74), channel_id=1, source_target_pairs={{0,232},{4,60},{8,224},{12,52},{16,248},{20,44},{24,240},{28,36},{... | collective-permute-start | bytes 196616 | tf_op jit(solution)/shard_map/ppermute | solution.py:292
  37.0 6.7 %collective-permute-start.13 = (bf16[8,16,256]{2,1,0:T(8,128)(2,1)S(1)}, bf16[8,16,256]{2,1,0:T(8,128)(2,1)S(1)}, u32[]{:S(2)}, u32[]{:S(2)}) collective-permute-start(bf16[8,16,256]{2,1,0:T(8,128)(2,1)S(1)} %get-tuple-element.75), channel_id=1, source_target_pairs={{0,8},{4,28},{8,0},{12,20},{16,24},{20,12},{24,16},{28,4},{32,40},... | collective-permute-start | bytes 196616 | tf_op jit(solution)/shard_map/ppermute | solution.py:292
  41.4 5.5 %collective-permute-start.14 = (bf16[8,16,256]{2,1,0:T(8,128)(2,1)S(1)}, bf16[8,16,256]{2,1,0:T(8,128)(2,1)S(1)}, u32[]{:S(2)}, u32[]{:S(2)}) collective-permute-start(bf16[8,16,256]{2,1,0:T(8,128)(2,1)S(1)} %get-tuple-element.76), channel_id=1, source_target_pairs={{0,224},{4,36},{8,232},{12,44},{16,240},{20,52},{24,248},{28,60},{... | collective-permute-start | bytes 196616 | tf_op jit(solution)/shard_map/ppermute | solution.py:292
  41.5 7.7 %collective-permute-start.8 = (bf16[2,256,256]{2,1,0:T(8,128)(2,1)S(1)}, bf16[2,256,256]{2,1,0:T(8,128)(2,1)S(1)}, u32[]{:S(2)}, u32[]{:S(2)}) collective-permute-start(bf16[2,256,256]{2,1,0:T(8,128)(2,1)S(1)} %get-tuple-element.65), channel_id=1, source_target_pairs={{0,3},{1,2},{2,1},{3,0},{4,5},{5,4},{6,7},{7,6},{8,11},{9,10},{10,... | collective-permute-start | bytes 786440 | tf_op jit(solution)/shard_map/ppermute | solution.py:292
  47.0 5.8 %collective-permute-start.15 = (bf16[4,16,256]{2,1,0:T(8,128)(2,1)S(1)}, bf16[4,16,256]{2,1,0:T(8,128)(2,1)S(1)}, u32[]{:S(2)}, u32[]{:S(2)}) collective-permute-start(bf16[4,16,256]{2,1,0:T(8,128)(2,1)S(1)} %get-tuple-element.78), channel_id=1, source_target_pairs={{0,96},{4,164},{8,104},{12,172},{16,112},{20,180},{24,120},{28,188... | collective-permute-start | bytes 98312 | tf_op jit(solution)/shard_map/ppermute | solution.py:292

commit v14 on v13

--- a/solution.py
+++ b/solution.py
@@ -123,9 +123,23 @@
     return total.astype(BF)
 
 
+def store_halves(out, rows, start, core):
+    for block in range(rows.shape[0] // 32):
+        for c in range(2):
+            half = jnp.where(core == c, D // 2, 0)
+            there = pl.ds(pl.multiple_of(half + start + 16 * block, 16), 16)
+            out[there, :] = rows[32 * block + 16 * c : 32 * block + 16 * (c + 1)]
+
+
+def spread_bias(bias, patches):
+    return jnp.concatenate(
+        [jnp.broadcast_to(bias[patch : patch + 1, :], (PATCH, ROW)) for patch in patches], axis=0
+    )
+
+
 def own_kernel(
     act, w_q, w_k, w_v, w_o, cot, slots, live, a_near,
-    wq, wk, wv, wo, query_out, keys_out, values_out, act_t, near_t, grad_out, cot_t, bias_out,
+    wq, wk, wv, wo, query_out, keys_out, values_out, exps_out, peaks_out, act_t, near_t, grad_out, cot_t, bias_out,
     act_s, cot_s, nb, mask, sems,
 ):
     core, y, z, x = places()
@@ -135,18 +149,28 @@
     copies = [pltpu.make_async_copy(a, b, sems.at[i]) for i, (a, b) in enumerate(pairs)]
     for copy in copies:
         copy.start()
-    near_t[...] = a_near[...].T
+    store_halves(near_t, a_near[...].T, 0, core)
     copies[0].wait()
     copies[1].wait()
-    bias_out[...] = slot_bias(nb, mask, core, y, z)
+    bias = slot_bias(nb, mask, core, y, z)
+    bias_out[...] = bias
     copies[2].wait()
-    act_t[...] = act_s[...].T
+    store_halves(act_t, act_s[...].T, 0, core)
     for index, weight, out in ((3, wk, keys_out), (4, wv, values_out)):
         copies[index].wait()
         out[:ROW, :] = mm(act_s[...], weight[...]).astype(BF)
         out[ROW:, :] = mm(a_near[...], weight[...]).astype(BF)
     copies[5].wait()
     stack_heads(mm(act_s[...], wq[...]).astype(BF), query_out)
+    bias_rows = spread_bias(bias, range(4, 12))
+    for head in range(HEADS):
+        scores = mm(keys_out[...], query_out[head * ROW : (head + 1) * ROW, :], NT)
+        scores = scores * (LOG2E * HD**-0.5) + bias_rows
+        peak = jnp.max(scores, axis=0, keepdims=True)
+        exps = jnp.exp2(scores - peak)
+        exps_out[head] = exps
+        peaks_out[head : head + 1, :] = peak
+        peaks_out[HEADS + head : HEADS + head + 1, :] = jnp.sum(exps, axis=0, keepdims=True)
     copies[6].wait()
     cot_t[...] = cot_s[...].T
     copies[7].wait()
@@ -154,33 +178,56 @@
 
 
 def forward_kernel(
-    a_far, wk, wv, query, keys_in, values_in, bias,
+    a_far, wk, wv, query, keys_in, values_in, exps, peaks, bias,
     keys, values, probs_out, att_out, far_t,
     probs_t,
 ):
+    core = places()[0]
     keys[ROW:, :] = keys_in[...]
     values[ROW:, :] = values_in[...]
     keys[:ROW, :] = mm(a_far[...], wk[...]).astype(BF)
     values[:ROW, :] = mm(a_far[...], wv[...]).astype(BF)
-    bias_rows = jnp.concatenate(
-        [jnp.broadcast_to(bias[patch : patch + 1, :], (PATCH, ROW)) for patch in range(KEYS // PATCH)],
-        axis=0,
-    )
+    bias_rows = spread_bias(bias, range(4))
     for head in range(HEADS):
         part = slice(head * ROW, (head + 1) * ROW)
-        scores = mm(keys[...], query[part, :], NT) * (LOG2E * HD**-0.5) + bias_rows
-        peak = jnp.max(scores, axis=0, keepdims=True)
+        scores = mm(keys[:ROW, :], query[part, :], NT) * (LOG2E * HD**-0.5) + bias_rows
+        peak_before = peaks[head : head + 1, :]
+        peak = jnp.maximum(peak_before, jnp.max(scores, axis=0, keepdims=True))
         weights = jnp.exp2(scores - peak)
-        probs = (weights * (1.0 / jnp.sum(weights, axis=0, keepdims=True))).astype(BF)
-        probs_out[:, part] = probs
-        probs_t[part, :] = probs.T
+        before = jnp.exp2(peak_before - peak)
+        total = before * peaks[HEADS + head : HEADS + head + 1, :] + jnp.sum(weights, axis=0, keepdims=True)
+        scale = 1.0 / total
+        far_probs = (weights * scale).astype(BF)
+        other_probs = (exps[head] * (before * scale)).astype(BF)
+        probs_out[:ROW, part] = far_probs
+        probs_out[ROW:, part] = other_probs
+        probs_t[part, :ROW] = far_probs.T
+        probs_t[part, ROW:] = other_probs.T
     att_out[...] = pick_heads(mm(probs_t[...], values[...]))
-    far_t[...] = a_far[...].T
+    store_halves(far_t, a_far[...].T, 0, core)
+
+
+def weight_terms(half, partners, act_t, far_t, near_t, cot_t, gq, grad_key, grad_value, att, out, dw_s):
+    rows = slice(half * (D // 2), (half + 1) * (D // 2))
+    dw_s[0] = mm(act_t[rows, :], gq[...])
+    for index, grad in ((1, grad_key), (2, grad_value)):
+        dw_s[index] = (
+            mm(act_t[rows, :], grad[ROW : 2 * ROW, :])
+            + mm(far_t[rows, :], grad[:ROW, :])
+            + mm(near_t[rows, :], grad[2 * ROW :, :])
+        )
+    dw_s[3] = mm(cot_t[rows, :], att[...])
+    core, y, z, _ = places()
+    tables = [target_rows(z, y, *pair) for pair in PARTNERS]
+    for number in range(32):
+        zero, one = (table[number] * 16 for table in tables)
+        row = pl.multiple_of(jnp.where(partners == 0, zero, one), 16)
+        out[4 * number : 4 * number + 4] = dw_s[:, pl.ds(row, 16), :].astype(BF)
 
 
 def backward_kernel(
-    keys, values, probs_in, att, far_t, near_t, wo, query, act_t, grad_in, cot_t, c2, c1, c3,
-    gq_out, far_out, own_out, send_out, keep_out,
+    keys, values, probs_in, att, far_t, near_t, wo, query, act_t, grad_in, cot_own, c2, c1, c3,
+    gq, far_out, own_out, grad_key, grad_value, cot_t, send_out,
     grad_s, scores_s, scores_t, dw_s,
 ):
     core, y, z, x = places()
@@ -197,34 +244,29 @@
         grad_scores = (probs * ((grad_probs - centre) * HD**-0.5)).astype(BF)
         scores_s[:, part] = grad_scores
         scores_t[part, :] = grad_scores.T
-    gq = pick_heads(mm(scores_t[...], keys[...]))
-    grad_key = mm(scores_s[...], query[...])
-    grad_value = mm(probs_in[...], grad_s[...])
-    gq_out[...] = gq
-    far_out[0], far_out[1] = grad_key[:ROW].astype(BF), grad_value[:ROW].astype(BF)
-    own_out[0], own_out[1] = grad_key[ROW : 2 * ROW], grad_value[ROW : 2 * ROW]
-    for part, grad in enumerate((grad_key, grad_value)):
+    gq[...] = pick_heads(mm(scores_t[...], keys[...]))
+    for index, (grad, out) in enumerate(
+        ((mm(scores_s[...], query[...]), grad_key), (mm(probs_in[...], grad_s[...]), grad_value))
+    ):
+        low = grad.astype(BF)
+        out[...] = low
+        far_out[index] = low[:ROW]
+        own_out[index] = grad[ROW : 2 * ROW]
         for block in range(16):
             rows = slice(2 * ROW + 16 * block, 2 * ROW + 16 * (block + 1))
-            send_out[128 + 16 * part + block] = grad[rows].astype(BF)
-
-    for place, block_t in ((x, cot_t[...]), *((place, block[...].T) for place, block in blocks)):
-        rows = pl.ds(pl.multiple_of(place * WIDTH, WIDTH), WIDTH)
-        dw_s[3, rows, :] = mm(block_t, att[...])
-    grad_key = grad_key.astype(BF)
-    grad_value = grad_value.astype(BF)
-    own = slice(ROW, 2 * ROW)
-    dw_s[0] = mm(act_t[...], gq)
-    for index, grad in ((1, grad_key), (2, grad_value)):
-        dw_s[index] = (
-            mm(act_t[...], grad[own]) + mm(far_t[...], grad[:ROW]) + mm(near_t[...], grad[2 * ROW :])
-        )
-    tables = [target_rows(z, y, *partners) for partners in PARTNERS]
-    for number in range(32):
-        first, second = (table[number] * 32 for table in tables)
-        for c, out in ((1 - core, send_out), (core, keep_out)):
-            row = pl.multiple_of(jnp.where(c == 0, first, second) + c * 16, 16)
-            out[4 * number : 4 * number + 4] = dw_s[:, pl.ds(row, 16), :].astype(BF)
+            send_out[128 + 16 * index + block] = low[rows]
+    for place, block_t in ((x, cot_own[...]), *((place, block[...].T) for place, block in blocks)):
+        store_halves(cot_t, block_t, place * (WIDTH // 2), core)
+    weight_terms(
+        0, 1 - core, act_t, far_t, near_t, cot_t, gq, grad_key, grad_value, att, send_out, dw_s
+    )
+
+
+def keep_kernel(act_t, far_t, near_t, cot_t, gq, grad_key, grad_value, att, keep_out, dw_s):
+    core = places()[0]
+    weight_terms(
+        1, core, act_t, far_t, near_t, cot_t, gq, grad_key, grad_value, att, keep_out, dw_s
+    )
 
 
 def share_kernel(count, *refs):
@@ -322,11 +364,12 @@
 
     square = (ROW, WIDTH)
     stacked = (HEADS * ROW, WIDTH)
-    wq, wk, wv, wo, query, keys, values, act_t, near_t, grad_own, cot_t, bias = call(
+    wq, wk, wv, wo, query, keys, values, exps, peaks, act_t, near_t, grad_own, cot_own, bias = call(
         own_kernel,
         "own_part",
         [((D, WIDTH), BF)] * 3
         + [((WIDTH, D), BF), (stacked, BF), ((2 * ROW, WIDTH), BF), ((2 * ROW, WIDTH), BF)]
+        + [((HEADS, 2 * ROW, ROW), F32), ((2 * HEADS, ROW), F32)]
         + [((D, ROW), BF), ((D, ROW), BF), (square, F32), (square, BF), ((16, ROW), F32)],
         [act_near],
         apart=(activations, w_query, w_key, w_value, w_out, grad_output, neighbours, pad_mask),
@@ -346,32 +389,43 @@
         forward_kernel,
         "forward",
         [((KEYS, WIDTH), BF)] * 2 + [((KEYS, HEADS * ROW), BF), (square, BF), ((D, ROW), BF)],
-        [act_far, wk, wv, query, keys, values, bias],
+        [act_far, wk, wv, query, keys, values, exps, peaks, bias],
         scratch=[pltpu.VMEM((HEADS * ROW, KEYS), BF)],
         limit=20,
         flops=2_000_000_000,
         moved=6_000_000,
     )
-    gq, far, own, dw_send, dw_keep = call(
+    gq, far, own, grad_key, grad_value, cot_t, dw_send = call(
         backward_kernel,
         "backward",
         [
             (square, BF),
             ((2, ROW, WIDTH), BF),
             ((2, ROW, WIDTH), F32),
+            ((KEYS, WIDTH), BF),
+            ((KEYS, WIDTH), BF),
+            ((D, ROW), BF),
             ((160,) + block, BF),
-            ((128,) + block, BF),
         ],
-        [keys, values, probs, att, far_t, near_t, wo, query, act_t, grad_own, cot_t, *cots],
+        [keys, values, probs, att, far_t, near_t, wo, query, act_t, grad_own, cot_own, *cots],
         scratch=[
             pltpu.VMEM(stacked, BF),
             pltpu.VMEM((KEYS, HEADS * ROW), BF),
             pltpu.VMEM((HEADS * ROW, KEYS), BF),
-            pltpu.VMEM((4, D, WIDTH), F32),
+            pltpu.VMEM((4, D // 2, WIDTH), F32),
         ],
         limit=24,
-        flops=3_000_000_000,
+        flops=2_000_000_000,
         moved=8_000_000,
+    )
+    (dw_keep,) = call(
+        keep_kernel,
+        "keep_terms",
+        [((128,) + block, BF)],
+        [act_t, far_t, near_t, cot_t, gq, grad_key, grad_value, att],
+        scratch=[pltpu.VMEM((4, D // 2, WIDTH), F32)],
+        flops=1_000_000_000,
+        moved=4_000_000,
     )
 
     def share(name, terms, ways, kept_as, flops=0):

time: 53.5 us -> 53.2 us (level)
  waiting for transfers between devices: 19.9 us -> 18.8 us
  Pallas kernels: 11.8 us -> 12.5 us
    ppermute x16, waiting for transfers between devices: 19.9 us -> 18.8 us  [move(): lax.ppermute(value, axis, [(i, target(i)) for i in range(count) if 0 <= t...]
    pallas_call x10 -> x11, Pallas kernels: 11.8 us -> 12.5 us  [call(): pl.pallas_call(kernel, out_shape=tuple(kept), in_specs=[pl.BlockSpec(memo...]
  transfers between devices with their start and end apart: 16 -> 16, of which waited for: 9 -> 9; matrix products, arithmetic and copies ran while one was open for 0% -> 0% of each run, Pallas kernels for 13% -> 16%
where the time goes in v14:
time: 53.2 us; the launch traced here: 53.1 us
  starting transfers between devices  21 us (39%)
  waiting for transfers between devices  18.8 us (35%)
  Pallas kernels  12.5 us (23%)
  between operations  0.72 us (1%)
    ppermute x16, starting transfers between devices, move(): lax.ppermute(value, axis, [(i, target(i)) for i in range(count) if 0 <= t...  21 us
    ppermute x16, waiting for transfers between devices, move(): lax.ppermute(value, axis, [(i, target(i)) for i in range(count) if 0 <= t...  18.8 us
    pallas_call x11, Pallas kernels, call(): pl.pallas_call(kernel, out_shape=tuple(kept), in_specs=[pl.BlockSpec(memo...  12.5 us
  transfers between devices with their start and end apart: 16, of which 9 were waited for; matrix products, arithmetic and copies ran while one was open for 0% of the time, Pallas kernels for 16%

profile of v14, /device:TPU:6, one launch (start us, length us, event | category | flops | bytes accessed | tf_op | source)
XLA Modules:
  0.0 53.1 jit_solution(491620030104850987)
XLA Ops:
  0.6 0.1 collective-permute-start.1
  0.7 0.9 %collective-permute-start = (bf16[256,1024]{1,0:T(8,128)(2,1)}, bf16[256,1024]{1,0:T(8,128)(2,1)S(1)}, u32[]{:S(2)}, u32[]{:S(2)}) collective-permute-start(bf16[256,1024]{1,0:T(8,128)(2,1)} %act.1), channel_id=1, source_target_pairs={{0,1},{1,0},{2,3},{3,2},{4,8},{5,9},{6,10},{7,11},{8,4},{9,5},{10,... | collective-permute-start | bytes 1572872 | tf_op jit(solution)/shard_map/ppermute | solution.py:334
  1.6 2.8 %collective-permute-start.2 = (bf16[256,256]{1,0:T(8,128)(2,1)}, bf16[256,256]{1,0:T(8,128)(2,1)S(1)}, u32[]{:S(2)}, u32[]{:S(2)}) collective-permute-start(bf16[256,256]{1,0:T(8,128)(2,1)} %cot.1), channel_id=1, source_target_pairs={{0,2},{1,3},{2,0},{3,1},{4,6},{5,7},{6,4},{7,5},{8,10},{9,11},{10,... | collective-permute-start | bytes 393224 | tf_op jit(solution)/shard_map/ppermute | solution.py:334
  4.5 1.0 %collective-permute-start.4 = (bf16[256,256]{1,0:T(8,128)(2,1)}, bf16[256,256]{1,0:T(8,128)(2,1)S(1)}, u32[]{:S(2)}, u32[]{:S(2)}) collective-permute-start(bf16[256,256]{1,0:T(8,128)(2,1)} %cot.1), channel_id=1, source_target_pairs={{0,3},{1,2},{2,1},{3,0},{4,7},{5,6},{6,5},{7,4},{8,11},{9,10},{10,... | collective-permute-start | bytes 393224 | tf_op jit(solution)/shard_map/ppermute | solution.py:334
  5.5 0.0 collective-permute-start.3
  5.5 0.0 collective-permute-done.1.a_near
  5.5 3.9 %own_part.1 = (bf16[1024,256]{1,0:T(8,128)(2,1)S(1)}, bf16[1024,256]{1,0:T(8,128)(2,1)S(1)}, bf16[1024,256]{1,0:T(8,128)(2,1)S(1)}, bf16[256,1024]{1,0:T(8,128)(...) custom-call(bf16[256,1024]{1,0:T(8,128)(2,1)} %act.1, ...), custom_call_target="tpu_custom_call" | custom-call | flops 600000000 | bytes 6000000 | tf_op jit(solution)/shard_map/own_part/pallas_call | solution.py:319
  9.5 3.5 %collective-permute-done.a_far = bf16[256,1024]{1,0:T(8,128)(2,1)S(1)} collective-permute-done((bf16[256,1024]{1,0:T(8,128)(2,1)}, bf16[256,1024]{1,0:T(8,128)(2,1)S(1)}, u32[]{:S(2)}, u32[]{:S(2)}) %collective-permute-start) | collective-permute-done | bytes 524320 | tf_op jit(solution)/shard_map/ppermute | solution.py:334
  13.0 1.6 %forward.1 = (bf16[768,256]{1,0:T(8,128)(2,1)S(1)}, bf16[768,256]{1,0:T(8,128)(2,1)S(1)}, bf16[768,1024]{1,0:T(8,128)(2,1)S(1)}, bf16[256,256]{1,0:T(8,128)(2,1)S(1)}, bf16[1024,256]{1,0:T(8,128)(2,1)S(1)}) custom-call(bf16[256,1024]{1,0:T(8,128)(2,1)S(1)} %collective-permute-done.a_far, bf16[1024,256]{1,0:T(8,128)(2,1)S(1)} %get-tuple-element.45.wk, ...), custom_call_target="tpu_custom_call" | custom-call | flops 2000000000 | bytes 6000000 | tf_op jit(solution)/shard_map/forward/pallas_call | solution.py:319
  14.6 1.5 %collective-permute-done.2.c2 = bf16[256,256]{1,0:T(8,128)(2,1)S(1)} collective-permute-done((bf16[256,256]{1,0:T(8,128)(2,1)}, bf16[256,256]{1,0:T(8,128)(2,1)S(1)}, u32[]{:S(2)}, u32[]{:S(2)}) %collective-permute-start.2) | collective-permute-done | bytes 131104 | tf_op jit(solution)/shard_map/ppermute | solution.py:334
  16.1 0.0 collective-permute-done.4.c3
  16.1 0.0 collective-permute-done.3.c1
  16.1 3.6 %backward.1 = (bf16[256,256]{1,0:T(8,128)(2,1)S(1)}, bf16[2,256,256]{2,1,0:T(8,128)(2,1)S(1)}, f32[2,256,256]{2,1,0:T(8,128)S(1)}, bf16[768,256]{1,0:T(8,128)(2,...) custom-call(bf16[768,256]{1,0:T(8,128)(2,1)S(1)} %get-tuple-element.54.keys, ...), custom_call_target="tpu_custom_call" | custom-call | flops 2000000000 | bytes 8000000 | tf_op jit(solution)/shard_map/backward/pallas_call | solution.py:319
  19.7 0.1 collective-permute-start.5
  19.8 0.7 %collective-permute-start.6 = (bf16[2,256,256]{2,1,0:T(8,128)(2,1)S(1)}, bf16[2,256,256]{2,1,0:T(8,128)(2,1)S(1)}, u32[]{:S(2)}, u32[]{:S(2)}) collective-permute-start(bf16[2,256,256]{2,1,0:T(8,128)(2,1)S(1)} %get-tuple-element.66), channel_id=1, source_target_pairs={{0,1},{1,0},{2,3},{3,2},{4,8},{5,9},{6,10},{7,11},{8,4},{9,5},{10,... | collective-permute-start | bytes 786440 | tf_op jit(solution)/shard_map/ppermute | solution.py:334
  20.5 0.8 %keep_terms.1.refs_0_ = bf16[128,16,256]{2,1,0:T(8,128)(2,1)S(1)} custom-call(bf16[1024,256]{1,0:T(8,128)(2,1)S(1)} %get-tuple-element.60.act_t, bf16[1024,256]{1,0:T(8,128)(2,1)S(1)} %get-tuple-element.57.far_t, bf16[1024,256]{1,0:T(8,128)(2,1)S(1)} %get-tuple-element.58.near_t, bf16[1024,256]{1,0:T(8,128)(2,1)S(1)} %get-tuple-element.74.cot_t, ...), custom_call_target="tpu_custom_call" | custom-call | flops 1000000000 | bytes 4000000 | tf_op jit(solution)/shard_map/keep_terms/pallas_call | solution.py:319
  21.3 1.5 %collective-permute-done.5.near.refs_1_ = bf16[160,16,256]{2,1,0:T(8,128)(2,1)S(1)} collective-permute-done((bf16[160,16,256]{2,1,0:T(8,128)(2,1)S(1)}, bf16[160,16,256]{2,1,0:T(8,128)(2,1)S(1)}, u32[]{:S(2)}, u32[]{:S(2)}) %collective-permute-start.5) | collective-permute-done | bytes 1310752 | tf_op jit(solution)/shard_map/ppermute | solution.py:334
  22.8 0.2 core_sum.1
  23.1 2.0 %collective-permute-start.9 = (bf16[32,16,256]{2,1,0:T(8,128)(2,1)S(1)}, bf16[32,16,256]{2,1,0:T(8,128)(2,1)S(1)}, u32[]{:S(2)}, u32[]{:S(2)}) collective-permute-start(bf16[32,16,256]{2,1,0:T(8,128)(2,1)S(1)} %get-tuple-element.78), channel_id=1, source_target_pairs={{0,56},{4,236},{8,48},{12,228},{16,40},{20,252},{24,32},{28,244},{... | collective-permute-start | bytes 786440 | tf_op jit(solution)/shard_map/ppermute | solution.py:334
  25.0 0.7 %collective-permute-start.10 = (bf16[32,16,256]{2,1,0:T(8,128)(2,1)S(1)}, bf16[32,16,256]{2,1,0:T(8,128)(2,1)S(1)}, u32[]{:S(2)}, u32[]{:S(2)}) collective-permute-start(bf16[32,16,256]{2,1,0:T(8,128)(2,1)S(1)} %get-tuple-element.79), channel_id=1, source_target_pairs={{0,24},{4,12},{8,16},{12,4},{16,8},{20,28},{24,0},{28,20},{32,56},... | collective-permute-start | bytes 786440 | tf_op jit(solution)/shard_map/ppermute | solution.py:334
  25.7 2.3 %collective-permute-start.11 = (bf16[32,16,256]{2,1,0:T(8,128)(2,1)S(1)}, bf16[32,16,256]{2,1,0:T(8,128)(2,1)S(1)}, u32[]{:S(2)}, u32[]{:S(2)}) collective-permute-start(bf16[32,16,256]{2,1,0:T(8,128)(2,1)S(1)} %get-tuple-element.80), channel_id=1, source_target_pairs={{0,32},{4,228},{8,40},{12,236},{16,48},{20,244},{24,56},{28,252},{... | collective-permute-start | bytes 786440 | tf_op jit(solution)/shard_map/ppermute | solution.py:334
  28.0 0.0 collective-permute-done.6.far
  28.0 0.7 %input_grad.1 = (f32[4,256,256]{2,1,0:T(8,128)S(1)}, bf16[4,256,256]{2,1,0:T(8,128)(2,1)S(1)}) custom-call(bf16[256,256]{1,0:T(8,128)(2,1)S(1)} %get-tuple-element.53.att, bf16[256,256]{1,0:T(8,128)(2,1)S(1)} %get-tuple-element.63.gq, f32[2,256,256]{2,1,0:T(8,128)S(1)} %get-tuple-element.64.own, ...), custom_call_target="tpu_custom_call" | custom-call | flops 540000000 | bytes 4000000 | tf_op jit(solution)/shard_map/input_grad/pallas_call | solution.py:319
  28.8 0.7 %collective-permute-start.7 = (bf16[4,256,256]{2,1,0:T(8,128)(2,1)S(1)}, bf16[4,256,256]{2,1,0:T(8,128)(2,1)S(1)}, u32[]{:S(2)}, u32[]{:S(2)}) collective-permute-start(bf16[4,256,256]{2,1,0:T(8,128)(2,1)S(1)} %get-tuple-element.69), channel_id=1, source_target_pairs={{0,1},{1,0},{2,3},{3,2},{4,7},{5,6},{6,5},{7,4},{8,9},{9,8},{10,11... | collective-permute-start | bytes 1572872 | tf_op jit(solution)/shard_map/ppermute | solution.py:334
  29.4 2.5 %collective-permute-done.9.refs_1_ = bf16[32,16,256]{2,1,0:T(8,128)(2,1)S(1)} collective-permute-done((bf16[32,16,256]{2,1,0:T(8,128)(2,1)S(1)}, bf16[32,16,256]{2,1,0:T(8,128)(2,1)S(1)}, u32[]{:S(2)}, u32[]{:S(2)}) %collective-permute-start.9) | collective-permute-done | bytes 262176 | tf_op jit(solution)/shard_map/ppermute | solution.py:334
  31.9 2.7 %collective-permute-done.10.refs_2_ = bf16[32,16,256]{2,1,0:T(8,128)(2,1)S(1)} collective-permute-done((bf16[32,16,256]{2,1,0:T(8,128)(2,1)S(1)}, bf16[32,16,256]{2,1,0:T(8,128)(2,1)S(1)}, u32[]{:S(2)}, u32[]{:S(2)}) %collective-permute-start.10) | collective-permute-done | bytes 262176 | tf_op jit(solution)/shard_map/ppermute | solution.py:334
  34.6 0.0 collective-permute-done.11.refs_3_
  34.6 0.1 first_sum.1
  34.7 2.0 %collective-permute-start.12 = (bf16[8,16,256]{2,1,0:T(8,128)(2,1)S(1)}, bf16[8,16,256]{2,1,0:T(8,128)(2,1)S(1)}, u32[]{:S(2)}, u32[]{:S(2)}) collective-permute-start(bf16[8,16,256]{2,1,0:T(8,128)(2,1)S(1)} %get-tuple-element.82), channel_id=1, source_target_pairs={{0,232},{4,60},{8,224},{12,52},{16,248},{20,44},{24,240},{28,36},{... | collective-permute-start | bytes 196616 | tf_op jit(solution)/shard_map/ppermute | solution.py:334
  36.7 4.5 %collective-permute-start.13 = (bf16[8,16,256]{2,1,0:T(8,128)(2,1)S(1)}, bf16[8,16,256]{2,1,0:T(8,128)(2,1)S(1)}, u32[]{:S(2)}, u32[]{:S(2)}) collective-permute-start(bf16[8,16,256]{2,1,0:T(8,128)(2,1)S(1)} %get-tuple-element.83), channel_id=1, source_target_pairs={{0,8},{4,28},{8,0},{12,20},{16,24},{20,12},{24,16},{28,4},{32,40},... | collective-permute-start | bytes 196616 | tf_op jit(solution)/shard_map/ppermute | solution.py:334
  41.2 0.0 collective-permute-start.14
  41.2 0.0 collective-permute-done.7.refs_1_
  41.2 0.1 mp_share.1
  41.3 1.4 %collective-permute-start.8 = (bf16[2,256,256]{2,1,0:T(8,128)(2,1)S(1)}, bf16[2,256,256]{2,1,0:T(8,128)(2,1)S(1)}, u32[]{:S(2)}, u32[]{:S(2)}) collective-permute-start(bf16[2,256,256]{2,1,0:T(8,128)(2,1)S(1)} %get-tuple-element.71), channel_id=1, source_target_pairs={{0,3},{1,2},{2,1},{3,0},{4,5},{5,4},{6,7},{7,6},{8,11},{9,10},{10,... | collective-permute-start | bytes 786440 | tf_op jit(solution)/shard_map/ppermute | solution.py:334
  42.6 0.0 collective-permute-done.12.refs_1_
  42.6 0.8 %collective-permute-done.13.refs_2_ = bf16[8,16,256]{2,1,0:T(8,128)(2,1)S(1)} collective-permute-done((bf16[8,16,256]{2,1,0:T(8,128)(2,1)S(1)}, bf16[8,16,256]{2,1,0:T(8,128)(2,1)S(1)}, u32[]{:S(2)}, u32[]{:S(2)}) %collective-permute-start.13) | collective-permute-done | bytes 65568 | tf_op jit(solution)/shard_map/ppermute | solution.py:334
  43.4 3.2 %collective-permute-done.14.refs_3_ = bf16[8,16,256]{2,1,0:T(8,128)(2,1)S(1)} collective-permute-done((bf16[8,16,256]{2,1,0:T(8,128)(2,1)S(1)}, bf16[8,16,256]{2,1,0:T(8,128)(2,1)S(1)}, u32[]{:S(2)}, u32[]{:S(2)}) %collective-permute-start.14) | collective-permute-done | bytes 65568 | tf_op jit(solution)/shard_map/ppermute | solution.py:334
  46.7 2.0 %collective-permute-start.15 = (bf16[4,16,256]{2,1,0:T(8,128)(2,1)S(1)}, bf16[4,16,256]{2,1,0:T(8,128)(2,1)S(1)}, u32[]{:S(2)}, u32[]{:S(2)}) collective-permute-start(bf16[4,16,256]{2,1,0:T(8,128)(2,1)S(1)} %get-tuple-element.86), channel_id=1, source_target_pairs={{0,96},{4,164},{8,104},{12,172},{16,112},{20,180},{24,120},{28,188... | collective-permute-start | bytes 98312 | tf_op jit(solution)/shard_map/ppermute | solution.py:334
  48.7 0.3 collective-permute-done.8.got
  49.0 0.7 %mp_sum.1 = (bf16[256,256]{1,0:T(8,128)(2,1)}, bf16[256,256]{1,0:T(8,128)(2,1)}) custom-call(f32[2,256,256]{2,1,0:T(8,128)S(1)} %get-tuple-element.70.kept, bf16[2,256,256]{2,1,0:T(8,128)(2,1)S(1)} %collective-permute-done.8.got), custom_call_target="tpu_custom_call" | custom-call | bytes 1000000 | tf_op jit(solution)/shard_map/mp_sum/pallas_call | solution.py:319
  49.7 2.8 %collective-permute-done.15.got = bf16[4,16,256]{2,1,0:T(8,128)(2,1)S(1)} collective-permute-done((bf16[4,16,256]{2,1,0:T(8,128)(2,1)S(1)}, bf16[4,16,256]{2,1,0:T(8,128)(2,1)S(1)}, u32[]{:S(2)}, u32[]{:S(2)}) %collective-permute-start.15) | collective-permute-done | bytes 32800 | tf_op jit(solution)/shard_map/ppermute | solution.py:334
  52.5 0.6 %last_sum.1 = f32[4,16,256]{2,1,0:T(8,128)} custom-call(bf16[256,256]{1,0:T(8,128)(2,1)} %get-tuple-element.42.after, f32[4,16,256]{2,1,0:T(8,128)S(1)} %get-tuple-element.85.kept, bf16[4,16,256]{2,1,0:T(8,128)(2,1)S(1)} %collective-permute-done.15.got), custom_call_target="tpu_custom_call" | custom-call | bytes 1000000 | tf_op jit(solution)/shard_map/last_sum/pallas_call | solution.py:319
  (1 shorter events, 0.0 us)
Async XLA Ops:
  0.6 4.9 %collective-permute-start.1 = (bf16[256,1024]{1,0:T(8,128)(2,1)}, bf16[256,1024]{1,0:T(8,128)(2,1)S(1)}, u32[]{:S(2)}, u32[]{:S(2)}) collective-permute-start(bf16[256,1024]{1,0:T(8,128)(2,1)} %act.1), channel_id=1, source_target_pairs={{0,4},{4,0},{8,12},{12,8},{16,20},{20,16},{24,28},{28,24},{32,36},... | collective-permute-start | bytes 1572872 | tf_op jit(solution)/shard_map/ppermute | solution.py:334
  0.7 12.3 %collective-permute-start = (bf16[256,1024]{1,0:T(8,128)(2,1)}, bf16[256,1024]{1,0:T(8,128)(2,1)S(1)}, u32[]{:S(2)}, u32[]{:S(2)}) collective-permute-start(bf16[256,1024]{1,0:T(8,128)(2,1)} %act.1), channel_id=1, source_target_pairs={{0,1},{1,0},{2,3},{3,2},{4,8},{5,9},{6,10},{7,11},{8,4},{9,5},{10,... | collective-permute-start | bytes 1572872 | tf_op jit(solution)/shard_map/ppermute | solution.py:334
  1.6 14.4 %collective-permute-start.2 = (bf16[256,256]{1,0:T(8,128)(2,1)}, bf16[256,256]{1,0:T(8,128)(2,1)S(1)}, u32[]{:S(2)}, u32[]{:S(2)}) collective-permute-start(bf16[256,256]{1,0:T(8,128)(2,1)} %cot.1), channel_id=1, source_target_pairs={{0,2},{1,3},{2,0},{3,1},{4,6},{5,7},{6,4},{7,5},{8,10},{9,11},{10,... | collective-permute-start | bytes 393224 | tf_op jit(solution)/shard_map/ppermute | solution.py:334
  4.5 11.6 %collective-permute-start.4 = (bf16[256,256]{1,0:T(8,128)(2,1)}, bf16[256,256]{1,0:T(8,128)(2,1)S(1)}, u32[]{:S(2)}, u32[]{:S(2)}) collective-permute-start(bf16[256,256]{1,0:T(8,128)(2,1)} %cot.1), channel_id=1, source_target_pairs={{0,3},{1,2},{2,1},{3,0},{4,7},{5,6},{6,5},{7,4},{8,11},{9,10},{10,... | collective-permute-start | bytes 393224 | tf_op jit(solution)/shard_map/ppermute | solution.py:334
  5.5 10.6 %collective-permute-start.3 = (bf16[256,256]{1,0:T(8,128)(2,1)}, bf16[256,256]{1,0:T(8,128)(2,1)S(1)}, u32[]{:S(2)}, u32[]{:S(2)}) collective-permute-start(bf16[256,256]{1,0:T(8,128)(2,1)} %cot.1), channel_id=1, source_target_pairs={{0,1},{1,0},{2,3},{3,2},{4,5},{5,4},{6,7},{7,6},{8,9},{9,8},{10,11... | collective-permute-start | bytes 393224 | tf_op jit(solution)/shard_map/ppermute | solution.py:334
  19.7 3.1 %collective-permute-start.5 = (bf16[160,16,256]{2,1,0:T(8,128)(2,1)S(1)}, bf16[160,16,256]{2,1,0:T(8,128)(2,1)S(1)}, u32[]{:S(2)}, u32[]{:S(2)}) collective-permute-start(bf16[160,16,256]{2,1,0:T(8,128)(2,1)S(1)} %get-tuple-element.65), channel_id=1, source_target_pairs={{0,4},{4,0},{8,12},{12,8},{16,20},{20,16},{24,28},{28,24},{32,36},... | collective-permute-start | bytes 3932168 | tf_op jit(solution)/shard_map/ppermute | solution.py:334
  19.8 8.2 %collective-permute-start.6 = (bf16[2,256,256]{2,1,0:T(8,128)(2,1)S(1)}, bf16[2,256,256]{2,1,0:T(8,128)(2,1)S(1)}, u32[]{:S(2)}, u32[]{:S(2)}) collective-permute-start(bf16[2,256,256]{2,1,0:T(8,128)(2,1)S(1)} %get-tuple-element.66), channel_id=1, source_target_pairs={{0,1},{1,0},{2,3},{3,2},{4,8},{5,9},{6,10},{7,11},{8,4},{9,5},{10,... | collective-permute-start | bytes 786440 | tf_op jit(solution)/shard_map/ppermute | solution.py:334
  23.1 8.9 %collective-permute-start.9 = (bf16[32,16,256]{2,1,0:T(8,128)(2,1)S(1)}, bf16[32,16,256]{2,1,0:T(8,128)(2,1)S(1)}, u32[]{:S(2)}, u32[]{:S(2)}) collective-permute-start(bf16[32,16,256]{2,1,0:T(8,128)(2,1)S(1)} %get-tuple-element.78), channel_id=1, source_target_pairs={{0,56},{4,236},{8,48},{12,228},{16,40},{20,252},{24,32},{28,244},{... | collective-permute-start | bytes 786440 | tf_op jit(solution)/shard_map/ppermute | solution.py:334
  25.0 9.6 %collective-permute-start.10 = (bf16[32,16,256]{2,1,0:T(8,128)(2,1)S(1)}, bf16[32,16,256]{2,1,0:T(8,128)(2,1)S(1)}, u32[]{:S(2)}, u32[]{:S(2)}) collective-permute-start(bf16[32,16,256]{2,1,0:T(8,128)(2,1)S(1)} %get-tuple-element.79), channel_id=1, source_target_pairs={{0,24},{4,12},{8,16},{12,4},{16,8},{20,28},{24,0},{28,20},{32,56},... | collective-permute-start | bytes 786440 | tf_op jit(solution)/shard_map/ppermute | solution.py:334
  25.7 8.9 %collective-permute-start.11 = (bf16[32,16,256]{2,1,0:T(8,128)(2,1)S(1)}, bf16[32,16,256]{2,1,0:T(8,128)(2,1)S(1)}, u32[]{:S(2)}, u32[]{:S(2)}) collective-permute-start(bf16[32,16,256]{2,1,0:T(8,128)(2,1)S(1)} %get-tuple-element.80), channel_id=1, source_target_pairs={{0,32},{4,228},{8,40},{12,236},{16,48},{20,244},{24,56},{28,252},{... | collective-permute-start | bytes 786440 | tf_op jit(solution)/shard_map/ppermute | solution.py:334
  28.8 12.4 %collective-permute-start.7 = (bf16[4,256,256]{2,1,0:T(8,128)(2,1)S(1)}, bf16[4,256,256]{2,1,0:T(8,128)(2,1)S(1)}, u32[]{:S(2)}, u32[]{:S(2)}) collective-permute-start(bf16[4,256,256]{2,1,0:T(8,128)(2,1)S(1)} %get-tuple-element.69), channel_id=1, source_target_pairs={{0,1},{1,0},{2,3},{3,2},{4,7},{5,6},{6,5},{7,4},{8,9},{9,8},{10,11... | collective-permute-start | bytes 1572872 | tf_op jit(solution)/shard_map/ppermute | solution.py:334
  34.7 7.9 %collective-permute-start.12 = (bf16[8,16,256]{2,1,0:T(8,128)(2,1)S(1)}, bf16[8,16,256]{2,1,0:T(8,128)(2,1)S(1)}, u32[]{:S(2)}, u32[]{:S(2)}) collective-permute-start(bf16[8,16,256]{2,1,0:T(8,128)(2,1)S(1)} %get-tuple-element.82), channel_id=1, source_target_pairs={{0,232},{4,60},{8,224},{12,52},{16,248},{20,44},{24,240},{28,36},{... | collective-permute-start | bytes 196616 | tf_op jit(solution)/shard_map/ppermute | solution.py:334
  36.7 6.7 %collective-permute-start.13 = (bf16[8,16,256]{2,1,0:T(8,128)(2,1)S(1)}, bf16[8,16,256]{2,1,0:T(8,128)(2,1)S(1)}, u32[]{:S(2)}, u32[]{:S(2)}) collective-permute-start(bf16[8,16,256]{2,1,0:T(8,128)(2,1)S(1)} %get-tuple-element.83), channel_id=1, source_target_pairs={{0,8},{4,28},{8,0},{12,20},{16,24},{20,12},{24,16},{28,4},{32,40},... | collective-permute-start | bytes 196616 | tf_op jit(solution)/shard_map/ppermute | solution.py:334
  41.2 5.5 %collective-permute-start.14 = (bf16[8,16,256]{2,1,0:T(8,128)(2,1)S(1)}, bf16[8,16,256]{2,1,0:T(8,128)(2,1)S(1)}, u32[]{:S(2)}, u32[]{:S(2)}) collective-permute-start(bf16[8,16,256]{2,1,0:T(8,128)(2,1)S(1)} %get-tuple-element.84), channel_id=1, source_target_pairs={{0,224},{4,36},{8,232},{12,44},{16,240},{20,52},{24,248},{28,60},{... | collective-permute-start | bytes 196616 | tf_op jit(solution)/shard_map/ppermute | solution.py:334
  41.3 7.7 %collective-permute-start.8 = (bf16[2,256,256]{2,1,0:T(8,128)(2,1)S(1)}, bf16[2,256,256]{2,1,0:T(8,128)(2,1)S(1)}, u32[]{:S(2)}, u32[]{:S(2)}) collective-permute-start(bf16[2,256,256]{2,1,0:T(8,128)(2,1)S(1)} %get-tuple-element.71), channel_id=1, source_target_pairs={{0,3},{1,2},{2,1},{3,0},{4,5},{5,4},{6,7},{7,6},{8,11},{9,10},{10,... | collective-permute-start | bytes 786440 | tf_op jit(solution)/shard_map/ppermute | solution.py:334
  46.7 5.8 %collective-permute-start.15 = (bf16[4,16,256]{2,1,0:T(8,128)(2,1)S(1)}, bf16[4,16,256]{2,1,0:T(8,128)(2,1)S(1)}, u32[]{:S(2)}, u32[]{:S(2)}) collective-permute-start(bf16[4,16,256]{2,1,0:T(8,128)(2,1)S(1)} %get-tuple-element.86), channel_id=1, source_target_pairs={{0,96},{4,164},{8,104},{12,172},{16,112},{20,180},{24,120},{28,188... | collective-permute-start | bytes 98312 | tf_op jit(solution)/shard_map/ppermute | solution.py:334

commit v15 on v14

--- a/solution.py
+++ b/solution.py
@@ -178,11 +178,11 @@
 
 
 def forward_kernel(
-    a_far, wk, wv, query, keys_in, values_in, exps, peaks, bias,
-    keys, values, probs_out, att_out, far_t,
+    a_far, wk, wv, wo, query, keys_in, values_in, exps, peaks, bias,
+    keys, values, probs_out, att_out, far_t, out_keep, out_send,
     probs_t,
 ):
-    core = places()[0]
+    core, _, _, x = places()
     keys[ROW:, :] = keys_in[...]
     values[ROW:, :] = values_in[...]
     keys[:ROW, :] = mm(a_far[...], wk[...]).astype(BF)
@@ -203,7 +203,12 @@
         probs_out[ROW:, part] = other_probs
         probs_t[part, :ROW] = far_probs.T
         probs_t[part, ROW:] = other_probs.T
-    att_out[...] = pick_heads(mm(probs_t[...], values[...]))
+    att = pick_heads(mm(probs_t[...], values[...]))
+    att_out[...] = att
+    first, second = (mp_partner(core, x, step) for step in range(2))
+    for out, targets in ((out_keep, (x, second)), (out_send, (first, x ^ 2))):
+        for place, target in enumerate(targets):
+            out[place] = mm(att, columns(wo, target)).astype(out.dtype)
     store_halves(far_t, a_far[...].T, 0, core)
 
 
@@ -280,7 +285,7 @@
         out[...] = total.astype(out.dtype)
 
 
-def input_kernel(att, gq, own, near, far, wq, wk, wv, wo, keep, send):
+def input_kernel(gq, own, near, far, wq, wk, wv, out_kept, out_got, keep, send):
     core, _, _, x = places()
     grads = []
     for part in range(2):
@@ -288,20 +293,26 @@
         grads.append((own[part] + from_near.astype(F32) + far[part].astype(F32)).astype(BF))
     grad_key, grad_value = grads
     first, second = (mp_partner(core, x, step) for step in range(2))
-    for out, targets in ((keep, (x, second)), (send, (first, x ^ 2))):
+    for out, targets in ((keep, (x, first)), (send, (second, x ^ 2))):
         for place, target in enumerate(targets):
             block = pl.ds(pl.multiple_of(target * WIDTH, WIDTH), WIDTH)
-            out[2 * place] = mm(att[...], wo[:, block]).astype(out.dtype)
-            out[2 * place + 1] = (
+            out[place] = (
                 mm(gq[...], wq[block, :], NT)
                 + mm(grad_key, wk[block, :], NT)
                 + mm(grad_value, wv[block, :], NT)
             ).astype(out.dtype)
-
-
-def mp_sum_kernel(kept, got, out, grad):
-    for part, ref in ((0, out), (1, grad)):
-        ref[...] = (kept[part] + got[part].astype(F32)).astype(BF)
+    for place, out in ((0, keep), (1, send)):
+        out[2] = (out_kept[place] + out_got[place].astype(F32)).astype(out.dtype)
+
+
+def mp_share_kernel(kept, got, out, keep, send):
+    out[...] = (kept[2] + got[2].astype(F32)).astype(BF)
+    keep[...] = kept[0] + got[0].astype(F32)
+    send[...] = (kept[1] + got[1].astype(F32)).astype(BF)
+
+
+def mp_sum_kernel(kept, got, grad):
+    grad[...] = (kept[...] + got[...].astype(F32)).astype(BF)
 
 
 def last_sum_kernel(after, kept, got, dw):
@@ -313,9 +324,10 @@
 
 
 def call(
-    kernel, name, outs, arrays, apart=(), scratch=(), limit=16, flops=0, moved=1_000_000, keep=True
+    kernel, name, outs, arrays, apart=(), scratch=(), limit=16, flops=0, moved=1_000_000, apart_outs=0
 ):
-    kept = [pltpu.VMEM(shape, dtype) if keep else jax.ShapeDtypeStruct(shape, dtype) for shape, dtype in outs]
+    kept = [jax.ShapeDtypeStruct(shape, dtype) for shape, dtype in outs[:apart_outs]]
+    kept += [pltpu.VMEM(shape, dtype) for shape, dtype in outs[apart_outs:]]
     return pl.pallas_call(
         kernel,
         out_shape=tuple(kept),
@@ -385,16 +397,19 @@
     )
 
     block = (16, WIDTH)
-    keys, values, probs, att, far_t = call(
+    pair = (2, ROW, WIDTH)
+    keys, values, probs, att, far_t, out_keep, out_send = call(
         forward_kernel,
         "forward",
-        [((KEYS, WIDTH), BF)] * 2 + [((KEYS, HEADS * ROW), BF), (square, BF), ((D, ROW), BF)],
-        [act_far, wk, wv, query, keys, values, exps, peaks, bias],
+        [((KEYS, WIDTH), BF)] * 2
+        + [((KEYS, HEADS * ROW), BF), (square, BF), ((D, ROW), BF), (pair, F32), (pair, BF)],
+        [act_far, wk, wv, wo, query, keys, values, exps, peaks, bias],
         scratch=[pltpu.VMEM((HEADS * ROW, KEYS), BF)],
         limit=20,
         flops=2_000_000_000,
         moved=6_000_000,
     )
+    out_got = over_mp(out_send, 0)
     gq, far, own, grad_key, grad_value, cot_t, dw_send = call(
         backward_kernel,
         "backward",
@@ -454,19 +469,25 @@
     mp_keep, mp_send = call(
         input_kernel,
         "input_grad",
-        [((4, ROW, WIDTH), F32), ((4, ROW, WIDTH), BF)],
-        [att, gq, own, from_core, grad_far, wq, wk, wv, wo],
+        [((3, ROW, WIDTH), F32), ((3, ROW, WIDTH), BF)],
+        [gq, own, from_core, grad_far, wq, wk, wv, out_keep, out_got],
         flops=540_000_000,
         moved=4_000_000,
     )
-    mp_keep, mp_send = share("mp_share", [mp_keep, over_mp(mp_send, 0)], 2, F32)
+    output, mp_keep, mp_send = call(
+        mp_share_kernel,
+        "mp_share",
+        [(square, BF), (square, F32), (square, BF)],
+        [mp_keep, over_mp(mp_send, 1)],
+        apart_outs=1,
+    )
     parts = four_ways(share("first_sum", parts, 4, F32, FIRST_FLOPS), 1)
     keep, send = share("second_sum", parts, 2, F32, SECOND_FLOPS)
     got = over_chips(send, None, 2)
-    output, grad_input = call(
-        mp_sum_kernel, "mp_sum", [(square, BF)] * 2, [mp_keep, over_mp(mp_send, 1)], keep=False
-    )
-    (dw,) = call(last_sum_kernel, "last_sum", [((4,) + block, F32)], [keep, got], apart=(output,), keep=False)
+    (grad_input,) = call(
+        mp_sum_kernel, "mp_sum", [(square, BF)], [mp_keep, over_mp(mp_send, 0)], apart_outs=1
+    )
+    (dw,) = call(last_sum_kernel, "last_sum", [((4,) + block, F32)], [keep, got], apart=(grad_input,), apart_outs=1)
     return output, grad_input, dw
 
 

time: 53.2 us -> 54.7 us (1.028); the launches traced: 53.1 us -> 53.9 us
  waiting for transfers between devices: 18.8 us -> 14.9 us
  starting transfers between devices: 21 us -> 24.8 us
  Pallas kernels: 12.5 us -> 13.5 us
    ppermute x16 -> x17, waiting for transfers between devices: 18.8 us -> 14.9 us  [move(): lax.ppermute(value, axis, [(i, target(i)) for i in range(count) if 0 <= t...]
    ppermute x16 -> x17, starting transfers between devices: 21 us -> 24.8 us  [move(): lax.ppermute(value, axis, [(i, target(i)) for i in range(count) if 0 <= t...]
    pallas_call x11, Pallas kernels: 12.5 us -> 13.5 us  [call(): pl.pallas_call(kernel, out_shape=tuple(kept), in_specs=[pl.BlockSpec(memo...]
  transfers between devices with their start and end apart: 16 -> 17, of which waited for: 9 -> 8; matrix products, arithmetic and copies ran while one was open for 0% -> 0% of each run, Pallas kernels for 16% -> 17%
where the time goes in v15:
time: 54.7 us; the launch traced here: 53.9 us
  starting transfers between devices  24.8 us (45%)
  waiting for transfers between devices  14.9 us (27%)
  Pallas kernels  13.5 us (25%)
  between operations  0.71 us (1%)
    ppermute x17, starting transfers between devices, move(): lax.ppermute(value, axis, [(i, target(i)) for i in range(count) if 0 <= t...  24.8 us
    ppermute x17, waiting for transfers between devices, move(): lax.ppermute(value, axis, [(i, target(i)) for i in range(count) if 0 <= t...  14.9 us
    pallas_call x11, Pallas kernels, call(): pl.pallas_call(kernel, out_shape=tuple(kept), in_specs=[pl.BlockSpec(memo...  13.5 us
  transfers between devices with their start and end apart: 17, of which 8 were waited for; matrix products, arithmetic and copies ran while one was open for 0% of the time, Pallas kernels for 17%

profile of v15, /device:TPU:6, one launch (start us, length us, event | category | flops | bytes accessed | tf_op | source)
XLA Modules:
  0.0 53.9 jit_solution(17296606576660603882)
XLA Ops:
  0.6 0.1 collective-permute-start.1
  0.7 0.9 %collective-permute-start = (bf16[256,1024]{1,0:T(8,128)(2,1)}, bf16[256,1024]{1,0:T(8,128)(2,1)S(1)}, u32[]{:S(2)}, u32[]{:S(2)}) collective-permute-start(bf16[256,1024]{1,0:T(8,128)(2,1)} %act.1), channel_id=1, source_target_pairs={{0,1},{1,0},{2,3},{3,2},{4,8},{5,9},{6,10},{7,11},{8,4},{9,5},{10,... | collective-permute-start | bytes 1572872 | tf_op jit(solution)/shard_map/ppermute | solution.py:346
  1.6 2.8 %collective-permute-start.2 = (bf16[256,256]{1,0:T(8,128)(2,1)}, bf16[256,256]{1,0:T(8,128)(2,1)S(1)}, u32[]{:S(2)}, u32[]{:S(2)}) collective-permute-start(bf16[256,256]{1,0:T(8,128)(2,1)} %cot.1), channel_id=1, source_target_pairs={{0,2},{1,3},{2,0},{3,1},{4,6},{5,7},{6,4},{7,5},{8,10},{9,11},{10,... | collective-permute-start | bytes 393224 | tf_op jit(solution)/shard_map/ppermute | solution.py:346
  4.5 1.0 %collective-permute-start.4 = (bf16[256,256]{1,0:T(8,128)(2,1)}, bf16[256,256]{1,0:T(8,128)(2,1)S(1)}, u32[]{:S(2)}, u32[]{:S(2)}) collective-permute-start(bf16[256,256]{1,0:T(8,128)(2,1)} %cot.1), channel_id=1, source_target_pairs={{0,3},{1,2},{2,1},{3,0},{4,7},{5,6},{6,5},{7,4},{8,11},{9,10},{10,... | collective-permute-start | bytes 393224 | tf_op jit(solution)/shard_map/ppermute | solution.py:346
  5.5 0.0 collective-permute-start.3
  5.5 0.0 collective-permute-done.1.a_near
  5.5 3.9 %own_part.1 = (bf16[1024,256]{1,0:T(8,128)(2,1)S(1)}, bf16[1024,256]{1,0:T(8,128)(2,1)S(1)}, bf16[1024,256]{1,0:T(8,128)(2,1)S(1)}, bf16[256,1024]{1,0:T(8,128)(...) custom-call(bf16[256,1024]{1,0:T(8,128)(2,1)} %act.1, ...), custom_call_target="tpu_custom_call" | custom-call | flops 600000000 | bytes 6000000 | tf_op jit(solution)/shard_map/own_part/pallas_call | solution.py:331
  9.5 3.5 %collective-permute-done.a_far = bf16[256,1024]{1,0:T(8,128)(2,1)S(1)} collective-permute-done((bf16[256,1024]{1,0:T(8,128)(2,1)}, bf16[256,1024]{1,0:T(8,128)(2,1)S(1)}, u32[]{:S(2)}, u32[]{:S(2)}) %collective-permute-start) | collective-permute-done | bytes 524320 | tf_op jit(solution)/shard_map/ppermute | solution.py:346
  13.0 2.0 %forward.1 = (bf16[768,256]{1,0:T(8,128)(2,1)S(1)}, bf16[768,256]{1,0:T(8,128)(2,1)S(1)}, bf16[768,1024]{1,0:T(8,128)(2,1)S(1)}, bf16[256,256]{1,0:T(8,128)(2,1)...) custom-call(bf16[256,1024]{1,0:T(8,128)(2,1)S(1)} %collective-permute-done.a_far, ...), custom_call_target="tpu_custom_call" | custom-call | flops 2000000000 | bytes 6000000 | tf_op jit(solution)/shard_map/forward/pallas_call | solution.py:331
  15.1 1.0 %collective-permute-done.2.c2 = bf16[256,256]{1,0:T(8,128)(2,1)S(1)} collective-permute-done((bf16[256,256]{1,0:T(8,128)(2,1)}, bf16[256,256]{1,0:T(8,128)(2,1)S(1)}, u32[]{:S(2)}, u32[]{:S(2)}) %collective-permute-start.2) | collective-permute-done | bytes 131104 | tf_op jit(solution)/shard_map/ppermute | solution.py:346
  16.1 0.0 collective-permute-done.4.c3
  16.1 0.0 collective-permute-done.3.c1
  16.1 3.6 %backward.1 = (bf16[256,256]{1,0:T(8,128)(2,1)S(1)}, bf16[2,256,256]{2,1,0:T(8,128)(2,1)S(1)}, f32[2,256,256]{2,1,0:T(8,128)S(1)}, bf16[768,256]{1,0:T(8,128)(2,...) custom-call(bf16[768,256]{1,0:T(8,128)(2,1)S(1)} %get-tuple-element.55.keys, ...), custom_call_target="tpu_custom_call" | custom-call | flops 2000000000 | bytes 8000000 | tf_op jit(solution)/shard_map/backward/pallas_call | solution.py:331
  19.7 0.1 collective-permute-start.5
  19.8 0.7 %collective-permute-start.6 = (bf16[2,256,256]{2,1,0:T(8,128)(2,1)S(1)}, bf16[2,256,256]{2,1,0:T(8,128)(2,1)S(1)}, u32[]{:S(2)}, u32[]{:S(2)}) collective-permute-start(bf16[2,256,256]{2,1,0:T(8,128)(2,1)S(1)} %get-tuple-element.67), channel_id=1, source_target_pairs={{0,1},{1,0},{2,3},{3,2},{4,8},{5,9},{6,10},{7,11},{8,4},{9,5},{10,... | collective-permute-start | bytes 786440 | tf_op jit(solution)/shard_map/ppermute | solution.py:346
  20.5 1.4 %collective-permute-start.7 = (bf16[2,256,256]{2,1,0:T(8,128)(2,1)S(1)}, bf16[2,256,256]{2,1,0:T(8,128)(2,1)S(1)}, u32[]{:S(2)}, u32[]{:S(2)}) collective-permute-start(bf16[2,256,256]{2,1,0:T(8,128)(2,1)S(1)} %get-tuple-element.70), channel_id=1, source_target_pairs={{0,1},{1,0},{2,3},{3,2},{4,7},{5,6},{6,5},{7,4},{8,9},{9,8},{10,11... | collective-permute-start | bytes 786440 | tf_op jit(solution)/shard_map/ppermute | solution.py:346
  21.9 0.8 %keep_terms.1.refs_0_ = bf16[128,16,256]{2,1,0:T(8,128)(2,1)S(1)} custom-call(bf16[1024,256]{1,0:T(8,128)(2,1)S(1)} %get-tuple-element.61.act_t, bf16[1024,256]{1,0:T(8,128)(2,1)S(1)} %get-tuple-element.59.far_t, bf16[1024,256]{1,0:T(8,128)(2,1)S(1)} %get-tuple-element.60.near_t, bf16[1024,256]{1,0:T(8,128)(2,1)S(1)} %get-tuple-element.76.cot_t, ...), custom_call_target="tpu_custom_call" | custom-call | flops 1000000000 | bytes 4000000 | tf_op jit(solution)/shard_map/keep_terms/pallas_call | solution.py:331
  22.8 0.1 collective-permute-done.5.near.refs_1_
  22.8 0.2 core_sum.1
  23.1 2.3 %collective-permute-start.10 = (bf16[32,16,256]{2,1,0:T(8,128)(2,1)S(1)}, bf16[32,16,256]{2,1,0:T(8,128)(2,1)S(1)}, u32[]{:S(2)}, u32[]{:S(2)}) collective-permute-start(bf16[32,16,256]{2,1,0:T(8,128)(2,1)S(1)} %get-tuple-element.80), channel_id=1, source_target_pairs={{0,56},{4,236},{8,48},{12,228},{16,40},{20,252},{24,32},{28,244},{... | collective-permute-start | bytes 786440 | tf_op jit(solution)/shard_map/ppermute | solution.py:346
  25.3 1.5 %collective-permute-start.11 = (bf16[32,16,256]{2,1,0:T(8,128)(2,1)S(1)}, bf16[32,16,256]{2,1,0:T(8,128)(2,1)S(1)}, u32[]{:S(2)}, u32[]{:S(2)}) collective-permute-start(bf16[32,16,256]{2,1,0:T(8,128)(2,1)S(1)} %get-tuple-element.81), channel_id=1, source_target_pairs={{0,24},{4,12},{8,16},{12,4},{16,8},{20,28},{24,0},{28,20},{32,56},... | collective-permute-start | bytes 786440 | tf_op jit(solution)/shard_map/ppermute | solution.py:346
  26.8 1.1 %collective-permute-start.12 = (bf16[32,16,256]{2,1,0:T(8,128)(2,1)S(1)}, bf16[32,16,256]{2,1,0:T(8,128)(2,1)S(1)}, u32[]{:S(2)}, u32[]{:S(2)}) collective-permute-start(bf16[32,16,256]{2,1,0:T(8,128)(2,1)S(1)} %get-tuple-element.82), channel_id=1, source_target_pairs={{0,32},{4,228},{8,40},{12,236},{16,48},{20,244},{24,56},{28,252},{... | collective-permute-start | bytes 786440 | tf_op jit(solution)/shard_map/ppermute | solution.py:346
  27.9 0.0 collective-permute-done.6.far
  27.9 1.2 %collective-permute-done.7.out_got = bf16[2,256,256]{2,1,0:T(8,128)(2,1)S(1)} collective-permute-done((bf16[2,256,256]{2,1,0:T(8,128)(2,1)S(1)}, bf16[2,256,256]{2,1,0:T(8,128)(2,1)S(1)}, u32[]{:S(2)}, u32[]{:S(2)}) %collective-permute-start.7) | collective-permute-done | bytes 262176 | tf_op jit(solution)/shard_map/ppermute | solution.py:346
  29.1 0.6 %input_grad.1 = (f32[3,256,256]{2,1,0:T(8,128)S(1)}, bf16[3,256,256]{2,1,0:T(8,128)(2,1)S(1)}) custom-call(bf16[256,256]{1,0:T(8,128)(2,1)S(1)} %get-tuple-element.64.gq, f32[2,256,256]{2,1,0:T(8,128)S(1)} %get-tuple-element.65.own, bf16[160,16,256]{2,1,0:T(8,128)(2,1)S(1)} %collective-permute-done.5.near.refs_1_, ...), custom_call_target="tpu_custom_call" | custom-call | flops 540000000 | bytes 4000000 | tf_op jit(solution)/shard_map/input_grad/pallas_call | solution.py:331
  29.7 2.1 %collective-permute-start.8 = (bf16[3,256,256]{2,1,0:T(8,128)(2,1)S(1)}, bf16[3,256,256]{2,1,0:T(8,128)(2,1)S(1)}, u32[]{:S(2)}, u32[]{:S(2)}) collective-permute-start(bf16[3,256,256]{2,1,0:T(8,128)(2,1)S(1)} %get-tuple-element.72), channel_id=1, source_target_pairs={{0,3},{1,2},{2,1},{3,0},{4,5},{5,4},{6,7},{7,6},{8,11},{9,10},{10,... | collective-permute-start | bytes 1179656 | tf_op jit(solution)/shard_map/ppermute | solution.py:346
  31.8 0.0 collective-permute-done.10.refs_1_
  31.8 2.7 %collective-permute-done.11.refs_2_ = bf16[32,16,256]{2,1,0:T(8,128)(2,1)S(1)} collective-permute-done((bf16[32,16,256]{2,1,0:T(8,128)(2,1)S(1)}, bf16[32,16,256]{2,1,0:T(8,128)(2,1)S(1)}, u32[]{:S(2)}, u32[]{:S(2)}) %collective-permute-start.11) | collective-permute-done | bytes 262176 | tf_op jit(solution)/shard_map/ppermute | solution.py:346
  34.5 0.0 collective-permute-done.12.refs_3_
  34.5 0.1 first_sum.1
  34.6 3.5 %collective-permute-start.13 = (bf16[8,16,256]{2,1,0:T(8,128)(2,1)S(1)}, bf16[8,16,256]{2,1,0:T(8,128)(2,1)S(1)}, u32[]{:S(2)}, u32[]{:S(2)}) collective-permute-start(bf16[8,16,256]{2,1,0:T(8,128)(2,1)S(1)} %get-tuple-element.84), channel_id=1, source_target_pairs={{0,232},{4,60},{8,224},{12,52},{16,248},{20,44},{24,240},{28,36},{... | collective-permute-start | bytes 196616 | tf_op jit(solution)/shard_map/ppermute | solution.py:346
  38.1 3.9 %collective-permute-start.14 = (bf16[8,16,256]{2,1,0:T(8,128)(2,1)S(1)}, bf16[8,16,256]{2,1,0:T(8,128)(2,1)S(1)}, u32[]{:S(2)}, u32[]{:S(2)}) collective-permute-start(bf16[8,16,256]{2,1,0:T(8,128)(2,1)S(1)} %get-tuple-element.85), channel_id=1, source_target_pairs={{0,8},{4,28},{8,0},{12,20},{16,24},{20,12},{24,16},{28,4},{32,40},... | collective-permute-start | bytes 196616 | tf_op jit(solution)/shard_map/ppermute | solution.py:346
  42.0 0.0 collective-permute-start.15
  42.0 0.0 collective-permute-done.8.got
  42.0 0.7 %mp_share.1 = (bf16[256,256]{1,0:T(8,128)(2,1)}, f32[256,256]{1,0:T(8,128)S(1)}, bf16[256,256]{1,0:T(8,128)(2,1)S(1)}) custom-call(f32[3,256,256]{2,1,0:T(8,128)S(1)} %get-tuple-element.71.kept, bf16[3,256,256]{2,1,0:T(8,128)(2,1)S(1)} %collective-permute-done.8.got), custom_call_target="tpu_custom_call" | custom-call | bytes 1000000 | tf_op jit(solution)/shard_map/mp_share/pallas_call | solution.py:331
  42.7 1.2 %collective-permute-start.9 = (bf16[256,256]{1,0:T(8,128)(2,1)S(1)}, bf16[256,256]{1,0:T(8,128)(2,1)S(1)}, u32[]{:S(2)}, u32[]{:S(2)}) collective-permute-start(bf16[256,256]{1,0:T(8,128)(2,1)S(1)} %get-tuple-element.75), channel_id=1, source_target_pairs={{0,1},{1,0},{2,3},{3,2},{4,7},{5,6},{6,5},{7,4},{8,9},{9,8},{10,11... | collective-permute-start | bytes 393224 | tf_op jit(solution)/shard_map/ppermute | solution.py:346
  43.9 0.0 collective-permute-done.13.refs_1_
  43.9 0.3 collective-permute-done.14.refs_2_
  44.2 3.2 %collective-permute-done.15.refs_3_ = bf16[8,16,256]{2,1,0:T(8,128)(2,1)S(1)} collective-permute-done((bf16[8,16,256]{2,1,0:T(8,128)(2,1)S(1)}, bf16[8,16,256]{2,1,0:T(8,128)(2,1)S(1)}, u32[]{:S(2)}, u32[]{:S(2)}) %collective-permute-start.15) | collective-permute-done | bytes 65568 | tf_op jit(solution)/shard_map/ppermute | solution.py:346
  47.5 2.3 %collective-permute-start.16 = (bf16[4,16,256]{2,1,0:T(8,128)(2,1)S(1)}, bf16[4,16,256]{2,1,0:T(8,128)(2,1)S(1)}, u32[]{:S(2)}, u32[]{:S(2)}) collective-permute-start(bf16[4,16,256]{2,1,0:T(8,128)(2,1)S(1)} %get-tuple-element.88), channel_id=1, source_target_pairs={{0,96},{4,164},{8,104},{12,172},{16,112},{20,180},{24,120},{28,188... | collective-permute-start | bytes 98312 | tf_op jit(solution)/shard_map/ppermute | solution.py:346
  49.8 0.0 collective-permute-done.9.got
  49.8 0.7 %mp_sum.1.after = bf16[256,256]{1,0:T(8,128)(2,1)} custom-call(f32[256,256]{1,0:T(8,128)S(1)} %get-tuple-element.74.kept, bf16[256,256]{1,0:T(8,128)(2,1)S(1)} %collective-permute-done.9.got), custom_call_target="tpu_custom_call" | custom-call | bytes 1000000 | tf_op jit(solution)/shard_map/mp_sum/pallas_call | solution.py:331
  50.5 2.8 %collective-permute-done.16.got = bf16[4,16,256]{2,1,0:T(8,128)(2,1)S(1)} collective-permute-done((bf16[4,16,256]{2,1,0:T(8,128)(2,1)S(1)}, bf16[4,16,256]{2,1,0:T(8,128)(2,1)S(1)}, u32[]{:S(2)}, u32[]{:S(2)}) %collective-permute-start.16) | collective-permute-done | bytes 32800 | tf_op jit(solution)/shard_map/ppermute | solution.py:346
  53.3 0.6 %last_sum.1 = f32[4,16,256]{2,1,0:T(8,128)} custom-call(bf16[256,256]{1,0:T(8,128)(2,1)} %mp_sum.1.after, f32[4,16,256]{2,1,0:T(8,128)S(1)} %get-tuple-element.87.kept, bf16[4,16,256]{2,1,0:T(8,128)(2,1)S(1)} %collective-permute-done.16.got), custom_call_target="tpu_custom_call" | custom-call | bytes 1000000 | tf_op jit(solution)/shard_map/last_sum/pallas_call | solution.py:331
  (1 shorter events, 0.0 us)
Async XLA Ops:
  0.6 4.9 %collective-permute-start.1 = (bf16[256,1024]{1,0:T(8,128)(2,1)}, bf16[256,1024]{1,0:T(8,128)(2,1)S(1)}, u32[]{:S(2)}, u32[]{:S(2)}) collective-permute-start(bf16[256,1024]{1,0:T(8,128)(2,1)} %act.1), channel_id=1, source_target_pairs={{0,4},{4,0},{8,12},{12,8},{16,20},{20,16},{24,28},{28,24},{32,36},... | collective-permute-start | bytes 1572872 | tf_op jit(solution)/shard_map/ppermute | solution.py:346
  0.7 12.3 %collective-permute-start = (bf16[256,1024]{1,0:T(8,128)(2,1)}, bf16[256,1024]{1,0:T(8,128)(2,1)S(1)}, u32[]{:S(2)}, u32[]{:S(2)}) collective-permute-start(bf16[256,1024]{1,0:T(8,128)(2,1)} %act.1), channel_id=1, source_target_pairs={{0,1},{1,0},{2,3},{3,2},{4,8},{5,9},{6,10},{7,11},{8,4},{9,5},{10,... | collective-permute-start | bytes 1572872 | tf_op jit(solution)/shard_map/ppermute | solution.py:346
  1.6 14.4 %collective-permute-start.2 = (bf16[256,256]{1,0:T(8,128)(2,1)}, bf16[256,256]{1,0:T(8,128)(2,1)S(1)}, u32[]{:S(2)}, u32[]{:S(2)}) collective-permute-start(bf16[256,256]{1,0:T(8,128)(2,1)} %cot.1), channel_id=1, source_target_pairs={{0,2},{1,3},{2,0},{3,1},{4,6},{5,7},{6,4},{7,5},{8,10},{9,11},{10,... | collective-permute-start | bytes 393224 | tf_op jit(solution)/shard_map/ppermute | solution.py:346
  4.5 11.6 %collective-permute-start.4 = (bf16[256,256]{1,0:T(8,128)(2,1)}, bf16[256,256]{1,0:T(8,128)(2,1)S(1)}, u32[]{:S(2)}, u32[]{:S(2)}) collective-permute-start(bf16[256,256]{1,0:T(8,128)(2,1)} %cot.1), channel_id=1, source_target_pairs={{0,3},{1,2},{2,1},{3,0},{4,7},{5,6},{6,5},{7,4},{8,11},{9,10},{10,... | collective-permute-start | bytes 393224 | tf_op jit(solution)/shard_map/ppermute | solution.py:346
  5.5 10.6 %collective-permute-start.3 = (bf16[256,256]{1,0:T(8,128)(2,1)}, bf16[256,256]{1,0:T(8,128)(2,1)S(1)}, u32[]{:S(2)}, u32[]{:S(2)}) collective-permute-start(bf16[256,256]{1,0:T(8,128)(2,1)} %cot.1), channel_id=1, source_target_pairs={{0,1},{1,0},{2,3},{3,2},{4,5},{5,4},{6,7},{7,6},{8,9},{9,8},{10,11... | collective-permute-start | bytes 393224 | tf_op jit(solution)/shard_map/ppermute | solution.py:346
  19.7 3.1 %collective-permute-start.5 = (bf16[160,16,256]{2,1,0:T(8,128)(2,1)S(1)}, bf16[160,16,256]{2,1,0:T(8,128)(2,1)S(1)}, u32[]{:S(2)}, u32[]{:S(2)}) collective-permute-start(bf16[160,16,256]{2,1,0:T(8,128)(2,1)S(1)} %get-tuple-element.66), channel_id=1, source_target_pairs={{0,4},{4,0},{8,12},{12,8},{16,20},{20,16},{24,28},{28,24},{32,36},... | collective-permute-start | bytes 3932168 | tf_op jit(solution)/shard_map/ppermute | solution.py:346
  19.8 8.1 %collective-permute-start.6 = (bf16[2,256,256]{2,1,0:T(8,128)(2,1)S(1)}, bf16[2,256,256]{2,1,0:T(8,128)(2,1)S(1)}, u32[]{:S(2)}, u32[]{:S(2)}) collective-permute-start(bf16[2,256,256]{2,1,0:T(8,128)(2,1)S(1)} %get-tuple-element.67), channel_id=1, source_target_pairs={{0,1},{1,0},{2,3},{3,2},{4,8},{5,9},{6,10},{7,11},{8,4},{9,5},{10,... | collective-permute-start | bytes 786440 | tf_op jit(solution)/shard_map/ppermute | solution.py:346
  20.5 8.6 %collective-permute-start.7 = (bf16[2,256,256]{2,1,0:T(8,128)(2,1)S(1)}, bf16[2,256,256]{2,1,0:T(8,128)(2,1)S(1)}, u32[]{:S(2)}, u32[]{:S(2)}) collective-permute-start(bf16[2,256,256]{2,1,0:T(8,128)(2,1)S(1)} %get-tuple-element.70), channel_id=1, source_target_pairs={{0,1},{1,0},{2,3},{3,2},{4,7},{5,6},{6,5},{7,4},{8,9},{9,8},{10,11... | collective-permute-start | bytes 786440 | tf_op jit(solution)/shard_map/ppermute | solution.py:346
  23.1 8.7 %collective-permute-start.10 = (bf16[32,16,256]{2,1,0:T(8,128)(2,1)S(1)}, bf16[32,16,256]{2,1,0:T(8,128)(2,1)S(1)}, u32[]{:S(2)}, u32[]{:S(2)}) collective-permute-start(bf16[32,16,256]{2,1,0:T(8,128)(2,1)S(1)} %get-tuple-element.80), channel_id=1, source_target_pairs={{0,56},{4,236},{8,48},{12,228},{16,40},{20,252},{24,32},{28,244},{... | collective-permute-start | bytes 786440 | tf_op jit(solution)/shard_map/ppermute | solution.py:346
  25.3 9.1 %collective-permute-start.11 = (bf16[32,16,256]{2,1,0:T(8,128)(2,1)S(1)}, bf16[32,16,256]{2,1,0:T(8,128)(2,1)S(1)}, u32[]{:S(2)}, u32[]{:S(2)}) collective-permute-start(bf16[32,16,256]{2,1,0:T(8,128)(2,1)S(1)} %get-tuple-element.81), channel_id=1, source_target_pairs={{0,24},{4,12},{8,16},{12,4},{16,8},{20,28},{24,0},{28,20},{32,56},... | collective-permute-start | bytes 786440 | tf_op jit(solution)/shard_map/ppermute | solution.py:346
  26.8 7.6 %collective-permute-start.12 = (bf16[32,16,256]{2,1,0:T(8,128)(2,1)S(1)}, bf16[32,16,256]{2,1,0:T(8,128)(2,1)S(1)}, u32[]{:S(2)}, u32[]{:S(2)}) collective-permute-start(bf16[32,16,256]{2,1,0:T(8,128)(2,1)S(1)} %get-tuple-element.82), channel_id=1, source_target_pairs={{0,32},{4,228},{8,40},{12,236},{16,48},{20,244},{24,56},{28,252},{... | collective-permute-start | bytes 786440 | tf_op jit(solution)/shard_map/ppermute | solution.py:346
  29.7 12.3 %collective-permute-start.8 = (bf16[3,256,256]{2,1,0:T(8,128)(2,1)S(1)}, bf16[3,256,256]{2,1,0:T(8,128)(2,1)S(1)}, u32[]{:S(2)}, u32[]{:S(2)}) collective-permute-start(bf16[3,256,256]{2,1,0:T(8,128)(2,1)S(1)} %get-tuple-element.72), channel_id=1, source_target_pairs={{0,3},{1,2},{2,1},{3,0},{4,5},{5,4},{6,7},{7,6},{8,11},{9,10},{10,... | collective-permute-start | bytes 1179656 | tf_op jit(solution)/shard_map/ppermute | solution.py:346
  34.6 9.3 %collective-permute-start.13 = (bf16[8,16,256]{2,1,0:T(8,128)(2,1)S(1)}, bf16[8,16,256]{2,1,0:T(8,128)(2,1)S(1)}, u32[]{:S(2)}, u32[]{:S(2)}) collective-permute-start(bf16[8,16,256]{2,1,0:T(8,128)(2,1)S(1)} %get-tuple-element.84), channel_id=1, source_target_pairs={{0,232},{4,60},{8,224},{12,52},{16,248},{20,44},{24,240},{28,36},{... | collective-permute-start | bytes 196616 | tf_op jit(solution)/shard_map/ppermute | solution.py:346
  38.1 6.1 %collective-permute-start.14 = (bf16[8,16,256]{2,1,0:T(8,128)(2,1)S(1)}, bf16[8,16,256]{2,1,0:T(8,128)(2,1)S(1)}, u32[]{:S(2)}, u32[]{:S(2)}) collective-permute-start(bf16[8,16,256]{2,1,0:T(8,128)(2,1)S(1)} %get-tuple-element.85), channel_id=1, source_target_pairs={{0,8},{4,28},{8,0},{12,20},{16,24},{20,12},{24,16},{28,4},{32,40},... | collective-permute-start | bytes 196616 | tf_op jit(solution)/shard_map/ppermute | solution.py:346
  42.0 5.5 %collective-permute-start.15 = (bf16[8,16,256]{2,1,0:T(8,128)(2,1)S(1)}, bf16[8,16,256]{2,1,0:T(8,128)(2,1)S(1)}, u32[]{:S(2)}, u32[]{:S(2)}) collective-permute-start(bf16[8,16,256]{2,1,0:T(8,128)(2,1)S(1)} %get-tuple-element.86), channel_id=1, source_target_pairs={{0,224},{4,36},{8,232},{12,44},{16,240},{20,52},{24,248},{28,60},{... | collective-permute-start | bytes 196616 | tf_op jit(solution)/shard_map/ppermute | solution.py:346
  42.7 7.1 %collective-permute-start.9 = (bf16[256,256]{1,0:T(8,128)(2,1)S(1)}, bf16[256,256]{1,0:T(8,128)(2,1)S(1)}, u32[]{:S(2)}, u32[]{:S(2)}) collective-permute-start(bf16[256,256]{1,0:T(8,128)(2,1)S(1)} %get-tuple-element.75), channel_id=1, source_target_pairs={{0,1},{1,0},{2,3},{3,2},{4,7},{5,6},{6,5},{7,4},{8,9},{9,8},{10,11... | collective-permute-start | bytes 393224 | tf_op jit(solution)/shard_map/ppermute | solution.py:346
  47.5 5.8 %collective-permute-start.16 = (bf16[4,16,256]{2,1,0:T(8,128)(2,1)S(1)}, bf16[4,16,256]{2,1,0:T(8,128)(2,1)S(1)}, u32[]{:S(2)}, u32[]{:S(2)}) collective-permute-start(bf16[4,16,256]{2,1,0:T(8,128)(2,1)S(1)} %get-tuple-element.88), channel_id=1, source_target_pairs={{0,96},{4,164},{8,104},{12,172},{16,112},{20,180},{24,120},{28,188... | collective-permute-start | bytes 98312 | tf_op jit(solution)/shard_map/ppermute | solution.py:346

commit v16 on v14

--- a/solution.py
+++ b/solution.py
@@ -262,7 +262,7 @@
     )
 
 
-def keep_kernel(act_t, far_t, near_t, cot_t, gq, grad_key, grad_value, att, keep_out, dw_s):
+def keep_kernel(far, act_t, far_t, near_t, cot_t, gq, grad_key, grad_value, att, far_out, keep_out, dw_s):
     core = places()[0]
     weight_terms(
         1, core, act_t, far_t, near_t, cot_t, gq, grad_key, grad_value, att, keep_out, dw_s
@@ -313,7 +313,8 @@
 
 
 def call(
-    kernel, name, outs, arrays, apart=(), scratch=(), limit=16, flops=0, moved=1_000_000, keep=True
+    kernel, name, outs, arrays, apart=(), scratch=(), limit=16, flops=0, moved=1_000_000, keep=True,
+    aliases=(),
 ):
     kept = [pltpu.VMEM(shape, dtype) if keep else jax.ShapeDtypeStruct(shape, dtype) for shape, dtype in outs]
     return pl.pallas_call(
@@ -323,6 +324,7 @@
         + [pl.BlockSpec(memory_space=pltpu.VMEM)] * len(arrays),
         out_specs=(pl.BlockSpec(memory_space=pltpu.VMEM),) * len(kept),
         scratch_shapes=list(scratch),
+        input_output_aliases=dict(aliases),
         compiler_params=pltpu.CompilerParams(vmem_limit_bytes=limit * 1024 * 1024),
         cost_estimate=pl.CostEstimate(flops=flops, bytes_accessed=moved, transcendentals=0),
         name=name,
@@ -418,14 +420,15 @@
         flops=2_000_000_000,
         moved=8_000_000,
     )
-    (dw_keep,) = call(
+    far, dw_keep = call(
         keep_kernel,
         "keep_terms",
-        [((128,) + block, BF)],
-        [act_t, far_t, near_t, cot_t, gq, grad_key, grad_value, att],
+        [((2, ROW, WIDTH), BF), ((128,) + block, BF)],
+        [far, act_t, far_t, near_t, cot_t, gq, grad_key, grad_value, att],
         scratch=[pltpu.VMEM((4, D // 2, WIDTH), F32)],
         flops=1_000_000_000,
         moved=4_000_000,
+        aliases={0: 0},
     )
 
     def share(name, terms, ways, kept_as, flops=0):

time: 53.2 us -> 53.2 us (level)
  transfers between devices with their start and end apart: 16 -> 16, of which waited for: 9 -> 8; matrix products, arithmetic and copies ran while one was open for 0% -> 0% of each run, Pallas kernels for 16% -> 16%
where the time goes in v16:
time: 53.2 us; the launch traced here: 53.1 us
  starting transfers between devices  21.4 us (40%)
  waiting for transfers between devices  18.5 us (35%)
  Pallas kernels  12.5 us (23%)
  between operations  0.72 us (1%)
    ppermute x16, starting transfers between devices, move(): lax.ppermute(value, axis, [(i, target(i)) for i in range(count) if 0 <= t...  21.4 us
    ppermute x16, waiting for transfers between devices, move(): lax.ppermute(value, axis, [(i, target(i)) for i in range(count) if 0 <= t...  18.5 us
    pallas_call x11, Pallas kernels, call(): pl.pallas_call(kernel, out_shape=tuple(kept), in_specs=[pl.BlockSpec(memo...  12.5 us
  transfers between devices with their start and end apart: 16, of which 8 were waited for; matrix products, arithmetic and copies ran while one was open for 0% of the time, Pallas kernels for 16%

profile of v16, /device:TPU:6, one launch (start us, length us, event | category | flops | bytes accessed | tf_op | source)
XLA Modules:
  0.0 53.1 jit_solution(4699100298967427441)
XLA Ops:
  0.6 0.1 collective-permute-start.1
  0.7 0.9 %collective-permute-start = (bf16[256,1024]{1,0:T(8,128)(2,1)}, bf16[256,1024]{1,0:T(8,128)(2,1)S(1)}, u32[]{:S(2)}, u32[]{:S(2)}) collective-permute-start(bf16[256,1024]{1,0:T(8,128)(2,1)} %act.1), channel_id=1, source_target_pairs={{0,1},{1,0},{2,3},{3,2},{4,8},{5,9},{6,10},{7,11},{8,4},{9,5},{10,... | collective-permute-start | bytes 1572872 | tf_op jit(solution)/shard_map/ppermute | solution.py:336
  1.6 2.8 %collective-permute-start.2 = (bf16[256,256]{1,0:T(8,128)(2,1)}, bf16[256,256]{1,0:T(8,128)(2,1)S(1)}, u32[]{:S(2)}, u32[]{:S(2)}) collective-permute-start(bf16[256,256]{1,0:T(8,128)(2,1)} %cot.1), channel_id=1, source_target_pairs={{0,2},{1,3},{2,0},{3,1},{4,6},{5,7},{6,4},{7,5},{8,10},{9,11},{10,... | collective-permute-start | bytes 393224 | tf_op jit(solution)/shard_map/ppermute | solution.py:336
  4.5 1.0 %collective-permute-start.4 = (bf16[256,256]{1,0:T(8,128)(2,1)}, bf16[256,256]{1,0:T(8,128)(2,1)S(1)}, u32[]{:S(2)}, u32[]{:S(2)}) collective-permute-start(bf16[256,256]{1,0:T(8,128)(2,1)} %cot.1), channel_id=1, source_target_pairs={{0,3},{1,2},{2,1},{3,0},{4,7},{5,6},{6,5},{7,4},{8,11},{9,10},{10,... | collective-permute-start | bytes 393224 | tf_op jit(solution)/shard_map/ppermute | solution.py:336
  5.5 0.0 collective-permute-start.3
  5.5 0.0 collective-permute-done.1.a_near
  5.5 3.9 %own_part.1 = (bf16[1024,256]{1,0:T(8,128)(2,1)S(1)}, bf16[1024,256]{1,0:T(8,128)(2,1)S(1)}, bf16[1024,256]{1,0:T(8,128)(2,1)S(1)}, bf16[256,1024]{1,0:T(8,128)(...) custom-call(bf16[256,1024]{1,0:T(8,128)(2,1)} %act.1, ...), custom_call_target="tpu_custom_call" | custom-call | flops 600000000 | bytes 6000000 | tf_op jit(solution)/shard_map/own_part/pallas_call | solution.py:320
  9.5 3.6 %collective-permute-done.a_far = bf16[256,1024]{1,0:T(8,128)(2,1)S(1)} collective-permute-done((bf16[256,1024]{1,0:T(8,128)(2,1)}, bf16[256,1024]{1,0:T(8,128)(2,1)S(1)}, u32[]{:S(2)}, u32[]{:S(2)}) %collective-permute-start) | collective-permute-done | bytes 524320 | tf_op jit(solution)/shard_map/ppermute | solution.py:336
  13.0 1.6 %forward.1 = (bf16[768,256]{1,0:T(8,128)(2,1)S(1)}, bf16[768,256]{1,0:T(8,128)(2,1)S(1)}, bf16[768,1024]{1,0:T(8,128)(2,1)S(1)}, bf16[256,256]{1,0:T(8,128)(2,1)S(1)}, bf16[1024,256]{1,0:T(8,128)(2,1)S(1)}) custom-call(bf16[256,1024]{1,0:T(8,128)(2,1)S(1)} %collective-permute-done.a_far, bf16[1024,256]{1,0:T(8,128)(2,1)S(1)} %get-tuple-element.47.wk, ...), custom_call_target="tpu_custom_call" | custom-call | flops 2000000000 | bytes 6000000 | tf_op jit(solution)/shard_map/forward/pallas_call | solution.py:320
  14.6 1.4 %collective-permute-done.2.c2 = bf16[256,256]{1,0:T(8,128)(2,1)S(1)} collective-permute-done((bf16[256,256]{1,0:T(8,128)(2,1)}, bf16[256,256]{1,0:T(8,128)(2,1)S(1)}, u32[]{:S(2)}, u32[]{:S(2)}) %collective-permute-start.2) | collective-permute-done | bytes 131104 | tf_op jit(solution)/shard_map/ppermute | solution.py:336
  16.1 0.0 collective-permute-done.4.c3
  16.1 0.0 collective-permute-done.3.c1
  16.1 3.6 %backward.1 = (bf16[256,256]{1,0:T(8,128)(2,1)S(1)}, bf16[2,256,256]{2,1,0:T(8,128)(2,1)S(1)}, f32[2,256,256]{2,1,0:T(8,128)S(1)}, bf16[768,256]{1,0:T(8,128)(2,...) custom-call(bf16[768,256]{1,0:T(8,128)(2,1)S(1)} %get-tuple-element.56.keys, ...), custom_call_target="tpu_custom_call" | custom-call | flops 2000000000 | bytes 8000000 | tf_op jit(solution)/shard_map/backward/pallas_call | solution.py:320
  19.7 0.1 collective-permute-start.5
  19.8 0.8 %keep_terms.1 = (bf16[2,256,256]{2,1,0:T(8,128)(2,1)S(1)}, bf16[128,16,256]{2,1,0:T(8,128)(2,1)S(1)}) custom-call(bf16[2,256,256]{2,1,0:T(8,128)(2,1)S(1)} %get-tuple-element.68.far, bf16[1024,256]{1,0:T(8,128)(2,1)S(1)} %get-tuple-element.62.act_t, bf16[1024,256]{1,0:T(8,128)(2,1)S(1)} %get-tuple-element.59.far_t, ...), custom_call_target="tpu_custom_call", output_to_operand_aliasing={{0}: (0, {})} | custom-call | flops 1000000000 | bytes 4000000 | tf_op jit(solution)/shard_map/keep_terms/pallas_call | solution.py:320
  20.6 0.7 %collective-permute-start.6 = (bf16[2,256,256]{2,1,0:T(8,128)(2,1)S(1)}, bf16[2,256,256]{2,1,0:T(8,128)(2,1)S(1)}, u32[]{:S(2)}, u32[]{:S(2)}) collective-permute-start(bf16[2,256,256]{2,1,0:T(8,128)(2,1)S(1)} %get-tuple-element.72), channel_id=1, source_target_pairs={{0,1},{1,0},{2,3},{3,2},{4,8},{5,9},{6,10},{7,11},{8,4},{9,5},{10,... | collective-permute-start | bytes 786440 | tf_op jit(solution)/shard_map/ppermute | solution.py:336
  21.3 1.5 %collective-permute-done.5.near.refs_1_ = bf16[160,16,256]{2,1,0:T(8,128)(2,1)S(1)} collective-permute-done((bf16[160,16,256]{2,1,0:T(8,128)(2,1)S(1)}, bf16[160,16,256]{2,1,0:T(8,128)(2,1)S(1)}, u32[]{:S(2)}, u32[]{:S(2)}) %collective-permute-start.5) | collective-permute-done | bytes 1310752 | tf_op jit(solution)/shard_map/ppermute | solution.py:336
  22.8 0.2 core_sum.1
  23.0 2.0 %collective-permute-start.9 = (bf16[32,16,256]{2,1,0:T(8,128)(2,1)S(1)}, bf16[32,16,256]{2,1,0:T(8,128)(2,1)S(1)}, u32[]{:S(2)}, u32[]{:S(2)}) collective-permute-start(bf16[32,16,256]{2,1,0:T(8,128)(2,1)S(1)} %get-tuple-element.82), channel_id=1, source_target_pairs={{0,56},{4,236},{8,48},{12,228},{16,40},{20,252},{24,32},{28,244},{... | collective-permute-start | bytes 786440 | tf_op jit(solution)/shard_map/ppermute | solution.py:336
  25.0 0.6 %collective-permute-start.10 = (bf16[32,16,256]{2,1,0:T(8,128)(2,1)S(1)}, bf16[32,16,256]{2,1,0:T(8,128)(2,1)S(1)}, u32[]{:S(2)}, u32[]{:S(2)}) collective-permute-start(bf16[32,16,256]{2,1,0:T(8,128)(2,1)S(1)} %get-tuple-element.83), channel_id=1, source_target_pairs={{0,24},{4,12},{8,16},{12,4},{16,8},{20,28},{24,0},{28,20},{32,56},... | collective-permute-start | bytes 786440 | tf_op jit(solution)/shard_map/ppermute | solution.py:336
  25.7 2.3 %collective-permute-start.11 = (bf16[32,16,256]{2,1,0:T(8,128)(2,1)S(1)}, bf16[32,16,256]{2,1,0:T(8,128)(2,1)S(1)}, u32[]{:S(2)}, u32[]{:S(2)}) collective-permute-start(bf16[32,16,256]{2,1,0:T(8,128)(2,1)S(1)} %get-tuple-element.84), channel_id=1, source_target_pairs={{0,32},{4,228},{8,40},{12,236},{16,48},{20,244},{24,56},{28,252},{... | collective-permute-start | bytes 786440 | tf_op jit(solution)/shard_map/ppermute | solution.py:336
  28.0 0.0 collective-permute-done.6.far
  28.0 0.7 %input_grad.1 = (f32[4,256,256]{2,1,0:T(8,128)S(1)}, bf16[4,256,256]{2,1,0:T(8,128)(2,1)S(1)}) custom-call(bf16[256,256]{1,0:T(8,128)(2,1)S(1)} %get-tuple-element.55.att, bf16[256,256]{1,0:T(8,128)(2,1)S(1)} %get-tuple-element.65.gq, f32[2,256,256]{2,1,0:T(8,128)S(1)} %get-tuple-element.66.own, ...), custom_call_target="tpu_custom_call" | custom-call | flops 540000000 | bytes 4000000 | tf_op jit(solution)/shard_map/input_grad/pallas_call | solution.py:320
  28.7 0.7 %collective-permute-start.7 = (bf16[4,256,256]{2,1,0:T(8,128)(2,1)S(1)}, bf16[4,256,256]{2,1,0:T(8,128)(2,1)S(1)}, u32[]{:S(2)}, u32[]{:S(2)}) collective-permute-start(bf16[4,256,256]{2,1,0:T(8,128)(2,1)S(1)} %get-tuple-element.75), channel_id=1, source_target_pairs={{0,1},{1,0},{2,3},{3,2},{4,7},{5,6},{6,5},{7,4},{8,9},{9,8},{10,11... | collective-permute-start | bytes 1572872 | tf_op jit(solution)/shard_map/ppermute | solution.py:336
  29.4 2.5 %collective-permute-done.9.refs_1_ = bf16[32,16,256]{2,1,0:T(8,128)(2,1)S(1)} collective-permute-done((bf16[32,16,256]{2,1,0:T(8,128)(2,1)S(1)}, bf16[32,16,256]{2,1,0:T(8,128)(2,1)S(1)}, u32[]{:S(2)}, u32[]{:S(2)}) %collective-permute-start.9) | collective-permute-done | bytes 262176 | tf_op jit(solution)/shard_map/ppermute | solution.py:336
  31.9 2.7 %collective-permute-done.10.refs_2_ = bf16[32,16,256]{2,1,0:T(8,128)(2,1)S(1)} collective-permute-done((bf16[32,16,256]{2,1,0:T(8,128)(2,1)S(1)}, bf16[32,16,256]{2,1,0:T(8,128)(2,1)S(1)}, u32[]{:S(2)}, u32[]{:S(2)}) %collective-permute-start.10) | collective-permute-done | bytes 262176 | tf_op jit(solution)/shard_map/ppermute | solution.py:336
  34.6 0.0 collective-permute-done.11.refs_3_
  34.6 0.1 first_sum.1
  34.7 2.0 %collective-permute-start.12 = (bf16[8,16,256]{2,1,0:T(8,128)(2,1)S(1)}, bf16[8,16,256]{2,1,0:T(8,128)(2,1)S(1)}, u32[]{:S(2)}, u32[]{:S(2)}) collective-permute-start(bf16[8,16,256]{2,1,0:T(8,128)(2,1)S(1)} %get-tuple-element.86), channel_id=1, source_target_pairs={{0,232},{4,60},{8,224},{12,52},{16,248},{20,44},{24,240},{28,36},{... | collective-permute-start | bytes 196616 | tf_op jit(solution)/shard_map/ppermute | solution.py:336
  36.7 4.5 %collective-permute-start.13 = (bf16[8,16,256]{2,1,0:T(8,128)(2,1)S(1)}, bf16[8,16,256]{2,1,0:T(8,128)(2,1)S(1)}, u32[]{:S(2)}, u32[]{:S(2)}) collective-permute-start(bf16[8,16,256]{2,1,0:T(8,128)(2,1)S(1)} %get-tuple-element.87), channel_id=1, source_target_pairs={{0,8},{4,28},{8,0},{12,20},{16,24},{20,12},{24,16},{28,4},{32,40},... | collective-permute-start | bytes 196616 | tf_op jit(solution)/shard_map/ppermute | solution.py:336
  41.2 0.0 collective-permute-start.14
  41.2 0.0 collective-permute-done.7.refs_1_
  41.2 0.1 mp_share.1
  41.3 1.4 %collective-permute-start.8 = (bf16[2,256,256]{2,1,0:T(8,128)(2,1)S(1)}, bf16[2,256,256]{2,1,0:T(8,128)(2,1)S(1)}, u32[]{:S(2)}, u32[]{:S(2)}) collective-permute-start(bf16[2,256,256]{2,1,0:T(8,128)(2,1)S(1)} %get-tuple-element.77), channel_id=1, source_target_pairs={{0,3},{1,2},{2,1},{3,0},{4,5},{5,4},{6,7},{7,6},{8,11},{9,10},{10,... | collective-permute-start | bytes 786440 | tf_op jit(solution)/shard_map/ppermute | solution.py:336
  42.6 0.0 collective-permute-done.12.refs_1_
  42.6 0.8 %collective-permute-done.13.refs_2_ = bf16[8,16,256]{2,1,0:T(8,128)(2,1)S(1)} collective-permute-done((bf16[8,16,256]{2,1,0:T(8,128)(2,1)S(1)}, bf16[8,16,256]{2,1,0:T(8,128)(2,1)S(1)}, u32[]{:S(2)}, u32[]{:S(2)}) %collective-permute-start.13) | collective-permute-done | bytes 65568 | tf_op jit(solution)/shard_map/ppermute | solution.py:336
  43.4 3.2 %collective-permute-done.14.refs_3_ = bf16[8,16,256]{2,1,0:T(8,128)(2,1)S(1)} collective-permute-done((bf16[8,16,256]{2,1,0:T(8,128)(2,1)S(1)}, bf16[8,16,256]{2,1,0:T(8,128)(2,1)S(1)}, u32[]{:S(2)}, u32[]{:S(2)}) %collective-permute-start.14) | collective-permute-done | bytes 65568 | tf_op jit(solution)/shard_map/ppermute | solution.py:336
  46.7 2.3 %collective-permute-start.15 = (bf16[4,16,256]{2,1,0:T(8,128)(2,1)S(1)}, bf16[4,16,256]{2,1,0:T(8,128)(2,1)S(1)}, u32[]{:S(2)}, u32[]{:S(2)}) collective-permute-start(bf16[4,16,256]{2,1,0:T(8,128)(2,1)S(1)} %get-tuple-element.90), channel_id=1, source_target_pairs={{0,96},{4,164},{8,104},{12,172},{16,112},{20,180},{24,120},{28,188... | collective-permute-start | bytes 98312 | tf_op jit(solution)/shard_map/ppermute | solution.py:336
  49.0 0.0 collective-permute-done.8.got
  49.0 0.7 %mp_sum.1 = (bf16[256,256]{1,0:T(8,128)(2,1)}, bf16[256,256]{1,0:T(8,128)(2,1)}) custom-call(f32[2,256,256]{2,1,0:T(8,128)S(1)} %get-tuple-element.76.kept, bf16[2,256,256]{2,1,0:T(8,128)(2,1)S(1)} %collective-permute-done.8.got), custom_call_target="tpu_custom_call" | custom-call | bytes 1000000 | tf_op jit(solution)/shard_map/mp_sum/pallas_call | solution.py:320
  49.7 2.8 %collective-permute-done.15.got = bf16[4,16,256]{2,1,0:T(8,128)(2,1)S(1)} collective-permute-done((bf16[4,16,256]{2,1,0:T(8,128)(2,1)S(1)}, bf16[4,16,256]{2,1,0:T(8,128)(2,1)S(1)}, u32[]{:S(2)}, u32[]{:S(2)}) %collective-permute-start.15) | collective-permute-done | bytes 32800 | tf_op jit(solution)/shard_map/ppermute | solution.py:336
  52.5 0.6 %last_sum.1 = f32[4,16,256]{2,1,0:T(8,128)} custom-call(bf16[256,256]{1,0:T(8,128)(2,1)} %get-tuple-element.44.after, f32[4,16,256]{2,1,0:T(8,128)S(1)} %get-tuple-element.89.kept, bf16[4,16,256]{2,1,0:T(8,128)(2,1)S(1)} %collective-permute-done.15.got), custom_call_target="tpu_custom_call" | custom-call | bytes 1000000 | tf_op jit(solution)/shard_map/last_sum/pallas_call | solution.py:320
  (1 shorter events, 0.0 us)
Async XLA Ops:
  0.6 4.9 %collective-permute-start.1 = (bf16[256,1024]{1,0:T(8,128)(2,1)}, bf16[256,1024]{1,0:T(8,128)(2,1)S(1)}, u32[]{:S(2)}, u32[]{:S(2)}) collective-permute-start(bf16[256,1024]{1,0:T(8,128)(2,1)} %act.1), channel_id=1, source_target_pairs={{0,4},{4,0},{8,12},{12,8},{16,20},{20,16},{24,28},{28,24},{32,36},... | collective-permute-start | bytes 1572872 | tf_op jit(solution)/shard_map/ppermute | solution.py:336
  0.7 12.3 %collective-permute-start = (bf16[256,1024]{1,0:T(8,128)(2,1)}, bf16[256,1024]{1,0:T(8,128)(2,1)S(1)}, u32[]{:S(2)}, u32[]{:S(2)}) collective-permute-start(bf16[256,1024]{1,0:T(8,128)(2,1)} %act.1), channel_id=1, source_target_pairs={{0,1},{1,0},{2,3},{3,2},{4,8},{5,9},{6,10},{7,11},{8,4},{9,5},{10,... | collective-permute-start | bytes 1572872 | tf_op jit(solution)/shard_map/ppermute | solution.py:336
  1.6 14.4 %collective-permute-start.2 = (bf16[256,256]{1,0:T(8,128)(2,1)}, bf16[256,256]{1,0:T(8,128)(2,1)S(1)}, u32[]{:S(2)}, u32[]{:S(2)}) collective-permute-start(bf16[256,256]{1,0:T(8,128)(2,1)} %cot.1), channel_id=1, source_target_pairs={{0,2},{1,3},{2,0},{3,1},{4,6},{5,7},{6,4},{7,5},{8,10},{9,11},{10,... | collective-permute-start | bytes 393224 | tf_op jit(solution)/shard_map/ppermute | solution.py:336
  4.5 11.6 %collective-permute-start.4 = (bf16[256,256]{1,0:T(8,128)(2,1)}, bf16[256,256]{1,0:T(8,128)(2,1)S(1)}, u32[]{:S(2)}, u32[]{:S(2)}) collective-permute-start(bf16[256,256]{1,0:T(8,128)(2,1)} %cot.1), channel_id=1, source_target_pairs={{0,3},{1,2},{2,1},{3,0},{4,7},{5,6},{6,5},{7,4},{8,11},{9,10},{10,... | collective-permute-start | bytes 393224 | tf_op jit(solution)/shard_map/ppermute | solution.py:336
  5.5 10.6 %collective-permute-start.3 = (bf16[256,256]{1,0:T(8,128)(2,1)}, bf16[256,256]{1,0:T(8,128)(2,1)S(1)}, u32[]{:S(2)}, u32[]{:S(2)}) collective-permute-start(bf16[256,256]{1,0:T(8,128)(2,1)} %cot.1), channel_id=1, source_target_pairs={{0,1},{1,0},{2,3},{3,2},{4,5},{5,4},{6,7},{7,6},{8,9},{9,8},{10,11... | collective-permute-start | bytes 393224 | tf_op jit(solution)/shard_map/ppermute | solution.py:336
  19.7 3.1 %collective-permute-start.5 = (bf16[160,16,256]{2,1,0:T(8,128)(2,1)S(1)}, bf16[160,16,256]{2,1,0:T(8,128)(2,1)S(1)}, u32[]{:S(2)}, u32[]{:S(2)}) collective-permute-start(bf16[160,16,256]{2,1,0:T(8,128)(2,1)S(1)} %get-tuple-element.67), channel_id=1, source_target_pairs={{0,4},{4,0},{8,12},{12,8},{16,20},{20,16},{24,28},{28,24},{32,36},... | collective-permute-start | bytes 3932168 | tf_op jit(solution)/shard_map/ppermute | solution.py:336
  20.6 7.4 %collective-permute-start.6 = (bf16[2,256,256]{2,1,0:T(8,128)(2,1)S(1)}, bf16[2,256,256]{2,1,0:T(8,128)(2,1)S(1)}, u32[]{:S(2)}, u32[]{:S(2)}) collective-permute-start(bf16[2,256,256]{2,1,0:T(8,128)(2,1)S(1)} %get-tuple-element.72), channel_id=1, source_target_pairs={{0,1},{1,0},{2,3},{3,2},{4,8},{5,9},{6,10},{7,11},{8,4},{9,5},{10,... | collective-permute-start | bytes 786440 | tf_op jit(solution)/shard_map/ppermute | solution.py:336
  23.0 8.9 %collective-permute-start.9 = (bf16[32,16,256]{2,1,0:T(8,128)(2,1)S(1)}, bf16[32,16,256]{2,1,0:T(8,128)(2,1)S(1)}, u32[]{:S(2)}, u32[]{:S(2)}) collective-permute-start(bf16[32,16,256]{2,1,0:T(8,128)(2,1)S(1)} %get-tuple-element.82), channel_id=1, source_target_pairs={{0,56},{4,236},{8,48},{12,228},{16,40},{20,252},{24,32},{28,244},{... | collective-permute-start | bytes 786440 | tf_op jit(solution)/shard_map/ppermute | solution.py:336
  25.0 9.6 %collective-permute-start.10 = (bf16[32,16,256]{2,1,0:T(8,128)(2,1)S(1)}, bf16[32,16,256]{2,1,0:T(8,128)(2,1)S(1)}, u32[]{:S(2)}, u32[]{:S(2)}) collective-permute-start(bf16[32,16,256]{2,1,0:T(8,128)(2,1)S(1)} %get-tuple-element.83), channel_id=1, source_target_pairs={{0,24},{4,12},{8,16},{12,4},{16,8},{20,28},{24,0},{28,20},{32,56},... | collective-permute-start | bytes 786440 | tf_op jit(solution)/shard_map/ppermute | solution.py:336
  25.7 8.9 %collective-permute-start.11 = (bf16[32,16,256]{2,1,0:T(8,128)(2,1)S(1)}, bf16[32,16,256]{2,1,0:T(8,128)(2,1)S(1)}, u32[]{:S(2)}, u32[]{:S(2)}) collective-permute-start(bf16[32,16,256]{2,1,0:T(8,128)(2,1)S(1)} %get-tuple-element.84), channel_id=1, source_target_pairs={{0,32},{4,228},{8,40},{12,236},{16,48},{20,244},{24,56},{28,252},{... | collective-permute-start | bytes 786440 | tf_op jit(solution)/shard_map/ppermute | solution.py:336
  28.7 12.4 %collective-permute-start.7 = (bf16[4,256,256]{2,1,0:T(8,128)(2,1)S(1)}, bf16[4,256,256]{2,1,0:T(8,128)(2,1)S(1)}, u32[]{:S(2)}, u32[]{:S(2)}) collective-permute-start(bf16[4,256,256]{2,1,0:T(8,128)(2,1)S(1)} %get-tuple-element.75), channel_id=1, source_target_pairs={{0,1},{1,0},{2,3},{3,2},{4,7},{5,6},{6,5},{7,4},{8,9},{9,8},{10,11... | collective-permute-start | bytes 1572872 | tf_op jit(solution)/shard_map/ppermute | solution.py:336
  34.7 7.9 %collective-permute-start.12 = (bf16[8,16,256]{2,1,0:T(8,128)(2,1)S(1)}, bf16[8,16,256]{2,1,0:T(8,128)(2,1)S(1)}, u32[]{:S(2)}, u32[]{:S(2)}) collective-permute-start(bf16[8,16,256]{2,1,0:T(8,128)(2,1)S(1)} %get-tuple-element.86), channel_id=1, source_target_pairs={{0,232},{4,60},{8,224},{12,52},{16,248},{20,44},{24,240},{28,36},{... | collective-permute-start | bytes 196616 | tf_op jit(solution)/shard_map/ppermute | solution.py:336
  36.7 6.7 %collective-permute-start.13 = (bf16[8,16,256]{2,1,0:T(8,128)(2,1)S(1)}, bf16[8,16,256]{2,1,0:T(8,128)(2,1)S(1)}, u32[]{:S(2)}, u32[]{:S(2)}) collective-permute-start(bf16[8,16,256]{2,1,0:T(8,128)(2,1)S(1)} %get-tuple-element.87), channel_id=1, source_target_pairs={{0,8},{4,28},{8,0},{12,20},{16,24},{20,12},{24,16},{28,4},{32,40},... | collective-permute-start | bytes 196616 | tf_op jit(solution)/shard_map/ppermute | solution.py:336
  41.2 5.5 %collective-permute-start.14 = (bf16[8,16,256]{2,1,0:T(8,128)(2,1)S(1)}, bf16[8,16,256]{2,1,0:T(8,128)(2,1)S(1)}, u32[]{:S(2)}, u32[]{:S(2)}) collective-permute-start(bf16[8,16,256]{2,1,0:T(8,128)(2,1)S(1)} %get-tuple-element.88), channel_id=1, source_target_pairs={{0,224},{4,36},{8,232},{12,44},{16,240},{20,52},{24,248},{28,60},{... | collective-permute-start | bytes 196616 | tf_op jit(solution)/shard_map/ppermute | solution.py:336
  41.3 7.7 %collective-permute-start.8 = (bf16[2,256,256]{2,1,0:T(8,128)(2,1)S(1)}, bf16[2,256,256]{2,1,0:T(8,128)(2,1)S(1)}, u32[]{:S(2)}, u32[]{:S(2)}) collective-permute-start(bf16[2,256,256]{2,1,0:T(8,128)(2,1)S(1)} %get-tuple-element.77), channel_id=1, source_target_pairs={{0,3},{1,2},{2,1},{3,0},{4,5},{5,4},{6,7},{7,6},{8,11},{9,10},{10,... | collective-permute-start | bytes 786440 | tf_op jit(solution)/shard_map/ppermute | solution.py:336
  46.7 5.8 %collective-permute-start.15 = (bf16[4,16,256]{2,1,0:T(8,128)(2,1)S(1)}, bf16[4,16,256]{2,1,0:T(8,128)(2,1)S(1)}, u32[]{:S(2)}, u32[]{:S(2)}) collective-permute-start(bf16[4,16,256]{2,1,0:T(8,128)(2,1)S(1)} %get-tuple-element.90), channel_id=1, source_target_pairs={{0,96},{4,164},{8,104},{12,172},{16,112},{20,180},{24,120},{28,188... | collective-permute-start | bytes 98312 | tf_op jit(solution)/shard_map/ppermute | solution.py:336

commit v17 on v14

--- a/solution.py
+++ b/solution.py
@@ -43,36 +43,35 @@
         named = jnp.zeros((16, ROW), jnp.int32)
         for patch in range(4):
             number = nb[patch, slot]
-            band = 1 + sign * (lax.div(number, 4) - row)
-            place = jnp.where(mask[patch, slot] > 0, band * 4 + lax.rem(number, 4), -1)
+            band = 1 + sign * ((number >> 2) - row)
+            place = jnp.where(mask[patch, slot] > 0, band * 4 + (number & 3), -1)
             named = jnp.where(patch_of_lane == patch, place, named)
         count += jnp.where(named == patch_of_row, 1.0, 0.0)
     return jnp.where(count > 0, jnp.where(count > 1, jnp.log(count) * LOG2E, 0.0), -1e30)
 
 
 def y_pair(y):
-    return y + 1 - 2 * (y % 2)
+    return y ^ 1
 
 
 def y_other(y):
-    return 3 - y
+    return y ^ 3
 
 
 def z_pair(z):
-    return z + 1 - 2 * (z % 2)
+    return z ^ 1
 
 
 def z_other(z):
-    return (z + 7 + 2 * (z % 2)) % 8
+    return (z + 2 * (z & 1) + 7) & 7
 
 
 def z_far(z):
-    middle = (z % 4) * (3 - z % 4) // 2
-    return (1 - middle) * (3 - 2 * (z % 4) + z) + middle * (7 - z)
+    return z ^ (3 + 4 * ((z ^ (z >> 1)) & 1))
 
 
 def z_far_too(z):
-    return z + 4 + (1 - 2 * (z % 2)) - 8 * (z // 4)
+    return z ^ 5
 
 
 def target_rows(z, y, y_partners, z_partners):

time: 53.2 us -> 53.1 us (level)
  no operation moved by 1% of the time
where the time goes in v17:
time: 53.1 us; the launch traced here: 53 us
  starting transfers between devices  20.9 us (39%)
  waiting for transfers between devices  18.8 us (35%)
  Pallas kernels  12.5 us (24%)
  between operations  0.72 us (1%)
    ppermute x16, starting transfers between devices, move(): lax.ppermute(value, axis, [(i, target(i)) for i in range(count) if 0 <= t...  20.9 us
    ppermute x16, waiting for transfers between devices, move(): lax.ppermute(value, axis, [(i, target(i)) for i in range(count) if 0 <= t...  18.8 us
    pallas_call x11, Pallas kernels, call(): pl.pallas_call(kernel, out_shape=tuple(kept), in_specs=[pl.BlockSpec(memo...  12.5 us
  transfers between devices with their start and end apart: 16, of which 9 were waited for; matrix products, arithmetic and copies ran while one was open for 0% of the time, Pallas kernels for 16%

profile of v17, /device:TPU:6, one launch (start us, length us, event | category | flops | bytes accessed | tf_op | source)
XLA Modules:
  0.0 53.0 jit_solution(2855231986246799079)
XLA Ops:
  0.6 0.1 collective-permute-start.1
  0.7 0.9 %collective-permute-start = (bf16[256,1024]{1,0:T(8,128)(2,1)}, bf16[256,1024]{1,0:T(8,128)(2,1)S(1)}, u32[]{:S(2)}, u32[]{:S(2)}) collective-permute-start(bf16[256,1024]{1,0:T(8,128)(2,1)} %act.1), channel_id=1, source_target_pairs={{0,1},{1,0},{2,3},{3,2},{4,8},{5,9},{6,10},{7,11},{8,4},{9,5},{10,... | collective-permute-start | bytes 1572872 | tf_op jit(solution)/shard_map/ppermute | solution.py:333
  1.6 2.8 %collective-permute-start.2 = (bf16[256,256]{1,0:T(8,128)(2,1)}, bf16[256,256]{1,0:T(8,128)(2,1)S(1)}, u32[]{:S(2)}, u32[]{:S(2)}) collective-permute-start(bf16[256,256]{1,0:T(8,128)(2,1)} %cot.1), channel_id=1, source_target_pairs={{0,2},{1,3},{2,0},{3,1},{4,6},{5,7},{6,4},{7,5},{8,10},{9,11},{10,... | collective-permute-start | bytes 393224 | tf_op jit(solution)/shard_map/ppermute | solution.py:333
  4.5 1.0 %collective-permute-start.4 = (bf16[256,256]{1,0:T(8,128)(2,1)}, bf16[256,256]{1,0:T(8,128)(2,1)S(1)}, u32[]{:S(2)}, u32[]{:S(2)}) collective-permute-start(bf16[256,256]{1,0:T(8,128)(2,1)} %cot.1), channel_id=1, source_target_pairs={{0,3},{1,2},{2,1},{3,0},{4,7},{5,6},{6,5},{7,4},{8,11},{9,10},{10,... | collective-permute-start | bytes 393224 | tf_op jit(solution)/shard_map/ppermute | solution.py:333
  5.5 0.0 collective-permute-start.3
  5.5 0.0 collective-permute-done.1.a_near
  5.5 3.9 %own_part.1 = (bf16[1024,256]{1,0:T(8,128)(2,1)S(1)}, bf16[1024,256]{1,0:T(8,128)(2,1)S(1)}, bf16[1024,256]{1,0:T(8,128)(2,1)S(1)}, bf16[256,1024]{1,0:T(8,128)(...) custom-call(bf16[256,1024]{1,0:T(8,128)(2,1)} %act.1, ...), custom_call_target="tpu_custom_call" | custom-call | flops 600000000 | bytes 6000000 | tf_op jit(solution)/shard_map/own_part/pallas_call | solution.py:318
  9.5 3.5 %collective-permute-done.a_far = bf16[256,1024]{1,0:T(8,128)(2,1)S(1)} collective-permute-done((bf16[256,1024]{1,0:T(8,128)(2,1)}, bf16[256,1024]{1,0:T(8,128)(2,1)S(1)}, u32[]{:S(2)}, u32[]{:S(2)}) %collective-permute-start) | collective-permute-done | bytes 524320 | tf_op jit(solution)/shard_map/ppermute | solution.py:333
  13.0 1.6 %forward.1 = (bf16[768,256]{1,0:T(8,128)(2,1)S(1)}, bf16[768,256]{1,0:T(8,128)(2,1)S(1)}, bf16[768,1024]{1,0:T(8,128)(2,1)S(1)}, bf16[256,256]{1,0:T(8,128)(2,1)S(1)}, bf16[1024,256]{1,0:T(8,128)(2,1)S(1)}) custom-call(bf16[256,1024]{1,0:T(8,128)(2,1)S(1)} %collective-permute-done.a_far, bf16[1024,256]{1,0:T(8,128)(2,1)S(1)} %get-tuple-element.45.wk, ...), custom_call_target="tpu_custom_call" | custom-call | flops 2000000000 | bytes 6000000 | tf_op jit(solution)/shard_map/forward/pallas_call | solution.py:318
  14.6 1.5 %collective-permute-done.2.c2 = bf16[256,256]{1,0:T(8,128)(2,1)S(1)} collective-permute-done((bf16[256,256]{1,0:T(8,128)(2,1)}, bf16[256,256]{1,0:T(8,128)(2,1)S(1)}, u32[]{:S(2)}, u32[]{:S(2)}) %collective-permute-start.2) | collective-permute-done | bytes 131104 | tf_op jit(solution)/shard_map/ppermute | solution.py:333
  16.1 0.0 collective-permute-done.4.c3
  16.1 0.0 collective-permute-done.3.c1
  16.1 3.6 %backward.1 = (bf16[256,256]{1,0:T(8,128)(2,1)S(1)}, bf16[2,256,256]{2,1,0:T(8,128)(2,1)S(1)}, f32[2,256,256]{2,1,0:T(8,128)S(1)}, bf16[768,256]{1,0:T(8,128)(2,...) custom-call(bf16[768,256]{1,0:T(8,128)(2,1)S(1)} %get-tuple-element.54.keys, ...), custom_call_target="tpu_custom_call" | custom-call | flops 2000000000 | bytes 8000000 | tf_op jit(solution)/shard_map/backward/pallas_call | solution.py:318
  19.7 0.1 collective-permute-start.5
  19.8 0.7 %collective-permute-start.6 = (bf16[2,256,256]{2,1,0:T(8,128)(2,1)S(1)}, bf16[2,256,256]{2,1,0:T(8,128)(2,1)S(1)}, u32[]{:S(2)}, u32[]{:S(2)}) collective-permute-start(bf16[2,256,256]{2,1,0:T(8,128)(2,1)S(1)} %get-tuple-element.66), channel_id=1, source_target_pairs={{0,1},{1,0},{2,3},{3,2},{4,8},{5,9},{6,10},{7,11},{8,4},{9,5},{10,... | collective-permute-start | bytes 786440 | tf_op jit(solution)/shard_map/ppermute | solution.py:333
  20.5 0.8 %keep_terms.1.refs_0_ = bf16[128,16,256]{2,1,0:T(8,128)(2,1)S(1)} custom-call(bf16[1024,256]{1,0:T(8,128)(2,1)S(1)} %get-tuple-element.60.act_t, bf16[1024,256]{1,0:T(8,128)(2,1)S(1)} %get-tuple-element.57.far_t, bf16[1024,256]{1,0:T(8,128)(2,1)S(1)} %get-tuple-element.58.near_t, bf16[1024,256]{1,0:T(8,128)(2,1)S(1)} %get-tuple-element.74.cot_t, ...), custom_call_target="tpu_custom_call" | custom-call | flops 1000000000 | bytes 4000000 | tf_op jit(solution)/shard_map/keep_terms/pallas_call | solution.py:318
  21.3 1.5 %collective-permute-done.5.near.refs_1_ = bf16[160,16,256]{2,1,0:T(8,128)(2,1)S(1)} collective-permute-done((bf16[160,16,256]{2,1,0:T(8,128)(2,1)S(1)}, bf16[160,16,256]{2,1,0:T(8,128)(2,1)S(1)}, u32[]{:S(2)}, u32[]{:S(2)}) %collective-permute-start.5) | collective-permute-done | bytes 1310752 | tf_op jit(solution)/shard_map/ppermute | solution.py:333
  22.8 0.2 core_sum.1
  23.1 1.8 %collective-permute-start.9 = (bf16[32,16,256]{2,1,0:T(8,128)(2,1)S(1)}, bf16[32,16,256]{2,1,0:T(8,128)(2,1)S(1)}, u32[]{:S(2)}, u32[]{:S(2)}) collective-permute-start(bf16[32,16,256]{2,1,0:T(8,128)(2,1)S(1)} %get-tuple-element.78), channel_id=1, source_target_pairs={{0,56},{4,236},{8,48},{12,228},{16,40},{20,252},{24,32},{28,244},{... | collective-permute-start | bytes 786440 | tf_op jit(solution)/shard_map/ppermute | solution.py:333
  24.9 0.7 %collective-permute-start.10 = (bf16[32,16,256]{2,1,0:T(8,128)(2,1)S(1)}, bf16[32,16,256]{2,1,0:T(8,128)(2,1)S(1)}, u32[]{:S(2)}, u32[]{:S(2)}) collective-permute-start(bf16[32,16,256]{2,1,0:T(8,128)(2,1)S(1)} %get-tuple-element.79), channel_id=1, source_target_pairs={{0,24},{4,12},{8,16},{12,4},{16,8},{20,28},{24,0},{28,20},{32,56},... | collective-permute-start | bytes 786440 | tf_op jit(solution)/shard_map/ppermute | solution.py:333
  25.5 2.3 %collective-permute-start.11 = (bf16[32,16,256]{2,1,0:T(8,128)(2,1)S(1)}, bf16[32,16,256]{2,1,0:T(8,128)(2,1)S(1)}, u32[]{:S(2)}, u32[]{:S(2)}) collective-permute-start(bf16[32,16,256]{2,1,0:T(8,128)(2,1)S(1)} %get-tuple-element.80), channel_id=1, source_target_pairs={{0,32},{4,228},{8,40},{12,236},{16,48},{20,244},{24,56},{28,252},{... | collective-permute-start | bytes 786440 | tf_op jit(solution)/shard_map/ppermute | solution.py:333
  27.8 0.0 collective-permute-done.6.far
  27.8 0.7 %input_grad.1 = (f32[4,256,256]{2,1,0:T(8,128)S(1)}, bf16[4,256,256]{2,1,0:T(8,128)(2,1)S(1)}) custom-call(bf16[256,256]{1,0:T(8,128)(2,1)S(1)} %get-tuple-element.53.att, bf16[256,256]{1,0:T(8,128)(2,1)S(1)} %get-tuple-element.63.gq, f32[2,256,256]{2,1,0:T(8,128)S(1)} %get-tuple-element.64.own, ...), custom_call_target="tpu_custom_call" | custom-call | flops 540000000 | bytes 4000000 | tf_op jit(solution)/shard_map/input_grad/pallas_call | solution.py:318
  28.6 0.7 %collective-permute-start.7 = (bf16[4,256,256]{2,1,0:T(8,128)(2,1)S(1)}, bf16[4,256,256]{2,1,0:T(8,128)(2,1)S(1)}, u32[]{:S(2)}, u32[]{:S(2)}) collective-permute-start(bf16[4,256,256]{2,1,0:T(8,128)(2,1)S(1)} %get-tuple-element.69), channel_id=1, source_target_pairs={{0,1},{1,0},{2,3},{3,2},{4,7},{5,6},{6,5},{7,4},{8,9},{9,8},{10,11... | collective-permute-start | bytes 1572872 | tf_op jit(solution)/shard_map/ppermute | solution.py:333
  29.3 2.5 %collective-permute-done.9.refs_1_ = bf16[32,16,256]{2,1,0:T(8,128)(2,1)S(1)} collective-permute-done((bf16[32,16,256]{2,1,0:T(8,128)(2,1)S(1)}, bf16[32,16,256]{2,1,0:T(8,128)(2,1)S(1)}, u32[]{:S(2)}, u32[]{:S(2)}) %collective-permute-start.9) | collective-permute-done | bytes 262176 | tf_op jit(solution)/shard_map/ppermute | solution.py:333
  31.7 2.7 %collective-permute-done.10.refs_2_ = bf16[32,16,256]{2,1,0:T(8,128)(2,1)S(1)} collective-permute-done((bf16[32,16,256]{2,1,0:T(8,128)(2,1)S(1)}, bf16[32,16,256]{2,1,0:T(8,128)(2,1)S(1)}, u32[]{:S(2)}, u32[]{:S(2)}) %collective-permute-start.10) | collective-permute-done | bytes 262176 | tf_op jit(solution)/shard_map/ppermute | solution.py:333
  34.4 0.0 collective-permute-done.11.refs_3_
  34.4 0.1 first_sum.1
  34.6 2.0 %collective-permute-start.12 = (bf16[8,16,256]{2,1,0:T(8,128)(2,1)S(1)}, bf16[8,16,256]{2,1,0:T(8,128)(2,1)S(1)}, u32[]{:S(2)}, u32[]{:S(2)}) collective-permute-start(bf16[8,16,256]{2,1,0:T(8,128)(2,1)S(1)} %get-tuple-element.82), channel_id=1, source_target_pairs={{0,232},{4,60},{8,224},{12,52},{16,248},{20,44},{24,240},{28,36},{... | collective-permute-start | bytes 196616 | tf_op jit(solution)/shard_map/ppermute | solution.py:333
  36.5 4.5 %collective-permute-start.13 = (bf16[8,16,256]{2,1,0:T(8,128)(2,1)S(1)}, bf16[8,16,256]{2,1,0:T(8,128)(2,1)S(1)}, u32[]{:S(2)}, u32[]{:S(2)}) collective-permute-start(bf16[8,16,256]{2,1,0:T(8,128)(2,1)S(1)} %get-tuple-element.83), channel_id=1, source_target_pairs={{0,8},{4,28},{8,0},{12,20},{16,24},{20,12},{24,16},{28,4},{32,40},... | collective-permute-start | bytes 196616 | tf_op jit(solution)/shard_map/ppermute | solution.py:333
  41.0 0.0 collective-permute-start.14
  41.0 0.0 collective-permute-done.7.refs_1_
  41.0 0.1 mp_share.1
  41.1 1.4 %collective-permute-start.8 = (bf16[2,256,256]{2,1,0:T(8,128)(2,1)S(1)}, bf16[2,256,256]{2,1,0:T(8,128)(2,1)S(1)}, u32[]{:S(2)}, u32[]{:S(2)}) collective-permute-start(bf16[2,256,256]{2,1,0:T(8,128)(2,1)S(1)} %get-tuple-element.71), channel_id=1, source_target_pairs={{0,3},{1,2},{2,1},{3,0},{4,5},{5,4},{6,7},{7,6},{8,11},{9,10},{10,... | collective-permute-start | bytes 786440 | tf_op jit(solution)/shard_map/ppermute | solution.py:333
  42.5 0.0 collective-permute-done.12.refs_1_
  42.5 0.8 %collective-permute-done.13.refs_2_ = bf16[8,16,256]{2,1,0:T(8,128)(2,1)S(1)} collective-permute-done((bf16[8,16,256]{2,1,0:T(8,128)(2,1)S(1)}, bf16[8,16,256]{2,1,0:T(8,128)(2,1)S(1)}, u32[]{:S(2)}, u32[]{:S(2)}) %collective-permute-start.13) | collective-permute-done | bytes 65568 | tf_op jit(solution)/shard_map/ppermute | solution.py:333
  43.2 3.2 %collective-permute-done.14.refs_3_ = bf16[8,16,256]{2,1,0:T(8,128)(2,1)S(1)} collective-permute-done((bf16[8,16,256]{2,1,0:T(8,128)(2,1)S(1)}, bf16[8,16,256]{2,1,0:T(8,128)(2,1)S(1)}, u32[]{:S(2)}, u32[]{:S(2)}) %collective-permute-start.14) | collective-permute-done | bytes 65568 | tf_op jit(solution)/shard_map/ppermute | solution.py:333
  46.5 2.0 %collective-permute-start.15 = (bf16[4,16,256]{2,1,0:T(8,128)(2,1)S(1)}, bf16[4,16,256]{2,1,0:T(8,128)(2,1)S(1)}, u32[]{:S(2)}, u32[]{:S(2)}) collective-permute-start(bf16[4,16,256]{2,1,0:T(8,128)(2,1)S(1)} %get-tuple-element.86), channel_id=1, source_target_pairs={{0,96},{4,164},{8,104},{12,172},{16,112},{20,180},{24,120},{28,188... | collective-permute-start | bytes 98312 | tf_op jit(solution)/shard_map/ppermute | solution.py:333
  48.5 0.3 collective-permute-done.8.got
  48.8 0.7 %mp_sum.1 = (bf16[256,256]{1,0:T(8,128)(2,1)}, bf16[256,256]{1,0:T(8,128)(2,1)}) custom-call(f32[2,256,256]{2,1,0:T(8,128)S(1)} %get-tuple-element.70.kept, bf16[2,256,256]{2,1,0:T(8,128)(2,1)S(1)} %collective-permute-done.8.got), custom_call_target="tpu_custom_call" | custom-call | bytes 1000000 | tf_op jit(solution)/shard_map/mp_sum/pallas_call | solution.py:318
  49.5 2.8 %collective-permute-done.15.got = bf16[4,16,256]{2,1,0:T(8,128)(2,1)S(1)} collective-permute-done((bf16[4,16,256]{2,1,0:T(8,128)(2,1)S(1)}, bf16[4,16,256]{2,1,0:T(8,128)(2,1)S(1)}, u32[]{:S(2)}, u32[]{:S(2)}) %collective-permute-start.15) | collective-permute-done | bytes 32800 | tf_op jit(solution)/shard_map/ppermute | solution.py:333
  52.3 0.6 %last_sum.1 = f32[4,16,256]{2,1,0:T(8,128)} custom-call(bf16[256,256]{1,0:T(8,128)(2,1)} %get-tuple-element.42.after, f32[4,16,256]{2,1,0:T(8,128)S(1)} %get-tuple-element.85.kept, bf16[4,16,256]{2,1,0:T(8,128)(2,1)S(1)} %collective-permute-done.15.got), custom_call_target="tpu_custom_call" | custom-call | bytes 1000000 | tf_op jit(solution)/shard_map/last_sum/pallas_call | solution.py:318
  (1 shorter events, 0.0 us)
Async XLA Ops:
  0.6 4.9 %collective-permute-start.1 = (bf16[256,1024]{1,0:T(8,128)(2,1)}, bf16[256,1024]{1,0:T(8,128)(2,1)S(1)}, u32[]{:S(2)}, u32[]{:S(2)}) collective-permute-start(bf16[256,1024]{1,0:T(8,128)(2,1)} %act.1), channel_id=1, source_target_pairs={{0,4},{4,0},{8,12},{12,8},{16,20},{20,16},{24,28},{28,24},{32,36},... | collective-permute-start | bytes 1572872 | tf_op jit(solution)/shard_map/ppermute | solution.py:333
  0.7 12.3 %collective-permute-start = (bf16[256,1024]{1,0:T(8,128)(2,1)}, bf16[256,1024]{1,0:T(8,128)(2,1)S(1)}, u32[]{:S(2)}, u32[]{:S(2)}) collective-permute-start(bf16[256,1024]{1,0:T(8,128)(2,1)} %act.1), channel_id=1, source_target_pairs={{0,1},{1,0},{2,3},{3,2},{4,8},{5,9},{6,10},{7,11},{8,4},{9,5},{10,... | collective-permute-start | bytes 1572872 | tf_op jit(solution)/shard_map/ppermute | solution.py:333
  1.6 14.4 %collective-permute-start.2 = (bf16[256,256]{1,0:T(8,128)(2,1)}, bf16[256,256]{1,0:T(8,128)(2,1)S(1)}, u32[]{:S(2)}, u32[]{:S(2)}) collective-permute-start(bf16[256,256]{1,0:T(8,128)(2,1)} %cot.1), channel_id=1, source_target_pairs={{0,2},{1,3},{2,0},{3,1},{4,6},{5,7},{6,4},{7,5},{8,10},{9,11},{10,... | collective-permute-start | bytes 393224 | tf_op jit(solution)/shard_map/ppermute | solution.py:333
  4.5 11.6 %collective-permute-start.4 = (bf16[256,256]{1,0:T(8,128)(2,1)}, bf16[256,256]{1,0:T(8,128)(2,1)S(1)}, u32[]{:S(2)}, u32[]{:S(2)}) collective-permute-start(bf16[256,256]{1,0:T(8,128)(2,1)} %cot.1), channel_id=1, source_target_pairs={{0,3},{1,2},{2,1},{3,0},{4,7},{5,6},{6,5},{7,4},{8,11},{9,10},{10,... | collective-permute-start | bytes 393224 | tf_op jit(solution)/shard_map/ppermute | solution.py:333
  5.5 10.6 %collective-permute-start.3 = (bf16[256,256]{1,0:T(8,128)(2,1)}, bf16[256,256]{1,0:T(8,128)(2,1)S(1)}, u32[]{:S(2)}, u32[]{:S(2)}) collective-permute-start(bf16[256,256]{1,0:T(8,128)(2,1)} %cot.1), channel_id=1, source_target_pairs={{0,1},{1,0},{2,3},{3,2},{4,5},{5,4},{6,7},{7,6},{8,9},{9,8},{10,11... | collective-permute-start | bytes 393224 | tf_op jit(solution)/shard_map/ppermute | solution.py:333
  19.7 3.1 %collective-permute-start.5 = (bf16[160,16,256]{2,1,0:T(8,128)(2,1)S(1)}, bf16[160,16,256]{2,1,0:T(8,128)(2,1)S(1)}, u32[]{:S(2)}, u32[]{:S(2)}) collective-permute-start(bf16[160,16,256]{2,1,0:T(8,128)(2,1)S(1)} %get-tuple-element.65), channel_id=1, source_target_pairs={{0,4},{4,0},{8,12},{12,8},{16,20},{20,16},{24,28},{28,24},{32,36},... | collective-permute-start | bytes 3932168 | tf_op jit(solution)/shard_map/ppermute | solution.py:333
  19.8 8.1 %collective-permute-start.6 = (bf16[2,256,256]{2,1,0:T(8,128)(2,1)S(1)}, bf16[2,256,256]{2,1,0:T(8,128)(2,1)S(1)}, u32[]{:S(2)}, u32[]{:S(2)}) collective-permute-start(bf16[2,256,256]{2,1,0:T(8,128)(2,1)S(1)} %get-tuple-element.66), channel_id=1, source_target_pairs={{0,1},{1,0},{2,3},{3,2},{4,8},{5,9},{6,10},{7,11},{8,4},{9,5},{10,... | collective-permute-start | bytes 786440 | tf_op jit(solution)/shard_map/ppermute | solution.py:333
  23.1 8.7 %collective-permute-start.9 = (bf16[32,16,256]{2,1,0:T(8,128)(2,1)S(1)}, bf16[32,16,256]{2,1,0:T(8,128)(2,1)S(1)}, u32[]{:S(2)}, u32[]{:S(2)}) collective-permute-start(bf16[32,16,256]{2,1,0:T(8,128)(2,1)S(1)} %get-tuple-element.78), channel_id=1, source_target_pairs={{0,56},{4,236},{8,48},{12,228},{16,40},{20,252},{24,32},{28,244},{... | collective-permute-start | bytes 786440 | tf_op jit(solution)/shard_map/ppermute | solution.py:333
  24.9 9.6 %collective-permute-start.10 = (bf16[32,16,256]{2,1,0:T(8,128)(2,1)S(1)}, bf16[32,16,256]{2,1,0:T(8,128)(2,1)S(1)}, u32[]{:S(2)}, u32[]{:S(2)}) collective-permute-start(bf16[32,16,256]{2,1,0:T(8,128)(2,1)S(1)} %get-tuple-element.79), channel_id=1, source_target_pairs={{0,24},{4,12},{8,16},{12,4},{16,8},{20,28},{24,0},{28,20},{32,56},... | collective-permute-start | bytes 786440 | tf_op jit(solution)/shard_map/ppermute | solution.py:333
  25.5 8.9 %collective-permute-start.11 = (bf16[32,16,256]{2,1,0:T(8,128)(2,1)S(1)}, bf16[32,16,256]{2,1,0:T(8,128)(2,1)S(1)}, u32[]{:S(2)}, u32[]{:S(2)}) collective-permute-start(bf16[32,16,256]{2,1,0:T(8,128)(2,1)S(1)} %get-tuple-element.80), channel_id=1, source_target_pairs={{0,32},{4,228},{8,40},{12,236},{16,48},{20,244},{24,56},{28,252},{... | collective-permute-start | bytes 786440 | tf_op jit(solution)/shard_map/ppermute | solution.py:333
  28.6 12.4 %collective-permute-start.7 = (bf16[4,256,256]{2,1,0:T(8,128)(2,1)S(1)}, bf16[4,256,256]{2,1,0:T(8,128)(2,1)S(1)}, u32[]{:S(2)}, u32[]{:S(2)}) collective-permute-start(bf16[4,256,256]{2,1,0:T(8,128)(2,1)S(1)} %get-tuple-element.69), channel_id=1, source_target_pairs={{0,1},{1,0},{2,3},{3,2},{4,7},{5,6},{6,5},{7,4},{8,9},{9,8},{10,11... | collective-permute-start | bytes 1572872 | tf_op jit(solution)/shard_map/ppermute | solution.py:333
  34.6 7.9 %collective-permute-start.12 = (bf16[8,16,256]{2,1,0:T(8,128)(2,1)S(1)}, bf16[8,16,256]{2,1,0:T(8,128)(2,1)S(1)}, u32[]{:S(2)}, u32[]{:S(2)}) collective-permute-start(bf16[8,16,256]{2,1,0:T(8,128)(2,1)S(1)} %get-tuple-element.82), channel_id=1, source_target_pairs={{0,232},{4,60},{8,224},{12,52},{16,248},{20,44},{24,240},{28,36},{... | collective-permute-start | bytes 196616 | tf_op jit(solution)/shard_map/ppermute | solution.py:333
  36.5 6.7 %collective-permute-start.13 = (bf16[8,16,256]{2,1,0:T(8,128)(2,1)S(1)}, bf16[8,16,256]{2,1,0:T(8,128)(2,1)S(1)}, u32[]{:S(2)}, u32[]{:S(2)}) collective-permute-start(bf16[8,16,256]{2,1,0:T(8,128)(2,1)S(1)} %get-tuple-element.83), channel_id=1, source_target_pairs={{0,8},{4,28},{8,0},{12,20},{16,24},{20,12},{24,16},{28,4},{32,40},... | collective-permute-start | bytes 196616 | tf_op jit(solution)/shard_map/ppermute | solution.py:333
  41.0 5.5 %collective-permute-start.14 = (bf16[8,16,256]{2,1,0:T(8,128)(2,1)S(1)}, bf16[8,16,256]{2,1,0:T(8,128)(2,1)S(1)}, u32[]{:S(2)}, u32[]{:S(2)}) collective-permute-start(bf16[8,16,256]{2,1,0:T(8,128)(2,1)S(1)} %get-tuple-element.84), channel_id=1, source_target_pairs={{0,224},{4,36},{8,232},{12,44},{16,240},{20,52},{24,248},{28,60},{... | collective-permute-start | bytes 196616 | tf_op jit(solution)/shard_map/ppermute | solution.py:333
  41.1 7.7 %collective-permute-start.8 = (bf16[2,256,256]{2,1,0:T(8,128)(2,1)S(1)}, bf16[2,256,256]{2,1,0:T(8,128)(2,1)S(1)}, u32[]{:S(2)}, u32[]{:S(2)}) collective-permute-start(bf16[2,256,256]{2,1,0:T(8,128)(2,1)S(1)} %get-tuple-element.71), channel_id=1, source_target_pairs={{0,3},{1,2},{2,1},{3,0},{4,5},{5,4},{6,7},{7,6},{8,11},{9,10},{10,... | collective-permute-start | bytes 786440 | tf_op jit(solution)/shard_map/ppermute | solution.py:333
  46.5 5.8 %collective-permute-start.15 = (bf16[4,16,256]{2,1,0:T(8,128)(2,1)S(1)}, bf16[4,16,256]{2,1,0:T(8,128)(2,1)S(1)}, u32[]{:S(2)}, u32[]{:S(2)}) collective-permute-start(bf16[4,16,256]{2,1,0:T(8,128)(2,1)S(1)} %get-tuple-element.86), channel_id=1, source_target_pairs={{0,96},{4,164},{8,104},{12,172},{16,112},{20,180},{24,120},{28,188... | collective-permute-start | bytes 98312 | tf_op jit(solution)/shard_map/ppermute | solution.py:333

commit v18 on v17

--- a/solution.py
+++ b/solution.py
@@ -90,8 +90,8 @@
 
 
 PARTNERS = (
-    ((y_other, y_pair), (z_pair, z_other, z_far)),
-    ((y_pair, y_other), (z_other, z_pair, z_far_too)),
+    ((y_pair, y_other), (z_pair, z_other, z_far)),
+    ((y_other, y_pair), (z_other, z_pair, z_far_too)),
 )
 
 

time: 53.1 us -> 52.9 us (level); the launches traced: 53 us -> 52.2 us
  waiting for transfers between devices: 18.8 us -> 17.8 us
    ppermute x16, waiting for transfers between devices: 18.8 us -> 17.8 us  [move(): lax.ppermute(value, axis, [(i, target(i)) for i in range(count) if 0 <= t...]
  transfers between devices with their start and end apart: 16 -> 16, of which waited for: 9 -> 10; matrix products, arithmetic and copies ran while one was open for 0% -> 0% of each run, Pallas kernels for 16% -> 16%
where the time goes in v18:
time: 52.9 us; the launch traced here: 52.2 us
  starting transfers between devices  21.2 us (40%)
  waiting for transfers between devices  17.8 us (34%)
  Pallas kernels  12.5 us (24%)
  between operations  0.72 us (1%)
    ppermute x16, starting transfers between devices, move(): lax.ppermute(value, axis, [(i, target(i)) for i in range(count) if 0 <= t...  21.2 us
    ppermute x16, waiting for transfers between devices, move(): lax.ppermute(value, axis, [(i, target(i)) for i in range(count) if 0 <= t...  17.8 us
    pallas_call x11, Pallas kernels, call(): pl.pallas_call(kernel, out_shape=tuple(kept), in_specs=[pl.BlockSpec(memo...  12.5 us
  transfers between devices with their start and end apart: 16, of which 10 were waited for; matrix products, arithmetic and copies ran while one was open for 0% of the time, Pallas kernels for 16%

profile of v18, /device:TPU:6, one launch (start us, length us, event | category | flops | bytes accessed | tf_op | source)
XLA Modules:
  0.0 52.2 jit_solution(17718660966958913446)
XLA Ops:
  0.6 0.1 collective-permute-start.1
  0.7 0.9 %collective-permute-start = (bf16[256,1024]{1,0:T(8,128)(2,1)}, bf16[256,1024]{1,0:T(8,128)(2,1)S(1)}, u32[]{:S(2)}, u32[]{:S(2)}) collective-permute-start(bf16[256,1024]{1,0:T(8,128)(2,1)} %act.1), channel_id=1, source_target_pairs={{0,1},{1,0},{2,3},{3,2},{4,8},{5,9},{6,10},{7,11},{8,4},{9,5},{10,... | collective-permute-start | bytes 1572872 | tf_op jit(solution)/shard_map/ppermute | solution.py:333
  1.6 2.8 %collective-permute-start.2 = (bf16[256,256]{1,0:T(8,128)(2,1)}, bf16[256,256]{1,0:T(8,128)(2,1)S(1)}, u32[]{:S(2)}, u32[]{:S(2)}) collective-permute-start(bf16[256,256]{1,0:T(8,128)(2,1)} %cot.1), channel_id=1, source_target_pairs={{0,2},{1,3},{2,0},{3,1},{4,6},{5,7},{6,4},{7,5},{8,10},{9,11},{10,... | collective-permute-start | bytes 393224 | tf_op jit(solution)/shard_map/ppermute | solution.py:333
  4.5 1.0 %collective-permute-start.4 = (bf16[256,256]{1,0:T(8,128)(2,1)}, bf16[256,256]{1,0:T(8,128)(2,1)S(1)}, u32[]{:S(2)}, u32[]{:S(2)}) collective-permute-start(bf16[256,256]{1,0:T(8,128)(2,1)} %cot.1), channel_id=1, source_target_pairs={{0,3},{1,2},{2,1},{3,0},{4,7},{5,6},{6,5},{7,4},{8,11},{9,10},{10,... | collective-permute-start | bytes 393224 | tf_op jit(solution)/shard_map/ppermute | solution.py:333
  5.5 0.0 collective-permute-start.3
  5.5 0.0 collective-permute-done.1.a_near
  5.5 3.9 %own_part.1 = (bf16[1024,256]{1,0:T(8,128)(2,1)S(1)}, bf16[1024,256]{1,0:T(8,128)(2,1)S(1)}, bf16[1024,256]{1,0:T(8,128)(2,1)S(1)}, bf16[256,1024]{1,0:T(8,128)(...) custom-call(bf16[256,1024]{1,0:T(8,128)(2,1)} %act.1, ...), custom_call_target="tpu_custom_call" | custom-call | flops 600000000 | bytes 6000000 | tf_op jit(solution)/shard_map/own_part/pallas_call | solution.py:318
  9.5 3.5 %collective-permute-done.a_far = bf16[256,1024]{1,0:T(8,128)(2,1)S(1)} collective-permute-done((bf16[256,1024]{1,0:T(8,128)(2,1)}, bf16[256,1024]{1,0:T(8,128)(2,1)S(1)}, u32[]{:S(2)}, u32[]{:S(2)}) %collective-permute-start) | collective-permute-done | bytes 524320 | tf_op jit(solution)/shard_map/ppermute | solution.py:333
  13.0 1.6 %forward.1 = (bf16[768,256]{1,0:T(8,128)(2,1)S(1)}, bf16[768,256]{1,0:T(8,128)(2,1)S(1)}, bf16[768,1024]{1,0:T(8,128)(2,1)S(1)}, bf16[256,256]{1,0:T(8,128)(2,1)S(1)}, bf16[1024,256]{1,0:T(8,128)(2,1)S(1)}) custom-call(bf16[256,1024]{1,0:T(8,128)(2,1)S(1)} %collective-permute-done.a_far, bf16[1024,256]{1,0:T(8,128)(2,1)S(1)} %get-tuple-element.45.wk, ...), custom_call_target="tpu_custom_call" | custom-call | flops 2000000000 | bytes 6000000 | tf_op jit(solution)/shard_map/forward/pallas_call | solution.py:318
  14.6 1.5 %collective-permute-done.2.c2 = bf16[256,256]{1,0:T(8,128)(2,1)S(1)} collective-permute-done((bf16[256,256]{1,0:T(8,128)(2,1)}, bf16[256,256]{1,0:T(8,128)(2,1)S(1)}, u32[]{:S(2)}, u32[]{:S(2)}) %collective-permute-start.2) | collective-permute-done | bytes 131104 | tf_op jit(solution)/shard_map/ppermute | solution.py:333
  16.1 0.0 collective-permute-done.4.c3
  16.1 0.0 collective-permute-done.3.c1
  16.1 3.6 %backward.1 = (bf16[256,256]{1,0:T(8,128)(2,1)S(1)}, bf16[2,256,256]{2,1,0:T(8,128)(2,1)S(1)}, f32[2,256,256]{2,1,0:T(8,128)S(1)}, bf16[768,256]{1,0:T(8,128)(2,...) custom-call(bf16[768,256]{1,0:T(8,128)(2,1)S(1)} %get-tuple-element.54.keys, ...), custom_call_target="tpu_custom_call" | custom-call | flops 2000000000 | bytes 8000000 | tf_op jit(solution)/shard_map/backward/pallas_call | solution.py:318
  19.7 0.1 collective-permute-start.5
  19.8 0.7 %collective-permute-start.6 = (bf16[2,256,256]{2,1,0:T(8,128)(2,1)S(1)}, bf16[2,256,256]{2,1,0:T(8,128)(2,1)S(1)}, u32[]{:S(2)}, u32[]{:S(2)}) collective-permute-start(bf16[2,256,256]{2,1,0:T(8,128)(2,1)S(1)} %get-tuple-element.66), channel_id=1, source_target_pairs={{0,1},{1,0},{2,3},{3,2},{4,8},{5,9},{6,10},{7,11},{8,4},{9,5},{10,... | collective-permute-start | bytes 786440 | tf_op jit(solution)/shard_map/ppermute | solution.py:333
  20.5 0.8 %keep_terms.1.refs_0_ = bf16[128,16,256]{2,1,0:T(8,128)(2,1)S(1)} custom-call(bf16[1024,256]{1,0:T(8,128)(2,1)S(1)} %get-tuple-element.60.act_t, bf16[1024,256]{1,0:T(8,128)(2,1)S(1)} %get-tuple-element.57.far_t, bf16[1024,256]{1,0:T(8,128)(2,1)S(1)} %get-tuple-element.58.near_t, bf16[1024,256]{1,0:T(8,128)(2,1)S(1)} %get-tuple-element.74.cot_t, ...), custom_call_target="tpu_custom_call" | custom-call | flops 1000000000 | bytes 4000000 | tf_op jit(solution)/shard_map/keep_terms/pallas_call | solution.py:318
  21.3 1.5 %collective-permute-done.5.near.refs_1_ = bf16[160,16,256]{2,1,0:T(8,128)(2,1)S(1)} collective-permute-done((bf16[160,16,256]{2,1,0:T(8,128)(2,1)S(1)}, bf16[160,16,256]{2,1,0:T(8,128)(2,1)S(1)}, u32[]{:S(2)}, u32[]{:S(2)}) %collective-permute-start.5) | collective-permute-done | bytes 1310752 | tf_op jit(solution)/shard_map/ppermute | solution.py:333
  22.8 0.2 core_sum.1
  23.1 0.1 collective-permute-start.9
  23.2 1.2 %collective-permute-start.10 = (bf16[32,16,256]{2,1,0:T(8,128)(2,1)S(1)}, bf16[32,16,256]{2,1,0:T(8,128)(2,1)S(1)}, u32[]{:S(2)}, u32[]{:S(2)}) collective-permute-start(bf16[32,16,256]{2,1,0:T(8,128)(2,1)S(1)} %get-tuple-element.79), channel_id=1, source_target_pairs={{0,8},{4,28},{8,0},{12,20},{16,24},{20,12},{24,16},{28,4},{32,40},... | collective-permute-start | bytes 786440 | tf_op jit(solution)/shard_map/ppermute | solution.py:333
  24.3 2.3 %collective-permute-start.11 = (bf16[32,16,256]{2,1,0:T(8,128)(2,1)S(1)}, bf16[32,16,256]{2,1,0:T(8,128)(2,1)S(1)}, u32[]{:S(2)}, u32[]{:S(2)}) collective-permute-start(bf16[32,16,256]{2,1,0:T(8,128)(2,1)S(1)} %get-tuple-element.80), channel_id=1, source_target_pairs={{0,32},{4,228},{8,40},{12,236},{16,48},{20,244},{24,56},{28,252},{... | collective-permute-start | bytes 786440 | tf_op jit(solution)/shard_map/ppermute | solution.py:333
  26.6 0.0 collective-permute-done.6.far
  26.6 0.7 %input_grad.1 = (f32[4,256,256]{2,1,0:T(8,128)S(1)}, bf16[4,256,256]{2,1,0:T(8,128)(2,1)S(1)}) custom-call(bf16[256,256]{1,0:T(8,128)(2,1)S(1)} %get-tuple-element.53.att, bf16[256,256]{1,0:T(8,128)(2,1)S(1)} %get-tuple-element.63.gq, f32[2,256,256]{2,1,0:T(8,128)S(1)} %get-tuple-element.64.own, ...), custom_call_target="tpu_custom_call" | custom-call | flops 540000000 | bytes 4000000 | tf_op jit(solution)/shard_map/input_grad/pallas_call | solution.py:318
  27.4 0.7 %collective-permute-start.7 = (bf16[4,256,256]{2,1,0:T(8,128)(2,1)S(1)}, bf16[4,256,256]{2,1,0:T(8,128)(2,1)S(1)}, u32[]{:S(2)}, u32[]{:S(2)}) collective-permute-start(bf16[4,256,256]{2,1,0:T(8,128)(2,1)S(1)} %get-tuple-element.69), channel_id=1, source_target_pairs={{0,1},{1,0},{2,3},{3,2},{4,7},{5,6},{6,5},{7,4},{8,9},{9,8},{10,11... | collective-permute-start | bytes 1572872 | tf_op jit(solution)/shard_map/ppermute | solution.py:333
  28.0 2.5 %collective-permute-done.9.refs_1_ = bf16[32,16,256]{2,1,0:T(8,128)(2,1)S(1)} collective-permute-done((bf16[32,16,256]{2,1,0:T(8,128)(2,1)S(1)}, bf16[32,16,256]{2,1,0:T(8,128)(2,1)S(1)}, u32[]{:S(2)}, u32[]{:S(2)}) %collective-permute-start.9) | collective-permute-done | bytes 262176 | tf_op jit(solution)/shard_map/ppermute | solution.py:333
  30.5 2.1 %collective-permute-done.10.refs_2_ = bf16[32,16,256]{2,1,0:T(8,128)(2,1)S(1)} collective-permute-done((bf16[32,16,256]{2,1,0:T(8,128)(2,1)S(1)}, bf16[32,16,256]{2,1,0:T(8,128)(2,1)S(1)}, u32[]{:S(2)}, u32[]{:S(2)}) %collective-permute-start.10) | collective-permute-done | bytes 262176 | tf_op jit(solution)/shard_map/ppermute | solution.py:333
  32.6 0.0 collective-permute-done.11.refs_3_
  32.6 0.1 first_sum.1
  32.7 7.0 %collective-permute-start.12 = (bf16[8,16,256]{2,1,0:T(8,128)(2,1)S(1)}, bf16[8,16,256]{2,1,0:T(8,128)(2,1)S(1)}, u32[]{:S(2)}, u32[]{:S(2)}) collective-permute-start(bf16[8,16,256]{2,1,0:T(8,128)(2,1)S(1)} %get-tuple-element.82), channel_id=1, source_target_pairs={{0,248},{4,44},{8,240},{12,36},{16,232},{20,60},{24,224},{28,52},{... | collective-permute-start | bytes 196616 | tf_op jit(solution)/shard_map/ppermute | solution.py:333
  39.8 0.4 collective-permute-start.13
  40.2 0.2 collective-permute-start.14
  40.4 0.0 collective-permute-done.7.refs_1_
  40.4 0.1 mp_share.1
  40.5 1.4 %collective-permute-start.8 = (bf16[2,256,256]{2,1,0:T(8,128)(2,1)S(1)}, bf16[2,256,256]{2,1,0:T(8,128)(2,1)S(1)}, u32[]{:S(2)}, u32[]{:S(2)}) collective-permute-start(bf16[2,256,256]{2,1,0:T(8,128)(2,1)S(1)} %get-tuple-element.71), channel_id=1, source_target_pairs={{0,3},{1,2},{2,1},{3,0},{4,5},{5,4},{6,7},{7,6},{8,11},{9,10},{10,... | collective-permute-start | bytes 786440 | tf_op jit(solution)/shard_map/ppermute | solution.py:333
  41.9 0.1 collective-permute-done.12.refs_1_
  42.0 3.2 %collective-permute-done.13.refs_2_ = bf16[8,16,256]{2,1,0:T(8,128)(2,1)S(1)} collective-permute-done((bf16[8,16,256]{2,1,0:T(8,128)(2,1)S(1)}, bf16[8,16,256]{2,1,0:T(8,128)(2,1)S(1)}, u32[]{:S(2)}, u32[]{:S(2)}) %collective-permute-start.13) | collective-permute-done | bytes 65568 | tf_op jit(solution)/shard_map/ppermute | solution.py:333
  45.3 0.4 collective-permute-done.14.refs_3_
  45.7 2.2 %collective-permute-start.15 = (bf16[4,16,256]{2,1,0:T(8,128)(2,1)S(1)}, bf16[4,16,256]{2,1,0:T(8,128)(2,1)S(1)}, u32[]{:S(2)}, u32[]{:S(2)}) collective-permute-start(bf16[4,16,256]{2,1,0:T(8,128)(2,1)S(1)} %get-tuple-element.86), channel_id=1, source_target_pairs={{0,96},{4,164},{8,104},{12,172},{16,112},{20,180},{24,120},{28,188... | collective-permute-start | bytes 98312 | tf_op jit(solution)/shard_map/ppermute | solution.py:333
  47.9 0.3 collective-permute-done.8.got
  48.2 0.7 %mp_sum.1 = (bf16[256,256]{1,0:T(8,128)(2,1)}, bf16[256,256]{1,0:T(8,128)(2,1)}) custom-call(f32[2,256,256]{2,1,0:T(8,128)S(1)} %get-tuple-element.70.kept, bf16[2,256,256]{2,1,0:T(8,128)(2,1)S(1)} %collective-permute-done.8.got), custom_call_target="tpu_custom_call" | custom-call | bytes 1000000 | tf_op jit(solution)/shard_map/mp_sum/pallas_call | solution.py:318
  48.9 2.6 %collective-permute-done.15.got = bf16[4,16,256]{2,1,0:T(8,128)(2,1)S(1)} collective-permute-done((bf16[4,16,256]{2,1,0:T(8,128)(2,1)S(1)}, bf16[4,16,256]{2,1,0:T(8,128)(2,1)S(1)}, u32[]{:S(2)}, u32[]{:S(2)}) %collective-permute-start.15) | collective-permute-done | bytes 32800 | tf_op jit(solution)/shard_map/ppermute | solution.py:333
  51.5 0.6 %last_sum.1 = f32[4,16,256]{2,1,0:T(8,128)} custom-call(bf16[256,256]{1,0:T(8,128)(2,1)} %get-tuple-element.42.after, f32[4,16,256]{2,1,0:T(8,128)S(1)} %get-tuple-element.85.kept, bf16[4,16,256]{2,1,0:T(8,128)(2,1)S(1)} %collective-permute-done.15.got), custom_call_target="tpu_custom_call" | custom-call | bytes 1000000 | tf_op jit(solution)/shard_map/last_sum/pallas_call | solution.py:318
  (1 shorter events, 0.0 us)
Async XLA Ops:
  0.6 4.9 %collective-permute-start.1 = (bf16[256,1024]{1,0:T(8,128)(2,1)}, bf16[256,1024]{1,0:T(8,128)(2,1)S(1)}, u32[]{:S(2)}, u32[]{:S(2)}) collective-permute-start(bf16[256,1024]{1,0:T(8,128)(2,1)} %act.1), channel_id=1, source_target_pairs={{0,4},{4,0},{8,12},{12,8},{16,20},{20,16},{24,28},{28,24},{32,36},... | collective-permute-start | bytes 1572872 | tf_op jit(solution)/shard_map/ppermute | solution.py:333
  0.7 12.3 %collective-permute-start = (bf16[256,1024]{1,0:T(8,128)(2,1)}, bf16[256,1024]{1,0:T(8,128)(2,1)S(1)}, u32[]{:S(2)}, u32[]{:S(2)}) collective-permute-start(bf16[256,1024]{1,0:T(8,128)(2,1)} %act.1), channel_id=1, source_target_pairs={{0,1},{1,0},{2,3},{3,2},{4,8},{5,9},{6,10},{7,11},{8,4},{9,5},{10,... | collective-permute-start | bytes 1572872 | tf_op jit(solution)/shard_map/ppermute | solution.py:333
  1.6 14.4 %collective-permute-start.2 = (bf16[256,256]{1,0:T(8,128)(2,1)}, bf16[256,256]{1,0:T(8,128)(2,1)S(1)}, u32[]{:S(2)}, u32[]{:S(2)}) collective-permute-start(bf16[256,256]{1,0:T(8,128)(2,1)} %cot.1), channel_id=1, source_target_pairs={{0,2},{1,3},{2,0},{3,1},{4,6},{5,7},{6,4},{7,5},{8,10},{9,11},{10,... | collective-permute-start | bytes 393224 | tf_op jit(solution)/shard_map/ppermute | solution.py:333
  4.5 11.6 %collective-permute-start.4 = (bf16[256,256]{1,0:T(8,128)(2,1)}, bf16[256,256]{1,0:T(8,128)(2,1)S(1)}, u32[]{:S(2)}, u32[]{:S(2)}) collective-permute-start(bf16[256,256]{1,0:T(8,128)(2,1)} %cot.1), channel_id=1, source_target_pairs={{0,3},{1,2},{2,1},{3,0},{4,7},{5,6},{6,5},{7,4},{8,11},{9,10},{10,... | collective-permute-start | bytes 393224 | tf_op jit(solution)/shard_map/ppermute | solution.py:333
  5.5 10.6 %collective-permute-start.3 = (bf16[256,256]{1,0:T(8,128)(2,1)}, bf16[256,256]{1,0:T(8,128)(2,1)S(1)}, u32[]{:S(2)}, u32[]{:S(2)}) collective-permute-start(bf16[256,256]{1,0:T(8,128)(2,1)} %cot.1), channel_id=1, source_target_pairs={{0,1},{1,0},{2,3},{3,2},{4,5},{5,4},{6,7},{7,6},{8,9},{9,8},{10,11... | collective-permute-start | bytes 393224 | tf_op jit(solution)/shard_map/ppermute | solution.py:333
  19.7 3.1 %collective-permute-start.5 = (bf16[160,16,256]{2,1,0:T(8,128)(2,1)S(1)}, bf16[160,16,256]{2,1,0:T(8,128)(2,1)S(1)}, u32[]{:S(2)}, u32[]{:S(2)}) collective-permute-start(bf16[160,16,256]{2,1,0:T(8,128)(2,1)S(1)} %get-tuple-element.65), channel_id=1, source_target_pairs={{0,4},{4,0},{8,12},{12,8},{16,20},{20,16},{24,28},{28,24},{32,36},... | collective-permute-start | bytes 3932168 | tf_op jit(solution)/shard_map/ppermute | solution.py:333
  19.8 6.8 %collective-permute-start.6 = (bf16[2,256,256]{2,1,0:T(8,128)(2,1)S(1)}, bf16[2,256,256]{2,1,0:T(8,128)(2,1)S(1)}, u32[]{:S(2)}, u32[]{:S(2)}) collective-permute-start(bf16[2,256,256]{2,1,0:T(8,128)(2,1)S(1)} %get-tuple-element.66), channel_id=1, source_target_pairs={{0,1},{1,0},{2,3},{3,2},{4,8},{5,9},{6,10},{7,11},{8,4},{9,5},{10,... | collective-permute-start | bytes 786440 | tf_op jit(solution)/shard_map/ppermute | solution.py:333
  23.1 7.5 %collective-permute-start.9 = (bf16[32,16,256]{2,1,0:T(8,128)(2,1)S(1)}, bf16[32,16,256]{2,1,0:T(8,128)(2,1)S(1)}, u32[]{:S(2)}, u32[]{:S(2)}) collective-permute-start(bf16[32,16,256]{2,1,0:T(8,128)(2,1)S(1)} %get-tuple-element.78), channel_id=1, source_target_pairs={{0,40},{4,252},{8,32},{12,244},{16,56},{20,236},{24,48},{28,228},{... | collective-permute-start | bytes 786440 | tf_op jit(solution)/shard_map/ppermute | solution.py:333
  23.2 9.4 %collective-permute-start.10 = (bf16[32,16,256]{2,1,0:T(8,128)(2,1)S(1)}, bf16[32,16,256]{2,1,0:T(8,128)(2,1)S(1)}, u32[]{:S(2)}, u32[]{:S(2)}) collective-permute-start(bf16[32,16,256]{2,1,0:T(8,128)(2,1)S(1)} %get-tuple-element.79), channel_id=1, source_target_pairs={{0,8},{4,28},{8,0},{12,20},{16,24},{20,12},{24,16},{28,4},{32,40},... | collective-permute-start | bytes 786440 | tf_op jit(solution)/shard_map/ppermute | solution.py:333
  24.3 8.3 %collective-permute-start.11 = (bf16[32,16,256]{2,1,0:T(8,128)(2,1)S(1)}, bf16[32,16,256]{2,1,0:T(8,128)(2,1)S(1)}, u32[]{:S(2)}, u32[]{:S(2)}) collective-permute-start(bf16[32,16,256]{2,1,0:T(8,128)(2,1)S(1)} %get-tuple-element.80), channel_id=1, source_target_pairs={{0,32},{4,228},{8,40},{12,236},{16,48},{20,244},{24,56},{28,252},{... | collective-permute-start | bytes 786440 | tf_op jit(solution)/shard_map/ppermute | solution.py:333
  27.4 13.1 %collective-permute-start.7 = (bf16[4,256,256]{2,1,0:T(8,128)(2,1)S(1)}, bf16[4,256,256]{2,1,0:T(8,128)(2,1)S(1)}, u32[]{:S(2)}, u32[]{:S(2)}) collective-permute-start(bf16[4,256,256]{2,1,0:T(8,128)(2,1)S(1)} %get-tuple-element.69), channel_id=1, source_target_pairs={{0,1},{1,0},{2,3},{3,2},{4,7},{5,6},{6,5},{7,4},{8,9},{9,8},{10,11... | collective-permute-start | bytes 1572872 | tf_op jit(solution)/shard_map/ppermute | solution.py:333
  32.7 9.3 %collective-permute-start.12 = (bf16[8,16,256]{2,1,0:T(8,128)(2,1)S(1)}, bf16[8,16,256]{2,1,0:T(8,128)(2,1)S(1)}, u32[]{:S(2)}, u32[]{:S(2)}) collective-permute-start(bf16[8,16,256]{2,1,0:T(8,128)(2,1)S(1)} %get-tuple-element.82), channel_id=1, source_target_pairs={{0,248},{4,44},{8,240},{12,36},{16,232},{20,60},{24,224},{28,52},{... | collective-permute-start | bytes 196616 | tf_op jit(solution)/shard_map/ppermute | solution.py:333
  39.8 5.5 %collective-permute-start.13 = (bf16[8,16,256]{2,1,0:T(8,128)(2,1)S(1)}, bf16[8,16,256]{2,1,0:T(8,128)(2,1)S(1)}, u32[]{:S(2)}, u32[]{:S(2)}) collective-permute-start(bf16[8,16,256]{2,1,0:T(8,128)(2,1)S(1)} %get-tuple-element.83), channel_id=1, source_target_pairs={{0,24},{4,12},{8,16},{12,4},{16,8},{20,28},{24,0},{28,20},{32,56},... | collective-permute-start | bytes 196616 | tf_op jit(solution)/shard_map/ppermute | solution.py:333
  40.2 5.5 %collective-permute-start.14 = (bf16[8,16,256]{2,1,0:T(8,128)(2,1)S(1)}, bf16[8,16,256]{2,1,0:T(8,128)(2,1)S(1)}, u32[]{:S(2)}, u32[]{:S(2)}) collective-permute-start(bf16[8,16,256]{2,1,0:T(8,128)(2,1)S(1)} %get-tuple-element.84), channel_id=1, source_target_pairs={{0,224},{4,36},{8,232},{12,44},{16,240},{20,52},{24,248},{28,60},{... | collective-permute-start | bytes 196616 | tf_op jit(solution)/shard_map/ppermute | solution.py:333
  40.5 7.7 %collective-permute-start.8 = (bf16[2,256,256]{2,1,0:T(8,128)(2,1)S(1)}, bf16[2,256,256]{2,1,0:T(8,128)(2,1)S(1)}, u32[]{:S(2)}, u32[]{:S(2)}) collective-permute-start(bf16[2,256,256]{2,1,0:T(8,128)(2,1)S(1)} %get-tuple-element.71), channel_id=1, source_target_pairs={{0,3},{1,2},{2,1},{3,0},{4,5},{5,4},{6,7},{7,6},{8,11},{9,10},{10,... | collective-permute-start | bytes 786440 | tf_op jit(solution)/shard_map/ppermute | solution.py:333
  45.7 5.8 %collective-permute-start.15 = (bf16[4,16,256]{2,1,0:T(8,128)(2,1)S(1)}, bf16[4,16,256]{2,1,0:T(8,128)(2,1)S(1)}, u32[]{:S(2)}, u32[]{:S(2)}) collective-permute-start(bf16[4,16,256]{2,1,0:T(8,128)(2,1)S(1)} %get-tuple-element.86), channel_id=1, source_target_pairs={{0,96},{4,164},{8,104},{12,172},{16,112},{20,180},{24,120},{28,188... | collective-permute-start | bytes 98312 | tf_op jit(solution)/shard_map/ppermute | solution.py:333

commit v19 on v18

--- a/solution.py
+++ b/solution.py
@@ -350,7 +350,7 @@
     def target(i):
         row, x = i // 4, i % 4
         if row in (0, 63):
-            return row * 4 + (x ^ 1)
+            return row * 4 + (x ^ 3)
         return (row + 1 if row % 2 else row - 1) * 4 + x
 
     return move(value, SPACE + ("mp",), target)

time: 52.9 us -> 53.9 us (1.019)
  waiting for transfers between devices: 17.8 us -> 18.5 us
    ppermute x16, waiting for transfers between devices: 17.8 us -> 18.5 us  [move(): lax.ppermute(value, axis, [(i, target(i)) for i in range(count) if 0 <= t...]
  transfers between devices with their start and end apart: 16 -> 16, of which waited for: 10 -> 9; matrix products, arithmetic and copies ran while one was open for 0% -> 0% of each run, Pallas kernels for 16% -> 16%
where the time goes in v19:
time: 53.9 us; the launch traced here: 53.2 us
  starting transfers between devices  21.4 us (40%)
  waiting for transfers between devices  18.5 us (34%)
  Pallas kernels  12.6 us (23%)
  between operations  0.76 us (1%)
    ppermute x16, starting transfers between devices, move(): lax.ppermute(value, axis, [(i, target(i)) for i in range(count) if 0 <= t...  21.4 us
    ppermute x16, waiting for transfers between devices, move(): lax.ppermute(value, axis, [(i, target(i)) for i in range(count) if 0 <= t...  18.5 us
    pallas_call x11, Pallas kernels, call(): pl.pallas_call(kernel, out_shape=tuple(kept), in_specs=[pl.BlockSpec(memo...  12.6 us
  transfers between devices with their start and end apart: 16, of which 9 were waited for; matrix products, arithmetic and copies ran while one was open for 0% of the time, Pallas kernels for 16%

profile of v19, /device:TPU:6, one launch (start us, length us, event | category | flops | bytes accessed | tf_op | source)
XLA Modules:
  0.0 53.2 jit_solution(10517585348352902075)
XLA Ops:
  0.6 0.1 collective-permute-start.1
  0.7 2.3 %collective-permute-start = (bf16[256,1024]{1,0:T(8,128)(2,1)}, bf16[256,1024]{1,0:T(8,128)(2,1)S(1)}, u32[]{:S(2)}, u32[]{:S(2)}) collective-permute-start(bf16[256,1024]{1,0:T(8,128)(2,1)} %act.1), channel_id=1, source_target_pairs={{0,3},{1,2},{2,1},{3,0},{4,8},{5,9},{6,10},{7,11},{8,4},{9,5},{10,... | collective-permute-start | bytes 1572872 | tf_op jit(solution)/shard_map/ppermute | solution.py:333
  3.0 0.7 %collective-permute-start.2 = (bf16[256,256]{1,0:T(8,128)(2,1)}, bf16[256,256]{1,0:T(8,128)(2,1)S(1)}, u32[]{:S(2)}, u32[]{:S(2)}) collective-permute-start(bf16[256,256]{1,0:T(8,128)(2,1)} %cot.1), channel_id=1, source_target_pairs={{0,2},{1,3},{2,0},{3,1},{4,6},{5,7},{6,4},{7,5},{8,10},{9,11},{10,... | collective-permute-start | bytes 393224 | tf_op jit(solution)/shard_map/ppermute | solution.py:333
  3.7 1.1 %collective-permute-start.4 = (bf16[256,256]{1,0:T(8,128)(2,1)}, bf16[256,256]{1,0:T(8,128)(2,1)S(1)}, u32[]{:S(2)}, u32[]{:S(2)}) collective-permute-start(bf16[256,256]{1,0:T(8,128)(2,1)} %cot.1), channel_id=1, source_target_pairs={{0,3},{1,2},{2,1},{3,0},{4,7},{5,6},{6,5},{7,4},{8,11},{9,10},{10,... | collective-permute-start | bytes 393224 | tf_op jit(solution)/shard_map/ppermute | solution.py:333
  4.9 1.7 %collective-permute-start.3 = (bf16[256,256]{1,0:T(8,128)(2,1)}, bf16[256,256]{1,0:T(8,128)(2,1)S(1)}, u32[]{:S(2)}, u32[]{:S(2)}) collective-permute-start(bf16[256,256]{1,0:T(8,128)(2,1)} %cot.1), channel_id=1, source_target_pairs={{0,1},{1,0},{2,3},{3,2},{4,5},{5,4},{6,7},{7,6},{8,9},{9,8},{10,11... | collective-permute-start | bytes 393224 | tf_op jit(solution)/shard_map/ppermute | solution.py:333
  6.5 0.0 collective-permute-done.1.a_near
  6.5 3.9 %own_part.1 = (bf16[1024,256]{1,0:T(8,128)(2,1)S(1)}, bf16[1024,256]{1,0:T(8,128)(2,1)S(1)}, bf16[1024,256]{1,0:T(8,128)(2,1)S(1)}, bf16[256,1024]{1,0:T(8,128)(...) custom-call(bf16[256,1024]{1,0:T(8,128)(2,1)} %act.1, ...), custom_call_target="tpu_custom_call" | custom-call | flops 600000000 | bytes 6000000 | tf_op jit(solution)/shard_map/own_part/pallas_call | solution.py:318
  10.5 5.2 %collective-permute-done.a_far = bf16[256,1024]{1,0:T(8,128)(2,1)S(1)} collective-permute-done((bf16[256,1024]{1,0:T(8,128)(2,1)}, bf16[256,1024]{1,0:T(8,128)(2,1)S(1)}, u32[]{:S(2)}, u32[]{:S(2)}) %collective-permute-start) | collective-permute-done | bytes 524320 | tf_op jit(solution)/shard_map/ppermute | solution.py:333
  15.6 1.6 %forward.1 = (bf16[768,256]{1,0:T(8,128)(2,1)S(1)}, bf16[768,256]{1,0:T(8,128)(2,1)S(1)}, bf16[768,1024]{1,0:T(8,128)(2,1)S(1)}, bf16[256,256]{1,0:T(8,128)(2,1)S(1)}, bf16[1024,256]{1,0:T(8,128)(2,1)S(1)}) custom-call(bf16[256,1024]{1,0:T(8,128)(2,1)S(1)} %collective-permute-done.a_far, bf16[1024,256]{1,0:T(8,128)(2,1)S(1)} %get-tuple-element.45.wk, ...), custom_call_target="tpu_custom_call" | custom-call | flops 2000000000 | bytes 6000000 | tf_op jit(solution)/shard_map/forward/pallas_call | solution.py:318
  17.2 0.0 collective-permute-done.2.c2
  17.2 0.0 collective-permute-done.4.c3
  17.3 0.0 collective-permute-done.3.c1
  17.3 3.6 %backward.1 = (bf16[256,256]{1,0:T(8,128)(2,1)S(1)}, bf16[2,256,256]{2,1,0:T(8,128)(2,1)S(1)}, f32[2,256,256]{2,1,0:T(8,128)S(1)}, bf16[768,256]{1,0:T(8,128)(2,...) custom-call(bf16[768,256]{1,0:T(8,128)(2,1)S(1)} %get-tuple-element.54.keys, ...), custom_call_target="tpu_custom_call" | custom-call | flops 2000000000 | bytes 8000000 | tf_op jit(solution)/shard_map/backward/pallas_call | solution.py:318
  20.9 0.1 collective-permute-start.5
  21.0 2.0 %collective-permute-start.6 = (bf16[2,256,256]{2,1,0:T(8,128)(2,1)S(1)}, bf16[2,256,256]{2,1,0:T(8,128)(2,1)S(1)}, u32[]{:S(2)}, u32[]{:S(2)}) collective-permute-start(bf16[2,256,256]{2,1,0:T(8,128)(2,1)S(1)} %get-tuple-element.66), channel_id=1, source_target_pairs={{0,3},{1,2},{2,1},{3,0},{4,8},{5,9},{6,10},{7,11},{8,4},{9,5},{10,... | collective-permute-start | bytes 786440 | tf_op jit(solution)/shard_map/ppermute | solution.py:333
  23.0 0.8 %keep_terms.1.refs_0_ = bf16[128,16,256]{2,1,0:T(8,128)(2,1)S(1)} custom-call(bf16[1024,256]{1,0:T(8,128)(2,1)S(1)} %get-tuple-element.60.act_t, bf16[1024,256]{1,0:T(8,128)(2,1)S(1)} %get-tuple-element.57.far_t, bf16[1024,256]{1,0:T(8,128)(2,1)S(1)} %get-tuple-element.58.near_t, bf16[1024,256]{1,0:T(8,128)(2,1)S(1)} %get-tuple-element.74.cot_t, ...), custom_call_target="tpu_custom_call" | custom-call | flops 1000000000 | bytes 4000000 | tf_op jit(solution)/shard_map/keep_terms/pallas_call | solution.py:318
  23.9 0.2 collective-permute-done.5.near.refs_1_
  24.0 0.2 core_sum.1
  24.3 0.1 collective-permute-start.9
  24.4 0.3 collective-permute-start.10
  24.6 3.2 %collective-permute-start.11 = (bf16[32,16,256]{2,1,0:T(8,128)(2,1)S(1)}, bf16[32,16,256]{2,1,0:T(8,128)(2,1)S(1)}, u32[]{:S(2)}, u32[]{:S(2)}) collective-permute-start(bf16[32,16,256]{2,1,0:T(8,128)(2,1)S(1)} %get-tuple-element.80), channel_id=1, source_target_pairs={{0,32},{4,228},{8,40},{12,236},{16,48},{20,244},{24,56},{28,252},{... | collective-permute-start | bytes 786440 | tf_op jit(solution)/shard_map/ppermute | solution.py:333
  27.8 0.8 %collective-permute-done.6.far = bf16[2,256,256]{2,1,0:T(8,128)(2,1)S(1)} collective-permute-done((bf16[2,256,256]{2,1,0:T(8,128)(2,1)S(1)}, bf16[2,256,256]{2,1,0:T(8,128)(2,1)S(1)}, u32[]{:S(2)}, u32[]{:S(2)}) %collective-permute-start.6) | collective-permute-done | bytes 262176 | tf_op jit(solution)/shard_map/ppermute | solution.py:333
  28.7 0.7 %input_grad.1 = (f32[4,256,256]{2,1,0:T(8,128)S(1)}, bf16[4,256,256]{2,1,0:T(8,128)(2,1)S(1)}) custom-call(bf16[256,256]{1,0:T(8,128)(2,1)S(1)} %get-tuple-element.53.att, bf16[256,256]{1,0:T(8,128)(2,1)S(1)} %get-tuple-element.63.gq, f32[2,256,256]{2,1,0:T(8,128)S(1)} %get-tuple-element.64.own, ...), custom_call_target="tpu_custom_call" | custom-call | flops 540000000 | bytes 4000000 | tf_op jit(solution)/shard_map/input_grad/pallas_call | solution.py:318
  29.4 0.1 collective-permute-start.7
  29.5 2.2 %collective-permute-done.9.refs_1_ = bf16[32,16,256]{2,1,0:T(8,128)(2,1)S(1)} collective-permute-done((bf16[32,16,256]{2,1,0:T(8,128)(2,1)S(1)}, bf16[32,16,256]{2,1,0:T(8,128)(2,1)S(1)}, u32[]{:S(2)}, u32[]{:S(2)}) %collective-permute-start.9) | collective-permute-done | bytes 262176 | tf_op jit(solution)/shard_map/ppermute | solution.py:333
  31.7 2.1 %collective-permute-done.10.refs_2_ = bf16[32,16,256]{2,1,0:T(8,128)(2,1)S(1)} collective-permute-done((bf16[32,16,256]{2,1,0:T(8,128)(2,1)S(1)}, bf16[32,16,256]{2,1,0:T(8,128)(2,1)S(1)}, u32[]{:S(2)}, u32[]{:S(2)}) %collective-permute-start.10) | collective-permute-done | bytes 262176 | tf_op jit(solution)/shard_map/ppermute | solution.py:333
  33.8 0.0 collective-permute-done.11.refs_3_
  33.8 0.1 first_sum.1
  34.0 7.3 %collective-permute-start.12 = (bf16[8,16,256]{2,1,0:T(8,128)(2,1)S(1)}, bf16[8,16,256]{2,1,0:T(8,128)(2,1)S(1)}, u32[]{:S(2)}, u32[]{:S(2)}) collective-permute-start(bf16[8,16,256]{2,1,0:T(8,128)(2,1)S(1)} %get-tuple-element.82), channel_id=1, source_target_pairs={{0,248},{4,44},{8,240},{12,36},{16,232},{20,60},{24,224},{28,52},{... | collective-permute-start | bytes 196616 | tf_op jit(solution)/shard_map/ppermute | solution.py:333
  41.2 0.0 collective-permute-start.13
  41.2 0.7 %collective-permute-start.14 = (bf16[8,16,256]{2,1,0:T(8,128)(2,1)S(1)}, bf16[8,16,256]{2,1,0:T(8,128)(2,1)S(1)}, u32[]{:S(2)}, u32[]{:S(2)}) collective-permute-start(bf16[8,16,256]{2,1,0:T(8,128)(2,1)S(1)} %get-tuple-element.84), channel_id=1, source_target_pairs={{0,224},{4,36},{8,232},{12,44},{16,240},{20,52},{24,248},{28,60},{... | collective-permute-start | bytes 196616 | tf_op jit(solution)/shard_map/ppermute | solution.py:333
  41.9 0.0 collective-permute-done.7.refs_1_
  41.9 0.1 mp_share.1
  42.0 0.6 %collective-permute-start.8 = (bf16[2,256,256]{2,1,0:T(8,128)(2,1)S(1)}, bf16[2,256,256]{2,1,0:T(8,128)(2,1)S(1)}, u32[]{:S(2)}, u32[]{:S(2)}) collective-permute-start(bf16[2,256,256]{2,1,0:T(8,128)(2,1)S(1)} %get-tuple-element.71), channel_id=1, source_target_pairs={{0,3},{1,2},{2,1},{3,0},{4,5},{5,4},{6,7},{7,6},{8,11},{9,10},{10,... | collective-permute-start | bytes 786440 | tf_op jit(solution)/shard_map/ppermute | solution.py:333
  42.6 0.9 %collective-permute-done.12.refs_1_ = bf16[8,16,256]{2,1,0:T(8,128)(2,1)S(1)} collective-permute-done((bf16[8,16,256]{2,1,0:T(8,128)(2,1)S(1)}, bf16[8,16,256]{2,1,0:T(8,128)(2,1)S(1)}, u32[]{:S(2)}, u32[]{:S(2)}) %collective-permute-start.12) | collective-permute-done | bytes 65568 | tf_op jit(solution)/shard_map/ppermute | solution.py:333
  43.5 3.2 %collective-permute-done.13.refs_2_ = bf16[8,16,256]{2,1,0:T(8,128)(2,1)S(1)} collective-permute-done((bf16[8,16,256]{2,1,0:T(8,128)(2,1)S(1)}, bf16[8,16,256]{2,1,0:T(8,128)(2,1)S(1)}, u32[]{:S(2)}, u32[]{:S(2)}) %collective-permute-start.13) | collective-permute-done | bytes 65568 | tf_op jit(solution)/shard_map/ppermute | solution.py:333
  46.7 0.0 collective-permute-done.14.refs_3_
  46.7 1.2 %collective-permute-start.15 = (bf16[4,16,256]{2,1,0:T(8,128)(2,1)S(1)}, bf16[4,16,256]{2,1,0:T(8,128)(2,1)S(1)}, u32[]{:S(2)}, u32[]{:S(2)}) collective-permute-start(bf16[4,16,256]{2,1,0:T(8,128)(2,1)S(1)} %get-tuple-element.86), channel_id=1, source_target_pairs={{0,96},{4,164},{8,104},{12,172},{16,112},{20,180},{24,120},{28,188... | collective-permute-start | bytes 98312 | tf_op jit(solution)/shard_map/ppermute | solution.py:333
  47.9 1.7 %collective-permute-done.8.got = bf16[2,256,256]{2,1,0:T(8,128)(2,1)S(1)} collective-permute-done((bf16[2,256,256]{2,1,0:T(8,128)(2,1)S(1)}, bf16[2,256,256]{2,1,0:T(8,128)(2,1)S(1)}, u32[]{:S(2)}, u32[]{:S(2)}) %collective-permute-start.8) | collective-permute-done | bytes 262176 | tf_op jit(solution)/shard_map/ppermute | solution.py:333
  49.7 0.7 %mp_sum.1 = (bf16[256,256]{1,0:T(8,128)(2,1)}, bf16[256,256]{1,0:T(8,128)(2,1)}) custom-call(f32[2,256,256]{2,1,0:T(8,128)S(1)} %get-tuple-element.70.kept, bf16[2,256,256]{2,1,0:T(8,128)(2,1)S(1)} %collective-permute-done.8.got), custom_call_target="tpu_custom_call" | custom-call | bytes 1000000 | tf_op jit(solution)/shard_map/mp_sum/pallas_call | solution.py:318
  50.4 2.2 %collective-permute-done.15.got = bf16[4,16,256]{2,1,0:T(8,128)(2,1)S(1)} collective-permute-done((bf16[4,16,256]{2,1,0:T(8,128)(2,1)S(1)}, bf16[4,16,256]{2,1,0:T(8,128)(2,1)S(1)}, u32[]{:S(2)}, u32[]{:S(2)}) %collective-permute-start.15) | collective-permute-done | bytes 32800 | tf_op jit(solution)/shard_map/ppermute | solution.py:333
  52.5 0.6 %last_sum.1 = f32[4,16,256]{2,1,0:T(8,128)} custom-call(bf16[256,256]{1,0:T(8,128)(2,1)} %get-tuple-element.42.after, f32[4,16,256]{2,1,0:T(8,128)S(1)} %get-tuple-element.85.kept, bf16[4,16,256]{2,1,0:T(8,128)(2,1)S(1)} %collective-permute-done.15.got), custom_call_target="tpu_custom_call" | custom-call | bytes 1000000 | tf_op jit(solution)/shard_map/last_sum/pallas_call | solution.py:318
  (1 shorter events, 0.0 us)
Async XLA Ops:
  0.6 5.9 %collective-permute-start.1 = (bf16[256,1024]{1,0:T(8,128)(2,1)}, bf16[256,1024]{1,0:T(8,128)(2,1)S(1)}, u32[]{:S(2)}, u32[]{:S(2)}) collective-permute-start(bf16[256,1024]{1,0:T(8,128)(2,1)} %act.1), channel_id=1, source_target_pairs={{0,4},{4,0},{8,12},{12,8},{16,20},{20,16},{24,28},{28,24},{32,36},... | collective-permute-start | bytes 1572872 | tf_op jit(solution)/shard_map/ppermute | solution.py:333
  0.7 14.9 %collective-permute-start = (bf16[256,1024]{1,0:T(8,128)(2,1)}, bf16[256,1024]{1,0:T(8,128)(2,1)S(1)}, u32[]{:S(2)}, u32[]{:S(2)}) collective-permute-start(bf16[256,1024]{1,0:T(8,128)(2,1)} %act.1), channel_id=1, source_target_pairs={{0,3},{1,2},{2,1},{3,0},{4,8},{5,9},{6,10},{7,11},{8,4},{9,5},{10,... | collective-permute-start | bytes 1572872 | tf_op jit(solution)/shard_map/ppermute | solution.py:333
  3.0 14.2 %collective-permute-start.2 = (bf16[256,256]{1,0:T(8,128)(2,1)}, bf16[256,256]{1,0:T(8,128)(2,1)S(1)}, u32[]{:S(2)}, u32[]{:S(2)}) collective-permute-start(bf16[256,256]{1,0:T(8,128)(2,1)} %cot.1), channel_id=1, source_target_pairs={{0,2},{1,3},{2,0},{3,1},{4,6},{5,7},{6,4},{7,5},{8,10},{9,11},{10,... | collective-permute-start | bytes 393224 | tf_op jit(solution)/shard_map/ppermute | solution.py:333
  3.7 13.5 %collective-permute-start.4 = (bf16[256,256]{1,0:T(8,128)(2,1)}, bf16[256,256]{1,0:T(8,128)(2,1)S(1)}, u32[]{:S(2)}, u32[]{:S(2)}) collective-permute-start(bf16[256,256]{1,0:T(8,128)(2,1)} %cot.1), channel_id=1, source_target_pairs={{0,3},{1,2},{2,1},{3,0},{4,7},{5,6},{6,5},{7,4},{8,11},{9,10},{10,... | collective-permute-start | bytes 393224 | tf_op jit(solution)/shard_map/ppermute | solution.py:333
  4.9 12.4 %collective-permute-start.3 = (bf16[256,256]{1,0:T(8,128)(2,1)}, bf16[256,256]{1,0:T(8,128)(2,1)S(1)}, u32[]{:S(2)}, u32[]{:S(2)}) collective-permute-start(bf16[256,256]{1,0:T(8,128)(2,1)} %cot.1), channel_id=1, source_target_pairs={{0,1},{1,0},{2,3},{3,2},{4,5},{5,4},{6,7},{7,6},{8,9},{9,8},{10,11... | collective-permute-start | bytes 393224 | tf_op jit(solution)/shard_map/ppermute | solution.py:333
  20.9 3.1 %collective-permute-start.5 = (bf16[160,16,256]{2,1,0:T(8,128)(2,1)S(1)}, bf16[160,16,256]{2,1,0:T(8,128)(2,1)S(1)}, u32[]{:S(2)}, u32[]{:S(2)}) collective-permute-start(bf16[160,16,256]{2,1,0:T(8,128)(2,1)S(1)} %get-tuple-element.65), channel_id=1, source_target_pairs={{0,4},{4,0},{8,12},{12,8},{16,20},{20,16},{24,28},{28,24},{32,36},... | collective-permute-start | bytes 3932168 | tf_op jit(solution)/shard_map/ppermute | solution.py:333
  21.0 7.7 %collective-permute-start.6 = (bf16[2,256,256]{2,1,0:T(8,128)(2,1)S(1)}, bf16[2,256,256]{2,1,0:T(8,128)(2,1)S(1)}, u32[]{:S(2)}, u32[]{:S(2)}) collective-permute-start(bf16[2,256,256]{2,1,0:T(8,128)(2,1)S(1)} %get-tuple-element.66), channel_id=1, source_target_pairs={{0,3},{1,2},{2,1},{3,0},{4,8},{5,9},{6,10},{7,11},{8,4},{9,5},{10,... | collective-permute-start | bytes 786440 | tf_op jit(solution)/shard_map/ppermute | solution.py:333
  24.3 7.5 %collective-permute-start.9 = (bf16[32,16,256]{2,1,0:T(8,128)(2,1)S(1)}, bf16[32,16,256]{2,1,0:T(8,128)(2,1)S(1)}, u32[]{:S(2)}, u32[]{:S(2)}) collective-permute-start(bf16[32,16,256]{2,1,0:T(8,128)(2,1)S(1)} %get-tuple-element.78), channel_id=1, source_target_pairs={{0,40},{4,252},{8,32},{12,244},{16,56},{20,236},{24,48},{28,228},{... | collective-permute-start | bytes 786440 | tf_op jit(solution)/shard_map/ppermute | solution.py:333
  24.4 9.4 %collective-permute-start.10 = (bf16[32,16,256]{2,1,0:T(8,128)(2,1)S(1)}, bf16[32,16,256]{2,1,0:T(8,128)(2,1)S(1)}, u32[]{:S(2)}, u32[]{:S(2)}) collective-permute-start(bf16[32,16,256]{2,1,0:T(8,128)(2,1)S(1)} %get-tuple-element.79), channel_id=1, source_target_pairs={{0,8},{4,28},{8,0},{12,20},{16,24},{20,12},{24,16},{28,4},{32,40},... | collective-permute-start | bytes 786440 | tf_op jit(solution)/shard_map/ppermute | solution.py:333
  24.6 9.2 %collective-permute-start.11 = (bf16[32,16,256]{2,1,0:T(8,128)(2,1)S(1)}, bf16[32,16,256]{2,1,0:T(8,128)(2,1)S(1)}, u32[]{:S(2)}, u32[]{:S(2)}) collective-permute-start(bf16[32,16,256]{2,1,0:T(8,128)(2,1)S(1)} %get-tuple-element.80), channel_id=1, source_target_pairs={{0,32},{4,228},{8,40},{12,236},{16,48},{20,244},{24,56},{28,252},{... | collective-permute-start | bytes 786440 | tf_op jit(solution)/shard_map/ppermute | solution.py:333
  29.4 12.5 %collective-permute-start.7 = (bf16[4,256,256]{2,1,0:T(8,128)(2,1)S(1)}, bf16[4,256,256]{2,1,0:T(8,128)(2,1)S(1)}, u32[]{:S(2)}, u32[]{:S(2)}) collective-permute-start(bf16[4,256,256]{2,1,0:T(8,128)(2,1)S(1)} %get-tuple-element.69), channel_id=1, source_target_pairs={{0,1},{1,0},{2,3},{3,2},{4,7},{5,6},{6,5},{7,4},{8,9},{9,8},{10,11... | collective-permute-start | bytes 1572872 | tf_op jit(solution)/shard_map/ppermute | solution.py:333
  34.0 9.5 %collective-permute-start.12 = (bf16[8,16,256]{2,1,0:T(8,128)(2,1)S(1)}, bf16[8,16,256]{2,1,0:T(8,128)(2,1)S(1)}, u32[]{:S(2)}, u32[]{:S(2)}) collective-permute-start(bf16[8,16,256]{2,1,0:T(8,128)(2,1)S(1)} %get-tuple-element.82), channel_id=1, source_target_pairs={{0,248},{4,44},{8,240},{12,36},{16,232},{20,60},{24,224},{28,52},{... | collective-permute-start | bytes 196616 | tf_op jit(solution)/shard_map/ppermute | solution.py:333
  41.2 5.5 %collective-permute-start.13 = (bf16[8,16,256]{2,1,0:T(8,128)(2,1)S(1)}, bf16[8,16,256]{2,1,0:T(8,128)(2,1)S(1)}, u32[]{:S(2)}, u32[]{:S(2)}) collective-permute-start(bf16[8,16,256]{2,1,0:T(8,128)(2,1)S(1)} %get-tuple-element.83), channel_id=1, source_target_pairs={{0,24},{4,12},{8,16},{12,4},{16,8},{20,28},{24,0},{28,20},{32,56},... | collective-permute-start | bytes 196616 | tf_op jit(solution)/shard_map/ppermute | solution.py:333
  41.2 5.5 %collective-permute-start.14 = (bf16[8,16,256]{2,1,0:T(8,128)(2,1)S(1)}, bf16[8,16,256]{2,1,0:T(8,128)(2,1)S(1)}, u32[]{:S(2)}, u32[]{:S(2)}) collective-permute-start(bf16[8,16,256]{2,1,0:T(8,128)(2,1)S(1)} %get-tuple-element.84), channel_id=1, source_target_pairs={{0,224},{4,36},{8,232},{12,44},{16,240},{20,52},{24,248},{28,60},{... | collective-permute-start | bytes 196616 | tf_op jit(solution)/shard_map/ppermute | solution.py:333
  42.0 7.7 %collective-permute-start.8 = (bf16[2,256,256]{2,1,0:T(8,128)(2,1)S(1)}, bf16[2,256,256]{2,1,0:T(8,128)(2,1)S(1)}, u32[]{:S(2)}, u32[]{:S(2)}) collective-permute-start(bf16[2,256,256]{2,1,0:T(8,128)(2,1)S(1)} %get-tuple-element.71), channel_id=1, source_target_pairs={{0,3},{1,2},{2,1},{3,0},{4,5},{5,4},{6,7},{7,6},{8,11},{9,10},{10,... | collective-permute-start | bytes 786440 | tf_op jit(solution)/shard_map/ppermute | solution.py:333
  46.7 5.8 %collective-permute-start.15 = (bf16[4,16,256]{2,1,0:T(8,128)(2,1)S(1)}, bf16[4,16,256]{2,1,0:T(8,128)(2,1)S(1)}, u32[]{:S(2)}, u32[]{:S(2)}) collective-permute-start(bf16[4,16,256]{2,1,0:T(8,128)(2,1)S(1)} %get-tuple-element.86), channel_id=1, source_target_pairs={{0,96},{4,164},{8,104},{12,172},{16,112},{20,180},{24,120},{28,188... | collective-permute-start | bytes 98312 | tf_op jit(solution)/shard_map/ppermute | solution.py:333

commit v20 on v18

--- a/solution.py
+++ b/solution.py
@@ -225,13 +225,13 @@
 
 
 def backward_kernel(
-    keys, values, probs_in, att, far_t, near_t, wo, query, act_t, grad_in, cot_own, c2, c1, c3,
+    keys, values, probs_in, att, far_t, near_t, wo, query, act_t, grad_in, cot_own, c3, c2, c1,
     gq, far_out, own_out, grad_key, grad_value, cot_t, send_out,
     grad_s, scores_s, scores_t, dw_s,
 ):
     core, y, z, x = places()
     grad_att = grad_in[...]
-    blocks = ((x ^ 2, c2), (x ^ 1, c1), (x ^ 3, c3))
+    blocks = ((x ^ 3, c3), (x ^ 2, c2), (x ^ 1, c1))
     for place, block in blocks:
         grad_att += mm(block[...], columns(wo, place), NT)
     stack_heads(grad_att.astype(BF), grad_s)
@@ -358,7 +358,7 @@
 
 def body(activations, w_query, w_key, w_value, w_out, grad_output, neighbours, pad_mask):
     act_far = far_row(activations)
-    cots = [move(grad_output, "mp", lambda i, step=step: i ^ step) for step in (2, 1, 3)]
+    cots = [move(grad_output, "mp", lambda i, step=step: i ^ step) for step in (3, 2, 1)]
     act_near = near_row(activations)
 
     square = (ROW, WIDTH)

time: 52.9 us -> 54.2 us (1.025)
  the two profiles are of different devices: /device:TPU:6 before, /device:TPU:24 now
where the time goes in v20:
time: 54.2 us; the launch traced here: 54.1 us
  starting transfers between devices  23.2 us (43%)
  waiting for transfers between devices  17.7 us (33%)
  Pallas kernels  12.5 us (23%)
  between operations  0.74 us (1%)
    ppermute x16, starting transfers between devices, move(): lax.ppermute(value, axis, [(i, target(i)) for i in range(count) if 0 <= t...  23.2 us
    ppermute x16, waiting for transfers between devices, move(): lax.ppermute(value, axis, [(i, target(i)) for i in range(count) if 0 <= t...  17.7 us
    pallas_call x11, Pallas kernels, call(): pl.pallas_call(kernel, out_shape=tuple(kept), in_specs=[pl.BlockSpec(memo...  12.5 us
  transfers between devices with their start and end apart: 16, of which 8 were waited for; matrix products, arithmetic and copies ran while one was open for 0% of the time, Pallas kernels for 15%

profile of v20, /device:TPU:24, one launch (start us, length us, event | category | flops | bytes accessed | tf_op | source)
XLA Modules:
  0.0 54.1 jit_solution(7415423713826899022)
XLA Ops:
  0.6 0.1 collective-permute-start.1
  0.7 0.8 %collective-permute-start = (bf16[256,1024]{1,0:T(8,128)(2,1)}, bf16[256,1024]{1,0:T(8,128)(2,1)S(1)}, u32[]{:S(2)}, u32[]{:S(2)}) collective-permute-start(bf16[256,1024]{1,0:T(8,128)(2,1)} %act.1), channel_id=1, source_target_pairs={{0,1},{1,0},{2,3},{3,2},{4,8},{5,9},{6,10},{7,11},{8,4},{9,5},{10,... | collective-permute-start | bytes 1572872 | tf_op jit(solution)/shard_map/ppermute | solution.py:333
  1.6 2.8 %collective-permute-start.2 = (bf16[256,256]{1,0:T(8,128)(2,1)}, bf16[256,256]{1,0:T(8,128)(2,1)S(1)}, u32[]{:S(2)}, u32[]{:S(2)}) collective-permute-start(bf16[256,256]{1,0:T(8,128)(2,1)} %cot.1), channel_id=1, source_target_pairs={{0,3},{1,2},{2,1},{3,0},{4,7},{5,6},{6,5},{7,4},{8,11},{9,10},{10,... | collective-permute-start | bytes 393224 | tf_op jit(solution)/shard_map/ppermute | solution.py:333
  4.3 0.2 collective-permute-start.4
  4.6 1.7 %collective-permute-start.3 = (bf16[256,256]{1,0:T(8,128)(2,1)}, bf16[256,256]{1,0:T(8,128)(2,1)S(1)}, u32[]{:S(2)}, u32[]{:S(2)}) collective-permute-start(bf16[256,256]{1,0:T(8,128)(2,1)} %cot.1), channel_id=1, source_target_pairs={{0,2},{1,3},{2,0},{3,1},{4,6},{5,7},{6,4},{7,5},{8,10},{9,11},{10,... | collective-permute-start | bytes 393224 | tf_op jit(solution)/shard_map/ppermute | solution.py:333
  6.3 0.0 collective-permute-done.1.a_near
  6.3 3.9 %own_part.1 = (bf16[1024,256]{1,0:T(8,128)(2,1)S(1)}, bf16[1024,256]{1,0:T(8,128)(2,1)S(1)}, bf16[1024,256]{1,0:T(8,128)(2,1)S(1)}, bf16[256,1024]{1,0:T(8,128)(...) custom-call(bf16[256,1024]{1,0:T(8,128)(2,1)} %act.1, ...), custom_call_target="tpu_custom_call" | custom-call | flops 600000000 | bytes 6000000 | tf_op jit(solution)/shard_map/own_part/pallas_call | solution.py:318
  10.2 0.0 collective-permute-done.a_far
  10.3 1.6 %forward.1 = (bf16[768,256]{1,0:T(8,128)(2,1)S(1)}, bf16[768,256]{1,0:T(8,128)(2,1)S(1)}, bf16[768,1024]{1,0:T(8,128)(2,1)S(1)}, bf16[256,256]{1,0:T(8,128)(2,1)S(1)}, bf16[1024,256]{1,0:T(8,128)(2,1)S(1)}) custom-call(bf16[256,1024]{1,0:T(8,128)(2,1)S(1)} %collective-permute-done.a_far, bf16[1024,256]{1,0:T(8,128)(2,1)S(1)} %get-tuple-element.45.wk, ...), custom_call_target="tpu_custom_call" | custom-call | flops 2000000000 | bytes 6000000 | tf_op jit(solution)/shard_map/forward/pallas_call | solution.py:318
  11.9 0.0 collective-permute-done.2.c3
  11.9 0.0 collective-permute-done.4.c1
  11.9 1.5 %collective-permute-done.3.c2 = bf16[256,256]{1,0:T(8,128)(2,1)S(1)} collective-permute-done((bf16[256,256]{1,0:T(8,128)(2,1)}, bf16[256,256]{1,0:T(8,128)(2,1)S(1)}, u32[]{:S(2)}, u32[]{:S(2)}) %collective-permute-start.3) | collective-permute-done | bytes 131104 | tf_op jit(solution)/shard_map/ppermute | solution.py:333
  13.3 3.6 %backward.1 = (bf16[256,256]{1,0:T(8,128)(2,1)S(1)}, bf16[2,256,256]{2,1,0:T(8,128)(2,1)S(1)}, f32[2,256,256]{2,1,0:T(8,128)S(1)}, bf16[768,256]{1,0:T(8,128)(2,...) custom-call(bf16[768,256]{1,0:T(8,128)(2,1)S(1)} %get-tuple-element.54.keys, ...), custom_call_target="tpu_custom_call" | custom-call | flops 2000000000 | bytes 8000000 | tf_op jit(solution)/shard_map/backward/pallas_call | solution.py:318
  16.9 0.9 %collective-permute-start.5 = (bf16[160,16,256]{2,1,0:T(8,128)(2,1)S(1)}, bf16[160,16,256]{2,1,0:T(8,128)(2,1)S(1)}, u32[]{:S(2)}, u32[]{:S(2)}) collective-permute-start(bf16[160,16,256]{2,1,0:T(8,128)(2,1)S(1)} %get-tuple-element.65), channel_id=1, source_target_pairs={{0,4},{4,0},{8,12},{12,8},{16,20},{20,16},{24,28},{28,24},{32,36},... | collective-permute-start | bytes 3932168 | tf_op jit(solution)/shard_map/ppermute | solution.py:333
  17.8 0.0 collective-permute-start.6
  17.8 0.8 %keep_terms.1.refs_0_ = bf16[128,16,256]{2,1,0:T(8,128)(2,1)S(1)} custom-call(bf16[1024,256]{1,0:T(8,128)(2,1)S(1)} %get-tuple-element.60.act_t, bf16[1024,256]{1,0:T(8,128)(2,1)S(1)} %get-tuple-element.57.far_t, bf16[1024,256]{1,0:T(8,128)(2,1)S(1)} %get-tuple-element.58.near_t, bf16[1024,256]{1,0:T(8,128)(2,1)S(1)} %get-tuple-element.74.cot_t, ...), custom_call_target="tpu_custom_call" | custom-call | flops 1000000000 | bytes 4000000 | tf_op jit(solution)/shard_map/keep_terms/pallas_call | solution.py:318
  18.6 1.8 %collective-permute-done.5.near.refs_1_ = bf16[160,16,256]{2,1,0:T(8,128)(2,1)S(1)} collective-permute-done((bf16[160,16,256]{2,1,0:T(8,128)(2,1)S(1)}, bf16[160,16,256]{2,1,0:T(8,128)(2,1)S(1)}, u32[]{:S(2)}, u32[]{:S(2)}) %collective-permute-start.5) | collective-permute-done | bytes 1310752 | tf_op jit(solution)/shard_map/ppermute | solution.py:333
  20.5 0.2 core_sum.1
  20.7 1.5 %collective-permute-start.9 = (bf16[32,16,256]{2,1,0:T(8,128)(2,1)S(1)}, bf16[32,16,256]{2,1,0:T(8,128)(2,1)S(1)}, u32[]{:S(2)}, u32[]{:S(2)}) collective-permute-start(bf16[32,16,256]{2,1,0:T(8,128)(2,1)S(1)} %get-tuple-element.78), channel_id=1, source_target_pairs={{0,40},{4,252},{8,32},{12,244},{16,56},{20,236},{24,48},{28,228},{... | collective-permute-start | bytes 786440 | tf_op jit(solution)/shard_map/ppermute | solution.py:333
  22.2 2.0 %collective-permute-start.10 = (bf16[32,16,256]{2,1,0:T(8,128)(2,1)S(1)}, bf16[32,16,256]{2,1,0:T(8,128)(2,1)S(1)}, u32[]{:S(2)}, u32[]{:S(2)}) collective-permute-start(bf16[32,16,256]{2,1,0:T(8,128)(2,1)S(1)} %get-tuple-element.79), channel_id=1, source_target_pairs={{0,8},{4,28},{8,0},{12,20},{16,24},{20,12},{24,16},{28,4},{32,40},... | collective-permute-start | bytes 786440 | tf_op jit(solution)/shard_map/ppermute | solution.py:333
  24.2 0.1 collective-permute-start.11
  24.3 0.0 collective-permute-done.6.far
  24.3 0.7 %input_grad.1 = (f32[4,256,256]{2,1,0:T(8,128)S(1)}, bf16[4,256,256]{2,1,0:T(8,128)(2,1)S(1)}) custom-call(bf16[256,256]{1,0:T(8,128)(2,1)S(1)} %get-tuple-element.53.att, bf16[256,256]{1,0:T(8,128)(2,1)S(1)} %get-tuple-element.63.gq, f32[2,256,256]{2,1,0:T(8,128)S(1)} %get-tuple-element.64.own, ...), custom_call_target="tpu_custom_call" | custom-call | flops 540000000 | bytes 4000000 | tf_op jit(solution)/shard_map/input_grad/pallas_call | solution.py:318
  25.0 1.3 %collective-permute-start.7 = (bf16[4,256,256]{2,1,0:T(8,128)(2,1)S(1)}, bf16[4,256,256]{2,1,0:T(8,128)(2,1)S(1)}, u32[]{:S(2)}, u32[]{:S(2)}) collective-permute-start(bf16[4,256,256]{2,1,0:T(8,128)(2,1)S(1)} %get-tuple-element.69), channel_id=1, source_target_pairs={{0,1},{1,0},{2,3},{3,2},{4,7},{5,6},{6,5},{7,4},{8,9},{9,8},{10,11... | collective-permute-start | bytes 1572872 | tf_op jit(solution)/shard_map/ppermute | solution.py:333
  26.3 1.9 %collective-permute-done.9.refs_1_ = bf16[32,16,256]{2,1,0:T(8,128)(2,1)S(1)} collective-permute-done((bf16[32,16,256]{2,1,0:T(8,128)(2,1)S(1)}, bf16[32,16,256]{2,1,0:T(8,128)(2,1)S(1)}, u32[]{:S(2)}, u32[]{:S(2)}) %collective-permute-start.9) | collective-permute-done | bytes 262176 | tf_op jit(solution)/shard_map/ppermute | solution.py:333
  28.2 2.7 %collective-permute-done.10.refs_2_ = bf16[32,16,256]{2,1,0:T(8,128)(2,1)S(1)} collective-permute-done((bf16[32,16,256]{2,1,0:T(8,128)(2,1)S(1)}, bf16[32,16,256]{2,1,0:T(8,128)(2,1)S(1)}, u32[]{:S(2)}, u32[]{:S(2)}) %collective-permute-start.10) | collective-permute-done | bytes 262176 | tf_op jit(solution)/shard_map/ppermute | solution.py:333
  30.9 0.0 collective-permute-done.11.refs_3_
  30.9 0.1 first_sum.1
  31.0 6.5 %collective-permute-start.12 = (bf16[8,16,256]{2,1,0:T(8,128)(2,1)S(1)}, bf16[8,16,256]{2,1,0:T(8,128)(2,1)S(1)}, u32[]{:S(2)}, u32[]{:S(2)}) collective-permute-start(bf16[8,16,256]{2,1,0:T(8,128)(2,1)S(1)} %get-tuple-element.82), channel_id=1, source_target_pairs={{0,248},{4,44},{8,240},{12,36},{16,232},{20,60},{24,224},{28,52},{... | collective-permute-start | bytes 196616 | tf_op jit(solution)/shard_map/ppermute | solution.py:333
  37.5 4.7 %collective-permute-start.13 = (bf16[8,16,256]{2,1,0:T(8,128)(2,1)S(1)}, bf16[8,16,256]{2,1,0:T(8,128)(2,1)S(1)}, u32[]{:S(2)}, u32[]{:S(2)}) collective-permute-start(bf16[8,16,256]{2,1,0:T(8,128)(2,1)S(1)} %get-tuple-element.83), channel_id=1, source_target_pairs={{0,24},{4,12},{8,16},{12,4},{16,8},{20,28},{24,0},{28,20},{32,56},... | collective-permute-start | bytes 196616 | tf_op jit(solution)/shard_map/ppermute | solution.py:333
  42.2 0.0 collective-permute-start.14
  42.2 0.0 collective-permute-done.7.refs_1_
  42.2 0.1 mp_share.1
  42.3 0.6 %collective-permute-start.8 = (bf16[2,256,256]{2,1,0:T(8,128)(2,1)S(1)}, bf16[2,256,256]{2,1,0:T(8,128)(2,1)S(1)}, u32[]{:S(2)}, u32[]{:S(2)}) collective-permute-start(bf16[2,256,256]{2,1,0:T(8,128)(2,1)S(1)} %get-tuple-element.71), channel_id=1, source_target_pairs={{0,3},{1,2},{2,1},{3,0},{4,5},{5,4},{6,7},{7,6},{8,11},{9,10},{10,... | collective-permute-start | bytes 786440 | tf_op jit(solution)/shard_map/ppermute | solution.py:333
  42.9 0.0 collective-permute-done.12.refs_1_
  42.9 1.6 %collective-permute-done.13.refs_2_ = bf16[8,16,256]{2,1,0:T(8,128)(2,1)S(1)} collective-permute-done((bf16[8,16,256]{2,1,0:T(8,128)(2,1)S(1)}, bf16[8,16,256]{2,1,0:T(8,128)(2,1)S(1)}, u32[]{:S(2)}, u32[]{:S(2)}) %collective-permute-start.13) | collective-permute-done | bytes 65568 | tf_op jit(solution)/shard_map/ppermute | solution.py:333
  44.4 3.2 %collective-permute-done.14.refs_3_ = bf16[8,16,256]{2,1,0:T(8,128)(2,1)S(1)} collective-permute-done((bf16[8,16,256]{2,1,0:T(8,128)(2,1)S(1)}, bf16[8,16,256]{2,1,0:T(8,128)(2,1)S(1)}, u32[]{:S(2)}, u32[]{:S(2)}) %collective-permute-start.14) | collective-permute-done | bytes 65568 | tf_op jit(solution)/shard_map/ppermute | solution.py:333
  47.7 0.1 collective-permute-start.15
  47.8 2.2 %collective-permute-done.8.got = bf16[2,256,256]{2,1,0:T(8,128)(2,1)S(1)} collective-permute-done((bf16[2,256,256]{2,1,0:T(8,128)(2,1)S(1)}, bf16[2,256,256]{2,1,0:T(8,128)(2,1)S(1)}, u32[]{:S(2)}, u32[]{:S(2)}) %collective-permute-start.8) | collective-permute-done | bytes 262176 | tf_op jit(solution)/shard_map/ppermute | solution.py:333
  50.0 0.7 %mp_sum.1 = (bf16[256,256]{1,0:T(8,128)(2,1)}, bf16[256,256]{1,0:T(8,128)(2,1)}) custom-call(f32[2,256,256]{2,1,0:T(8,128)S(1)} %get-tuple-element.70.kept, bf16[2,256,256]{2,1,0:T(8,128)(2,1)S(1)} %collective-permute-done.8.got), custom_call_target="tpu_custom_call" | custom-call | bytes 1000000 | tf_op jit(solution)/shard_map/mp_sum/pallas_call | solution.py:318
  50.7 2.8 %collective-permute-done.15.got = bf16[4,16,256]{2,1,0:T(8,128)(2,1)S(1)} collective-permute-done((bf16[4,16,256]{2,1,0:T(8,128)(2,1)S(1)}, bf16[4,16,256]{2,1,0:T(8,128)(2,1)S(1)}, u32[]{:S(2)}, u32[]{:S(2)}) %collective-permute-start.15) | collective-permute-done | bytes 32800 | tf_op jit(solution)/shard_map/ppermute | solution.py:333
  53.5 0.6 %last_sum.1 = f32[4,16,256]{2,1,0:T(8,128)} custom-call(bf16[256,256]{1,0:T(8,128)(2,1)} %get-tuple-element.42.after, f32[4,16,256]{2,1,0:T(8,128)S(1)} %get-tuple-element.85.kept, bf16[4,16,256]{2,1,0:T(8,128)(2,1)S(1)} %collective-permute-done.15.got), custom_call_target="tpu_custom_call" | custom-call | bytes 1000000 | tf_op jit(solution)/shard_map/last_sum/pallas_call | solution.py:318
  (1 shorter events, 0.0 us)
Async XLA Ops:
  0.6 5.7 %collective-permute-start.1 = (bf16[256,1024]{1,0:T(8,128)(2,1)}, bf16[256,1024]{1,0:T(8,128)(2,1)S(1)}, u32[]{:S(2)}, u32[]{:S(2)}) collective-permute-start(bf16[256,1024]{1,0:T(8,128)(2,1)} %act.1), channel_id=1, source_target_pairs={{0,4},{4,0},{8,12},{12,8},{16,20},{20,16},{24,28},{28,24},{32,36},... | collective-permute-start | bytes 1572872 | tf_op jit(solution)/shard_map/ppermute | solution.py:333
  0.7 9.5 %collective-permute-start = (bf16[256,1024]{1,0:T(8,128)(2,1)}, bf16[256,1024]{1,0:T(8,128)(2,1)S(1)}, u32[]{:S(2)}, u32[]{:S(2)}) collective-permute-start(bf16[256,1024]{1,0:T(8,128)(2,1)} %act.1), channel_id=1, source_target_pairs={{0,1},{1,0},{2,3},{3,2},{4,8},{5,9},{6,10},{7,11},{8,4},{9,5},{10,... | collective-permute-start | bytes 1572872 | tf_op jit(solution)/shard_map/ppermute | solution.py:333
  1.6 10.3 %collective-permute-start.2 = (bf16[256,256]{1,0:T(8,128)(2,1)}, bf16[256,256]{1,0:T(8,128)(2,1)S(1)}, u32[]{:S(2)}, u32[]{:S(2)}) collective-permute-start(bf16[256,256]{1,0:T(8,128)(2,1)} %cot.1), channel_id=1, source_target_pairs={{0,3},{1,2},{2,1},{3,0},{4,7},{5,6},{6,5},{7,4},{8,11},{9,10},{10,... | collective-permute-start | bytes 393224 | tf_op jit(solution)/shard_map/ppermute | solution.py:333
  4.3 7.5 %collective-permute-start.4 = (bf16[256,256]{1,0:T(8,128)(2,1)}, bf16[256,256]{1,0:T(8,128)(2,1)S(1)}, u32[]{:S(2)}, u32[]{:S(2)}) collective-permute-start(bf16[256,256]{1,0:T(8,128)(2,1)} %cot.1), channel_id=1, source_target_pairs={{0,1},{1,0},{2,3},{3,2},{4,5},{5,4},{6,7},{7,6},{8,9},{9,8},{10,11... | collective-permute-start | bytes 393224 | tf_op jit(solution)/shard_map/ppermute | solution.py:333
  4.6 8.8 %collective-permute-start.3 = (bf16[256,256]{1,0:T(8,128)(2,1)}, bf16[256,256]{1,0:T(8,128)(2,1)S(1)}, u32[]{:S(2)}, u32[]{:S(2)}) collective-permute-start(bf16[256,256]{1,0:T(8,128)(2,1)} %cot.1), channel_id=1, source_target_pairs={{0,2},{1,3},{2,0},{3,1},{4,6},{5,7},{6,4},{7,5},{8,10},{9,11},{10,... | collective-permute-start | bytes 393224 | tf_op jit(solution)/shard_map/ppermute | solution.py:333
  16.9 3.5 %collective-permute-start.5 = (bf16[160,16,256]{2,1,0:T(8,128)(2,1)S(1)}, bf16[160,16,256]{2,1,0:T(8,128)(2,1)S(1)}, u32[]{:S(2)}, u32[]{:S(2)}) collective-permute-start(bf16[160,16,256]{2,1,0:T(8,128)(2,1)S(1)} %get-tuple-element.65), channel_id=1, source_target_pairs={{0,4},{4,0},{8,12},{12,8},{16,20},{20,16},{24,28},{28,24},{32,36},... | collective-permute-start | bytes 3932168 | tf_op jit(solution)/shard_map/ppermute | solution.py:333
  17.8 6.5 %collective-permute-start.6 = (bf16[2,256,256]{2,1,0:T(8,128)(2,1)S(1)}, bf16[2,256,256]{2,1,0:T(8,128)(2,1)S(1)}, u32[]{:S(2)}, u32[]{:S(2)}) collective-permute-start(bf16[2,256,256]{2,1,0:T(8,128)(2,1)S(1)} %get-tuple-element.66), channel_id=1, source_target_pairs={{0,1},{1,0},{2,3},{3,2},{4,8},{5,9},{6,10},{7,11},{8,4},{9,5},{10,... | collective-permute-start | bytes 786440 | tf_op jit(solution)/shard_map/ppermute | solution.py:333
  20.7 7.5 %collective-permute-start.9 = (bf16[32,16,256]{2,1,0:T(8,128)(2,1)S(1)}, bf16[32,16,256]{2,1,0:T(8,128)(2,1)S(1)}, u32[]{:S(2)}, u32[]{:S(2)}) collective-permute-start(bf16[32,16,256]{2,1,0:T(8,128)(2,1)S(1)} %get-tuple-element.78), channel_id=1, source_target_pairs={{0,40},{4,252},{8,32},{12,244},{16,56},{20,236},{24,48},{28,228},{... | collective-permute-start | bytes 786440 | tf_op jit(solution)/shard_map/ppermute | solution.py:333
  22.2 8.7 %collective-permute-start.10 = (bf16[32,16,256]{2,1,0:T(8,128)(2,1)S(1)}, bf16[32,16,256]{2,1,0:T(8,128)(2,1)S(1)}, u32[]{:S(2)}, u32[]{:S(2)}) collective-permute-start(bf16[32,16,256]{2,1,0:T(8,128)(2,1)S(1)} %get-tuple-element.79), channel_id=1, source_target_pairs={{0,8},{4,28},{8,0},{12,20},{16,24},{20,12},{24,16},{28,4},{32,40},... | collective-permute-start | bytes 786440 | tf_op jit(solution)/shard_map/ppermute | solution.py:333
  24.2 6.7 %collective-permute-start.11 = (bf16[32,16,256]{2,1,0:T(8,128)(2,1)S(1)}, bf16[32,16,256]{2,1,0:T(8,128)(2,1)S(1)}, u32[]{:S(2)}, u32[]{:S(2)}) collective-permute-start(bf16[32,16,256]{2,1,0:T(8,128)(2,1)S(1)} %get-tuple-element.80), channel_id=1, source_target_pairs={{0,32},{4,228},{8,40},{12,236},{16,48},{20,244},{24,56},{28,252},{... | collective-permute-start | bytes 786440 | tf_op jit(solution)/shard_map/ppermute | solution.py:333
  25.0 17.2 %collective-permute-start.7 = (bf16[4,256,256]{2,1,0:T(8,128)(2,1)S(1)}, bf16[4,256,256]{2,1,0:T(8,128)(2,1)S(1)}, u32[]{:S(2)}, u32[]{:S(2)}) collective-permute-start(bf16[4,256,256]{2,1,0:T(8,128)(2,1)S(1)} %get-tuple-element.69), channel_id=1, source_target_pairs={{0,1},{1,0},{2,3},{3,2},{4,7},{5,6},{6,5},{7,4},{8,9},{9,8},{10,11... | collective-permute-start | bytes 1572872 | tf_op jit(solution)/shard_map/ppermute | solution.py:333
  31.0 11.8 %collective-permute-start.12 = (bf16[8,16,256]{2,1,0:T(8,128)(2,1)S(1)}, bf16[8,16,256]{2,1,0:T(8,128)(2,1)S(1)}, u32[]{:S(2)}, u32[]{:S(2)}) collective-permute-start(bf16[8,16,256]{2,1,0:T(8,128)(2,1)S(1)} %get-tuple-element.82), channel_id=1, source_target_pairs={{0,248},{4,44},{8,240},{12,36},{16,232},{20,60},{24,224},{28,52},{... | collective-permute-start | bytes 196616 | tf_op jit(solution)/shard_map/ppermute | solution.py:333
  37.5 6.9 %collective-permute-start.13 = (bf16[8,16,256]{2,1,0:T(8,128)(2,1)S(1)}, bf16[8,16,256]{2,1,0:T(8,128)(2,1)S(1)}, u32[]{:S(2)}, u32[]{:S(2)}) collective-permute-start(bf16[8,16,256]{2,1,0:T(8,128)(2,1)S(1)} %get-tuple-element.83), channel_id=1, source_target_pairs={{0,24},{4,12},{8,16},{12,4},{16,8},{20,28},{24,0},{28,20},{32,56},... | collective-permute-start | bytes 196616 | tf_op jit(solution)/shard_map/ppermute | solution.py:333
  42.2 5.5 %collective-permute-start.14 = (bf16[8,16,256]{2,1,0:T(8,128)(2,1)S(1)}, bf16[8,16,256]{2,1,0:T(8,128)(2,1)S(1)}, u32[]{:S(2)}, u32[]{:S(2)}) collective-permute-start(bf16[8,16,256]{2,1,0:T(8,128)(2,1)S(1)} %get-tuple-element.84), channel_id=1, source_target_pairs={{0,224},{4,36},{8,232},{12,44},{16,240},{20,52},{24,248},{28,60},{... | collective-permute-start | bytes 196616 | tf_op jit(solution)/shard_map/ppermute | solution.py:333
  42.3 7.7 %collective-permute-start.8 = (bf16[2,256,256]{2,1,0:T(8,128)(2,1)S(1)}, bf16[2,256,256]{2,1,0:T(8,128)(2,1)S(1)}, u32[]{:S(2)}, u32[]{:S(2)}) collective-permute-start(bf16[2,256,256]{2,1,0:T(8,128)(2,1)S(1)} %get-tuple-element.71), channel_id=1, source_target_pairs={{0,3},{1,2},{2,1},{3,0},{4,5},{5,4},{6,7},{7,6},{8,11},{9,10},{10,... | collective-permute-start | bytes 786440 | tf_op jit(solution)/shard_map/ppermute | solution.py:333
  47.7 5.8 %collective-permute-start.15 = (bf16[4,16,256]{2,1,0:T(8,128)(2,1)S(1)}, bf16[4,16,256]{2,1,0:T(8,128)(2,1)S(1)}, u32[]{:S(2)}, u32[]{:S(2)}) collective-permute-start(bf16[4,16,256]{2,1,0:T(8,128)(2,1)S(1)} %get-tuple-element.86), channel_id=1, source_target_pairs={{0,96},{4,164},{8,104},{12,172},{16,112},{20,180},{24,120},{28,188... | collective-permute-start | bytes 98312 | tf_op jit(solution)/shard_map/ppermute | solution.py:333
